TPU v7x, 32 devices: a whole 2x2x4 slice. The times are simulated.
32 devices in a mesh: dp: 8 (over z, core), seq: 4 (over y, x).
Axes of the slice: x: 2, y: 2, z: 4, core: 2. Of those that a mesh axis runs over, the one named last changes fastest.
Arguments:
- hidden_in: bfloat16 [8, 1024, 2048], P('dp', 'seq'), may hold values from -6 to 6
- out_grads: bfloat16 [4, 8, 1024, 2048], P(None, 'dp', 'seq'), may hold values from -6 to 6
- w_in: float32 [2048, 8512], P(('dp', 'seq')), may hold values from -0.125 to 0.125
- w_in_m: float32 [2048, 8512], P(('dp', 'seq')), may hold values from -0.0012207031 to 0.0012207031
- w_in_v: float32 [2048, 8512], P(('dp', 'seq')), may hold values from 3.872789e-08 to 1.5491156e-07
- w_out: float32 [4096, 2048], P(('dp', 'seq')), may hold values from -0.1875 to 0.1875
- w_out_m: float32 [4096, 2048], P(('dp', 'seq')), may hold values from -0.0012207031 to 0.0012207031
- w_out_v: float32 [4096, 2048], P(('dp', 'seq')), may hold values from 3.872789e-08 to 1.5491156e-07
- chan_params: float32 [27904], P(('dp', 'seq')), may hold values from -1 to 6.5
- chan_m: float32 [27904], P(('dp', 'seq')), may hold values from -0.0034179688 to 0.0034179688
- chan_v: float32 [27904], P(('dp', 'seq')), may hold values from 3.4855103e-07 to 1.3942041e-06
- head_params: float32 [3, 64], replicated, may hold values from -7 to 1.5
- head_m: float32 [3, 64], replicated, may hold values from -0.009765625 to 0.009765625
- head_v: float32 [3, 64], replicated, may hold values from 2.478585e-06 to 9.91434e-06
Outputs:
- block_out: bfloat16 [4, 8, 1024, 2048], P(None, 'dp', 'seq')
- hidden_grad: float32 [8, 1024, 2048], P('dp', 'seq')
- grad_norm: float32 [], replicated
- w_in_new: float32 [2048, 8512], P(('dp', 'seq'))
- w_in_m_new: float32 [2048, 8512], P(('dp', 'seq'))
- w_in_v_new: float32 [2048, 8512], P(('dp', 'seq'))
- w_in_copy: bfloat16 [2048, 8512], P(('dp', 'seq'))
- w_out_new: float32 [4096, 2048], P(('dp', 'seq'))
- w_out_m_new: float32 [4096, 2048], P(('dp', 'seq'))
- w_out_v_new: float32 [4096, 2048], P(('dp', 'seq'))
- w_out_copy: bfloat16 [4096, 2048], P(('dp', 'seq'))
- chan_new: float32 [27904], P(('dp', 'seq'))
- chan_m_new: float32 [27904], P(('dp', 'seq'))
- chan_v_new: float32 [27904], P(('dp', 'seq'))
- head_new: float32 [3, 64], replicated
- head_m_new: float32 [3, 64], replicated
- head_v_new: float32 [3, 64], replicated
All inputs are finite; a program needn't handle non-finite values.
Results may differ from a plain program's by a relative error of at most 0.012.
The roundings to bfloat16 on the way count: a program that leaves them out, or rounds other values in their place, can miss the bound.
Values may be sent and summed in bfloat16 or wider, within the bound.
A program may use at most 320 MiB of HBM per device.

v0:
```python
import jax
import jax.numpy as jnp
from jax import lax
from jax.sharding import PartitionSpec as P

D = 2048
INNER = 4096
H = 64
P_SIZE = 64
N = 128
TAPS = 4
STEP = 10
E_IN = 8512
CONV_CH = 4352


EXACT = lax.Precision.HIGHEST
EPS_IN = 1e-06
EPS_OUT = 1e-05
ADAM_EPS = 1e-08
BETA = 0.5
CLIP = 1.0


def from_behind(shard, axis, by):
    devices = lax.axis_size(axis)
    pairs = [(i, i + by) for i in range(devices) if 0 <= i + by < devices]
    return lax.ppermute(shard, axis, pairs)


def entering_2(shard, axis, combine, identity, reverse):
    devices, position = (lax.axis_size(axis), lax.axis_index(axis))
    everything = jax.tree.map(lambda part: lax.all_gather(part, axis), shard)
    start = jax.tree.map(
        lambda part, zero: jnp.broadcast_to(jnp.asarray(zero, part.dtype), part.shape),
        shard,
        identity,
    )

    def step(k, before):
        at = devices - 1 - k if reverse else k
        reached = at > position if reverse else at < position
        new = combine(before, jax.tree.map(lambda part: part[at], everything))
        return jax.tree.map(lambda a, b: jnp.where(reached, a, b), new, before)

    return lax.fori_loop(0, devices, step, start)


def unpack(chan_vec):
    conv_taps = chan_vec[: TAPS * CONV_CH].reshape(TAPS, CONV_CH)
    offset = TAPS * CONV_CH
    conv_bias = chan_vec[offset : offset + CONV_CH]
    offset = offset + CONV_CH
    gain_in = chan_vec[offset : offset + D]
    gain_out = chan_vec[offset + D : offset + D + INNER]
    return (conv_taps, conv_bias, gain_in, gain_out)


def in_norm(tokens, gain_in):
    square = jnp.mean(tokens * tokens, axis=-1, keepdims=True)
    return tokens * lax.rsqrt(square + EPS_IN) * gain_in


def prepare(conv_in, previous, conv_taps, conv_bias, rate_in, rate_bias, rate_log):
    row_count = conv_in.shape[1]
    padded = jnp.concatenate([previous, conv_in], axis=1)
    conv_out = conv_bias
    for tap_index in range(TAPS):
        conv_out = conv_out + conv_taps[tap_index] * padded[:, tap_index : tap_index + row_count]
    activated = jax.nn.silu(conv_out)
    head_in = activated[..., :INNER].reshape(activated.shape[0], row_count, H, P_SIZE)
    state_in = activated[..., INNER : INNER + N]
    state_out = activated[..., INNER + N :]
    step_size = jax.nn.softplus(rate_in + rate_bias)
    log_decay = jnp.cumsum(-step_size * jnp.exp(rate_log), axis=1)
    return (head_in, state_in, state_out, step_size, log_decay)


def tail_state(head_in, state_in, step_size, log_decay):
    end_decay = log_decay[:, -1]
    tail_weight = jnp.exp(end_decay[:, None, :] - log_decay) * step_size
    fresh_state = jnp.einsum("sjh,sjhp,sjn->shpn", tail_weight, head_in, state_in, precision=EXACT)
    return (jnp.exp(end_decay), fresh_state)


def mix_heads(head_in, state_in, state_out, step_size, log_decay, skip_gain, entering):
    row_count = head_in.shape[1]
    places = jnp.arange(row_count)
    causal = (places[:, None] >= places[None, :])[None, None]
    decay_heads = jnp.swapaxes(log_decay, 1, 2)
    spread = decay_heads[:, :, :, None] - decay_heads[:, :, None, :]
    decay_mat = jnp.where(causal, jnp.exp(jnp.where(causal, spread, 0.0)), 0.0)
    scores = jnp.einsum("sin,sjn->sij", state_out, state_in, precision=EXACT)
    mixing = decay_mat * scores[:, None] * jnp.swapaxes(step_size, 1, 2)[:, :, None, :]
    inner_part = jnp.einsum("shij,sjhp->sihp", mixing, head_in, precision=EXACT)
    carried = jnp.exp(log_decay)[..., None] * jnp.einsum(
        "shpn,sin->sihp", entering, state_out, precision=EXACT
    )
    result = inner_part + carried + skip_gain[None, None, :, None] * head_in
    return result.reshape(result.shape[0], row_count, INNER)


def gate_norms(mixed_out, gate_in, gain_out):
    gate_act = jax.nn.silu(gate_in)
    outputs = []
    for width_level in range(4):
        span_width = INNER * 2**width_level // 8
        gated_rows = mixed_out[:, :span_width] * gate_act[:, :span_width]
        outputs.append(
            gated_rows
            * lax.rsqrt(jnp.mean(gated_rows * gated_rows, axis=-1, keepdims=True) + EPS_OUT)
            * gain_out[:span_width]
        )
    return tuple(outputs)


def chain_combine(earlier, later):
    return (earlier[0] * later[0], later[0][:, :, None, None] * earlier[1] + later[1])


def adam_step(weight, gradient, moment, second, step_rate, weight_decay):
    new_moment = BETA * moment + (1.0 - BETA) * gradient
    new_second = BETA * second + (1.0 - BETA) * gradient * gradient
    correction = 1.0 - BETA**STEP
    update = new_moment / correction / (jnp.sqrt(new_second / correction) + ADAM_EPS)
    return (weight - step_rate * (update + weight_decay * weight), new_moment, new_second)


def on_device(
    hidden_in,
    out_grads,
    w_in,
    w_in_m,
    w_in_v,
    w_out,
    w_out_m,
    w_out_v,
    chan_params,
    chan_m,
    chan_v,
    head_params,
    head_m,
    head_v,
):
    seq_count, row_count, model_width = hidden_in.shape
    in_low = w_in.astype(jnp.bfloat16)
    out_low = w_out.astype(jnp.bfloat16)
    full_in, full_out, chan_full = (
        lax.all_gather(in_low, ("dp", "seq"), axis=0, tiled=True),
        lax.all_gather(out_low, ("dp", "seq"), axis=0, tiled=True),
        lax.all_gather(chan_params.astype(jnp.bfloat16), ("dp", "seq"), axis=0, tiled=True),
    )
    conv_taps, conv_bias, gain_in, gain_out = unpack(chan_full.astype(jnp.float32))
    tokens = hidden_in.astype(jnp.float32).reshape(seq_count * row_count, model_width)
    normed_exact, norm_pull = jax.vjp(in_norm, tokens, gain_in)
    normed = normed_exact.astype(jnp.bfloat16)
    projected = jnp.dot(normed, full_in, preferred_element_type=jnp.float32).reshape(
        seq_count, row_count, E_IN
    )
    gate_in = projected[..., :INNER]
    conv_in = projected[..., INNER : INNER + CONV_CH]
    rate_in = projected[..., INNER + CONV_CH :]
    previous = from_behind(conv_in[:, row_count - TAPS + 1 :], "seq", 1)
    prepared, prepare_pull = jax.vjp(
        prepare, conv_in, previous, conv_taps, conv_bias, rate_in, head_params[0], head_params[1]
    )
    head_in, state_in, state_out, step_size, log_decay = prepared
    (ends_exp, fresh_state), tail_pull = jax.vjp(
        tail_state, head_in, state_in, step_size, log_decay
    )
    scanned = entering_2(
        (ends_exp, fresh_state),
        "seq",
        chain_combine,
        (jnp.ones_like(ends_exp), jnp.zeros_like(fresh_state)),
        False,
    )
    entering = scanned[1]
    mixed_out, mix_pull = jax.vjp(
        mix_heads, head_in, state_in, state_out, step_size, log_decay, head_params[2], entering
    )
    flat_mixed = mixed_out.reshape(seq_count * row_count, INNER)
    flat_gate = gate_in.reshape(seq_count * row_count, INNER)
    scaled, gate_pull = jax.vjp(gate_norms, flat_mixed, flat_gate, gain_out)
    scaled_low = tuple((scaled_piece.astype(jnp.bfloat16) for scaled_piece in scaled))
    branch_out = []
    for width_level in range(4):
        span_width = INNER * 2**width_level // 8
        branch = jnp.dot(
            scaled_low[width_level], full_out[:span_width], preferred_element_type=jnp.float32
        )
        branch_out.append((tokens + branch).astype(jnp.bfloat16))
    block_out = jnp.stack(branch_out).reshape(4, seq_count, row_count, model_width)
    back_in, back_out = (
        lax.all_gather(in_low, ("dp", "seq"), axis=0, tiled=True),
        lax.all_gather(out_low, ("dp", "seq"), axis=0, tiled=True),
    )
    cotangent = out_grads.reshape(4, seq_count * row_count, model_width)
    scaled_grads = []
    out_grad = jnp.zeros((INNER, model_width), jnp.float32)
    for width_level in range(4):
        span_width = INNER * 2**width_level // 8
        scaled_grads.append(
            jnp.einsum(
                "td,kd->tk",
                cotangent[width_level],
                back_out[:span_width],
                preferred_element_type=jnp.float32,
            )
        )
        out_grad = out_grad.at[:span_width].add(
            jnp.einsum(
                "tk,td->kd",
                scaled_low[width_level],
                cotangent[width_level],
                preferred_element_type=jnp.float32,
            )
        )
    mixed_grad, gate_grad, gain_out_grad = gate_pull(tuple(scaled_grads))
    mix_grads = mix_pull(mixed_grad.reshape(seq_count, row_count, INNER))
    reverse = entering_2(
        (ends_exp, mix_grads[6]),
        "seq",
        chain_combine,
        (jnp.ones_like(ends_exp), jnp.zeros_like(fresh_state)),
        True,
    )
    later_grad = reverse[1]
    ends_grad = jnp.sum(later_grad * entering, axis=(2, 3))
    tail_grads = tail_pull((ends_grad, later_grad))
    prep_grads = prepare_pull(
        (
            mix_grads[0] + tail_grads[0],
            mix_grads[1] + tail_grads[1],
            mix_grads[2],
            mix_grads[3] + tail_grads[2],
            mix_grads[4] + tail_grads[3],
        )
    )
    returned = from_behind(prep_grads[1].astype(jnp.bfloat16), "seq", -1).astype(jnp.float32)
    conv_grad = jnp.concatenate(
        [
            prep_grads[0][:, : row_count - TAPS + 1],
            prep_grads[0][:, row_count - TAPS + 1 :] + returned,
        ],
        axis=1,
    )
    proj_grad = jnp.concatenate(
        [gate_grad.reshape(seq_count, row_count, INNER), conv_grad, prep_grads[4]], axis=-1
    )
    proj_grad = proj_grad.reshape(seq_count * row_count, E_IN).astype(jnp.bfloat16)
    group_normed = lax.all_gather(normed, "seq", axis=0, tiled=True)
    group_cols = lax.all_to_all(proj_grad, "seq", split_axis=1, concat_axis=0, tiled=True)
    in_term = jnp.einsum("td,te->de", group_normed, group_cols, preferred_element_type=jnp.float32)
    in_rows = lax.psum_scatter(in_term, "dp", scatter_dimension=0, tiled=True)
    in_part = lax.all_to_all(in_rows, "seq", split_axis=0, concat_axis=1, tiled=True)
    normed_grad = jnp.einsum("te,de->td", proj_grad, back_in, preferred_element_type=jnp.float32)
    token_grad, gain_in_grad = norm_pull(normed_grad)
    hidden_grad = (token_grad + jnp.sum(cotangent.astype(jnp.float32), axis=0)).reshape(
        seq_count, row_count, model_width
    )
    chan_grad = jnp.concatenate(
        [prep_grads[2].reshape(-1), prep_grads[3], gain_in_grad, gain_out_grad]
    )
    head_grad = jnp.stack([prep_grads[5], prep_grads[6], mix_grads[5]])
    out_part, chan_part = (
        lax.psum_scatter(out_grad, ("dp", "seq"), scatter_dimension=0, tiled=True),
        lax.psum_scatter(chan_grad, ("dp", "seq"), scatter_dimension=0, tiled=True),
    )
    local_squares = (
        jnp.sum(in_part * in_part) + jnp.sum(out_part * out_part) + jnp.sum(chan_part * chan_part)
    )
    total_squares, head_total = lax.psum((local_squares, head_grad), ("dp", "seq"))
    grad_norm = jnp.sqrt(total_squares + jnp.sum(head_total * head_total))
    clip_factor = jnp.minimum(1.0, CLIP / grad_norm)
    w_in_new, w_in_m_new, w_in_v_new = adam_step(
        w_in, clip_factor * in_part, w_in_m, w_in_v, 0.02, 0.1
    )
    w_out_new, w_out_m_new, w_out_v_new = adam_step(
        w_out, clip_factor * out_part, w_out_m, w_out_v, 0.03, 0.1
    )
    chan_new, chan_m_new, chan_v_new = adam_step(
        chan_params, clip_factor * chan_part, chan_m, chan_v, 0.2, 0.0
    )
    head_new, head_m_new, head_v_new = adam_step(
        head_params, clip_factor * head_total, head_m, head_v, 1.0, 0.0
    )
    return (
        block_out,
        hidden_grad,
        grad_norm,
        w_in_new,
        w_in_m_new,
        w_in_v_new,
        w_in_new.astype(jnp.bfloat16),
        w_out_new,
        w_out_m_new,
        w_out_v_new,
        w_out_new.astype(jnp.bfloat16),
        chan_new,
        chan_m_new,
        chan_v_new,
        head_new,
        head_m_new,
        head_v_new,
    )


def solution(mesh):
    in_specs = (
        P("dp", "seq", None),
        P(None, "dp", "seq", None),
        P(("dp", "seq"), None),
        P(("dp", "seq"), None),
        P(("dp", "seq"), None),
        P(("dp", "seq"), None),
        P(("dp", "seq"), None),
        P(("dp", "seq"), None),
        P(("dp", "seq")),
        P(("dp", "seq")),
        P(("dp", "seq")),
        P(),
        P(),
        P(),
    )
    out_specs = (
        P(None, "dp", "seq", None),
        P("dp", "seq", None),
        P(),
        P(("dp", "seq"), None),
        P(("dp", "seq"), None),
        P(("dp", "seq"), None),
        P(("dp", "seq"), None),
        P(("dp", "seq"), None),
        P(("dp", "seq"), None),
        P(("dp", "seq"), None),
        P(("dp", "seq"), None),
        P(("dp", "seq")),
        P(("dp", "seq")),
        P(("dp", "seq")),
        P(),
        P(),
        P(),
    )
    return jax.shard_map(
        on_device, mesh=mesh, in_specs=in_specs, out_specs=out_specs, check_vma=False
    )
```

profile of v0, /device:TPU:1, one launch (start us, length us, event | category | flops | bytes accessed | tf_op | source)
XLA Modules:
  0.0 1915.4 jit_solution(9121491327295784997)
XLA Ops:
  10.4 43.7 %all-reduce.22 = bf16[27904]{0:T(1024)(128)(2,1)S(1)} all-reduce(bf16[27904]{0:T(1024)(128)(2,1)S(1)} %dynamic-update-slice.11), channel_id=1, replica_groups=mesh['dp'=8,'seq'=4] {'dp','seq'}, use_global_device_ids=true, to_apply=%add.22 | all-reduce | flops 27904 | bytes 111616
  54.9 162.5 %all-gather.8.cloned.1.call-done = bf16[2048,8512]{1,0:T(8,128)(2,1)} async-done(((bf16[64,8512]{1,0:T(8,128)(2,1)}), bf16[2048,8512]{1,0:T(8,128)(2,1)}) %all-gather.8.cloned.1.call-update) | async-done | bytes 34865168 | tf_op jit(solution)/shard_map/all_gather | solution.py:149
  217.4 17.8 convolution_bitcast_fusion
  243.3 4.6 slice.281
  248.0 9.6 fusion.34
  262.2 5.6 copy.263
  267.8 7.0 fusion.50
  276.0 4.7 slice.296
  280.7 6.1 copy.277
  289.5 5.6 copy.279
  295.1 7.1 all_gather.34
  303.6 57.1 %all-gather.14.cloned.1.call-done = f32[256,64,128]{2,1,0:T(8,128)} async-done(((f32[64,64,128]{2,1,0:T(8,128)}), f32[256,64,128]{2,1,0:T(8,128)}) %all-gather.14.cloned.1.call-update) | async-done | bytes 8388624 | tf_op jit(solution)/shard_map/all_gather | solution.py:33
  360.7 8.5 while.35
  369.2 4.5 fusion.94
  373.8 23.6 %multiply_reduce_fusion.9 = (f32[256]{0:T(256)S(1)}, f32[1,256,64,64]{1,3,2,0:T(8,128)}, f32[1,256,64,64]{1,3,2,0:T(8,128)}) fusion(f32[1,256,64,64]{1,3,2,0:T(8,128)} %bitcast.367, f32[1,256,64,64]{1,3,2,0:T(8,128)S(1)} %bitcast.351, f32[64]{0:T(128)S(1)} %get-tuple-element.652, f32[256,64,64]{0,2,1:T(8,128)S(1)} %fusion.94, f32[256,64]{0,1:T(8,128)S(1)} %copy.269, ...), kind=kOutput, calls=%fused_computation.96 | convolution fusion | flops 3253731072 | bytes 25691392 | tf_op jit(solution)/shard_map/jvp(shij,sjhp->sihp)/dot_general | solution.py:95
  397.4 5.7 copy.273
  403.1 76.4 %all-gather.10.cloned.1.call-done = bf16[4096,2048]{1,0:T(8,128)(2,1)} async-done(((bf16[128,2048]{1,0:T(8,128)(2,1)}), bf16[4096,2048]{1,0:T(8,128)(2,1)}) %all-gather.10.cloned.1.call-update) | async-done | bytes 16777232 | tf_op jit(solution)/shard_map/all_gather | solution.py:150
  479.5 14.9 multiply_reduce_fusion.6
  501.9 3.3 multiply_reduce_fusion.19
  505.2 4.4 multiply_reduce_fusion.15
  509.7 8.2 multiply_reduce_fusion.11
  519.4 4.6 slice_multiply_fusion.2
  525.9 5.1 fusion.42
  535.6 5.6 copy.280
  541.2 6.9 fusion.146
  548.8 5.8 copy.281
  554.6 9.6 fusion.103
  564.2 3.3 multiply_reduce_fusion.7
  568.3 29.1 %fusion.11 = (f32[64,256]{1,0:T(8,128)}, f32[64,256]{1,0:T(8,128)}, f32[64,256]{1,0:T(8,128)}, f32[256,256]{1,0:T(8,128)S(1)}) fusion(f32[64,256]{1,0:T(8,128)S(1)} %copy.267, f32[256,256]{1,0:T(8,128)} %copy-done.48, f32[64,256]{1,0:T(8,128)S(1)} %bitcast_add_fusion.8, pred[256,256]{1,0:T(8,128)(4,1)} %copy-done.71, f32[64,64,256]{2,1,0:T(8,128)} %bitcast.358, ...), kind=kOutput, calls=%fused_computation.21 | convolution fusion | flops 3284025344 | bytes 9306112 | tf_op jit(solution)/shard_map/transpose(jvp(shij,sjhp->sihp))/dot_general | solution.py:95
  605.7 9.3 fusion.39
  614.9 18.7 all-gather.16.cloned.1.call-done
  633.6 18.0 while.36
  638.2 3.9 fusion.207
  642.7 4.4 fusion.207
  647.7 3.9 fusion.207
  651.6 8.6 fusion.44
  666.0 19.2 %fusion.40 = f32[1,256,64,64]{1,3,2,0:T(8,128)} fusion(f32[64,64,256]{2,1,0:T(8,128)} %get-tuple-element.661, f32[1,256,64,64]{1,3,2,0:T(8,128)} %bitcast.360, f32[64,64,256]{2,1,0:T(8,128)} %bitcast.359, f32[64,256]{1,0:T(8,128)S(1)} %copy-done.68, f32[256,256]{1,0:T(8,128)S(1)} %copy-done.49, f32[64,256]{1,0:T(8,128)S(1)} %copy-done.70, ...), kind=kOutput, calls=%fused_computation.75 | convolution fusion | flops 3246391296 | bytes 17301760 | tf_op jit(solution)/shard_map/transpose(jvp(shij,sjhp->sihp))/dot_general | solution.py:95
  685.2 5.8 copy.284
  691.0 8.8 fusion.111
  699.9 10.8 multiply_reduce_fusion.5
  710.7 5.1 broadcast_multiply_fusion
  715.8 8.4 pad_add_fusion
  732.1 4.6 maximum_convert_fusion
  736.6 6.5 copy.292
  743.1 56.1 %all_to_all.29 = bf16[256,4,2128]{0,2,1:T(8,128)(2,1)} all-to-all(bf16[256,4,2128]{0,2,1:T(8,128)(2,1)} %bitcast.357), channel_id=1, replica_groups=mesh['dp'=8,'seq'=4] {'seq'}, dimensions={1} | all-to-all | bytes 8716288 | tf_op jit(solution)/shard_map/all_to_all | solution.py:253
  799.3 6.5 copy.293
  805.8 15.8 fusion.187
  824.7 12.6 scatter-add.10
  840.7 4.7 fusion.13
  845.4 10.9 fusion.2
  856.5 17.6 fusion.84
  874.9 25.6 %convolution_add_fusion = f32[4096,2048]{1,0:T(8,128)} fusion(f32[4096,2048]{1,0:T(8,128)} %fusion.2, bf16[256,4096]{0,1:T(8,128)(2,1)} %bitcast.364, bf16[4,1,256,2048]{3,2,1,0:T(8,128)(2,1)} %param.29), kind=kOutput, calls=%fused_computation.17 | convolution fusion | flops 4303355904 | bytes 70254592 | tf_op jit(solution)/shard_map/tk,td->kd/dot_general | solution.py:212
  900.6 4.5 convert_reduce_fusion
  905.3 4.0 fusion.77
  909.2 4.8 fusion.74
  914.0 9.5 fusion.70
  923.6 71.0 %reduce-scatter.3.cloned.1.call-done = f32[256,2128]{0,1:T(8,128)} async-done(((f32[2048,2128]{0,1:T(8,128)}), f32[256,2128]{0,1:T(8,128)}) %reduce-scatter.3.cloned.1.call-update) | async-done | bytes 2179088 | tf_op jit(solution)/shard_map/reduce_scatter | solution.py:255
  997.6 4.5 all-to-all-start.1
  1002.2 5.9 fusion.71
  1010.5 120.0 %all-reduce.27.cloned.1.call-done = f32[27904]{0:T(1024)} async-done(((f32[27904]{0:T(1024)}), f32[27904]{0:T(1024)}) %all-reduce.27.cloned.1.call-update) | async-done | bytes 111632
  1134.7 704.3 %reduce-scatter.5.cloned.1.call-done = f32[128,2048]{1,0:T(8,128)} async-done(((f32[4096,2048]{1,0:T(8,128)}), f32[128,2048]{1,0:T(8,128)}) %reduce-scatter.5.cloned.1.call-update) | async-done | bytes 1048592 | tf_op jit(solution)/shard_map/reduce_scatter | solution.py:267
  1843.1 3.5 fusion.86
  1846.5 40.5 %all-reduce.24 = (f32[]{:T(128)}, f32[3,64]{1,0:T(4,128)S(1)}) all-reduce(f32[]{:T(128)S(6)} %add.393, f32[3,64]{1,0:T(4,128)S(1)} %pad_maximum_fusion.2), channel_id=1, replica_groups=mesh['dp'=8,'seq'=4] {'dp','seq'}, use_global_device_ids=true, to_apply=%region_42.43 | all-reduce | flops 193 | bytes 1544 | tf_op jit(solution)/shard_map/psum | solution.py:273
  1895.1 8.1 fusion.179
  (363 shorter events, 103.9 us)
Async XLA Ops:
  7.2 46.9 %copy-start.20 = (bf16[1,256,2048]{2,1,0:T(8,128)(2,1)S(1)}, bf16[1,256,2048]{2,1,0:T(8,128)(2,1)}, u32[]{:S(2)}) copy-start(bf16[1,256,2048]{2,1,0:T(8,128)(2,1)} %param.28) | copy-start | bytes 3145732
  7.2 47.2 %copy-start.96 = (f32[3,64]{1,0:T(4,128)S(1)}, f32[3,64]{1,0:T(4,128)}, u32[]{:S(2)}) copy-start(f32[3,64]{1,0:T(4,128)} %param.39) | copy-start | bytes 2308
  7.2 210.2 %all-gather.8.cloned.1.call-start = ((), (), s32[]{:S(2)}) async-start(), calls=%async_computation.4 | async-start | bytes 36225024 | tf_op jit(solution)/shard_map/all_gather | solution.py:149
  10.1 350.6 %all-gather.14.cloned.1.call-start = ((), (), s32[]{:S(2)}) async-start(), calls=%async_computation.9 | async-start | bytes 10485760 | tf_op jit(solution)/shard_map/all_gather | solution.py:33
  54.4 180.8 %copy-start.90 = (f32[256]{0:T(256)}, f32[256]{0:T(256)S(1)}, u32[]{:S(2)}) copy-start(f32[256]{0:T(256)S(1)} %fusion.87) | copy-start | bytes 3076
  54.5 180.8 %copy-start.88 = (f32[256]{0:T(256)}, f32[256]{0:T(256)S(1)}, u32[]{:S(2)}) copy-start(f32[256]{0:T(256)S(1)} %fusion.165) | copy-start | bytes 3076
  54.5 181.7 %copy-start.98 = (f32[64]{0:T(128)}, f32[64]{0:T(128)S(1)}, u32[]{:S(2)}) copy-start(f32[64]{0:T(128)S(1)} %get-tuple-element.653) | copy-start | bytes 772
  54.5 187.1 %copy-start.73 = (f32[64]{0:T(128)}, f32[64]{0:T(128)S(1)}, u32[]{:S(2)}) copy-start(f32[64]{0:T(128)S(1)} %get-tuple-element.654) | copy-start | bytes 772
  54.5 319.3 %copy-start.109 = (f32[64]{0:T(128)}, f32[64]{0:T(128)S(1)}, u32[]{:S(2)}) copy-start(f32[64]{0:T(128)S(1)} %get-tuple-element.652) | copy-start | bytes 772
  54.5 180.7 %copy-start.62 = (f32[2048]{0:T(1024)}, f32[2048]{0:T(1024)S(1)}, u32[]{:S(2)}) copy-start(f32[2048]{0:T(1024)S(1)} %get-tuple-element.646) | copy-start | bytes 24580
  54.5 464.8 %copy-start.50 = (f32[2048]{0:T(1024)}, f32[2048]{0:T(1024)S(1)}, u32[]{:S(2)}) copy-start(f32[2048]{0:T(1024)S(1)} %get-tuple-element.645) | copy-start | bytes 24580
  54.6 193.4 %copy-start.52 = (f32[4352]{0:T(1024)}, f32[4352]{0:T(1024)S(1)}, u32[]{:S(2)}) copy-start(f32[4352]{0:T(1024)S(1)} %get-tuple-element.648) | copy-start | bytes 52228
  54.6 193.4 %copy-start.54 = (f32[4352]{0:T(1024)}, f32[4352]{0:T(1024)S(1)}, u32[]{:S(2)}) copy-start(f32[4352]{0:T(1024)S(1)} %get-tuple-element.649) | copy-start | bytes 52228
  54.6 193.4 %copy-start.56 = (f32[4352]{0:T(1024)}, f32[4352]{0:T(1024)S(1)}, u32[]{:S(2)}) copy-start(f32[4352]{0:T(1024)S(1)} %get-tuple-element.650) | copy-start | bytes 52228
  54.6 193.4 %copy-start.58 = (f32[4352]{0:T(1024)}, f32[4352]{0:T(1024)S(1)}, u32[]{:S(2)}) copy-start(f32[4352]{0:T(1024)S(1)} %get-tuple-element.651) | copy-start | bytes 52228
  54.9 180.3 %copy-start.31 = (bf16[256,2048]{1,0:T(8,128)(2,1)}, bf16[256,2048]{1,0:T(8,128)(2,1)S(1)}, u32[]{:S(2)}) copy-start(bf16[256,2048]{1,0:T(8,128)(2,1)S(1)} %fusion.83) | copy-start | bytes 3145732
  238.2 9.7 collective-permute-start
  247.9 19.9 %copy-start.41 = (f32[256,64]{0,1:T(8,128)}, f32[256,64]{0,1:T(8,128)S(1)}, u32[]{:S(2)}) copy-start(f32[256,64]{0,1:T(8,128)S(1)} %copy.270) | copy-start | bytes 196612
  248.0 9.6 copy-start.39
  274.9 204.6 %all-gather.10.cloned.1.call-start = ((), (), s32[]{:S(2)}) async-start(), calls=%async_computation.5 | async-start | bytes 17301504 | tf_op jit(solution)/shard_map/all_gather | solution.py:150
  275.8 357.8 %all-gather.16.cloned.1.call-start = ((), (), s32[]{:S(2)}) async-start(), calls=%async_computation.10 | async-start | bytes 10485760 | tf_op jit(solution)/shard_map/all_gather | solution.py:33
  275.9 243.1 %copy-start.60 = (f32[1024]{0:T(1024)}, f32[1024]{0:T(1024)S(1)}, u32[]{:S(2)}) copy-start(f32[1024]{0:T(1024)S(1)} %slice.302) | copy-start | bytes 12292
  275.9 242.0 %copy-start.64 = (f32[512]{0:T(512)}, f32[512]{0:T(512)S(1)}, u32[]{:S(2)}) copy-start(f32[512]{0:T(512)S(1)} %slice.298) | copy-start | bytes 6148
  276.0 97.8 %copy-start.71 = (pred[256,256]{1,0:T(8,128)(4,1)}, pred[256,256]{1,0:T(8,128)(4,1)S(1)}, u32[]{:S(2)}) copy-start(pred[256,256]{1,0:T(8,128)(4,1)S(1)} %iota_compare_fusion) | copy-start | bytes 196612
  287.0 281.2 %copy-start.67 = (f32[64,256]{1,0:T(8,128)}, f32[64,256]{1,0:T(8,128)S(1)}, u32[]{:S(2)}) copy-start(f32[64,256]{1,0:T(8,128)S(1)} %copy.267) | copy-start | bytes 196612
  302.2 266.1 %copy-start.69 = (f32[64,256]{1,0:T(8,128)}, f32[64,256]{1,0:T(8,128)S(1)}, u32[]{:S(2)}) copy-start(f32[64,256]{1,0:T(8,128)S(1)} %bitcast_add_fusion.8) | copy-start | bytes 196612
  303.6 70.2 %copy-start.48 = (f32[256,256]{1,0:T(8,128)}, f32[256,256]{1,0:T(8,128)S(1)}, u32[]{:S(2)}) copy-start(f32[256,256]{1,0:T(8,128)S(1)} %fusion.150) | copy-start | bytes 786436
  369.2 28.2 %copy-start.105 = (f32[4,1,64]{2,1,0:T(1,128)}, f32[4,1,64]{2,1,0:T(1,128)S(1)}, u32[]{:S(2)}) copy-start(f32[4,1,64]{2,1,0:T(1,128)S(1)} %get-tuple-element.810) | copy-start | bytes 3076
  373.7 23.7 %copy-start.16 = (f32[256,64,64]{0,2,1:T(8,128)}, f32[256,64,64]{0,2,1:T(8,128)S(1)}, u32[]{:S(2)}) copy-start(f32[256,64,64]{0,2,1:T(8,128)S(1)} %fusion.94) | copy-start | bytes 12582916
  403.1 120.9 %copy-start.83 = (f32[256]{0:T(256)}, f32[256]{0:T(256)S(1)}, u32[]{:S(2)}) copy-start(f32[256]{0:T(256)S(1)} %fusion.169) | copy-start | bytes 3076
  497.8 21.5 %copy-start.6 = (f32[256,2048]{1,0:T(8,128)}, f32[256,2048]{1,0:T(8,128)S(1)}, u32[]{:S(2)}) copy-start(f32[256,2048]{1,0:T(8,128)S(1)} %get-tuple-element.622) | copy-start | bytes 6291460
  500.3 18.7 copy-start.17
  501.8 16.1 copy-start.25
  501.9 17.5 copy-start.76
  501.9 17.1 copy-start.78
  501.9 16.0 copy-start.85
  509.7 8.3 copy-start.19
  548.1 257.6 %all-gather.12.cloned.1.call-start = ((), (), s32[]{:S(2)}) async-start(), calls=%async_computation.6 | async-start | bytes 5242880 | tf_op jit(solution)/shard_map/all_gather | solution.py:252
  548.7 445.9 %reduce-scatter.3.cloned.1.call-start = ((), (), s32[]{:S(2)}) async-start(), calls=%async_computation.7 | async-start | bytes 19611648 | tf_op jit(solution)/shard_map/reduce_scatter | solution.py:255
  554.6 9.6 copy-start.15
  651.6 8.6 copy-start
  691.0 8.8 copy-start.14
  691.0 8.8 copy-start.40
  699.9 10.8 copy-start.53
  699.9 10.8 copy-start.55
  699.9 10.8 copy-start.57
  699.9 10.8 copy-start.59
  725.4 5.7 collective-permute-start.1
  821.6 308.9 %all-reduce.27.cloned.1.call-start = ((), (), s32[]{:S(2)}) async-start(), calls=%async_computation.11 | async-start | bytes 229376
  824.7 12.7 copy-start.80
  824.7 12.7 copy-start.92
  824.7 12.7 copy-start.100
  824.7 12.7 copy-start.104
  824.7 12.7 copy-start.30
  824.7 12.7 copy-start.84
  845.4 11.1 copy-start.63
  845.4 11.1 copy-start.89
  874.9 964.2 %reduce-scatter.5.cloned.1.call-start = ((), (), s32[]{:S(2)}) async-start(), calls=%async_computation.8 | async-start | bytes 34603008 | tf_op jit(solution)/shard_map/reduce_scatter | solution.py:267
  923.6 78.5 %copy-start.22 = (bf16[1,256,2048]{2,1,0:T(8,128)(2,1)S(1)}, bf16[1,256,2048]{2,1,0:T(8,128)(2,1)}, u32[]{:S(2)}) copy-start(bf16[1,256,2048]{2,1,0:T(8,128)(2,1)} %param.28) | copy-start | bytes 3145732
  997.6 134.3 %all-to-all-start.1 = ((f32[4,64,2128]{2,1,0:T(8,128)}), f32[4,64,2128]{2,1,0:T(8,128)}, u32[]{:S(2)}, u32[]{:S(2)}) async-start(f32[4,64,2128]{2,1,0:T(8,128)} %bitcast.365), calls=%async_computation.2 | async-start | bytes 4456448 | tf_op jit(solution)/shard_map/all_to_all | solution.py:256
  1008.2 834.9 %copy-start.24 = (f32[256,2048]{1,0:T(8,128)S(1)}, f32[256,2048]{1,0:T(8,128)}, u32[]{:S(2)}) copy-start(f32[256,2048]{1,0:T(8,128)} %convert_reduce_fusion) | copy-start | bytes 6291460
  1895.1 8.1 copy-start.29
  1895.1 8.1 copy-start.34
  1895.1 8.1 copy-start.35
  (59 other events, 241.8 us)
Sparse Core Ops, SparseCore 0:
  11.5 205.9 all-gather.7
  275.0 85.6 all-gather.13
  364.2 115.2 all-gather.9
  548.2 85.3 all-gather.15
  635.9 52.6 all-gather.11
  821.7 172.8 reduce-scatter.2
  1001.7 128.7 all-reduce.26
  1132.9 706.0 reduce-scatter.4
where the time goes:
time: 1920 us
  waiting for transfers between devices  1210 us (63%)
  matrix products  272 us (14%)
  blocking collectives  147 us (8%)
  other arithmetic  144 us (8%)
  local copies, waits for them, and re-layouts  112 us (6%)
  between operations  20.5 us (1%)
    reduce_scatter x1, waiting for transfers between devices, on_device(): lax.psum_scatter(out_grad, ('dp', 'seq'), scatter_dimension=0, tiled=True)  704 us
    all_gather x1, waiting for transfers between devices, on_device(): lax.all_gather(in_low, ('dp', 'seq'), axis=0, tiled=True)  163 us
    unnamed x9, waiting for transfers between devices  121 us
    all_gather x1, waiting for transfers between devices, on_device(): lax.all_gather(out_low, ('dp', 'seq'), axis=0, tiled=True)  76.4 us
    all_gather x2, waiting for transfers between devices, entering_2(): everything = jax.tree.map(lambda part: lax.all_gather(part, axis), shard)  75.8 us
    dot_general x3, matrix products, mix_heads(): inner_part = jnp.einsum('shij,sjhp->sihp', mixing, head_in, precision=EXACT)  71.9 us
    reduce_scatter x1, waiting for transfers between devices, on_device(): in_rows = lax.psum_scatter(in_term, 'dp', scatter_dimension=0, tiled=True)  71 us
    all_to_all x1, blocking collectives, on_device(): lax.all_to_all(proj_grad, 'seq', split_axis=1, concat_axis=0, tiled=True)  56.1 us
  transfers between devices with their start and end apart: 11, of which 7 were waited for; matrix products, arithmetic and copies ran while one was open for 19% of the time, Pallas kernels for 0%

commit v1 on v0

v1 whole, which is shorter than its diff:
```python
import functools

import jax
import jax.numpy as jnp
from jax import lax
from jax.experimental import pallas as pl
from jax.experimental.pallas import tpu as pltpu
from jax.sharding import PartitionSpec as P

D = 2048
INNER = 4096
H = 64
P_SIZE = 64
N = 128
TAPS = 4
STEP = 10
E_IN = 8512
CONV_CH = 4352
LANES = 128
CHUNK = 128
LEVELS = 4

EXACT = lax.Precision.HIGHEST
EPS_IN = 1e-06
EPS_OUT = 1e-05
ADAM_EPS = 1e-08
BETA = 0.5
CLIP = 1.0
F32 = jnp.float32
BF16 = jnp.bfloat16
MASKED = -1e30


def level_width(level):
    return INNER * 2**level // 8


SEGMENTS = tuple(
    (0 if level == 0 else level_width(level - 1), level_width(level)) for level in range(LEVELS)
)


def dot(a, b, dims=((1,), (0,)), precision=None):
    return lax.dot_general(a, b, (dims, ((), ())), precision=precision, preferred_element_type=F32)


NT = ((1,), (1,))
TN = ((0,), (0,))


def softplus(v):
    return jnp.maximum(v, 0.0) + jnp.log1p(jnp.exp(-jnp.abs(v)))


def two_terms(v):
    high = v.astype(BF16)
    return high, (v - high.astype(F32)).astype(BF16)


def spread_heads(v, spread):
    high, rest = two_terms(v)
    return dot(high, spread) + dot(rest, spread)


def rates(dt_raw, heads):
    step = softplus(dt_raw + heads[0:1, :])
    return step, step * heads[1:2, :]


def triangle(size):
    row = lax.broadcasted_iota(jnp.int32, (size, size), 0)
    col = lax.broadcasted_iota(jnp.int32, (size, size), 1)
    return row, col


def conv_block(taps, xbuf, lanes):
    out = taps[TAPS : TAPS + 1, lanes]
    for tap in range(TAPS):
        out = out + taps[tap : tap + 1, lanes] * xbuf[5 + tap : 5 + tap + CHUNK, lanes]
    return out


def pair_decay(cum, cum_t, causal, head):
    gap = cum[:, head : head + 1] - cum_t[head : head + 1, :]
    return jnp.exp(jnp.where(causal, gap, MASKED))


def scan_forward_kernel(cw, px, taps, heads, skip, spread, y, states, xbuf, state, xdt, carried):
    cc = cw + 2 * N

    @pl.when(pl.program_id(0) == 0)
    def _():
        state[...] = jnp.zeros_like(state)
        xbuf[0:8, :] = jnp.zeros((8, cc), F32)

    xbuf[8 : 8 + CHUNK, :] = px[:, :cc]
    step, rate = rates(px[:, cc:], heads)
    row, col = triangle(CHUNK)
    causal = row >= col
    cum = dot(causal.astype(F32), rate, precision=EXACT)
    cum_t = cum.T
    spread_m = spread[...]
    last = cum[CHUNK - 1 : CHUNK, :]
    step_x = spread_heads(step, spread_m)
    grow_x = spread_heads(jnp.exp(cum), spread_m)
    tail_x = spread_heads(jnp.exp(last - cum), spread_m)

    def activated(lanes):
        conv = conv_block(taps, xbuf, lanes)
        return conv * jax.nn.sigmoid(conv)

    state_in = activated(slice(cw, cw + N))
    state_out = activated(slice(cw + N, cw + 2 * N))
    scores = dot(state_out, state_in, NT, EXACT)
    states[0] = state[...].astype(BF16)
    carried[...] = dot(state_out.astype(BF16), state[...].astype(BF16))
    first = lax.broadcasted_iota(jnp.int32, (1, LANES), 1) < P_SIZE
    for pair in range(cw // LANES):
        lanes = slice(pair * LANES, (pair + 1) * LANES)
        x = activated(lanes)
        xd = (x * step_x[:, lanes]).astype(BF16).astype(F32)
        xdt[:, lanes] = (xd * tail_x[:, lanes]).astype(BF16)
        stacked = jnp.concatenate([jnp.where(first, xd, 0.0), jnp.where(first, 0.0, xd)], axis=0)
        mixing = jnp.concatenate(
            [
                (pair_decay(cum, cum_t, causal, 2 * pair + k) * scores).astype(BF16)
                for k in range(2)
            ],
            axis=1,
        )
        y[:, lanes] = (
            dot(mixing, stacked.astype(BF16))
            + grow_x[:, lanes] * carried[:, lanes]
            + skip[:, lanes] * x
        )
    state[...] = grow_x[CHUNK - 1 : CHUNK, :] * state[...] + dot(
        state_in.astype(BF16), xdt[...], TN
    )
    xbuf[0:8, :] = xbuf[CHUNK : CHUNK + 8, :]


def scan_backward_kernel(
    cw, px, halo, taps, heads, skip, spread, gather, dy, y, states,
    dpx, dtaps, dheads, dskip,
    xbuf, dstate, dcbuf, slope, xact, xd_s, dxd_s, acc_s,
):
    cc = cw + 2 * N
    at = pl.program_id(0)

    @pl.when(at == 0)
    def _():
        dstate[...] = jnp.zeros_like(dstate)
        dcbuf[CHUNK : CHUNK + 8, :] = jnp.zeros((8, cc), F32)
        dtaps[...] = jnp.zeros_like(dtaps)
        dheads[...] = jnp.zeros_like(dheads)
        dskip[...] = jnp.zeros_like(dskip)

    xbuf[0:8, :] = jnp.where(at == pl.num_programs(0) - 1, 0.0, halo[:, :cc])
    xbuf[8 : 8 + CHUNK, :] = px[:, :cc]
    dt_raw = px[:, cc:]
    step, rate = rates(dt_raw, heads)
    row, col = triangle(CHUNK)
    causal = row >= col
    cum = dot(causal.astype(F32), rate, precision=EXACT)
    cum_t = cum.T
    spread_m = spread[...]
    last = cum[CHUNK - 1 : CHUNK, :]
    step_x = spread_heads(step, spread_m)
    grow_x = spread_heads(jnp.exp(cum), spread_m)
    tail_x = spread_heads(jnp.exp(last - cum), spread_m)

    for block in range(cc // LANES):
        lanes = slice(block * LANES, (block + 1) * LANES)
        conv = conv_block(taps, xbuf, lanes)
        sig = jax.nn.sigmoid(conv)
        act = conv * sig
        xact[:, lanes] = act
        slope[:, lanes] = sig + act * (1.0 - sig)
    state_in = xact[:, cw : cw + N]
    state_out = xact[:, cw + N : cc]
    scores = dot(state_out, state_in, NT, EXACT)
    in_low = state_in.astype(BF16)
    out_low = state_out.astype(BF16)
    dstate_low = dstate[...].astype(BF16)
    acc_s[...] = jnp.zeros_like(acc_s)
    dxd_s[...] = tail_x * dot(in_low, dstate_low)
    dskip[0:1, :] += jnp.sum(xact[:, :cw] * dy[...], axis=0, keepdims=True)
    first = lax.broadcasted_iota(jnp.int32, (1, LANES), 1) < P_SIZE
    xd_s[...] = (xact[:, :cw] * step_x).astype(BF16)
    total = jnp.sum(xd_s[...].astype(F32) * dxd_s[...], axis=0, keepdims=True) + grow_x[
        CHUNK - 1 : CHUNK, :
    ] * jnp.sum(dstate[...] * states[0].astype(F32), axis=0, keepdims=True)
    dscores = jnp.zeros((CHUNK, CHUNK), F32)
    for pair in range(cw // LANES):
        lanes = slice(pair * LANES, (pair + 1) * LANES)
        dyp = dy[:, lanes]
        stacked = jnp.concatenate(
            [jnp.where(first, dyp, 0.0), jnp.where(first, 0.0, dyp)], axis=0
        ).astype(BF16)
        decays = [pair_decay(cum, cum_t, causal, 2 * pair + k) for k in range(2)]
        mixing = jnp.concatenate([(decay * scores).astype(BF16) for decay in decays], axis=0)
        dxd_s[:, lanes] += dot(mixing, stacked, TN)
        dmix = dot(stacked, xd_s[:, lanes], NT)
        dscores = dscores + decays[0] * dmix[:CHUNK] + decays[1] * dmix[CHUNK:]
    dy_low = dy[...].astype(BF16)
    dy_f = dy_low.astype(F32)
    xd_f = xd_s[...].astype(F32)
    dxd = dxd_s[...]
    y_scan = y[...] - skip[...] * xact[:, :cw]
    final = lax.broadcasted_iota(jnp.int32, (CHUNK, 1), 0) == CHUNK - 1
    gather_m = gather[...]
    dcum = spread_heads(dy_f * y_scan - xd_f * dxd + jnp.where(final, total, 0.0), gather_m)
    dstep = spread_heads(xact[:, :cw] * dxd, gather_m)
    drate = dot((row <= col).astype(F32), dcum, precision=EXACT)
    dstep = dstep + drate * heads[1:2, :]
    ddt = dstep * jax.nn.sigmoid(dt_raw + heads[0:1, :])
    dheads[0:1, :] += jnp.sum(ddt, axis=0, keepdims=True)
    dheads[1:2, :] += jnp.sum(drate * rate, axis=0, keepdims=True)
    grown = (grow_x * dy_f).astype(BF16)
    dscores_low = dscores.astype(BF16)
    dout = dot(dscores_low, in_low) + dot(grown, states[0], NT)
    din = dot(dscores_low, out_low, TN) + dot((tail_x * xd_f).astype(BF16), dstate_low, NT)
    dstate[...] = grow_x[CHUNK - 1 : CHUNK, :] * dstate[...] + dot(out_low, grown, TN)
    dcbuf[:CHUNK, :cw] = (step_x * dxd + skip[...] * dy[...]) * slope[:, :cw]
    dcbuf[:CHUNK, cw : cw + N] = din * slope[:, cw : cw + N]
    dcbuf[:CHUNK, cw + N :] = dout * slope[:, cw + N :]
    for block in range(cc // LANES):
        lanes = slice(block * LANES, (block + 1) * LANES)
        dconv = dcbuf[:CHUNK, lanes]
        dtaps[TAPS : TAPS + 1, lanes] += jnp.sum(dconv, axis=0, keepdims=True)
        back = taps[TAPS - 1 : TAPS, lanes] * dconv
        for tap in range(TAPS):
            dtaps[tap : tap + 1, lanes] += jnp.sum(
                dconv * xbuf[5 + tap : 5 + tap + CHUNK, lanes], axis=0, keepdims=True
            )
            if tap < TAPS - 1:
                reach = TAPS - 1 - tap
                back = back + taps[tap : tap + 1, lanes] * dcbuf[reach : reach + CHUNK, lanes]
        dpx[:, lanes] = back.astype(BF16)
    dpx[:, cc:] = ddt.astype(BF16)
    dcbuf[CHUNK : CHUNK + 8, :] = dcbuf[0:8, :]


def whole(shape):
    return pl.BlockSpec(shape, lambda i: (0,) * len(shape))


def scan_forward(px, taps, heads, skip, spread):
    length, width = px.shape
    cw = skip.shape[1]
    cc = cw + 2 * N
    chunks = length // CHUNK
    return pl.pallas_call(
        functools.partial(scan_forward_kernel, cw),
        grid=(chunks,),
        in_specs=[
            pl.BlockSpec((CHUNK, width), lambda i: (i, 0)),
            whole(taps.shape),
            whole(heads.shape),
            whole(skip.shape),
            whole(spread.shape),
        ],
        out_specs=[
            pl.BlockSpec((CHUNK, cw), lambda i: (i, 0)),
            pl.BlockSpec((1, N, cw), lambda i: (i, 0, 0)),
        ],
        out_shape=[
            jax.ShapeDtypeStruct((length, cw), F32),
            jax.ShapeDtypeStruct((chunks, N, cw), BF16),
        ],
        scratch_shapes=[
            pltpu.VMEM((CHUNK + 8, cc), F32),
            pltpu.VMEM((N, cw), F32),
            pltpu.VMEM((CHUNK, cw), BF16),
            pltpu.VMEM((CHUNK, cw), F32),
        ],
        compiler_params=pltpu.CompilerParams(vmem_limit_bytes=48 * 2**20),
        name="scan_forward",
    )(px, taps, heads, skip, spread)


def scan_backward(px, taps, heads, skip, spread, gather, dy, y, states):
    length, width = px.shape
    cw = skip.shape[1]
    cc = cw + 2 * N
    chunks = length // CHUNK
    eighths = CHUNK // 8
    return pl.pallas_call(
        functools.partial(scan_backward_kernel, cw),
        grid=(chunks,),
        in_specs=[
            pl.BlockSpec((CHUNK, width), lambda i: (chunks - 1 - i, 0)),
            pl.BlockSpec(
                (8, width), lambda i: (jnp.maximum((chunks - 1 - i) * eighths - 1, 0), 0)
            ),
            whole(taps.shape),
            whole(heads.shape),
            whole(skip.shape),
            whole(spread.shape),
            whole(gather.shape),
            pl.BlockSpec((CHUNK, cw), lambda i: (chunks - 1 - i, 0)),
            pl.BlockSpec((CHUNK, cw), lambda i: (chunks - 1 - i, 0)),
            pl.BlockSpec((1, N, cw), lambda i: (chunks - 1 - i, 0, 0)),
        ],
        out_specs=[
            pl.BlockSpec((CHUNK, width), lambda i: (chunks - 1 - i, 0)),
            whole((8, cc)),
            whole((8, LANES)),
            whole((8, cw)),
        ],
        out_shape=[
            jax.ShapeDtypeStruct((length, width), BF16),
            jax.ShapeDtypeStruct((8, cc), F32),
            jax.ShapeDtypeStruct((8, LANES), F32),
            jax.ShapeDtypeStruct((8, cw), F32),
        ],
        scratch_shapes=[
            pltpu.VMEM((CHUNK + 8, cc), F32),
            pltpu.VMEM((N, cw), F32),
            pltpu.VMEM((CHUNK + 8, cc), F32),
            pltpu.VMEM((CHUNK, cc), F32),
            pltpu.VMEM((CHUNK, cc), F32),
            pltpu.VMEM((CHUNK, cw), BF16),
            pltpu.VMEM((CHUNK, cw), F32),
            pltpu.VMEM((CHUNK, CHUNK), F32),
        ],
        compiler_params=pltpu.CompilerParams(vmem_limit_bytes=48 * 2**20),
        name="scan_backward",
    )(px, px, taps, heads, skip, spread, gather, dy, y, states)


def adam_step(weight, gradient, moment, second, step_rate, weight_decay):
    new_moment = BETA * moment + (1.0 - BETA) * gradient
    new_second = BETA * second + (1.0 - BETA) * gradient * gradient
    correction = 1.0 - BETA**STEP
    update = new_moment / correction / (jnp.sqrt(new_second / correction) + ADAM_EPS)
    return (weight - step_rate * (update + weight_decay * weight), new_moment, new_second)


def all_sum(value, axis):
    size = lax.axis_size(axis)
    by = 1
    while by < size:
        value = value + lax.ppermute(value, axis, [(i, i ^ by) for i in range(size)])
        by *= 2
    return value


def swap_blocks(blocks):
    return lax.all_to_all(blocks, "seq", split_axis=0, concat_axis=0, tiled=True)


def pack_terms(values):
    high = lax.reduce_precision(values, 8, 7)
    packed = jnp.concatenate([high, values - high], axis=-1).astype(BF16)
    return jnp.pad(packed, ((0, 0), (0, LANES - packed.shape[-1])))


def unpack_terms(packed, count):
    packed = packed.astype(F32)
    return packed[..., :count] + packed[..., count : 2 * count]


def on_device(
    hidden_in, out_grads, w_in, w_in_m, w_in_v, w_out, w_out_m, w_out_v,
    chan_params, chan_m, chan_v, head_params, head_m, head_v,
):
    parts = lax.axis_size("seq")
    groups = lax.axis_size("dp")
    q = lax.axis_index("seq")
    rows = hidden_in.shape[1]
    length = rows * parts
    cw = INNER // parts
    hq = H // parts
    cc = cw + 2 * N
    in_rows = w_in.shape[0]
    out_rows = w_out.shape[0]

    in_low = w_in.astype(BF16)
    out_low = w_out.astype(BF16)
    z_blocks = in_low[:, :INNER].reshape(in_rows, parts, cw).transpose(1, 0, 2)
    x_blocks = in_low[:, INNER : 2 * INNER].reshape(in_rows, parts, cw).transpose(1, 0, 2)
    bc_block = jnp.broadcast_to(
        in_low[None, :, 2 * INNER : 2 * INNER + 2 * N], (parts, in_rows, 2 * N)
    )
    dt_blocks = in_low[:, 2 * INNER + 2 * N :].reshape(in_rows, parts, hq).transpose(1, 0, 2)
    dt_blocks = jnp.pad(dt_blocks, ((0, 0), (0, 0), (0, LANES - hq)))
    x_blocks = jnp.concatenate([x_blocks, bc_block, dt_blocks], axis=2)
    wx = lax.all_gather(swap_blocks(x_blocks), "dp", axis=0).reshape(D, cc + LANES)
    hidden = lax.all_gather(hidden_in[0], "seq", axis=0, tiled=True)
    chan_full = lax.all_gather(chan_params.astype(BF16), ("dp", "seq"), axis=0, tiled=True).astype(
        F32
    )
    wz = lax.all_gather(swap_blocks(z_blocks), "dp", axis=0).reshape(D, cw)
    wo = lax.all_gather(out_low, ("dp", "seq"), axis=0, tiled=True)

    conv_taps = chan_full[: TAPS * CONV_CH].reshape(TAPS, CONV_CH)
    conv_bias = chan_full[TAPS * CONV_CH : (TAPS + 1) * CONV_CH].reshape(1, CONV_CH)
    offset = (TAPS + 1) * CONV_CH
    gain_in = chan_full[offset : offset + D]
    gain_out = chan_full[offset + D : offset + D + INNER]
    taps_all = jnp.concatenate(
        [conv_taps, conv_bias, jnp.zeros((8 - TAPS - 1, CONV_CH), F32)], axis=0
    )
    taps = jnp.concatenate(
        [lax.dynamic_slice(taps_all, (0, q * cw), (8, cw)), taps_all[:, INNER:]], axis=1
    )
    own_gain = lax.dynamic_slice(gain_out, (q * cw,), (cw,))
    own_heads = lax.dynamic_slice(head_params, (0, q * hq), (3, hq))
    heads = jnp.pad(
        jnp.stack([own_heads[0], -jnp.exp(own_heads[1])]), ((0, 6), (0, LANES - hq))
    )
    skip = jnp.repeat(own_heads[2], P_SIZE).reshape(1, cw)
    spread = (
        jnp.arange(LANES)[:, None] == (jnp.arange(cw) // P_SIZE)[None, :]
    ).astype(BF16)

    tokens = hidden.astype(F32)
    scale = lax.rsqrt(jnp.mean(tokens * tokens, axis=-1, keepdims=True) + EPS_IN)
    normed = (tokens * scale * gain_in).astype(BF16)
    px = dot(normed, wx)
    y, states = scan_forward(px, taps, heads, skip, spread)
    z = dot(normed, wz)
    sig = jax.nn.sigmoid(z)
    gate = z * sig
    gated = y * gate
    channel = q * cw + jnp.arange(cw)
    squares = jnp.stack(
        [
            jnp.sum(jnp.where((channel >= low) & (channel < high), gated * gated, 0.0), axis=-1)
            for low, high in SEGMENTS
        ],
        axis=-1,
    )
    u_blocks = jnp.concatenate([(gated * own_gain).astype(BF16), pack_terms(squares)], axis=-1)
    u_blocks = swap_blocks(u_blocks.reshape(parts, rows, cw + LANES))
    u = u_blocks[:, :, :cw].transpose(1, 0, 2).reshape(rows, INNER)
    squares = jnp.cumsum(
        jnp.sum(unpack_terms(u_blocks[:, :, cw:], LEVELS), axis=0), axis=-1
    )

    own_tokens = hidden_in[0].astype(F32)
    cotangent = out_grads[:, 0]
    norms = [
        lax.rsqrt(squares[:, k : k + 1] / level_width(k) + EPS_OUT) for k in range(LEVELS)
    ]
    branch = jnp.zeros((rows, D), F32)
    block_out = []
    pulls = []
    for k, (low, high) in enumerate(SEGMENTS):
        branch = branch + dot(u[:, low:high], wo[low:high])
        block_out.append((own_tokens + norms[k] * branch).astype(BF16))
        inner = jnp.sum(cotangent[k].astype(F32) * branch, axis=-1, keepdims=True)
        pulls.append(norms[k] ** 3 * (inner / level_width(k)))
    block_out = jnp.stack(block_out)[:, None]
    mixed = [None] * LEVELS
    coefs = [None] * LEVELS
    running = jnp.zeros((rows, D), F32)
    coef = jnp.zeros((rows, 1), F32)
    for k in reversed(range(LEVELS)):
        running = running + norms[k] * cotangent[k].astype(F32)
        coef = coef + pulls[k]
        mixed[k] = running.astype(BF16)
        coefs[k] = coef
    back = jnp.concatenate(
        [dot(mixed[k], wo[low:high], NT).astype(BF16) for k, (low, high) in enumerate(SEGMENTS)],
        axis=-1,
    )
    coefs = jnp.concatenate(coefs, axis=-1)
    back_blocks = jnp.concatenate(
        [
            back.reshape(rows, parts, cw).transpose(1, 0, 2),
            jnp.broadcast_to(pack_terms(coefs)[None], (parts, rows, LANES)),
        ],
        axis=-1,
    )
    back_own = swap_blocks(back_blocks).reshape(length, cw + LANES)
    dwo = jnp.concatenate(
        [dot(u[:, low:high], mixed[k], TN).astype(BF16) for k, (low, high) in enumerate(SEGMENTS)],
        axis=0,
    )
    dwo = lax.psum_scatter(
        dwo.reshape(groups, parts, out_rows, D).transpose(1, 0, 2, 3), "seq", scatter_dimension=0
    )
    out_part = lax.psum_scatter(dwo, "dp", scatter_dimension=0).astype(F32)

    coefs = unpack_terms(back_own[:, cw:], LEVELS)
    pull = coefs[:, LEVELS - 1 :]
    for k in reversed(range(LEVELS - 1)):
        pull = jnp.where(channel[None, :] < level_width(k), coefs[:, k : k + 1], pull)
    back = back_own[:, :cw].astype(F32)
    dgated = own_gain * back - gated * pull
    dgain_out = jnp.sum(back * gated, axis=0)
    dz = (dgated * y * (sig + gate * (1.0 - sig))).astype(BF16)
    dy = dgated * gate
    dwz = dot(normed, dz, TN).astype(BF16)
    dwz = lax.psum_scatter(dwz, "dp", scatter_dimension=0, tiled=True)
    dpx, dtaps, dheads, dskip = scan_backward(
        px, taps, heads, skip, spread, spread.T, dy, y, states
    )
    dwx = dot(normed, dpx, TN).astype(BF16)
    dwx = lax.psum_scatter(dwx, "dp", scatter_dimension=0, tiled=True)
    dnormed = (dot(dz, wz, NT) + dot(dpx, wx, NT)).astype(BF16)
    dnormed = jnp.sum(swap_blocks(dnormed.reshape(parts, rows, D)).astype(F32), axis=0)
    own_scale = lax.rsqrt(jnp.mean(own_tokens * own_tokens, axis=-1, keepdims=True) + EPS_IN)
    dgain_in = jnp.sum(dnormed * own_tokens * own_scale, axis=0)
    scaled = dnormed * gain_in
    hidden_grad = (
        own_scale * scaled
        - own_tokens
        * (own_scale**3 * (jnp.sum(scaled * own_tokens, axis=-1, keepdims=True) / D))
        + jnp.sum(cotangent.astype(F32), axis=0)
    )[None]

    z_part = swap_blocks(dwz.reshape(parts, in_rows, cw)).astype(F32)
    x_part = swap_blocks(dwx.reshape(parts, in_rows, cc + LANES)).astype(F32)
    in_part = jnp.concatenate(
        [
            z_part.transpose(1, 0, 2).reshape(in_rows, INNER),
            x_part[:, :, :cw].transpose(1, 0, 2).reshape(in_rows, INNER),
            jnp.sum(x_part[:, :, cw:cc], axis=0),
            x_part[:, :, cc : cc + hq].transpose(1, 0, 2).reshape(in_rows, H),
        ],
        axis=1,
    )
    taps_grad = jnp.zeros((TAPS + 1, CONV_CH), F32)
    taps_grad = lax.dynamic_update_slice(taps_grad, dtaps[: TAPS + 1, :cw], (0, q * cw))
    taps_grad = taps_grad.at[:, INNER:].set(dtaps[: TAPS + 1, cw:])
    gain_grad = lax.dynamic_update_slice(jnp.zeros((INNER,), F32), dgain_out, (q * cw,))
    skip_grad = jnp.sum(dskip[0].reshape(hq, P_SIZE), axis=-1)
    head_grad = lax.dynamic_update_slice(
        jnp.zeros((3, H), F32),
        jnp.stack([dheads[0, :hq], dheads[1, :hq], skip_grad]),
        (0, q * hq),
    )
    small = jnp.concatenate(
        [taps_grad.reshape(-1), dgain_in, gain_grad, head_grad.reshape(-1)]
    )
    small = all_sum(all_sum(small, "seq"), "dp")
    chan_len = chan_params.shape[0]
    chan_total = small[: small.shape[0] - 3 * H]
    head_total = small[small.shape[0] - 3 * H :].reshape(3, H)
    owner = lax.axis_index("dp") * parts + q
    chan_part = lax.dynamic_slice(chan_total, (owner * chan_len,), (chan_len,))
    local_squares = jnp.sum(in_part * in_part) + jnp.sum(out_part * out_part)
    total_squares = all_sum(all_sum(local_squares.reshape(1, 1), "seq"), "dp")[0, 0]
    grad_norm = jnp.sqrt(
        total_squares + jnp.sum(chan_total * chan_total) + jnp.sum(head_total * head_total)
    )
    clip_factor = jnp.minimum(1.0, CLIP / grad_norm)
    w_in_new, w_in_m_new, w_in_v_new = adam_step(
        w_in, clip_factor * in_part, w_in_m, w_in_v, 0.02, 0.1
    )
    w_out_new, w_out_m_new, w_out_v_new = adam_step(
        w_out, clip_factor * out_part, w_out_m, w_out_v, 0.03, 0.1
    )
    chan_new, chan_m_new, chan_v_new = adam_step(
        chan_params, clip_factor * chan_part, chan_m, chan_v, 0.2, 0.0
    )
    head_new, head_m_new, head_v_new = adam_step(
        head_params, clip_factor * head_total, head_m, head_v, 1.0, 0.0
    )
    return (
        block_out, hidden_grad, grad_norm,
        w_in_new, w_in_m_new, w_in_v_new, w_in_new.astype(BF16),
        w_out_new, w_out_m_new, w_out_v_new, w_out_new.astype(BF16),
        chan_new, chan_m_new, chan_v_new, head_new, head_m_new, head_v_new,
    )


def solution(mesh):
    rows = P(("dp", "seq"), None)
    flat = P(("dp", "seq"))
    in_specs = (
        P("dp", "seq", None),
        P(None, "dp", "seq", None),
        *([rows] * 6),
        *([flat] * 3),
        *([P()] * 3),
    )
    out_specs = (
        P(None, "dp", "seq", None),
        P("dp", "seq", None),
        P(),
        *([rows] * 8),
        *([flat] * 3),
        *([P()] * 3),
    )
    return jax.shard_map(
        on_device, mesh=mesh, in_specs=in_specs, out_specs=out_specs, check_vma=False
    )
```

time: 1920 us -> 753 us (0.39)
  waiting for transfers between devices: 1210 us -> 313 us
  matrix products: 272 us -> 97.3 us
  other arithmetic: 144 us -> 67.4 us
  local copies, waits for them, and re-layouts: 112 us -> 37.9 us
  Pallas kernels: 0 us -> 46.5 us
  starting transfers between devices: 9.37 us -> 38.3 us
  blocking collectives: 147 us -> 120 us
    reduce_scatter x2 -> x3, waiting for transfers between devices: 775 us -> 47.2 us  [the longest x1 31.3 us: on_device(): out_part = lax.psum_scatter(dwo, 'dp', scatter_dimension=0).astype(F32)]
    all_gather x5 -> x4, waiting for transfers between devices: 315 us -> 117 us  [the longest x1 57.5 us: on_device(): wo = lax.all_gather(out_low, ('dp', 'seq'), axis=0, tiled=True)]
    dot_general x27 -> x18, matrix products: 272 us -> 97.3 us  [dot(): lax.dot_general(a, b, (dims, ((), ())), precision=precision, preferred_el...]
    all_to_all x1 -> x4, waiting for transfers between devices: 0.01 us -> 104 us  [swap_blocks(): lax.all_to_all(blocks, 'seq', split_axis=0, concat_axis=0, tiled=True)]
    unnamed x9, waiting for transfers between devices: 121 us -> 26.2 us
    pallas_call x0 -> x2, Pallas kernels: none -> 46.5 us  [the longest x1 29.2 us: scan_backward(): pl.pallas_call(functools.partial(scan_backward_kernel, cw), grid=(chunks,...]
    psum x1 -> x0, blocking collectives: 40.5 us -> none  [on_device(): lax.psum((local_squares, head_grad), ('dp', 'seq'))]
    select_n x8 -> x1, other arithmetic: 23.6 us -> 0.01 us  [on_device(): jnp.arange(cw) // P_SIZE]
  transfers between devices with their start and end apart: 11 -> 22, of which waited for: 7 -> 17; matrix products, arithmetic and copies ran while one was open for 19% -> 19% of each run, Pallas kernels for 0% -> 6%
where the time goes in v1:
time: 753 us; the launch traced here: 743 us
  waiting for transfers between devices  313 us (42%)
  blocking collectives  120 us (16%)
  matrix products  97.3 us (13%)
  other arithmetic  67.4 us (9%)
  Pallas kernels  46.5 us (6%)
  starting transfers between devices  38.3 us (5%)
  local copies, waits for them, and re-layouts  37.9 us (5%)
  between operations  22.3 us (3%)
    all_to_all x4, waiting for transfers between devices, swap_blocks(): lax.all_to_all(blocks, 'seq', split_axis=0, concat_axis=0, tiled=True)  104 us
    dot_general x18, matrix products, dot(): lax.dot_general(a, b, (dims, ((), ())), precision=precision, preferred_el...  97.3 us
    all_to_all x3, blocking collectives, swap_blocks(): lax.all_to_all(blocks, 'seq', split_axis=0, concat_axis=0, tiled=True)  75.4 us
    all_gather x1, waiting for transfers between devices, on_device(): wo = lax.all_gather(out_low, ('dp', 'seq'), axis=0, tiled=True)  57.5 us
    unnamed x1, blocking collectives  44.5 us
    all_gather x1, waiting for transfers between devices, on_device(): lax.all_gather(swap_blocks(x_blocks), 'dp', axis=0).reshape(D, cc + LANES)  40.8 us
    reduce_scatter x1, waiting for transfers between devices, on_device(): out_part = lax.psum_scatter(dwo, 'dp', scatter_dimension=0).astype(F32)  31.3 us
    pallas_call x1, Pallas kernels, scan_backward(): pl.pallas_call(functools.partial(scan_backward_kernel, cw), grid=(chunks,...  29.2 us
  transfers between devices with their start and end apart: 22, of which 17 were waited for; matrix products, arithmetic and copies ran while one was open for 19% of the time, Pallas kernels for 6%

profile of v1, /device:TPU:1, one launch (start us, length us, event | category | flops | bytes accessed | tf_op | source)
XLA Modules:
  0.0 742.6 jit_solution(6250013553499093472)
XLA Ops:
  8.0 3.4 copy.59
  14.3 18.8 %all_to_all.35 = bf16[4,64,1408]{2,1,0:T(8,128)(2,1)} all-to-all(bf16[4,64,1408]{2,1,0:T(8,128)(2,1)S(1)} %fusion.81), channel_id=1, replica_groups=mesh['dp'=8,'seq'=4] {'seq'}, dimensions={0} | all-to-all | bytes 1441792 | tf_op jit(solution)/shard_map/all_to_all | solution.py:350
  33.6 10.0 %all_to_all.36 = bf16[4,64,1024]{2,1,0:T(8,128)(2,1)} all-to-all(bf16[4,64,1024]{2,1,0:T(8,128)(2,1)S(1)} %bitcast.216), channel_id=1, replica_groups=mesh['dp'=8,'seq'=4] {'seq'}, dimensions={0} | all-to-all | bytes 1048576 | tf_op jit(solution)/shard_map/all_to_all | solution.py:350
  44.9 44.5 %all-reduce.4 = bf16[27904]{0:T(1024)(128)(2,1)S(1)} all-reduce(bf16[27904]{0:T(1024)(128)(2,1)S(1)} %dynamic-update-slice.3), channel_id=1, replica_groups=mesh['dp'=8,'seq'=4] {'dp','seq'}, use_global_device_ids=true, to_apply=%add.4 | all-reduce | flops 27904 | bytes 111616
  90.2 3.1 fusion
  93.3 40.8 %all-gather.12.cloned.1.call-done = bf16[32,64,1408]{2,1,0:T(8,128)(2,1)} async-done(((bf16[4,64,1408]{2,1,0:T(8,128)(2,1)}), bf16[32,64,1408]{2,1,0:T(8,128)(2,1)}) %all-gather.12.cloned.1.call-update) | async-done | bytes 5767184 | tf_op jit(solution)/shard_map/all_gather | solution.py:389
  134.2 11.9 %fusion.139.px.halo = f32[1024,1408]{1,0:T(8,128)} fusion(bf16[2048,1408]{1,0:T(8,128)(2,1)} %bitcast.251, bf16[1,1024,2048]{2,1,0:T(8,128)(2,1)} %all-gather.10.cloned.1.call-done, f32[2048]{0:T(1024)S(1)} %slice.239, f32[1024]{0:T(1024)S(1)} %add_rsqrt_fusion), kind=kOutput, calls=%fused_computation.232 | convolution fusion | flops 5913968640 | bytes 15740928 | tf_op jit(solution)/shard_map/dot_general | solution.py:44
  146.1 17.3 %scan_forward.1 = (f32[1024,1024]{1,0:T(8,128)}, bf16[8,128,1024]{2,1,0:T(8,128)(2,1)S(1)}) custom-call(f32[1024,1408]{1,0:T(8,128)} %fusion.139.px.halo, f32[8,1280]{1,0:T(8,128)S(1)} %pad_maximum_fusion.5.taps, f32[8,128]{1,0:T(8,128)S(1)} %select_maximum_fusion.heads, f32[1,1024]{1,0:T(1,128)S(1)} %reshape_reshape.3.skip, bf16[128,1024]{1,0:T(8,128)(2,1)S(1)} %fusion.84.spread), custom_call_target="tpu_custom_call" | custom-call | tf_op jit(solution)/shard_map/scan_forward/pallas_call | solution.py:253
  163.4 18.3 %all-gather.14.cloned.1.call-done = bf16[32,64,1024]{2,1,0:T(8,128)(2,1)} async-done(((bf16[4,64,1024]{2,1,0:T(8,128)(2,1)}), bf16[32,64,1024]{2,1,0:T(8,128)(2,1)}) %all-gather.14.cloned.1.call-update) | async-done | bytes 4194320 | tf_op jit(solution)/shard_map/all_gather | solution.py:394
  181.7 12.3 %multiply_convert_fusion.1 = (bf16[1024,1024]{1,0:T(8,128)(2,1)}, f32[1024,1024]{1,0:T(8,128)S(1)}, f32[1024,1024]{1,0:T(8,128)}) fusion(f32[1024]{0:T(1024)S(1)} %dynamic_slice.14, f32[1024,1024]{1,0:T(8,128)} %get-tuple-element.35.y, bf16[2048,1024]{1,0:T(8,128)(2,1)} %bitcast.253, bf16[1,1024,2048]{2,1,0:T(8,128)(2,1)} %all-gather.10.cloned.1.call-done, ...), kind=kOutput, calls=%fused_computation.29 | convolution fusion | flops 4310695936 | bytes 23085056 | tf_op jit(solution)/shard_map/dot_general | solution.py:44
  194.0 2.0 copy-done.5
  197.6 3.3 fusion.34
  200.8 4.3 copy.67
  205.1 46.6 %all_to_all.37 = bf16[4,256,1152]{1,2,0:T(8,128)(2,1)S(1)} all-to-all(bf16[4,256,1152]{1,2,0:T(8,128)(2,1)} %copy.67), channel_id=1, replica_groups=mesh['dp'=8,'seq'=4] {'seq'}, dimensions={0} | all-to-all | bytes 4718592 | tf_op jit(solution)/shard_map/all_to_all | solution.py:350
  253.3 3.0 slice.252
  256.4 57.5 %all-gather.8.cloned.1.call-done = bf16[4096,2048]{1,0:T(8,128)(2,1)} async-done(((bf16[128,2048]{1,0:T(8,128)(2,1)}), bf16[4096,2048]{1,0:T(8,128)(2,1)}) %all-gather.8.cloned.1.call-update) | async-done | bytes 16777232 | tf_op jit(solution)/shard_map/all_gather | solution.py:395
  313.9 2.5 fusion.59
  316.4 2.3 convolution_add_fusion
  318.8 3.5 fusion.16
  322.3 5.9 fusion.19
  328.2 3.8 fusion.52
  333.0 2.4 convolution_convert_fusion.4
  336.7 2.4 convolution_convert_fusion
  339.9 5.3 pad_maximum_fusion
  345.2 6.7 copy.84
  352.0 2.8 fusion.66
  355.1 2.5 fusion.69
  357.6 3.5 fusion.63
  361.1 6.0 fusion.29
  369.1 3.2 pad_maximum_fusion.1
  372.4 4.5 all-to-all-start.3
  377.0 53.2 %all-to-all-done.3 = bf16[4,256,1152]{2,1,0:T(8,128)(2,1)} async-done(((bf16[4,256,1152]{2,1,0:T(8,128)(2,1)}), bf16[4,256,1152]{2,1,0:T(8,128)(2,1)}, u32[]{:S(2)}, u32[]{:S(2)}) %all-to-all-start.3) | async-done | bytes 2359328 | tf_op jit(solution)/shard_map/all_to_all | solution.py:350
  432.5 11.9 %fusion.10 = (f32[1024,1024]{1,0:T(8,128)}, bf16[1024,1024]{1,0:T(8,128)(2,1)S(1)}, f32[1024]{0:T(1024)S(1)}) fusion(f32[1024,1024]{1,0:T(8,128)} %copy-done.5, f32[1024]{0:T(1024)S(1)} %get-tuple-element.103, f32[1024]{0:T(1024)S(1)} %get-tuple-element.104, f32[1024]{0:T(1024)S(1)} %get-tuple-element.105, f32[1024]{0:T(1024)S(1)} %get-tuple-element.102, ...), kind=kLoop, calls=%fused_computation.24 | loop fusion | flops 20970496 | bytes 20999168 | tf_op jit(solution)/shard_map/mul | solution.py:495
  445.8 6.8 convolution_convert_fusion.3
  452.9 29.2 %scan_backward.1 = (bf16[1024,1408]{1,0:T(8,128)(2,1)S(1)}, f32[8,1280]{1,0:T(8,128)S(1)}, f32[8,128]{1,0:T(8,128)S(1)}, f32[8,1024]{1,0:T(8,128)S(1)}) custom-call(f32[1024,1408]{1,0:T(8,128)} %fusion.139.px.halo, f32[1024,1408]{1,0:T(8,128)} %fusion.139.px.halo, f32[8,1280]{1,0:T(8,128)S(1)} %pad_maximum_fusion.5.taps, ...), custom_call_target="tpu_custom_call" | custom-call | tf_op jit(solution)/shard_map/scan_backward/pallas_call | solution.py:288
  483.7 9.0 %convolution_convert_fusion.1 = bf16[2048,1408]{1,0:T(8,128)(2,1)} fusion(bf16[1024,1408]{1,0:T(8,128)(2,1)S(1)} %get-tuple-element.37, bf16[1,1024,2048]{2,1,0:T(8,128)(2,1)S(1)} %copy-done.12, f32[2048]{0:T(1024)S(1)} %slice.239, f32[1024]{0:T(1024)S(1)} %copy-done.35), kind=kOutput, calls=%fused_computation.11 | convolution fusion | flops 5916852224 | bytes 12857344 | tf_op jit(solution)/shard_map/dot_general | solution.py:44
  494.3 9.2 %fusion.154 = f32[1024,2048]{1,0:T(8,128)} fusion(bf16[1024,1024]{1,0:T(8,128)(2,1)S(1)} %copy-done.21, bf16[2048,1024]{1,0:T(8,128)(2,1)} %bitcast.254), kind=kOutput, calls=%fused_computation.237 | convolution fusion | flops 4294967296 | bytes 14680064 | tf_op jit(solution)/shard_map/dot_general | solution.py:44
  503.5 25.4 %reduce-scatter.13.cloned.1.call-done = bf16[1,8,128,2048]{3,2,1,0:T(8,128)(2,1)} async-done(((bf16[4,8,128,2048]{3,2,1,0:T(8,128)(2,1)}), bf16[1,8,128,2048]{3,2,1,0:T(8,128)(2,1)}) %reduce-scatter.13.cloned.1.call-update) | async-done | bytes 4194320
  529.0 12.1 %add_convert_fusion = bf16[1024,2048]{1,0:T(8,128)(2,1)} fusion(f32[1024,2048]{1,0:T(8,128)} %fusion.154, bf16[1024,1408]{1,0:T(8,128)(2,1)} %copy-done, bf16[2048,1408]{1,0:T(8,128)(2,1)} %bitcast.252), kind=kOutput, calls=%fused_computation.9 | convolution fusion | flops 5909774336 | bytes 21233664 | tf_op jit(solution)/shard_map/dot_general | solution.py:44
  541.1 5.3 all-to-all-start.4
  547.2 46.1 %all-to-all-done.4 = bf16[4,256,2048]{2,1,0:T(8,128)(2,1)} async-done(((bf16[4,256,2048]{2,1,0:T(8,128)(2,1)}), bf16[4,256,2048]{2,1,0:T(8,128)(2,1)}, u32[]{:S(2)}, u32[]{:S(2)}) %all-to-all-start.4) | async-done | bytes 4194336 | tf_op jit(solution)/shard_map/all_to_all | solution.py:350
  593.3 3.4 convert_reduce_fusion.1
  596.7 1.8 fusion.43
  599.5 3.1 collective-permute-done.5
  603.8 2.1 convert_reduce_fusion
  606.8 2.9 collective-permute-start.7
  612.0 4.1 all-to-all-start.5
  616.2 3.6 fusion.45
  619.9 2.1 collective-permute-start.9
  622.0 2.3 maximum_bitcast_fusion
  624.3 9.1 %collective-permute-done.9 = f32[28096]{0:T(1024)S(1)} collective-permute-done((f32[28096]{0:T(1024)S(1)}, f32[28096]{0:T(1024)S(1)}, u32[]{:S(2)}, u32[]{:S(2)}) %collective-permute-start.9) | collective-permute-done | bytes 112416 | tf_op jit(solution)/shard_map/ppermute | solution.py:344
  633.4 15.8 %reduce-scatter.9.cloned.1.call-done = bf16[256,1408]{1,0:T(8,128)(2,1)} async-done(((bf16[2048,1408]{1,0:T(8,128)(2,1)}), bf16[256,1408]{1,0:T(8,128)(2,1)}) %reduce-scatter.9.cloned.1.call-update) | async-done | bytes 720912 | tf_op jit(solution)/shard_map/reduce_scatter | solution.py:502
  649.3 3.5 all-to-all-start.6
  655.2 4.7 all-to-all-done.6
  662.2 1.8 convert_element_type.202
  664.0 2.2 copy.72
  668.6 31.3 %reduce-scatter.11.cloned.1.call-done = bf16[1,128,2048]{2,1,0:T(8,128)(2,1)} async-done(((bf16[8,128,2048]{2,1,0:T(8,128)(2,1)}), bf16[1,128,2048]{2,1,0:T(8,128)(2,1)}) %reduce-scatter.11.cloned.1.call-update) | async-done | bytes 524304 | tf_op jit(solution)/shard_map/reduce_scatter | solution.py:485
  700.0 1.9 fusion.72
  703.2 2.0 collective-permute-start
  706.1 2.0 collective-permute-start.1
  709.1 6.5 collective-permute-start.2
  719.9 2.5 collective-permute-done.4
  724.5 5.8 fusion.145
  731.7 2.5 fusion.143
  (212 shorter events, 40.5 us)
Async XLA Ops:
  7.2 83.0 %all-gather.10.cloned.1.call-start = ((), (), s32[]{:S(2)}) async-start(), calls=%async_computation.15 | async-start | bytes 5242880 | tf_op jit(solution)/shard_map/all_gather | solution.py:390
  7.9 126.3 %all-gather.12.cloned.1.call-start = ((), (), s32[]{:S(2)}) async-start(), calls=%async_computation.16 | async-start | bytes 6488064 | tf_op jit(solution)/shard_map/all_gather | solution.py:389
  14.3 29.3 %copy-start.15 = (f32[128,2048]{1,0:T(8,128)S(1)}, f32[128,2048]{1,0:T(8,128)}, u32[]{:S(2)}) copy-start(f32[128,2048]{1,0:T(8,128)} %param.21) | copy-start | bytes 3145732
  33.2 148.4 %all-gather.14.cloned.1.call-start = ((), (), s32[]{:S(2)}) async-start(), calls=%async_computation.17 | async-start | bytes 4718592 | tf_op jit(solution)/shard_map/all_gather | solution.py:394
  33.3 11.3 %copy-start.25 = (f32[872]{0:T(1024)S(1)}, f32[872]{0:T(1024)}, u32[]{:S(2)}) copy-start(f32[872]{0:T(1024)} %param.24) | copy-start | bytes 10468
  33.6 56.1 %copy-start.31 = (f32[3,64]{1,0:T(4,128)S(1)}, f32[3,64]{1,0:T(4,128)}, u32[]{:S(2)}) copy-start(f32[3,64]{1,0:T(4,128)} %param.27) | copy-start | bytes 2308
  43.6 270.2 %all-gather.8.cloned.1.call-start = ((), (), s32[]{:S(2)}) async-start(), calls=%async_computation.11 | async-start | bytes 17301504 | tf_op jit(solution)/shard_map/all_gather | solution.py:395
  44.5 484.4 %reduce-scatter.13.cloned.1.call-start = ((), (), s32[]{:S(2)}) async-start(), calls=%async_computation.18 | async-start | bytes 20971520
  93.3 88.3 %copy-start.33 = (f32[1024]{0:T(1024)}, f32[1024]{0:T(1024)S(1)}, u32[]{:S(2)}) copy-start(f32[1024]{0:T(1024)S(1)} %add_rsqrt_fusion) | copy-start | bytes 12292
  194.0 2.0 copy-start.5
  251.8 1.5 copy-start.8
  313.9 2.6 copy-start.7
  322.2 5.9 copy-start.1
  322.2 5.9 copy-start.6
  328.2 3.9 copy-start.9
  332.9 6.3 copy-start.13
  352.0 3.1 copy-start.2
  372.4 57.8 %all-to-all-start.3 = ((bf16[4,256,1152]{2,1,0:T(8,128)(2,1)}), bf16[4,256,1152]{2,1,0:T(8,128)(2,1)}, u32[]{:S(2)}, u32[]{:S(2)}) async-start(bf16[4,256,1152]{2,1,0:T(8,128)(2,1)} %pad_maximum_fusion.1), calls=%async_computation.3 | async-start | bytes 4718592 | tf_op jit(solution)/shard_map/all_to_all | solution.py:350
  376.9 235.2 %reduce-scatter.7.cloned.1.call-start = ((), (), s32[]{:S(2)}) async-start(), calls=%async_computation.12 | async-start | bytes 4718592 | tf_op jit(solution)/shard_map/reduce_scatter | solution.py:497
  430.1 2.4 copy-start.4
  432.5 13.3 %copy-start.11 = (bf16[1,1024,2048]{2,1,0:T(8,128)(2,1)S(1)}, bf16[1,1024,2048]{2,1,0:T(8,128)(2,1)}, u32[]{:S(2)}) copy-start(bf16[1,1024,2048]{2,1,0:T(8,128)(2,1)} %all-gather.10.cloned.1.call-done) | copy-start | bytes 12582916
  432.5 13.3 %copy-start.34 = (f32[1024]{0:T(1024)S(1)}, f32[1024]{0:T(1024)}, u32[]{:S(2)}) copy-start(f32[1024]{0:T(1024)} %copy-done.33) | copy-start | bytes 12292
  444.5 1.3 copy-start.20
  452.6 196.7 %reduce-scatter.9.cloned.1.call-start = ((), (), s32[]{:S(2)}) async-start(), calls=%async_computation.13 | async-start | bytes 6488064 | tf_op jit(solution)/shard_map/reduce_scatter | solution.py:502
  452.8 30.8 %copy-start.12 = (bf16[1,1024,2048]{2,1,0:T(8,128)(2,1)S(1)}, bf16[1,1024,2048]{2,1,0:T(8,128)(2,1)}, u32[]{:S(2)}) copy-start(bf16[1,1024,2048]{2,1,0:T(8,128)(2,1)} %all-gather.10.cloned.1.call-done) | copy-start | bytes 12582916
  452.8 30.8 %copy-start.35 = (f32[1024]{0:T(1024)S(1)}, f32[1024]{0:T(1024)}, u32[]{:S(2)}) copy-start(f32[1024]{0:T(1024)} %copy-done.33) | copy-start | bytes 12292
  482.1 1.6 copy-start
  492.7 1.6 copy-start.21
  492.7 207.2 %reduce-scatter.11.cloned.1.call-start = ((), (), s32[]{:S(2)}) async-start(), calls=%async_computation.14 | async-start | bytes 4718592 | tf_op jit(solution)/shard_map/reduce_scatter | solution.py:485
  541.1 5.3 copy-start.29
  541.1 52.2 %all-to-all-start.4 = ((bf16[4,256,2048]{2,1,0:T(8,128)(2,1)}), bf16[4,256,2048]{2,1,0:T(8,128)(2,1)}, u32[]{:S(2)}, u32[]{:S(2)}) async-start(bf16[4,256,2048]{2,1,0:T(8,128)(2,1)} %bitcast.213), calls=%async_computation.4 | async-start | bytes 8388608 | tf_op jit(solution)/shard_map/all_to_all | solution.py:350
  546.4 50.3 %copy-start.27 = (f32[256]{0:T(256)}, f32[256]{0:T(256)S(1)}, u32[]{:S(2)}) copy-start(f32[256]{0:T(256)S(1)} %add_rsqrt_fusion.1) | copy-start | bytes 3076
  593.3 3.4 copy-start.10
  596.7 7.1 copy-start.3
  598.5 4.1 collective-permute-start.5
  602.6 7.1 copy-start.30
  602.6 13.6 %copy-start.28 = (f32[256]{0:T(256)S(1)}, f32[256]{0:T(256)}, u32[]{:S(2)}) copy-start(f32[256]{0:T(256)} %copy-done.27) | copy-start | bytes 3076
  602.7 4.1 collective-permute-start.6
  606.8 3.9 collective-permute-start.7
  610.7 9.2 %collective-permute-start.8 = (f32[28096]{0:T(1024)S(1)}, f32[28096]{0:T(1024)S(1)}, u32[]{:S(2)}, u32[]{:S(2)}) collective-permute-start(f32[28096]{0:T(1024)S(1)} %add.291), channel_id=1, source_target_pairs={{0,8},{4,12},{8,0},{12,4},{16,24},{20,28},{24,16},{28,20},{1,9},{5... | collective-permute-start | bytes 337160 | tf_op jit(solution)/shard_map/ppermute | solution.py:344
  612.0 21.4 %all-to-all-start.5 = ((bf16[4,64,1024]{2,1,0:T(8,128)(2,1)}), bf16[4,64,1024]{2,1,0:T(8,128)(2,1)}, u32[]{:S(2)}, u32[]{:S(2)}) async-start(bf16[4,64,1024]{2,1,0:T(8,128)(2,1)} %bitcast.219), calls=%async_computation.6 | async-start | bytes 1048576 | tf_op jit(solution)/shard_map/all_to_all | solution.py:350
  616.2 5.8 copy-start.14
  616.2 5.8 copy-start.17
  616.2 5.8 copy-start.18
  616.2 5.8 copy-start.19
  619.9 13.5 %collective-permute-start.9 = (f32[28096]{0:T(1024)S(1)}, f32[28096]{0:T(1024)S(1)}, u32[]{:S(2)}, u32[]{:S(2)}) collective-permute-start(f32[28096]{0:T(1024)S(1)} %add.292), channel_id=1, source_target_pairs={{0,16},{4,20},{8,24},{12,28},{16,0},{20,4},{24,8},{28,12},{1,17},{... | collective-permute-start | bytes 337160 | tf_op jit(solution)/shard_map/ppermute | solution.py:344
  649.3 10.6 %all-to-all-start.6 = ((bf16[4,64,1408]{2,1,0:T(8,128)(2,1)}), bf16[4,64,1408]{2,1,0:T(8,128)(2,1)S(1)}, u32[]{:S(2)}, u32[]{:S(2)}) async-start(bf16[4,64,1408]{2,1,0:T(8,128)(2,1)} %bitcast.218), calls=%async_computation.8 | async-start | bytes 1441792 | tf_op jit(solution)/shard_map/all_to_all | solution.py:350
  703.2 2.4 collective-permute-start
  706.1 2.4 collective-permute-start.1
  709.1 6.5 collective-permute-start.2
  716.1 2.4 collective-permute-start.3
  719.1 3.3 collective-permute-start.4
  724.5 5.9 copy-start.32
  724.5 5.9 copy-start.38
  724.5 5.9 copy-start.39
  724.5 6.5 copy-start.26
  724.5 6.5 copy-start.36
  724.5 6.5 copy-start.37
  724.5 7.2 copy-start.16
  724.5 7.2 copy-start.22
  724.5 7.2 copy-start.23
  724.5 7.1 copy-start.24
Sparse Core Ops, SparseCore 0:
  9.9 61.7 all-gather.9
  73.3 60.8 all-gather.11
  135.8 45.8 all-gather.13
  185.0 128.8 all-gather.7
  352.1 176.8 reduce-scatter.12
  531.1 47.8 reduce-scatter.6
  581.3 67.9 reduce-scatter.8
  651.6 48.3 reduce-scatter.10

commit v2 on v1

--- a/solution.py
+++ b/solution.py
@@ -329,25 +329,506 @@
     )(px, px, taps, heads, skip, spread, gather, dy, y, states)
 
 
+WIDE = 512
+
+
+def widths_kernel(cw, u, wo, cotangent, tokens, block_out, back, mixed, branch, norms, pulls):
+    at = pl.program_id(0)
+    ends = [level_width(k) // WIDE - 1 for k in range(LEVELS)]
+
+    @pl.when(at == 0)
+    def _():
+        terms = u[0, :, cw:].astype(F32)
+        for part in range(1, u.shape[0]):
+            terms = terms + u[part, :, cw:].astype(F32)
+        squares = jnp.zeros((terms.shape[0], 1), F32)
+        for k in range(LEVELS):
+            squares = squares + terms[:, k : k + 1] + terms[:, LEVELS + k : LEVELS + k + 1]
+            norms[:, k : k + 1] = lax.rsqrt(squares / level_width(k) + EPS_OUT)
+        running = jnp.zeros(branch.shape, F32)
+        for k in reversed(range(LEVELS)):
+            running = running + norms[:, k : k + 1] * cotangent[k].astype(F32)
+            mixed[k] = running.astype(BF16)
+        branch[...] = jnp.zeros_like(branch)
+
+    part = at * WIDE // cw
+    lanes = pl.ds(pl.multiple_of(lax.rem(at * WIDE, cw), WIDE), WIDE)
+    level = sum((at > end).astype(jnp.int32) for end in ends[:-1])
+    branch[...] += dot(u[part, :, lanes], wo[...])
+    back[part, :, lanes] = dot(mixed[level], wo[...], NT).astype(BF16)
+    for k in range(LEVELS):
+
+        @pl.when(at == ends[k])
+        def _():
+            norm = norms[:, k : k + 1]
+            block_out[k] = (tokens[...].astype(F32) + norm * branch[...]).astype(BF16)
+            inner = jnp.sum(cotangent[k].astype(F32) * branch[...], axis=-1, keepdims=True)
+            pulls[:, k : k + 1] = norm * norm * norm * (inner / level_width(k))
+
+    @pl.when(at == ends[-1])
+    def _():
+        coef = jnp.zeros((branch.shape[0], 1), F32)
+        lane = lax.broadcasted_iota(jnp.int32, (1, LANES), 1)
+        packed = jnp.zeros((branch.shape[0], LANES), F32)
+        for k in reversed(range(LEVELS)):
+            coef = coef + pulls[:, k : k + 1]
+            high, rest = two_terms(coef)
+            packed = jnp.where(lane == k, high.astype(F32), packed)
+            packed = jnp.where(lane == LEVELS + k, rest.astype(F32), packed)
+        for p in range(back.shape[0]):
+            back[p, :, cw:] = packed.astype(BF16)
+
+
+def widths(u, wo, cotangent, tokens):
+    parts, rows, wide = u.shape
+    cw = wide - LANES
+
+    def full(shape):
+        return pl.BlockSpec(shape, lambda i: (0,) * len(shape), pipeline_mode=pl.Buffered(1))
+
+    return pl.pallas_call(
+        functools.partial(widths_kernel, cw),
+        grid=(INNER // WIDE,),
+        in_specs=[
+            full(u.shape),
+            pl.BlockSpec((WIDE, D), lambda i: (i, 0)),
+            full(cotangent.shape),
+            full(tokens.shape),
+        ],
+        out_specs=[full(cotangent.shape), full(u.shape), full(cotangent.shape)],
+        out_shape=[
+            jax.ShapeDtypeStruct(cotangent.shape, BF16),
+            jax.ShapeDtypeStruct(u.shape, BF16),
+            jax.ShapeDtypeStruct(cotangent.shape, BF16),
+        ],
+        scratch_shapes=[
+            pltpu.VMEM((rows, D), F32),
+            pltpu.VMEM((rows, LANES), F32),
+            pltpu.VMEM((rows, LANES), F32),
+        ],
+        compiler_params=pltpu.CompilerParams(vmem_limit_bytes=48 * 2**20),
+        name="widths",
+    )(u, wo, cotangent, tokens)
+
+
+MESH = pl.DeviceIdType.MESH
+
+
+def remote(src, dst, sends, recvs, index, device):
+    return pltpu.make_async_remote_copy(
+        src_ref=src,
+        dst_ref=dst,
+        send_sem=sends.at[index],
+        recv_sem=recvs.at[index],
+        device_id=device,
+        device_id_type=MESH,
+    )
+
+
+def greet(devices):
+    barrier = pltpu.get_barrier_semaphore()
+    for device in devices:
+        pl.semaphore_signal(barrier, inc=1, device_id=device, device_id_type=MESH)
+    pl.semaphore_wait(barrier, len(devices))
+
+
+def seq_peers(parts):
+    group, q = lax.axis_index("dp"), lax.axis_index("seq")
+    return [(group, lax.rem(q + k, parts)) for k in range(1, parts)]
+
+
+def dp_peers(groups):
+    group, q = lax.axis_index("dp"), lax.axis_index("seq")
+    return [(lax.rem(group + k, groups), q) for k in range(1, groups)]
+
+
+def swap_kernel(parts, count, *refs):
+    sources, results = refs[:count], refs[count : 2 * count]
+    sends, recvs, local = refs[2 * count :]
+    q = lax.axis_index("seq")
+    peers = seq_peers(parts)
+    greet(peers)
+    copies = []
+    for k, peer in enumerate(peers):
+        for a in range(count):
+            copy = remote(
+                sources[a].at[peer[1]], results[a].at[q], sends, recvs, k * count + a, peer
+            )
+            copy.start()
+            copies.append(copy)
+    own = [
+        pltpu.make_async_copy(sources[a].at[q], results[a].at[q], local.at[a])
+        for a in range(count)
+    ]
+    for copy in own:
+        copy.start()
+    for copy in own + copies:
+        copy.wait()
+
+
+def swap(collective_id, *arrays):
+    parts = arrays[0].shape[0]
+    count = len(arrays)
+    return pl.pallas_call(
+        functools.partial(swap_kernel, parts, count),
+        in_specs=[pl.BlockSpec(memory_space=pl.ANY)] * count,
+        out_specs=[pl.BlockSpec(memory_space=pl.ANY)] * count,
+        out_shape=[jax.ShapeDtypeStruct(a.shape, a.dtype) for a in arrays],
+        scratch_shapes=[
+            pltpu.SemaphoreType.DMA(((parts - 1) * count,)),
+            pltpu.SemaphoreType.DMA(((parts - 1) * count,)),
+            pltpu.SemaphoreType.DMA((count,)),
+        ],
+        compiler_params=pltpu.CompilerParams(collective_id=collective_id, has_side_effects=True),
+        name="swap",
+    )(*arrays)
+
+
+def all_peers(groups, parts):
+    devices = groups * parts
+    me = lax.axis_index("dp") * parts + lax.axis_index("seq")
+    peers = []
+    for k in range(1, devices):
+        other = lax.rem(me + k, devices)
+        peers.append((other // parts, lax.rem(other, parts)))
+    return peers
+
+
+def broadcast_kernel(
+    groups, parts, block, near, total, near_out, out, sends, recvs, near_s, near_r, local
+):
+    group, q = lax.axis_index("dp"), lax.axis_index("seq")
+    me = group * parts + q
+    everyone = all_peers(groups, parts)
+    greet(everyone)
+    copies = [
+        remote(block, out.at[me], sends, recvs, k, peer) for k, peer in enumerate(everyone)
+    ]
+    copies += [
+        remote(near, near_out.at[q], near_s, near_r, k, peer)
+        for k, peer in enumerate(seq_peers(parts))
+    ]
+    copies += [
+        pltpu.make_async_copy(block, out.at[me], local.at[0]),
+        pltpu.make_async_copy(near, near_out.at[q], local.at[1]),
+    ]
+    for copy in copies:
+        copy.start()
+    for copy in copies:
+        copy.wait()
+    total[...] = jnp.sum(out[...], axis=0)
+
+
+def broadcast(collective_id, block, near, groups, parts):
+    devices = groups * parts
+    sem = pltpu.SemaphoreType.DMA
+    return pl.pallas_call(
+        functools.partial(broadcast_kernel, groups, parts),
+        in_specs=[pl.BlockSpec(memory_space=pltpu.VMEM)] * 2,
+        out_specs=[pl.BlockSpec(memory_space=pltpu.VMEM)] * 2,
+        out_shape=[
+            jax.ShapeDtypeStruct(block.shape, block.dtype),
+            jax.ShapeDtypeStruct((parts,) + near.shape, near.dtype),
+        ],
+        scratch_shapes=[
+            pltpu.VMEM((devices,) + block.shape, block.dtype),
+            sem((devices - 1,)), sem((devices - 1,)), sem((parts - 1,)), sem((parts - 1,)),
+            sem((2,)),
+        ],
+        compiler_params=pltpu.CompilerParams(collective_id=collective_id, has_side_effects=True),
+        name="broadcast",
+    )(block, near)
+
+
+def collect_kernel(
+    groups, parts, hidden, blocks, chan, hid_out, w_out, chan_out,
+    chan_s, chan_r, hid_s, hid_r, swap_s, swap_r, line_s, line_r, core_s, core_r, local,
+):
+    line = groups // 2
+    group, q = lax.axis_index("dp"), lax.axis_index("seq")
+    z, core = group // 2, lax.rem(group, 2)
+    sibling = (2 * z + 1 - core, q)
+    peers = seq_peers(parts)
+    everyone = all_peers(groups, parts)
+    greet(everyone)
+    swaps = []
+    for k, peer in enumerate(peers):
+        copy = remote(blocks.at[peer[1]], w_out.at[group, q], swap_s, swap_r, k, peer)
+        copy.start()
+        swaps.append(copy)
+    mine = pltpu.make_async_copy(blocks.at[q], w_out.at[group, q], local.at[0])
+    mine.start()
+    keep = pltpu.make_async_copy(hidden, hid_out.at[q], local.at[1])
+    keep.start()
+    chans = []
+    for k, peer in enumerate(everyone):
+        copy = remote(chan, chan_out.at[group * parts + q], chan_s, chan_r, k, peer)
+        copy.start()
+        chans.append(copy)
+    chan_keep = pltpu.make_async_copy(chan, chan_out.at[group * parts + q], local.at[2])
+    chan_keep.start()
+    mine.wait()
+    for copy in swaps:
+        copy.wait()
+    hids = []
+    for k, peer in enumerate(peers):
+        copy = remote(hidden, hid_out.at[q], hid_s, hid_r, k, peer)
+        copy.start()
+        hids.append(copy)
+
+    def along(from_z, up):
+        block = w_out.at[2 * from_z + core]
+        to = z + 1 if up else z - 1
+        return remote(
+            block, block, line_s.at[0 if up else 1], line_r.at[0 if up else 1], from_z,
+            (2 * to + core, q),
+        )
+
+    def across(from_z):
+        block = w_out.at[2 * from_z + core]
+        return remote(block, block, core_s, core_r, from_z, sibling)
+
+    for t in range(line):
+        low, high = z - t, z + t
+        if t == 0:
+            across(z).start()
+
+            @pl.when(z < line - 1)
+            def _():
+                along(z, True).start()
+
+            @pl.when(z > 0)
+            def _():
+                along(z, False).start()
+
+            continue
+
+        @pl.when(low >= 0)
+        def _():
+            along(low, True).wait_recv()
+
+            @pl.when(z < line - 1)
+            def _():
+                along(low, True).start()
+
+            across(low).start()
+
+        @pl.when(high <= line - 1)
+        def _():
+            along(high, False).wait_recv()
+
+            @pl.when(z > 0)
+            def _():
+                along(high, False).start()
+
+            across(high).start()
+
+    for from_z in range(line):
+        across(from_z).wait_send()
+        block = w_out.at[2 * from_z + 1 - core]
+        remote(block, block, core_s, core_r, from_z, sibling).wait_recv()
+
+        @pl.when((from_z <= z) & (z < line - 1))
+        def _():
+            along(from_z, True).wait_send()
+
+        @pl.when((from_z >= z) & (z > 0))
+        def _():
+            along(from_z, False).wait_send()
+
+    keep.wait()
+    chan_keep.wait()
+    for copy in hids + chans:
+        copy.wait()
+
+
+def collect(collective_id, hidden, blocks, chan, groups):
+    parts, rows, width = blocks.shape
+    line = groups // 2
+    sem = pltpu.SemaphoreType.DMA
+    return pl.pallas_call(
+        functools.partial(collect_kernel, groups, parts),
+        in_specs=[pl.BlockSpec(memory_space=pl.ANY)] * 3,
+        out_specs=[pl.BlockSpec(memory_space=pl.ANY)] * 3,
+        out_shape=[
+            jax.ShapeDtypeStruct((parts,) + hidden.shape, hidden.dtype),
+            jax.ShapeDtypeStruct((groups, parts, rows, width), blocks.dtype),
+            jax.ShapeDtypeStruct((groups * parts,) + chan.shape, chan.dtype),
+        ],
+        scratch_shapes=[
+            sem((groups * parts - 1,)), sem((groups * parts - 1,)), sem((parts - 1,)), sem((parts - 1,)), sem((parts - 1,)), sem((parts - 1,)),
+            sem((2, line)), sem((2, line)), sem((line,)), sem((line,)), sem((3,)),
+        ],
+        compiler_params=pltpu.CompilerParams(collective_id=collective_id, has_side_effects=True),
+        name="collect",
+    )(hidden, blocks, chan)
+
+
+def add_blocks(out, a, b, rows, steps):
+    def step(i, carry):
+        at = pl.ds(pl.multiple_of(i * rows, rows), rows)
+        out[at] = (a[at].astype(F32) + b[at].astype(F32)).astype(out.dtype)
+        return carry
+
+    lax.fori_loop(0, steps, step, 0)
+
+
+def reduce_kernel(
+    groups, parts, rows, grad, back, small, part, back_out, small_all,
+    held, acc, down, up,
+    core_s, core_r, up_s, up_r, down_s, down_r, part_s, part_r, back_s, back_r,
+    small_s, small_r, local,
+):
+    line = groups // 2
+    span = parts * rows
+    group, q = lax.axis_index("dp"), lax.axis_index("seq")
+    z, core = group // 2, lax.rem(group, 2)
+    sibling = (2 * z + 1 - core, q)
+    peers, others = seq_peers(parts), dp_peers(groups)
+    greet(peers + others)
+
+    def share(of):
+        return grad.at[pl.ds(pl.multiple_of(of * span, span), span)]
+
+    cores = []
+    for d in range(line):
+        copy = remote(share(2 * d + 1 - core), held.at[d], core_s, core_r, d, sibling)
+        copy.start()
+        cores.append(copy)
+    waiting = []
+    for k, peer in enumerate(peers):
+        copy = remote(back.at[peer[1]], back_out.at[q], back_s, back_r, k, peer)
+        copy.start()
+        waiting.append(copy)
+    for k, peer in enumerate(others):
+        copy = remote(small, small_all.at[group], small_s, small_r, k, peer)
+        copy.start()
+        waiting.append(copy)
+    own_back = pltpu.make_async_copy(back.at[q], back_out.at[q], local.at[0])
+    own_back.start()
+    own_small = pltpu.make_async_copy(small, small_all.at[group], local.at[1])
+    own_small.start()
+    for d in range(line):
+        cores[d].wait()
+        add_blocks(acc.at[d], share(2 * d + core), held.at[d], rows, parts)
+
+    def ahead(d, first):
+        block = acc.at[d] if first else up.at[d]
+        return remote(block, up.at[d], up_s, up_r, d, (2 * (z + 1) + core, q))
+
+    def behind(d, first):
+        block = acc.at[d] if first else down.at[d]
+        return remote(block, down.at[d], down_s, down_r, d, (2 * (z - 1) + core, q))
+
+    for t in range(line - 1):
+        far = line - 1 - t + z
+
+        @pl.when((z == 0) & (z < line - 1))
+        def _():
+            ahead(line - 1 - t, True).start()
+
+        @pl.when((z > 0) & (z <= t) & (z < line - 1))
+        def _():
+            ahead(far, False).wait_recv()
+            add_blocks(up.at[far], up.at[far], acc.at[far], rows, parts)
+            ahead(far, False).start()
+
+        near = t - (line - 1 - z)
+
+        @pl.when((z == line - 1) & (z > 0))
+        def _():
+            behind(t, True).start()
+
+        @pl.when((z < line - 1) & (line - 1 - z <= t) & (z > 0))
+        def _():
+            behind(near, False).wait_recv()
+            add_blocks(down.at[near], down.at[near], acc.at[near], rows, parts)
+            behind(near, False).start()
+
+    @pl.when(z > 0)
+    def _():
+        ahead(z, False).wait_recv()
+        add_blocks(acc.at[z], acc.at[z], up.at[z], rows, parts)
+
+    @pl.when(z < line - 1)
+    def _():
+        behind(z, False).wait_recv()
+        add_blocks(acc.at[z], acc.at[z], down.at[z], rows, parts)
+
+    parts_copies = []
+    for k, peer in enumerate(peers):
+        block = acc.at[z, pl.ds(pl.multiple_of(peer[1] * rows, rows), rows)]
+        copy = remote(block, part.at[q], part_s, part_r, k, peer)
+        copy.start()
+        parts_copies.append(copy)
+    own = pltpu.make_async_copy(
+        acc.at[z, pl.ds(pl.multiple_of(q * rows, rows), rows)], part.at[q], local.at[2]
+    )
+    own.start()
+    for t in range(line - 1):
+        far = line - 1 - t + z
+        near = t - (line - 1 - z)
+
+        @pl.when((z == 0) & (z < line - 1))
+        def _():
+            ahead(line - 1 - t, True).wait_send()
+
+        @pl.when((z > 0) & (z <= t) & (z < line - 1))
+        def _():
+            ahead(far, False).wait_send()
+
+        @pl.when((z == line - 1) & (z > 0))
+        def _():
+            behind(t, True).wait_send()
+
+        @pl.when((z < line - 1) & (line - 1 - z <= t) & (z > 0))
+        def _():
+            behind(near, False).wait_send()
+
+    own.wait()
+    own_back.wait()
+    own_small.wait()
+    for copy in parts_copies + waiting:
+        copy.wait()
+
+
+def reduce_to_owners(collective_id, grad, back, small, groups):
+    parts = back.shape[0]
+    line = groups // 2
+    rows = grad.shape[0] // (groups * parts)
+    span, width = rows * parts, grad.shape[1]
+    sem = pltpu.SemaphoreType.DMA
+    vmem = pl.BlockSpec(memory_space=pltpu.VMEM)
+    hbm = pl.BlockSpec(memory_space=pl.ANY)
+    return pl.pallas_call(
+        functools.partial(reduce_kernel, groups, parts, rows),
+        in_specs=[vmem, hbm, vmem],
+        out_specs=[hbm, hbm, vmem],
+        out_shape=[
+            jax.ShapeDtypeStruct((parts, rows, width), grad.dtype),
+            jax.ShapeDtypeStruct(back.shape, back.dtype),
+            jax.ShapeDtypeStruct((groups,) + small.shape, small.dtype),
+        ],
+        scratch_shapes=[
+            pltpu.VMEM((line, span, width), grad.dtype),
+            pltpu.VMEM((line, span, width), grad.dtype),
+            pltpu.VMEM((line, span, width), grad.dtype),
+            pltpu.VMEM((line, span, width), grad.dtype),
+            sem((line,)), sem((line,)), sem((line,)), sem((line,)), sem((line,)), sem((line,)),
+            sem((parts - 1,)), sem((parts - 1,)), sem((parts - 1,)), sem((parts - 1,)),
+            sem((groups - 1,)), sem((groups - 1,)), sem((3,)),
+        ],
+        compiler_params=pltpu.CompilerParams(
+            collective_id=collective_id, has_side_effects=True, vmem_limit_bytes=48 * 2**20
+        ),
+        name="reduce_to_owners",
+    )(grad, back, small)
 def adam_step(weight, gradient, moment, second, step_rate, weight_decay):
     new_moment = BETA * moment + (1.0 - BETA) * gradient
     new_second = BETA * second + (1.0 - BETA) * gradient * gradient
     correction = 1.0 - BETA**STEP
     update = new_moment / correction / (jnp.sqrt(new_second / correction) + ADAM_EPS)
     return (weight - step_rate * (update + weight_decay * weight), new_moment, new_second)
-
-
-def all_sum(value, axis):
-    size = lax.axis_size(axis)
-    by = 1
-    while by < size:
-        value = value + lax.ppermute(value, axis, [(i, i ^ by) for i in range(size)])
-        by *= 2
-    return value
-
-
-def swap_blocks(blocks):
-    return lax.all_to_all(blocks, "seq", split_axis=0, concat_axis=0, tiled=True)
 
 
 def pack_terms(values):
@@ -386,12 +867,16 @@
     dt_blocks = in_low[:, 2 * INNER + 2 * N :].reshape(in_rows, parts, hq).transpose(1, 0, 2)
     dt_blocks = jnp.pad(dt_blocks, ((0, 0), (0, 0), (0, LANES - hq)))
     x_blocks = jnp.concatenate([x_blocks, bc_block, dt_blocks], axis=2)
-    wx = lax.all_gather(swap_blocks(x_blocks), "dp", axis=0).reshape(D, cc + LANES)
-    hidden = lax.all_gather(hidden_in[0], "seq", axis=0, tiled=True)
-    chan_full = lax.all_gather(chan_params.astype(BF16), ("dp", "seq"), axis=0, tiled=True).astype(
-        F32
-    )
-    wz = lax.all_gather(swap_blocks(z_blocks), "dp", axis=0).reshape(D, cw)
+    chan_len = chan_params.shape[0]
+    chan_rows = -(-chan_len // (8 * LANES)) * 8
+    chan_block = jnp.pad(
+        lax.reduce_precision(chan_params, 8, 7), (0, chan_rows * LANES - chan_len)
+    ).reshape(chan_rows, LANES)
+    hidden, wx, chan_full = collect(0, hidden_in[0], x_blocks, chan_block, groups)
+    hidden = hidden.reshape(length, D)
+    wx = wx.reshape(D, cc + LANES)
+    chan_full = chan_full.reshape(groups * parts, chan_rows * LANES)[:, :chan_len].reshape(-1)
+    wz = lax.all_gather(swap(1, z_blocks)[0], "dp", axis=0).reshape(D, cw)
     wo = lax.all_gather(out_low, ("dp", "seq"), axis=0, tiled=True)
 
     conv_taps = chan_full[: TAPS * CONV_CH].reshape(TAPS, CONV_CH)
@@ -433,48 +918,14 @@
         axis=-1,
     )
     u_blocks = jnp.concatenate([(gated * own_gain).astype(BF16), pack_terms(squares)], axis=-1)
-    u_blocks = swap_blocks(u_blocks.reshape(parts, rows, cw + LANES))
-    u = u_blocks[:, :, :cw].transpose(1, 0, 2).reshape(rows, INNER)
-    squares = jnp.cumsum(
-        jnp.sum(unpack_terms(u_blocks[:, :, cw:], LEVELS), axis=0), axis=-1
-    )
+    u = swap(2, u_blocks.reshape(parts, rows, cw + LANES))[0]
 
     own_tokens = hidden_in[0].astype(F32)
     cotangent = out_grads[:, 0]
-    norms = [
-        lax.rsqrt(squares[:, k : k + 1] / level_width(k) + EPS_OUT) for k in range(LEVELS)
-    ]
-    branch = jnp.zeros((rows, D), F32)
-    block_out = []
-    pulls = []
-    for k, (low, high) in enumerate(SEGMENTS):
-        branch = branch + dot(u[:, low:high], wo[low:high])
-        block_out.append((own_tokens + norms[k] * branch).astype(BF16))
-        inner = jnp.sum(cotangent[k].astype(F32) * branch, axis=-1, keepdims=True)
-        pulls.append(norms[k] ** 3 * (inner / level_width(k)))
-    block_out = jnp.stack(block_out)[:, None]
-    mixed = [None] * LEVELS
-    coefs = [None] * LEVELS
-    running = jnp.zeros((rows, D), F32)
-    coef = jnp.zeros((rows, 1), F32)
-    for k in reversed(range(LEVELS)):
-        running = running + norms[k] * cotangent[k].astype(F32)
-        coef = coef + pulls[k]
-        mixed[k] = running.astype(BF16)
-        coefs[k] = coef
-    back = jnp.concatenate(
-        [dot(mixed[k], wo[low:high], NT).astype(BF16) for k, (low, high) in enumerate(SEGMENTS)],
-        axis=-1,
-    )
-    coefs = jnp.concatenate(coefs, axis=-1)
-    back_blocks = jnp.concatenate(
-        [
-            back.reshape(rows, parts, cw).transpose(1, 0, 2),
-            jnp.broadcast_to(pack_terms(coefs)[None], (parts, rows, LANES)),
-        ],
-        axis=-1,
-    )
-    back_own = swap_blocks(back_blocks).reshape(length, cw + LANES)
+    block_out, back_blocks, mixed = widths(u, wo, cotangent, hidden_in[0])
+    block_out = block_out[:, None]
+    back_own = swap(3, back_blocks)[0].reshape(length, cw + LANES)
+    u = u[:, :, :cw].transpose(1, 0, 2).reshape(rows, INNER)
     dwo = jnp.concatenate(
         [dot(u[:, low:high], mixed[k], TN).astype(BF16) for k, (low, high) in enumerate(SEGMENTS)],
         axis=0,
@@ -499,9 +950,16 @@
         px, taps, heads, skip, spread, spread.T, dy, y, states
     )
     dwx = dot(normed, dpx, TN).astype(BF16)
-    dwx = lax.psum_scatter(dwx, "dp", scatter_dimension=0, tiled=True)
     dnormed = (dot(dz, wz, NT) + dot(dpx, wx, NT)).astype(BF16)
-    dnormed = jnp.sum(swap_blocks(dnormed.reshape(parts, rows, D)).astype(F32), axis=0)
+    skip_grad = jnp.sum(dskip[0].reshape(hq, P_SIZE), axis=-1)
+    small = jnp.concatenate(
+        [dtaps[: TAPS + 1].reshape(-1), dgain_out, dheads[0, :hq], dheads[1, :hq], skip_grad]
+    )
+    small_rows = -(-small.shape[0] // (8 * LANES)) * 8
+    small = jnp.pad(small, (0, small_rows * LANES - small.shape[0])).reshape(small_rows, LANES)
+    x_part, dnormed, small = reduce_to_owners(4, dwx, dnormed.reshape(parts, rows, D), small, groups)
+    dnormed = jnp.sum(dnormed.astype(F32), axis=0)
+    small = jnp.sum(small, axis=0)
     own_scale = lax.rsqrt(jnp.mean(own_tokens * own_tokens, axis=-1, keepdims=True) + EPS_IN)
     dgain_in = jnp.sum(dnormed * own_tokens * own_scale, axis=0)
     scaled = dnormed * gain_in
@@ -512,8 +970,8 @@
         + jnp.sum(cotangent.astype(F32), axis=0)
     )[None]
 
-    z_part = swap_blocks(dwz.reshape(parts, in_rows, cw)).astype(F32)
-    x_part = swap_blocks(dwx.reshape(parts, in_rows, cc + LANES)).astype(F32)
+    z_part = swap(5, dwz.reshape(parts, in_rows, cw))[0].astype(F32)
+    x_part = x_part.astype(F32)
     in_part = jnp.concatenate(
         [
             z_part.transpose(1, 0, 2).reshape(in_rows, INNER),
@@ -523,29 +981,36 @@
         ],
         axis=1,
     )
-    taps_grad = jnp.zeros((TAPS + 1, CONV_CH), F32)
-    taps_grad = lax.dynamic_update_slice(taps_grad, dtaps[: TAPS + 1, :cw], (0, q * cw))
-    taps_grad = taps_grad.at[:, INNER:].set(dtaps[: TAPS + 1, cw:])
-    gain_grad = lax.dynamic_update_slice(jnp.zeros((INNER,), F32), dgain_out, (q * cw,))
-    skip_grad = jnp.sum(dskip[0].reshape(hq, P_SIZE), axis=-1)
-    head_grad = lax.dynamic_update_slice(
-        jnp.zeros((3, H), F32),
-        jnp.stack([dheads[0, :hq], dheads[1, :hq], skip_grad]),
-        (0, q * hq),
-    )
-    small = jnp.concatenate(
-        [taps_grad.reshape(-1), dgain_in, gain_grad, head_grad.reshape(-1)]
-    )
-    small = all_sum(all_sum(small, "seq"), "dp")
-    chan_len = chan_params.shape[0]
-    chan_total = small[: small.shape[0] - 3 * H]
-    head_total = small[small.shape[0] - 3 * H :].reshape(3, H)
+    local_squares = jnp.sum(in_part * in_part) + jnp.sum(out_part * out_part)
+    block = jnp.concatenate(
+        [dgain_in.reshape(D // LANES, LANES), jnp.full((8, LANES), local_squares)], axis=0
+    )
+    block, small = broadcast(6, block, small, groups, parts)
+    small = small.reshape(parts, small_rows * LANES)
+    taps_size = (TAPS + 1) * cc
+    taps_grad = small[:, :taps_size].reshape(parts, TAPS + 1, cc)
+    taps_grad = jnp.concatenate(
+        [
+            taps_grad[:, :, :cw].transpose(1, 0, 2).reshape(TAPS + 1, INNER),
+            jnp.sum(taps_grad[:, :, cw:], axis=0),
+        ],
+        axis=1,
+    )
+    head_total = small[:, taps_size + cw : taps_size + cw + 3 * hq]
+    head_total = head_total.reshape(parts, 3, hq).transpose(1, 0, 2).reshape(3, H)
+    chan_total = jnp.concatenate(
+        [
+            taps_grad.reshape(-1),
+            block[: D // LANES].reshape(-1),
+            small[:, taps_size : taps_size + cw].reshape(-1),
+        ]
+    )
     owner = lax.axis_index("dp") * parts + q
     chan_part = lax.dynamic_slice(chan_total, (owner * chan_len,), (chan_len,))
-    local_squares = jnp.sum(in_part * in_part) + jnp.sum(out_part * out_part)
-    total_squares = all_sum(all_sum(local_squares.reshape(1, 1), "seq"), "dp")[0, 0]
     grad_norm = jnp.sqrt(
-        total_squares + jnp.sum(chan_total * chan_total) + jnp.sum(head_total * head_total)
+        block[D // LANES, 0]
+        + jnp.sum(chan_total * chan_total)
+        + jnp.sum(head_total * head_total)
     )
     clip_factor = jnp.minimum(1.0, CLIP / grad_norm)
     w_in_new, w_in_m_new, w_in_v_new = adam_step(

time: 753 us -> 663 us (0.88)
  Pallas kernels: 46.5 us -> 410 us
  waiting for transfers between devices: 313 us -> 63.5 us
  blocking collectives: 120 us -> 0 us
  starting transfers between devices: 38.3 us -> 0.38 us
  matrix products: 97.3 us -> 63.3 us
    pallas_call x0 -> x8, Pallas kernels: none -> 364 us  [the longest x1 117 us: collect(): pl.pallas_call(functools.partial(collect_kernel, groups, parts), in_specs...]
    all_to_all x4 -> x0, waiting for transfers between devices: 104 us -> none  [swap_blocks(): lax.all_to_all(blocks, 'seq', split_axis=0, concat_axis=0, tiled=True)]
    all_to_all x3 -> x0, blocking collectives: 75.4 us -> none  [swap_blocks(): lax.all_to_all(blocks, 'seq', split_axis=0, concat_axis=0, tiled=True)]
    all_gather x3 -> x1, waiting for transfers between devices: 59.1 us -> 0.02 us  [on_device(): wz = lax.all_gather(swap(1, z_blocks)[0], 'dp', axis=0).reshape(D, cw)]
    all_gather x1, waiting for transfers between devices: 57.5 us -> 0.01 us  [on_device(): wo = lax.all_gather(out_low, ('dp', 'seq'), axis=0, tiled=True)]
    unnamed x1 -> x0, blocking collectives: 44.5 us -> none
    unnamed x9 -> x6, waiting for transfers between devices: 26.2 us -> 63.5 us
    dot_general x18 -> x10, matrix products: 97.3 us -> 63.3 us  [dot(): lax.dot_general(a, b, (dims, ((), ())), precision=precision, preferred_el...]
  transfers between devices with their start and end apart: 22 -> 5, of which waited for: 17 -> 1; matrix products, arithmetic and copies ran while one was open for 19% -> 17% of each run, Pallas kernels for 6% -> 54%
where the time goes in v2:
time: 663 us; the launch traced here: 658 us
  Pallas kernels  410 us (62%)
  waiting for transfers between devices  63.5 us (10%)
  matrix products  63.3 us (10%)
  other arithmetic  60.9 us (9%)
  local copies, waits for them, and re-layouts  39.8 us (6%)
  between operations  19.4 us (3%)
    pallas_call x1, Pallas kernels, collect(): pl.pallas_call(functools.partial(collect_kernel, groups, parts), in_specs...  117 us
    pallas_call x1, Pallas kernels, reduce_to_owners(): pl.pallas_call(functools.partial(reduce_kernel, groups, parts, rows), in_...  103 us
    pallas_call x4, Pallas kernels, swap(): pl.pallas_call(functools.partial(swap_kernel, parts, count), in_specs=[pl...  98.4 us
    unnamed x6, waiting for transfers between devices  63.5 us
    dot_general x10, matrix products, dot(): lax.dot_general(a, b, (dims, ((), ())), precision=precision, preferred_el...  63.3 us
    pallas_call x1, Pallas kernels, scan_backward(): pl.pallas_call(functools.partial(scan_backward_kernel, cw), grid=(chunks,...  29.1 us
    pallas_call x1, Pallas kernels, broadcast(): pl.pallas_call(functools.partial(broadcast_kernel, groups, parts), in_spe...  23.7 us
    pallas_call x1, Pallas kernels, widths(): pl.pallas_call(functools.partial(widths_kernel, cw), grid=(INNER // WIDE,...  22.1 us
  transfers between devices with their start and end apart: 5, of which 1 were waited for; matrix products, arithmetic and copies ran while one was open for 17% of the time, Pallas kernels for 54%

profile of v2, /device:TPU:1, one launch (start us, length us, event | category | flops | bytes accessed | tf_op | source)
XLA Modules:
  0.0 657.7 jit_solution(6282955810902115456)
XLA Ops:
  7.2 3.4 copy.77
  10.6 1.1 fusion.62
  11.7 2.4 copy.83
  14.1 10.4 %swap.4 = bf16[4,64,1024]{2,1,0:T(8,128)(2,1)} custom-call(bf16[4,64,1024]{2,1,0:T(8,128)(2,1)} %bitcast.154), custom_call_target="tpu_custom_call" | custom-call | tf_op jit(solution)/shard_map/swap/pallas_call | solution.py:472
  24.6 2.1 convert_element_type.109
  27.9 0.9 fusion.28.blocks
  28.9 117.4 %collect.1 = (bf16[4,256,2048]{2,1,0:T(8,128)(2,1)}, bf16[8,4,64,1408]{3,2,1,0:T(8,128)(2,1)}, f32[32,8,128]{2,1,0:T(8,128)}) custom-call(bf16[256,2048]{1,0:T(8,128)(2,1)} %bitcast.131, bf16[4,64,1408]{2,1,0:T(8,128)(2,1)} %fusion.28.blocks, f32[8,128]{1,0:T(8,128)} %pad_bitcast_fusion.1.chan), custom_call_target="tpu_custom_call" | custom-call | tf_op jit(solution)/shard_map/collect/pallas_call | solution.py:649
  146.2 0.9 copy.112
  147.9 3.2 multiply_reduce_fusion
  151.3 1.0 multiply_convert_fusion
  152.4 3.1 copy-done.34
  155.5 8.8 %fusion.63.px.halo = f32[1024,1408]{1,0:T(8,128)} fusion(bf16[1024,2048]{1,0:T(8,128)(2,1)S(1)} %bitcast.149, bf16[2048,1408]{1,0:T(8,128)(2,1)S(1)} %bitcast.176), kind=kOutput, calls=%fused_computation.155 | convolution fusion | flops 5905580032 | bytes 15728640 | tf_op jit(solution)/shard_map/dot_general | solution.py:44
  164.3 17.0 %scan_forward.1 = (f32[1024,1024]{1,0:T(8,128)}, bf16[8,128,1024]{2,1,0:T(8,128)(2,1)S(1)}) custom-call(f32[1024,1408]{1,0:T(8,128)} %fusion.63.px.halo, f32[8,1280]{1,0:T(8,128)S(1)} %pad_maximum_fusion.4.taps, f32[8,128]{1,0:T(8,128)S(1)} %select_maximum_fusion.heads, f32[1,1024]{1,0:T(1,128)S(1)} %reshape_reshape.3.skip, bf16[128,1024]{1,0:T(8,128)(2,1)S(1)} %fusion.30.spread), custom_call_target="tpu_custom_call" | custom-call | tf_op jit(solution)/shard_map/scan_forward/pallas_call | solution.py:253
  181.3 1.3 copy-done.6
  182.7 11.6 %multiply_convert_fusion.2 = (bf16[1024,1024]{1,0:T(8,128)(2,1)S(1)}, f32[1024,1024]{1,0:T(8,128)S(1)}, f32[1024,1024]{1,0:T(8,128)}) fusion(f32[1024]{0:T(1024)S(1)} %dynamic_slice.14, f32[1024,1024]{1,0:T(8,128)} %get-tuple-element.37.y, bf16[1024,2048]{1,0:T(8,128)(2,1)} %bitcast.150, bf16[2048,1024]{1,0:T(8,128)(2,1)} %bitcast.180), kind=kOutput, calls=%fused_computation.24 | convolution fusion | flops 4302307328 | bytes 23072768 | tf_op jit(solution)/shard_map/dot_general | solution.py:44
  194.3 2.0 copy-done.12
  196.2 1.4 select_reduce_fusion.3
  197.9 1.6 fusion.7
  199.5 27.8 %swap.5.u = bf16[4,256,1152]{2,1,0:T(8,128)(2,1)} custom-call(bf16[4,256,1152]{2,1,0:T(8,128)(2,1)} %bitcast.147), custom_call_target="tpu_custom_call" | custom-call | tf_op jit(solution)/shard_map/swap/pallas_call | solution.py:472
  227.3 3.2 slice_bitcast_fusion
  230.6 3.9 copy.91
  234.5 22.1 %widths.1 = (bf16[4,256,2048]{2,1,0:T(8,128)(2,1)}, bf16[4,256,1152]{2,1,0:T(8,128)(2,1)S(1)}, bf16[4,256,2048]{2,1,0:T(8,128)(2,1)}) custom-call(bf16[4,256,1152]{2,1,0:T(8,128)(2,1)S(1)} %copy-done.1, bf16[4096,2048]{1,0:T(8,128)(2,1)} %all-gather.4.cloned.1.call-done.wo, bf16[4,256,2048]{2,1,0:T(8,128)(2,1)} %bitcast.136, bf16[256,2048]{1,0:T(8,128)(2,1)S(1)} %bitcast.132), custom_call_target="tpu_custom_call" | custom-call | tf_op jit(solution)/shard_map/widths/pallas_call | solution.py:389
  256.6 4.3 convolution_convert_fusion
  260.9 2.6 convolution_convert_fusion.2
  263.6 0.7 convolution_convert_fusion.4
  264.3 0.7 convolution_convert_fusion.5
  265.0 3.3 pad_maximum_fusion
  268.3 6.6 %copy.110 = bf16[8,4,128,2048]{3,2,0,1:T(8,128)(2,1)} copy(bf16[8,4,128,2048]{3,2,1,0:T(8,128)(2,1)S(1)} %bitcast.135) | data formatting | bytes 33554432 | tf_op jit(solution)/shard_map/reshape | solution.py:934
  275.2 5.2 fusion.1
  280.5 53.8 %swap.6 = bf16[4,256,1152]{2,1,0:T(8,128)(2,1)} custom-call(bf16[4,256,1152]{2,1,0:T(8,128)(2,1)} %copy-done.5), custom_call_target="tpu_custom_call" | custom-call | tf_op jit(solution)/shard_map/swap/pallas_call | solution.py:472
  334.2 1.1 slice_convert_fusion
  335.6 1.0 slice_reduce_fusion.3
  336.7 12.5 %multiply_convert_fusion.1 = (bf16[1024,1024]{1,0:T(8,128)(2,1)S(1)}, f32[1024,1024]{1,0:T(8,128)}, f32[1024]{0:T(1024)S(1)}) fusion(f32[1024,1024]{1,0:T(8,128)S(1)} %copy-done.11, f32[1024,1024]{1,0:T(8,128)} %copy-done.12, f32[1024,1024]{1,0:T(8,128)} %get-tuple-element.161, f32[1024]{0:T(1024)S(1)} %get-tuple-element.126, ...), kind=kLoop, calls=%fused_computation.18 | loop fusion | flops 20970496 | bytes 20999168 | tf_op jit(solution)/shard_map/convert_element_type | solution.py:945
  349.2 6.2 convolution_convert_fusion.3
  356.0 4.6 convert_reduce_fusion
  360.7 29.1 %scan_backward.1 = (bf16[1024,1408]{1,0:T(8,128)(2,1)S(1)}, f32[8,1280]{1,0:T(8,128)S(1)}, f32[8,128]{1,0:T(8,128)S(1)}, f32[8,1024]{1,0:T(8,128)S(1)}) custom-call(f32[1024,1408]{1,0:T(8,128)} %fusion.63.px.halo, f32[1024,1408]{1,0:T(8,128)} %fusion.63.px.halo, f32[8,1280]{1,0:T(8,128)S(1)} %pad_maximum_fusion.4.taps, ...), custom_call_target="tpu_custom_call" | custom-call | tf_op jit(solution)/shard_map/scan_backward/pallas_call | solution.py:288
  389.7 1.5 copy-done.8
  391.3 63.4 %reduce-scatter.10.cloned.1.call-done = bf16[1,8,128,2048]{3,2,1,0:T(8,128)(2,1)} async-done(((bf16[4,8,128,2048]{3,2,1,0:T(8,128)(2,1)}), bf16[1,8,128,2048]{3,2,1,0:T(8,128)(2,1)}) %reduce-scatter.10.cloned.1.call-update) | async-done | bytes 4194320
  455.0 9.1 %fusion.64 = f32[1024,2048]{1,0:T(8,128)} fusion(bf16[1024,1024]{1,0:T(8,128)(2,1)S(1)} %copy-done.22, bf16[2048,1024]{1,0:T(8,128)(2,1)} %bitcast.181), kind=kOutput, calls=%fused_computation.156 | convolution fusion | flops 4294967296 | bytes 14680064 | tf_op jit(solution)/shard_map/dot_general | solution.py:44
  464.1 8.7 %convolution_convert_fusion.1.grad = bf16[2048,1408]{1,0:T(8,128)(2,1)} fusion(bf16[1024,2048]{1,0:T(8,128)(2,1)S(1)} %copy-done.17, bf16[1024,1408]{1,0:T(8,128)(2,1)S(1)} %copy-done.9), kind=kOutput, calls=%fused_computation.11 | convolution fusion | flops 5908463616 | bytes 12845056 | tf_op jit(solution)/shard_map/dot_general | solution.py:44
  472.8 10.6 %add_convert_fusion = bf16[1024,2048]{1,0:T(8,128)(2,1)} fusion(f32[1024,2048]{1,0:T(8,128)} %fusion.64, bf16[1024,1408]{1,0:T(8,128)(2,1)S(1)} %copy-done.9, bf16[2048,1408]{1,0:T(8,128)(2,1)S(1)} %bitcast.179), kind=kOutput, calls=%fused_computation.7 | convolution fusion | flops 5909774336 | bytes 21233664 | tf_op jit(solution)/shard_map/dot_general | solution.py:44
  483.4 102.8 %reduce_to_owners.1 = (bf16[4,64,1408]{2,1,0:T(8,128)(2,1)S(1)}, bf16[4,256,2048]{2,1,0:T(8,128)(2,1)S(1)}, f32[8,64,128]{2,1,0:T(8,128)S(1)}) custom-call(bf16[2048,1408]{1,0:T(8,128)(2,1)} %convolution_convert_fusion.1.grad, bf16[4,256,2048]{2,1,0:T(8,128)(2,1)} %bitcast.151, f32[64,128]{1,0:T(8,128)S(1)} %pad_bitcast_fusion.small), custom_call_target="tpu_custom_call" | custom-call | tf_op jit(solution)/shard_map/reduce_to_owners/pallas_call | solution.py:803
  586.2 2.0 copy-done.2
  588.4 0.9 copy-done.15
  589.6 0.6 reduce_sum.192.near
  590.2 1.0 slice_reduce_fusion.4
  591.2 3.4 convert_reduce_fusion.1
  594.6 0.6 fusion.12
  595.3 1.9 bitcast_add_fusion
  597.2 6.4 swap.7
  603.6 1.1 convert_bitcast_fusion
  604.8 1.2 multiply_reduce_fusion.1
  606.0 1.9 fusion.16
  609.2 0.6 concatenate.42.block
  609.8 23.7 %broadcast.309 = (f32[24,128]{1,0:T(8,128)}, f32[4,64,128]{2,1,0:T(8,128)}) custom-call(f32[24,128]{1,0:T(8,128)} %concatenate.42.block, f32[64,128]{1,0:T(8,128)} %reduce_sum.192.near), custom_call_target="tpu_custom_call" | custom-call | tf_op jit(solution)/shard_map/broadcast/pallas_call | solution.py:525
  633.5 1.2 slice.169
  634.7 0.7 slice_bitcast_fusion.4
  635.4 1.0 copy.111
  636.5 0.6 multiply_reduce_fusion.3
  637.2 0.6 pad_maximum_fusion.3
  640.1 5.8 fusion.59
  645.9 0.6 add_subtract_fusion
  646.5 0.7 multiply_subtract_fusion.2
  647.2 2.5 fusion.57
  (153 shorter events, 4.7 us)
Async XLA Ops:
  7.2 175.5 %all-gather.6.cloned.1.call-start = ((), (), s32[]{:S(2)}) async-start(), calls=%async_computation.6 | async-start | bytes 4718592 | tf_op jit(solution)/shard_map/all_gather | solution.py:879
  11.7 15.6 %copy-start.26 = (f32[872]{0:T(1024)S(1)}, f32[872]{0:T(1024)}, u32[]{:S(2)}) copy-start(f32[872]{0:T(1024)} %param.22) | copy-start | bytes 10468
  24.5 123.1 %copy-start.28 = (f32[3,64]{1,0:T(4,128)S(1)}, f32[3,64]{1,0:T(4,128)}, u32[]{:S(2)}) copy-start(f32[3,64]{1,0:T(4,128)} %param.25) | copy-start | bytes 2308
  24.5 210.0 %all-gather.4.cloned.1.call-start = ((), (), s32[]{:S(2)}) async-start(), calls=%async_computation.3 | async-start | bytes 17301504 | tf_op jit(solution)/shard_map/all_gather | solution.py:880
  26.7 428.0 %reduce-scatter.10.cloned.1.call-start = ((), (), s32[]{:S(2)}) async-start(), calls=%async_computation.7 | async-start | bytes 20971520
  147.9 3.5 copy-start.10
  151.2 13.0 %copy-start.3 = (bf16[128,1024]{1,0:T(8,128)(2,1)}, bf16[128,1024]{1,0:T(8,128)(2,1)S(1)}, u32[]{:S(2)}) copy-start(bf16[128,1024]{1,0:T(8,128)(2,1)S(1)} %fusion.30.spread) | copy-start | bytes 786436
  151.3 4.2 copy-start.34
  152.4 11.9 %copy-start.18 = (bf16[4,256,2048]{2,1,0:T(8,128)(2,1)}, bf16[4,256,2048]{2,1,0:T(8,128)(2,1)S(1)}, u32[]{:S(2)}) copy-start(bf16[4,256,2048]{2,1,0:T(8,128)(2,1)S(1)} %multiply_convert_fusion) | copy-start | bytes 12582916
  181.3 1.3 copy-start.6
  194.3 2.0 copy-start.12
  227.3 7.2 %copy-start = (bf16[1,256,2048]{2,1,0:T(8,128)(2,1)S(1)}, bf16[1,256,2048]{2,1,0:T(8,128)(2,1)}, u32[]{:S(2)}) copy-start(bf16[1,256,2048]{2,1,0:T(8,128)(2,1)} %param.14) | copy-start | bytes 3145732
  227.3 7.2 %copy-start.1 = (bf16[4,256,1152]{2,1,0:T(8,128)(2,1)S(1)}, bf16[4,256,1152]{2,1,0:T(8,128)(2,1)}, u32[]{:S(2)}) copy-start(bf16[4,256,1152]{2,1,0:T(8,128)(2,1)} %swap.5.u) | copy-start | bytes 7077892
  234.5 22.1 %copy-start.13 = (bf16[256,4,1024]{0,2,1:T(8,128)(2,1)S(1)}, bf16[256,4,1024]{0,2,1:T(8,128)(2,1)}, u32[]{:S(2)}) copy-start(bf16[256,4,1024]{0,2,1:T(8,128)(2,1)} %copy.91) | copy-start | bytes 6291460
  256.6 4.3 copy-start.5
  260.9 2.7 copy-start.19
  275.0 322.2 %reduce-scatter.6.cloned.1.call-start = ((), (), s32[]{:S(2)}) async-start(), calls=%async_computation.4 | async-start | bytes 4718592 | tf_op jit(solution)/shard_map/reduce_scatter | solution.py:948
  334.2 2.4 copy-start.11
  336.6 12.5 %copy-start.16 = (bf16[1024,2048]{1,0:T(8,128)(2,1)S(1)}, bf16[1024,2048]{1,0:T(8,128)(2,1)}, u32[]{:S(2)}) copy-start(bf16[1024,2048]{1,0:T(8,128)(2,1)} %fusion.1) | copy-start | bytes 12582916
  349.1 6.2 copy-start.21
  355.4 5.2 copy-start.4
  355.4 5.2 copy-start.7
  355.4 250.6 %reduce-scatter.8.cloned.1.call-start = ((), (), s32[]{:S(2)}) async-start(), calls=%async_computation.5 | async-start | bytes 4718592 | tf_op jit(solution)/shard_map/reduce_scatter | solution.py:936
  389.7 1.5 copy-start.8
  391.3 63.7 %copy-start.22 = (bf16[1024,1024]{1,0:T(8,128)(2,1)S(1)}, bf16[1024,1024]{1,0:T(8,128)(2,1)}, u32[]{:S(2)}) copy-start(bf16[1024,1024]{1,0:T(8,128)(2,1)} %copy-done.21) | copy-start | bytes 6291460
  455.0 9.1 %copy-start.9 = (bf16[1024,1408]{1,0:T(8,128)(2,1)S(1)}, bf16[1024,1408]{1,0:T(8,128)(2,1)}, u32[]{:S(2)}) copy-start(bf16[1024,1408]{1,0:T(8,128)(2,1)} %copy-done.8) | copy-start | bytes 8650756
  455.0 9.1 %copy-start.17 = (bf16[1024,2048]{1,0:T(8,128)(2,1)S(1)}, bf16[1024,2048]{1,0:T(8,128)(2,1)}, u32[]{:S(2)}) copy-start(bf16[1024,2048]{1,0:T(8,128)(2,1)} %fusion.1) | copy-start | bytes 12582916
  455.0 17.8 %slice-start = ((s8[5767168]{0:T(1024)(128)(4,1)}), s8[4194304]{0:T(1024)(128)(4,1)S(1)}, s32[]{:S(2)}) async-start(s8[5767168]{0:T(1024)(128)(4,1)} %bitcast.177), calls=%async_computation.8 | async-start | bytes 8388608
  464.1 8.7 %slice-start.1 = ((s8[5767168]{0:T(1024)(128)(4,1)}), s8[1572864]{0:T(1024)(128)(4,1)S(1)}, s32[]{:S(2)}) async-start(s8[5767168]{0:T(1024)(128)(4,1)} %bitcast.177), calls=%async_computation.9 | async-start | bytes 3145728
  586.2 2.0 copy-start.2
  588.3 1.1 copy-start.15
  591.2 4.1 copy-start.14
  640.0 5.9 copy-start.29
  640.0 5.9 copy-start.32
  640.0 5.9 copy-start.33
  640.0 6.5 copy-start.27
  640.0 6.5 copy-start.30
  640.0 6.5 copy-start.31
  640.0 7.2 %copy-start.20 = (f32[128,2048]{1,0:T(8,128)S(1)}, f32[128,2048]{1,0:T(8,128)}, u32[]{:S(2)}) copy-start(f32[128,2048]{1,0:T(8,128)} %param.19) | copy-start | bytes 3145732
  640.1 7.2 %copy-start.23 = (bf16[1,128,2048]{2,1,0:T(8,128)(2,1)S(1)}, bf16[1,128,2048]{2,1,0:T(8,128)(2,1)}, u32[]{:S(2)}) copy-start(bf16[1,128,2048]{2,1,0:T(8,128)(2,1)} %reduce-scatter.8.cloned.1.call-done) | copy-start | bytes 1572868
  640.1 7.2 %copy-start.24 = (f32[128,2048]{1,0:T(8,128)S(1)}, f32[128,2048]{1,0:T(8,128)}, u32[]{:S(2)}) copy-start(f32[128,2048]{1,0:T(8,128)} %param.20) | copy-start | bytes 3145732
  640.1 7.1 %copy-start.25 = (f32[128,2048]{1,0:T(8,128)S(1)}, f32[128,2048]{1,0:T(8,128)}, u32[]{:S(2)}) copy-start(f32[128,2048]{1,0:T(8,128)} %param.21) | copy-start | bytes 3145732
Sparse Core Ops, SparseCore 0:
  24.6 61.6 all-gather.5
  89.7 122.7 all-gather.3
  275.1 179.5 reduce-scatter.9
  456.8 56.3 reduce-scatter.5
  515.3 80.1 reduce-scatter.7

commit v3 on v2

--- a/solution.py
+++ b/solution.py
@@ -62,6 +62,11 @@
     return dot(high, spread) + dot(rest, spread)
 
 
+def own_heads_first(dt_raw, hq, back=False):
+    by = lax.axis_index("seq") * hq
+    return pltpu.roll(dt_raw, by if back else lax.rem(LANES - by, LANES), 1)
+
+
 def rates(dt_raw, heads):
     step = softplus(dt_raw + heads[0:1, :])
     return step, step * heads[1:2, :]
@@ -94,7 +99,7 @@
         xbuf[0:8, :] = jnp.zeros((8, cc), F32)
 
     xbuf[8 : 8 + CHUNK, :] = px[:, :cc]
-    step, rate = rates(px[:, cc:], heads)
+    step, rate = rates(own_heads_first(px[:, cc:], cw // P_SIZE), heads)
     row, col = triangle(CHUNK)
     causal = row >= col
     cum = dot(causal.astype(F32), rate, precision=EXACT)
@@ -140,6 +145,67 @@
 
 
 def scan_backward_kernel(
+    groups, parts, cw,
+    px, halo, taps, heads, skip, spread, gather, dy, y, states, wide, gate,
+    dpx, dtaps, dheads, dskip, wide_sum, gate_sum,
+    xbuf, dstate, dcbuf, slope, xact, xd_s, dxd_s, acc_s,
+    wide_in, gate_held, gate_acc, gate_in,
+    wide_s, wide_r, core_s, core_r, gate_s, gate_r,
+):
+    line = groups // 2
+    group, q = lax.axis_index("dp"), lax.axis_index("seq")
+    z, core = group // 2, lax.rem(group, 2)
+    sibling = (2 * z + 1 - core, q)
+    peers = seq_peers(parts)
+    places = [lax.rem(z + k, line) for k in range(1, line)]
+
+    def wide_copy(k):
+        return remote(wide.at[peers[k][1]], wide_in.at[k], wide_s, wide_r, k, peers[k])
+
+    def core_copy(d):
+        return remote(gate.at[d, 1 - core], gate_held.at[d], core_s, core_r, d, sibling)
+
+    def gate_copy(k):
+        to = (2 * places[k] + core, q)
+        return remote(gate_acc.at[places[k]], gate_in.at[k], gate_s, gate_r, k, to)
+
+    @pl.when(pl.program_id(0) == 0)
+    def _():
+        greet(peers + dp_peers(groups))
+        for d in range(line):
+            core_copy(d).start()
+        for k in range(parts - 1):
+            wide_copy(k).start()
+
+    @pl.when(pl.program_id(0) == 1)
+    def _():
+        for d in range(line):
+            core_copy(d).wait()
+            add_blocks(gate_acc.at[d], gate.at[d, core], gate_held.at[d], 32, gate.shape[2] // 32)
+        for k in range(line - 1):
+            gate_copy(k).start()
+
+    scan_backward_step(
+        cw, px, halo, taps, heads, skip, spread, gather, dy, y, states,
+        dpx, dtaps, dheads, dskip, xbuf, dstate, dcbuf, slope, xact, xd_s, dxd_s, acc_s,
+    )
+
+    @pl.when(pl.program_id(0) == pl.num_programs(0) - 1)
+    def _():
+        for k in range(line - 1):
+            gate_copy(k).wait()
+        sum_blocks(gate_sum, [gate_acc.at[z]] + [gate_in.at[k] for k in range(line - 1)], 32)
+        for k in range(parts - 1):
+            wide_copy(k).wait()
+        for d in range(line):
+            sum_blocks(
+                wide_sum.at[d],
+                [wide.at[q, d]] + [wide_in.at[k, d] for k in range(parts - 1)],
+                16,
+            )
+
+
+def scan_backward_step(
     cw, px, halo, taps, heads, skip, spread, gather, dy, y, states,
     dpx, dtaps, dheads, dskip,
     xbuf, dstate, dcbuf, slope, xact, xd_s, dxd_s, acc_s,
@@ -157,7 +223,7 @@
 
     xbuf[0:8, :] = jnp.where(at == pl.num_programs(0) - 1, 0.0, halo[:, :cc])
     xbuf[8 : 8 + CHUNK, :] = px[:, :cc]
-    dt_raw = px[:, cc:]
+    dt_raw = own_heads_first(px[:, cc:], cw // P_SIZE)
     step, rate = rates(dt_raw, heads)
     row, col = triangle(CHUNK)
     causal = row >= col
@@ -237,6 +303,8 @@
                 reach = TAPS - 1 - tap
                 back = back + taps[tap : tap + 1, lanes] * dcbuf[reach : reach + CHUNK, lanes]
         dpx[:, lanes] = back.astype(BF16)
+    ours = lax.broadcasted_iota(jnp.int32, (1, LANES), 1) < cw // P_SIZE
+    ddt = own_heads_first(jnp.where(ours, ddt, 0.0), cw // P_SIZE, back=True)
     dpx[:, cc:] = ddt.astype(BF16)
     dcbuf[CHUNK : CHUNK + 8, :] = dcbuf[0:8, :]
 
@@ -275,18 +343,25 @@
             pltpu.VMEM((CHUNK, cw), F32),
         ],
         compiler_params=pltpu.CompilerParams(vmem_limit_bytes=48 * 2**20),
+        cost_estimate=pl.CostEstimate(
+            flops=3 * 10**9, bytes_accessed=40 * 10**6, transcendentals=10**7
+        ),
         name="scan_forward",
     )(px, taps, heads, skip, spread)
 
 
-def scan_backward(px, taps, heads, skip, spread, gather, dy, y, states):
+def scan_backward(collective_id, px, taps, heads, skip, spread, gather, dy, y, states, wide, gate):
     length, width = px.shape
     cw = skip.shape[1]
     cc = cw + 2 * N
     chunks = length // CHUNK
     eighths = CHUNK // 8
+    parts, line, out_rows, half = wide.shape
+    span = gate.shape[2]
+    sem = pltpu.SemaphoreType.DMA
+    vmem = pl.BlockSpec(memory_space=pltpu.VMEM)
     return pl.pallas_call(
-        functools.partial(scan_backward_kernel, cw),
+        functools.partial(scan_backward_kernel, 2 * line, parts, cw),
         grid=(chunks,),
         in_specs=[
             pl.BlockSpec((CHUNK, width), lambda i: (chunks - 1 - i, 0)),
@@ -301,18 +376,24 @@
             pl.BlockSpec((CHUNK, cw), lambda i: (chunks - 1 - i, 0)),
             pl.BlockSpec((CHUNK, cw), lambda i: (chunks - 1 - i, 0)),
             pl.BlockSpec((1, N, cw), lambda i: (chunks - 1 - i, 0, 0)),
+            vmem,
+            vmem,
         ],
         out_specs=[
             pl.BlockSpec((CHUNK, width), lambda i: (chunks - 1 - i, 0)),
             whole((8, cc)),
             whole((8, LANES)),
             whole((8, cw)),
+            vmem,
+            vmem,
         ],
         out_shape=[
             jax.ShapeDtypeStruct((length, width), BF16),
             jax.ShapeDtypeStruct((8, cc), F32),
             jax.ShapeDtypeStruct((8, LANES), F32),
             jax.ShapeDtypeStruct((8, cw), F32),
+            jax.ShapeDtypeStruct(wide.shape[1:], BF16),
+            jax.ShapeDtypeStruct((span, cw), BF16),
         ],
         scratch_shapes=[
             pltpu.VMEM((CHUNK + 8, cc), F32),
@@ -323,10 +404,21 @@
             pltpu.VMEM((CHUNK, cw), BF16),
             pltpu.VMEM((CHUNK, cw), F32),
             pltpu.VMEM((CHUNK, CHUNK), F32),
-        ],
-        compiler_params=pltpu.CompilerParams(vmem_limit_bytes=48 * 2**20),
+            pltpu.VMEM((parts - 1,) + wide.shape[1:], BF16),
+            pltpu.VMEM((line, span, cw), BF16),
+            pltpu.VMEM((line, span, cw), BF16),
+            pltpu.VMEM((line - 1, span, cw), BF16),
+            sem((parts - 1,)), sem((parts - 1,)), sem((line,)), sem((line,)),
+            sem((line - 1,)), sem((line - 1,)),
+        ],
+        compiler_params=pltpu.CompilerParams(
+            collective_id=collective_id, has_side_effects=True, vmem_limit_bytes=56 * 2**20
+        ),
+        cost_estimate=pl.CostEstimate(
+            flops=10**10, bytes_accessed=100 * 10**6, transcendentals=10**7
+        ),
         name="scan_backward",
-    )(px, px, taps, heads, skip, spread, gather, dy, y, states)
+    )(px, px, taps, heads, skip, spread, gather, dy, y, states, wide, gate)
 
 
 WIDE = 512
@@ -541,15 +633,24 @@
 
 
 def collect_kernel(
-    groups, parts, hidden, blocks, chan, hid_out, w_out, chan_out,
-    chan_s, chan_r, hid_s, hid_r, swap_s, swap_r, line_s, line_r, core_s, core_r, local,
+    groups, parts, hidden, w_in, chan, hid_out, w_out, gate_out, chan_out,
+    blocks, gates, chan_s, chan_r, hid_s, hid_r, swap_s, swap_r, gate_s, gate_r,
+    line_s, line_r, core_s, core_r, local,
 ):
     line = groups // 2
+    cw = INNER // parts
+    cc = cw + 2 * N
     group, q = lax.axis_index("dp"), lax.axis_index("seq")
     z, core = group // 2, lax.rem(group, 2)
     sibling = (2 * z + 1 - core, q)
     peers = seq_peers(parts)
     everyone = all_peers(groups, parts)
+    shared = w_in[:, 2 * INNER :].astype(BF16)
+    for part in range(parts):
+        at = INNER + part * cw
+        blocks[part, :, :cw] = w_in[:, at : at + cw].astype(BF16)
+        blocks[part, :, cw : cc + H] = shared
+        blocks[part, :, cc + H :] = jnp.zeros((w_in.shape[0], LANES - H), BF16)
     greet(everyone)
     swaps = []
     for k, peer in enumerate(peers):
@@ -567,6 +668,8 @@
         chans.append(copy)
     chan_keep = pltpu.make_async_copy(chan, chan_out.at[group * parts + q], local.at[2])
     chan_keep.start()
+    for part in range(parts):
+        gates[part] = w_in[:, part * cw : (part + 1) * cw].astype(BF16)
     mine.wait()
     for copy in swaps:
         copy.wait()
@@ -575,6 +678,12 @@
         copy = remote(hidden, hid_out.at[q], hid_s, hid_r, k, peer)
         copy.start()
         hids.append(copy)
+    for k, peer in enumerate(peers):
+        copy = remote(gates.at[peer[1]], gate_out.at[q], gate_s, gate_r, k, peer)
+        copy.start()
+        hids.append(copy)
+    gate_keep = pltpu.make_async_copy(gates.at[q], gate_out.at[q], local.at[3])
+    gate_keep.start()
 
     def along(from_z, up):
         block = w_out.at[2 * from_z + core]
@@ -638,30 +747,40 @@
 
     keep.wait()
     chan_keep.wait()
+    gate_keep.wait()
     for copy in hids + chans:
         copy.wait()
 
 
-def collect(collective_id, hidden, blocks, chan, groups):
-    parts, rows, width = blocks.shape
+def collect(collective_id, hidden, w_in, chan, groups, parts):
+    rows = w_in.shape[0]
     line = groups // 2
+    cw = INNER // parts
+    width = cw + 2 * N + LANES
     sem = pltpu.SemaphoreType.DMA
+    hbm = pl.BlockSpec(memory_space=pl.ANY)
     return pl.pallas_call(
         functools.partial(collect_kernel, groups, parts),
-        in_specs=[pl.BlockSpec(memory_space=pl.ANY)] * 3,
-        out_specs=[pl.BlockSpec(memory_space=pl.ANY)] * 3,
+        in_specs=[hbm, pl.BlockSpec(memory_space=pltpu.VMEM), hbm],
+        out_specs=[hbm] * 4,
         out_shape=[
             jax.ShapeDtypeStruct((parts,) + hidden.shape, hidden.dtype),
-            jax.ShapeDtypeStruct((groups, parts, rows, width), blocks.dtype),
+            jax.ShapeDtypeStruct((groups, parts, rows, width), BF16),
+            jax.ShapeDtypeStruct((parts, rows, cw), BF16),
             jax.ShapeDtypeStruct((groups * parts,) + chan.shape, chan.dtype),
         ],
         scratch_shapes=[
-            sem((groups * parts - 1,)), sem((groups * parts - 1,)), sem((parts - 1,)), sem((parts - 1,)), sem((parts - 1,)), sem((parts - 1,)),
-            sem((2, line)), sem((2, line)), sem((line,)), sem((line,)), sem((3,)),
-        ],
-        compiler_params=pltpu.CompilerParams(collective_id=collective_id, has_side_effects=True),
+            pltpu.VMEM((parts, rows, width), BF16),
+            pltpu.VMEM((parts, rows, cw), BF16),
+            *([sem((groups * parts - 1,))] * 2),
+            *([sem((parts - 1,))] * 6),
+            sem((2, line)), sem((2, line)), sem((line,)), sem((line,)), sem((4,)),
+        ],
+        compiler_params=pltpu.CompilerParams(
+            collective_id=collective_id, has_side_effects=True, vmem_limit_bytes=48 * 2**20
+        ),
         name="collect",
-    )(hidden, blocks, chan)
+    )(hidden, w_in, chan)
 
 
 def add_blocks(out, a, b, rows, steps):
@@ -673,11 +792,203 @@
     lax.fori_loop(0, steps, step, 0)
 
 
-def reduce_kernel(
-    groups, parts, rows, grad, back, small, part, back_out, small_all,
-    held, acc, down, up,
-    core_s, core_r, up_s, up_r, down_s, down_r, part_s, part_r, back_s, back_r,
-    small_s, small_r, local,
+def level_of(channel, width):
+    return sum((channel >= level_width(k)).astype(jnp.int32) for k in range(LEVELS - 1))
+
+
+def swap_back_kernel(
+    groups, parts, cw, back, u, mixed, back_out, left, right,
+    sent, held, sends, recvs, core_s, core_r, local,
+):
+    line = groups // 2
+    group, q = lax.axis_index("dp"), lax.axis_index("seq")
+    z, core = group // 2, lax.rem(group, 2)
+    sibling = (2 * z + 1 - core, q)
+    peers = seq_peers(parts)
+    greet(peers + [sibling])
+    copies = [
+        remote(back.at[peer[1]], back_out.at[q], sends, recvs, k, peer)
+        for k, peer in enumerate(peers)
+    ]
+    copies.append(pltpu.make_async_copy(back.at[q], back_out.at[q], local))
+    for copy in copies:
+        copy.start()
+    width = INNER // groups
+    rows = width // parts
+    tile = 512
+    halves = D // 2 // tile
+
+    def product(of, j):
+        channel = of * width
+        lanes = pl.ds(pl.multiple_of(lax.rem(channel, cw), width), width)
+        cols = pl.ds(pl.multiple_of(j * tile, tile), tile)
+        return dot(u[channel // cw, :, lanes], mixed[level_of(channel, width), :, cols], TN)
+
+    cores = []
+    for d in range(line):
+
+        def send_step(j, carry, d=d):
+            cols = pl.ds(pl.multiple_of(j * tile, tile), tile)
+            sent[d, :, cols] = product(2 * d + 1 - core, j).astype(BF16)
+            return carry
+
+        lax.fori_loop(0, 2 * halves, send_step, 0)
+        copy = remote(sent.at[d], held.at[d], core_s, core_r, d, sibling)
+        copy.start()
+        cores.append(copy)
+    for d in range(line):
+        cores[d].wait_recv()
+        for out, first in ((left, 0), (right, halves)):
+
+            def keep_step(j, carry, d=d, out=out, first=first):
+                at = pl.ds(pl.multiple_of((j + first) * tile, tile), tile)
+                cols = pl.ds(pl.multiple_of(j * tile, tile), tile)
+                total = product(2 * d + core, j + first) + held[d, :, at].astype(F32)
+                total = total.astype(BF16)
+                for part in range(parts):
+                    out[part, d, :, cols] = total[part * rows : (part + 1) * rows]
+                return carry
+
+            lax.fori_loop(0, halves, keep_step, 0)
+    for copy in cores:
+        copy.wait_send()
+    for copy in copies:
+        copy.wait()
+
+
+def swap_back(collective_id, back, u, mixed, groups):
+    parts, rows, wide = back.shape
+    line, width = groups // 2, INNER // groups
+    sem = pltpu.SemaphoreType.DMA
+    vmem = pl.BlockSpec(memory_space=pltpu.VMEM)
+    hbm = pl.BlockSpec(memory_space=pl.ANY)
+    return pl.pallas_call(
+        functools.partial(swap_back_kernel, groups, parts, wide - LANES),
+        in_specs=[hbm, vmem, vmem],
+        out_specs=[hbm, vmem, vmem],
+        out_shape=[
+            jax.ShapeDtypeStruct(back.shape, back.dtype),
+            *([jax.ShapeDtypeStruct((parts, line, width // parts, D // 2), BF16)] * 2),
+        ],
+        scratch_shapes=[
+            pltpu.VMEM((line, width, D), BF16),
+            pltpu.VMEM((line, width, D), BF16),
+            sem((parts - 1,)), sem((parts - 1,)), sem((line,)), sem((line,)), sem,
+        ],
+        compiler_params=pltpu.CompilerParams(
+            collective_id=collective_id, has_side_effects=True, vmem_limit_bytes=56 * 2**20
+        ),
+        name="swap_back",
+    )(back, u, mixed)
+
+
+def sum_blocks(out, blocks, rows):
+    def step(i, carry):
+        at = pl.ds(pl.multiple_of(i * rows, rows), rows)
+        total = blocks[0][at].astype(F32)
+        for block in blocks[1:]:
+            total = total + block[at].astype(F32)
+        out[at] = total.astype(out.dtype)
+        return carry
+
+    lax.fori_loop(0, out.shape[0] // rows, step, 0)
+
+
+class LineSum:
+    def __init__(self, line, z, core, q, acc, up, down, up_s, up_r, down_s, down_r, rows, steps):
+        self.line, self.z, self.core, self.q = line, z, core, q
+        self.acc, self.up, self.down = acc, up, down
+        self.up_s, self.up_r, self.down_s, self.down_r = up_s, up_r, down_s, down_r
+        self.rows, self.steps = rows, steps
+
+    def ahead(self, d, first):
+        block = self.acc.at[d] if first else self.up.at[d]
+        to = (2 * (self.z + 1) + self.core, self.q)
+        return remote(block, self.up.at[d], self.up_s, self.up_r, d, to)
+
+    def behind(self, d, first):
+        block = self.acc.at[d] if first else self.down.at[d]
+        to = (2 * (self.z - 1) + self.core, self.q)
+        return remote(block, self.down.at[d], self.down_s, self.down_r, d, to)
+
+    def add(self, into, d):
+        add_blocks(into.at[d], into.at[d], self.acc.at[d], self.rows, self.steps)
+
+    def step(self, t):
+        line, z = self.line, self.z
+        far, near = line - 1 - t + z, t - (line - 1 - z)
+
+        @pl.when(z == 0)
+        def _():
+            self.ahead(line - 1 - t, True).start()
+
+        @pl.when((z > 0) & (z <= t))
+        def _():
+            self.ahead(far, False).wait_recv()
+            self.add(self.up, far)
+            self.ahead(far, False).start()
+
+        @pl.when(z == line - 1)
+        def _():
+            self.behind(t, True).start()
+
+        @pl.when((z < line - 1) & (line - 1 - z <= t))
+        def _():
+            self.behind(near, False).wait_recv()
+            self.add(self.down, near)
+            self.behind(near, False).start()
+
+    def sent(self, t):
+        line, z = self.line, self.z
+        far, near = line - 1 - t + z, t - (line - 1 - z)
+
+        @pl.when(z == 0)
+        def _():
+            self.ahead(line - 1 - t, True).wait_send()
+
+        @pl.when((z > 0) & (z <= t))
+        def _():
+            self.ahead(far, False).wait_send()
+
+        @pl.when(z == line - 1)
+        def _():
+            self.behind(t, True).wait_send()
+
+        @pl.when((z < line - 1) & (line - 1 - z <= t))
+        def _():
+            self.behind(near, False).wait_send()
+
+    def finish(self, out):
+        line, z = self.line, self.z
+
+        @pl.when(z == 0)
+        def _():
+            self.behind(z, False).wait_recv()
+            add_blocks(out, self.acc.at[z], self.down.at[z], self.rows, self.steps)
+
+        @pl.when(z == line - 1)
+        def _():
+            self.ahead(z, False).wait_recv()
+            add_blocks(out, self.acc.at[z], self.up.at[z], self.rows, self.steps)
+
+        @pl.when((z > 0) & (z < line - 1))
+        def _():
+            self.ahead(z, False).wait_recv()
+            self.add(self.up, z)
+            self.behind(z, False).wait_recv()
+            add_blocks(out, self.up.at[z], self.down.at[z], self.rows, self.steps)
+
+
+def owners_kernel(
+    groups, parts, rows,
+    normed, left, right, gate, small, dz, dpx, wz, wx,
+    part, left_out, right_out, gate_out, back_out, small_all,
+    made, held, acc, up, down, final, left_up, left_down, right_in, right_acc, right_up, right_down,
+    normed_v, dz_v, dpx_v, wz_v, wx_v, back,
+    core_s, core_r, up_s, up_r, down_s, down_r, lup_s, lup_r, ldown_s, ldown_r,
+    rup_s, rup_r, rdown_s, rdown_r,
+    part_s, part_r, back_s, back_r, gate_s, gate_r, right_s, right_r, small_s, small_r,
+    load, local,
 ):
     line = groups // 2
     span = parts * rows
@@ -685,144 +996,170 @@
     z, core = group // 2, lax.rem(group, 2)
     sibling = (2 * z + 1 - core, q)
     peers, others = seq_peers(parts), dp_peers(groups)
+    tokens = back.shape[1]
+    loads = [
+        pltpu.make_async_copy(source, target, load.at[k])
+        for k, (source, target) in enumerate(
+            [(normed, normed_v), (dpx, dpx_v), (dz, dz_v), (wz, wz_v), (wx, wx_v)]
+        )
+    ]
+    for copy in loads:
+        copy.start()
     greet(peers + others)
-
-    def share(of):
-        return grad.at[pl.ds(pl.multiple_of(of * span, span), span)]
-
-    cores = []
-    for d in range(line):
-        copy = remote(share(2 * d + 1 - core), held.at[d], core_s, core_r, d, sibling)
-        copy.start()
-        cores.append(copy)
+    half_rows = left.shape[1] // 2
+    lefts = LineSum(
+        line, z, core, q, left, left_up, left_down, lup_s, lup_r, ldown_s, ldown_r, half_rows, 2
+    )
+    rights = LineSum(
+        line, z, core, q, right_acc, right_up, right_down, rup_s, rup_r, rdown_s, rdown_r,
+        half_rows, 2,
+    )
+    wholes = LineSum(
+        line, z, core, q, acc, up, down, up_s, up_r, down_s, down_r, rows, parts
+    )
+    lefts.step(0)
+    rights_in = []
+    for k, peer in enumerate(peers):
+        copy = remote(right.at[peer[1]], right_in.at[k], right_s, right_r, k, peer)
+        copy.start()
+        rights_in.append(copy)
     waiting = []
     for k, peer in enumerate(peers):
-        copy = remote(back.at[peer[1]], back_out.at[q], back_s, back_r, k, peer)
+        copy = remote(gate.at[peer[1]], gate_out.at[q], gate_s, gate_r, k, peer)
         copy.start()
         waiting.append(copy)
     for k, peer in enumerate(others):
         copy = remote(small, small_all.at[group], small_s, small_r, k, peer)
         copy.start()
         waiting.append(copy)
-    own_back = pltpu.make_async_copy(back.at[q], back_out.at[q], local.at[0])
-    own_back.start()
-    own_small = pltpu.make_async_copy(small, small_all.at[group], local.at[1])
-    own_small.start()
+    own = [
+        pltpu.make_async_copy(gate.at[q], gate_out.at[q], local.at[0]),
+        pltpu.make_async_copy(small, small_all.at[group], local.at[1]),
+    ]
+    for copy in own:
+        copy.start()
+    loads[0].wait()
+    loads[1].wait()
+    tile = 512
+
+    def dweight(of, out):
+        at = pl.ds(pl.multiple_of(of * span, span), span)
+        out[...] = dot(normed_v[:, at], dpx_v[...], TN).astype(BF16)
+
+    cores = []
+    for d in range(line):
+        dweight(2 * d + 1 - core, made.at[d])
+        copy = remote(made.at[d], held.at[d], core_s, core_r, d, sibling)
+        copy.start()
+        cores.append(copy)
+    for d in range(line):
+        dweight(2 * d + core, acc.at[d])
     for d in range(line):
         cores[d].wait()
-        add_blocks(acc.at[d], share(2 * d + core), held.at[d], rows, parts)
-
-    def ahead(d, first):
-        block = acc.at[d] if first else up.at[d]
-        return remote(block, up.at[d], up_s, up_r, d, (2 * (z + 1) + core, q))
-
-    def behind(d, first):
-        block = acc.at[d] if first else down.at[d]
-        return remote(block, down.at[d], down_s, down_r, d, (2 * (z - 1) + core, q))
-
-    for t in range(line - 1):
-        far = line - 1 - t + z
-
-        @pl.when((z == 0) & (z < line - 1))
-        def _():
-            ahead(line - 1 - t, True).start()
-
-        @pl.when((z > 0) & (z <= t) & (z < line - 1))
-        def _():
-            ahead(far, False).wait_recv()
-            add_blocks(up.at[far], up.at[far], acc.at[far], rows, parts)
-            ahead(far, False).start()
-
-        near = t - (line - 1 - z)
-
-        @pl.when((z == line - 1) & (z > 0))
-        def _():
-            behind(t, True).start()
-
-        @pl.when((z < line - 1) & (line - 1 - z <= t) & (z > 0))
-        def _():
-            behind(near, False).wait_recv()
-            add_blocks(down.at[near], down.at[near], acc.at[near], rows, parts)
-            behind(near, False).start()
-
-    @pl.when(z > 0)
-    def _():
-        ahead(z, False).wait_recv()
-        add_blocks(acc.at[z], acc.at[z], up.at[z], rows, parts)
-
-    @pl.when(z < line - 1)
-    def _():
-        behind(z, False).wait_recv()
-        add_blocks(acc.at[z], acc.at[z], down.at[z], rows, parts)
-
-    parts_copies = []
+        add_blocks(acc.at[d], acc.at[d], held.at[d], rows, parts)
+    lefts.sent(0)
+    wholes.step(0)
+    for copy in loads[2:]:
+        copy.wait()
+
+    def dnormed(of):
+        at = pl.ds(pl.multiple_of(of * tokens, tokens), tokens)
+
+        def step(j, carry):
+            cols = pl.ds(pl.multiple_of(j * tile, tile), tile)
+            back[of, :, cols] = (
+                dot(dz_v[at, :], wz_v[cols, :], NT) + dot(dpx_v[at, :], wx_v[cols, :], NT)
+            ).astype(BF16)
+            return carry
+
+        lax.fori_loop(0, D // tile, step, 0)
+
     for k, peer in enumerate(peers):
-        block = acc.at[z, pl.ds(pl.multiple_of(peer[1] * rows, rows), rows)]
+        dnormed(peer[1])
+        copy = remote(back.at[peer[1]], back_out.at[q], back_s, back_r, k, peer)
+        copy.start()
+        waiting.append(copy)
+    dnormed(q)
+    copy = pltpu.make_async_copy(back.at[q], back_out.at[q], local.at[2])
+    copy.start()
+    own.append(copy)
+    for t in range(1, line - 1):
+        wholes.sent(t - 1)
+        lefts.step(t)
+        lefts.sent(t)
+        wholes.step(t)
+    lefts.finish(left_out)
+    for copy in rights_in:
+        copy.wait()
+    for d in range(line):
+        sum_blocks(
+            right_acc.at[d],
+            [right.at[q, d]] + [right_in.at[k, d] for k in range(parts - 1)],
+            16,
+        )
+    wholes.sent(line - 2)
+    rights.step(0)
+    wholes.finish(final)
+    for k, peer in enumerate(peers):
+        block = final.at[pl.ds(pl.multiple_of(peer[1] * rows, rows), rows)]
         copy = remote(block, part.at[q], part_s, part_r, k, peer)
         copy.start()
-        parts_copies.append(copy)
-    own = pltpu.make_async_copy(
-        acc.at[z, pl.ds(pl.multiple_of(q * rows, rows), rows)], part.at[q], local.at[2]
-    )
-    own.start()
-    for t in range(line - 1):
-        far = line - 1 - t + z
-        near = t - (line - 1 - z)
-
-        @pl.when((z == 0) & (z < line - 1))
-        def _():
-            ahead(line - 1 - t, True).wait_send()
-
-        @pl.when((z > 0) & (z <= t) & (z < line - 1))
-        def _():
-            ahead(far, False).wait_send()
-
-        @pl.when((z == line - 1) & (z > 0))
-        def _():
-            behind(t, True).wait_send()
-
-        @pl.when((z < line - 1) & (line - 1 - z <= t) & (z > 0))
-        def _():
-            behind(near, False).wait_send()
-
-    own.wait()
-    own_back.wait()
-    own_small.wait()
-    for copy in parts_copies + waiting:
+        waiting.append(copy)
+    copy = pltpu.make_async_copy(
+        final.at[pl.ds(pl.multiple_of(q * rows, rows), rows)], part.at[q], local.at[3]
+    )
+    copy.start()
+    own.append(copy)
+    for t in range(1, line - 1):
+        rights.sent(t - 1)
+        rights.step(t)
+    rights.finish(right_out)
+    rights.sent(line - 2)
+    for copy in own + waiting:
         copy.wait()
 
 
-def reduce_to_owners(collective_id, grad, back, small, groups):
-    parts = back.shape[0]
-    line = groups // 2
-    rows = grad.shape[0] // (groups * parts)
-    span, width = rows * parts, grad.shape[1]
+def sum_to_owners(collective_id, normed, left, right, gate, small, dz, dpx, wz, wx):
+    parts, line, out_rows, half = right.shape
+    groups = 2 * line
+    rows = gate.shape[1]
+    span, width = rows * parts, dpx.shape[1]
+    tokens = dz.shape[0] // parts
     sem = pltpu.SemaphoreType.DMA
     vmem = pl.BlockSpec(memory_space=pltpu.VMEM)
     hbm = pl.BlockSpec(memory_space=pl.ANY)
     return pl.pallas_call(
-        functools.partial(reduce_kernel, groups, parts, rows),
-        in_specs=[vmem, hbm, vmem],
-        out_specs=[hbm, hbm, vmem],
+        functools.partial(owners_kernel, groups, parts, rows),
+        in_specs=[hbm, vmem, vmem, hbm, vmem, hbm, hbm, hbm, hbm],
+        out_specs=[hbm, vmem, vmem, hbm, hbm, vmem],
         out_shape=[
-            jax.ShapeDtypeStruct((parts, rows, width), grad.dtype),
-            jax.ShapeDtypeStruct(back.shape, back.dtype),
-            jax.ShapeDtypeStruct((groups,) + small.shape, small.dtype),
+            jax.ShapeDtypeStruct((parts, rows, width), BF16),
+            *([jax.ShapeDtypeStruct((out_rows, half), F32)] * 2),
+            jax.ShapeDtypeStruct(gate.shape, BF16),
+            jax.ShapeDtypeStruct((parts, tokens, D), BF16),
+            jax.ShapeDtypeStruct((groups,) + small.shape, F32),
         ],
         scratch_shapes=[
-            pltpu.VMEM((line, span, width), grad.dtype),
-            pltpu.VMEM((line, span, width), grad.dtype),
-            pltpu.VMEM((line, span, width), grad.dtype),
-            pltpu.VMEM((line, span, width), grad.dtype),
-            sem((line,)), sem((line,)), sem((line,)), sem((line,)), sem((line,)), sem((line,)),
-            sem((parts - 1,)), sem((parts - 1,)), sem((parts - 1,)), sem((parts - 1,)),
-            sem((groups - 1,)), sem((groups - 1,)), sem((3,)),
+            *([pltpu.VMEM((line, span, width), BF16)] * 5),
+            pltpu.VMEM((span, width), BF16),
+            *([pltpu.VMEM(left.shape, BF16)] * 2),
+            pltpu.VMEM((parts - 1,) + left.shape, BF16),
+            *([pltpu.VMEM(left.shape, BF16)] * 3),
+            *[pltpu.VMEM(a.shape, BF16) for a in (normed, dz, dpx, wz, wx)],
+            pltpu.VMEM((parts, tokens, D), BF16),
+            *([sem((line,))] * 14),
+            *([sem((parts - 1,))] * 8),
+            *([sem((groups - 1,))] * 2),
+            sem((5,)),
+            sem((4,)),
         ],
         compiler_params=pltpu.CompilerParams(
-            collective_id=collective_id, has_side_effects=True, vmem_limit_bytes=48 * 2**20
+            collective_id=collective_id, has_side_effects=True, vmem_limit_bytes=63 * 2**20
         ),
-        name="reduce_to_owners",
-    )(grad, back, small)
+        name="sum_to_owners",
+    )(normed, left, right, gate, small, dz, dpx, wz, wx)
+
+
 def adam_step(weight, gradient, moment, second, step_rate, weight_decay):
     new_moment = BETA * moment + (1.0 - BETA) * gradient
     new_second = BETA * second + (1.0 - BETA) * gradient * gradient
@@ -857,27 +1194,28 @@
     in_rows = w_in.shape[0]
     out_rows = w_out.shape[0]
 
-    in_low = w_in.astype(BF16)
-    out_low = w_out.astype(BF16)
-    z_blocks = in_low[:, :INNER].reshape(in_rows, parts, cw).transpose(1, 0, 2)
-    x_blocks = in_low[:, INNER : 2 * INNER].reshape(in_rows, parts, cw).transpose(1, 0, 2)
-    bc_block = jnp.broadcast_to(
-        in_low[None, :, 2 * INNER : 2 * INNER + 2 * N], (parts, in_rows, 2 * N)
-    )
-    dt_blocks = in_low[:, 2 * INNER + 2 * N :].reshape(in_rows, parts, hq).transpose(1, 0, 2)
-    dt_blocks = jnp.pad(dt_blocks, ((0, 0), (0, 0), (0, LANES - hq)))
-    x_blocks = jnp.concatenate([x_blocks, bc_block, dt_blocks], axis=2)
     chan_len = chan_params.shape[0]
     chan_rows = -(-chan_len // (8 * LANES)) * 8
     chan_block = jnp.pad(
         lax.reduce_precision(chan_params, 8, 7), (0, chan_rows * LANES - chan_len)
     ).reshape(chan_rows, LANES)
-    hidden, wx, chan_full = collect(0, hidden_in[0], x_blocks, chan_block, groups)
+    hidden, wx, wz, chan_full = collect(0, hidden_in[0], w_in, chan_block, groups, parts)
+    out_low, chan_full = lax.optimization_barrier((w_out.astype(BF16), chan_full))
+    wo = lax.all_gather(out_low, ("dp", "seq"), axis=0, tiled=True)
     hidden = hidden.reshape(length, D)
     wx = wx.reshape(D, cc + LANES)
     chan_full = chan_full.reshape(groups * parts, chan_rows * LANES)[:, :chan_len].reshape(-1)
-    wz = lax.all_gather(swap(1, z_blocks)[0], "dp", axis=0).reshape(D, cw)
-    wo = lax.all_gather(out_low, ("dp", "seq"), axis=0, tiled=True)
+    line = groups // 2
+    group = lax.axis_index("dp")
+    core, place = group % 2, group // 2
+    wz_line = jnp.zeros((line,) + wz.shape, BF16)
+    wz_line = lax.dynamic_update_index_in_dim(wz_line, wz, place, 0)
+    for k in range(1, line):
+        block = lax.ppermute(wz, "dp", [(i, i ^ (2 * k)) for i in range(groups)])
+        wz_line = lax.dynamic_update_index_in_dim(wz_line, block, place ^ k, 0)
+    other = lax.ppermute(wz_line, "dp", [(i, i ^ 1) for i in range(groups)])
+    wz = jnp.where(core == 0, jnp.stack([wz_line, other], 1), jnp.stack([other, wz_line], 1))
+    wz = wz.reshape(D, cw)
 
     conv_taps = chan_full[: TAPS * CONV_CH].reshape(TAPS, CONV_CH)
     conv_bias = chan_full[TAPS * CONV_CH : (TAPS + 1) * CONV_CH].reshape(1, CONV_CH)
@@ -924,16 +1262,8 @@
     cotangent = out_grads[:, 0]
     block_out, back_blocks, mixed = widths(u, wo, cotangent, hidden_in[0])
     block_out = block_out[:, None]
-    back_own = swap(3, back_blocks)[0].reshape(length, cw + LANES)
-    u = u[:, :, :cw].transpose(1, 0, 2).reshape(rows, INNER)
-    dwo = jnp.concatenate(
-        [dot(u[:, low:high], mixed[k], TN).astype(BF16) for k, (low, high) in enumerate(SEGMENTS)],
-        axis=0,
-    )
-    dwo = lax.psum_scatter(
-        dwo.reshape(groups, parts, out_rows, D).transpose(1, 0, 2, 3), "seq", scatter_dimension=0
-    )
-    out_part = lax.psum_scatter(dwo, "dp", scatter_dimension=0).astype(F32)
+    back_own, dwo_left, dwo_right = swap_back(3, back_blocks, u, mixed, groups)
+    back_own = back_own.reshape(length, cw + LANES)
 
     coefs = unpack_terms(back_own[:, cw:], LEVELS)
     pull = coefs[:, LEVELS - 1 :]
@@ -945,19 +1275,20 @@
     dz = (dgated * y * (sig + gate * (1.0 - sig))).astype(BF16)
     dy = dgated * gate
     dwz = dot(normed, dz, TN).astype(BF16)
-    dwz = lax.psum_scatter(dwz, "dp", scatter_dimension=0, tiled=True)
-    dpx, dtaps, dheads, dskip = scan_backward(
-        px, taps, heads, skip, spread, spread.T, dy, y, states
-    )
-    dwx = dot(normed, dpx, TN).astype(BF16)
-    dnormed = (dot(dz, wz, NT) + dot(dpx, wx, NT)).astype(BF16)
+    dwz = dwz.reshape(line, 2, parts * in_rows, cw)
+    dpx, dtaps, dheads, dskip, dwo_left, dwz = scan_backward(
+        5, px, taps, heads, skip, spread, spread.T, dy, y, states, dwo_left, dwz
+    )
     skip_grad = jnp.sum(dskip[0].reshape(hq, P_SIZE), axis=-1)
     small = jnp.concatenate(
         [dtaps[: TAPS + 1].reshape(-1), dgain_out, dheads[0, :hq], dheads[1, :hq], skip_grad]
     )
     small_rows = -(-small.shape[0] // (8 * LANES)) * 8
     small = jnp.pad(small, (0, small_rows * LANES - small.shape[0])).reshape(small_rows, LANES)
-    x_part, dnormed, small = reduce_to_owners(4, dwx, dnormed.reshape(parts, rows, D), small, groups)
+    x_part, left_part, right_part, z_part, dnormed, small = sum_to_owners(
+        4, normed, dwo_left, dwo_right, dwz.reshape(parts, in_rows, cw), small, dz, dpx, wz, wx
+    )
+    out_part = jnp.concatenate([left_part, right_part], axis=1)
     dnormed = jnp.sum(dnormed.astype(F32), axis=0)
     small = jnp.sum(small, axis=0)
     own_scale = lax.rsqrt(jnp.mean(own_tokens * own_tokens, axis=-1, keepdims=True) + EPS_IN)
@@ -970,14 +1301,13 @@
         + jnp.sum(cotangent.astype(F32), axis=0)
     )[None]
 
-    z_part = swap(5, dwz.reshape(parts, in_rows, cw))[0].astype(F32)
+    z_part = z_part.astype(F32)
     x_part = x_part.astype(F32)
     in_part = jnp.concatenate(
         [
             z_part.transpose(1, 0, 2).reshape(in_rows, INNER),
             x_part[:, :, :cw].transpose(1, 0, 2).reshape(in_rows, INNER),
-            jnp.sum(x_part[:, :, cw:cc], axis=0),
-            x_part[:, :, cc : cc + hq].transpose(1, 0, 2).reshape(in_rows, H),
+            jnp.sum(x_part[:, :, cw : cc + H], axis=0),
         ],
         axis=1,
     )

time: 663 us -> 576 us (0.87)
  matrix products: 63.3 us -> 21.8 us
  waiting for transfers between devices: 63.5 us -> 40.3 us
  Pallas kernels: 410 us -> 387 us
    pallas_call x2 -> x3, Pallas kernels: 132 us -> 213 us  [the longest x1 116 us: sum_to_owners(): pl.pallas_call(functools.partial(owners_kernel, groups, parts, rows), in_...]
    unnamed x6 -> x1, waiting for transfers between devices: 63.5 us -> 0.02 us
    pallas_call x4 -> x1, Pallas kernels: 98.4 us -> 49.2 us  [swap(): pl.pallas_call(functools.partial(swap_kernel, parts, count), in_specs=[pl...]
    pallas_call x1, Pallas kernels: 117 us -> 71.6 us  [collect(): pl.pallas_call(functools.partial(collect_kernel, groups, parts), in_specs...]
    dot_general x10 -> x3, matrix products: 63.3 us -> 21.8 us  [dot(): lax.dot_general(a, b, (dims, ((), ())), precision=precision, preferred_el...]
    ppermute x0 -> x4, waiting for transfers between devices: none -> 25.1 us  [the longest x3 25.1 us: on_device(): block = lax.ppermute(wz, 'dp', [(i, i ^ 2 * k) for i in range(groups)])]
    all_gather x1, waiting for transfers between devices: 0.01 us -> 15.2 us  [on_device(): wo = lax.all_gather(out_low, ('dp', 'seq'), axis=0, tiled=True)]
    pallas_call x1, Pallas kernels: 23.7 us -> 13.8 us  [broadcast(): pl.pallas_call(functools.partial(broadcast_kernel, groups, parts), in_spe...]
  transfers between devices with their start and end apart: 5 -> 5, of which waited for: 1 -> 3; matrix products, arithmetic and copies ran while one was open for 17% -> 7% of each run, Pallas kernels for 54% -> 12%
where the time goes in v3:
time: 576 us; the launch traced here: 566 us
  Pallas kernels  387 us (67%)
  other arithmetic  57.7 us (10%)
  waiting for transfers between devices  40.3 us (7%)
  local copies, waits for them, and re-layouts  33.9 us (6%)
  matrix products  21.8 us (4%)
  between operations  19.7 us (3%)
  starting transfers between devices  6.48 us (1%)
    pallas_call x1, Pallas kernels, sum_to_owners(): pl.pallas_call(functools.partial(owners_kernel, groups, parts, rows), in_...  116 us
    pallas_call x1, Pallas kernels, collect(): pl.pallas_call(functools.partial(collect_kernel, groups, parts), in_specs...  71.6 us
    pallas_call x1, Pallas kernels, scan_backward(): pl.pallas_call(functools.partial(scan_backward_kernel, 2 * line, parts, c...  62.6 us
    pallas_call x1, Pallas kernels, swap(): pl.pallas_call(functools.partial(swap_kernel, parts, count), in_specs=[pl...  49.2 us
    pallas_call x1, Pallas kernels, swap_back(): pl.pallas_call(functools.partial(swap_back_kernel, groups, parts, wide -...  33.6 us
    ppermute x3, waiting for transfers between devices, on_device(): block = lax.ppermute(wz, 'dp', [(i, i ^ 2 * k) for i in range(groups)])  25.1 us
    dot_general x3, matrix products, dot(): lax.dot_general(a, b, (dims, ((), ())), precision=precision, preferred_el...  21.8 us
    pallas_call x1, Pallas kernels, widths(): pl.pallas_call(functools.partial(widths_kernel, cw), grid=(INNER // WIDE,...  21.4 us
  transfers between devices with their start and end apart: 5, of which 3 were waited for; matrix products, arithmetic and copies ran while one was open for 7% of the time, Pallas kernels for 12%

profile of v3, /device:TPU:1, one launch (start us, length us, event | category | flops | bytes accessed | tf_op | source)
XLA Modules:
  0.0 566.4 jit_solution(8465362000968657527)
XLA Ops:
  7.3 0.8 reduce_precision.6
  8.0 2.1 convert_element_type.75
  10.1 1.2 copy-done
  11.3 1.6 copy-done.4
  13.0 71.6 %collect.1 = (bf16[4,256,2048]{2,1,0:T(8,128)(2,1)}, bf16[8,4,64,1408]{3,2,1,0:T(8,128)(2,1)}, bf16[4,64,1024]{2,1,0:T(8,128)(2,1)S(1)}, f32[32,8,128]{2,1,0:T(8,128)S(1)}) custom-call(bf16[256,2048]{1,0:T(8,128)(2,1)S(1)} %bitcast.95, f32[64,8512]{1,0:T(8,128)S(1)} %copy-done.4, f32[8,128]{1,0:T(8,128)S(1)} %pad_bitcast_fusion.1.chan), custom_call_target="tpu_custom_call" | custom-call | tf_op jit(solution)/shard_map/collect/pallas_call | solution.py:762
  84.7 1.7 collective-permute-start.1
  86.4 1.8 collective-permute-start.2
  89.0 3.2 multiply_reduce_fusion
  92.2 1.6 broadcast_in_dim.119
  93.8 0.8 bitcast_dynamic-update-slice_fusion.3
  94.6 1.0 multiply_convert_fusion
  96.3 8.5 %fusion.46.px.halo = f32[1024,1408]{1,0:T(8,128)} fusion(bf16[1024,2048]{1,0:T(8,128)(2,1)S(1)} %bitcast.110, bf16[2048,1408]{1,0:T(8,128)(2,1)S(1)} %bitcast.109), kind=kOutput, calls=%fused_computation.133 | convolution fusion | flops 5905580032 | bytes 15728640 | tf_op jit(solution)/shard_map/dot_general | solution.py:44
  104.8 13.5 %collective-permute-done = bf16[4,64,1024]{2,1,0:T(8,128)(2,1)S(1)} collective-permute-done((bf16[4,64,1024]{2,1,0:T(8,128)(2,1)S(1)}, bf16[4,64,1024]{2,1,0:T(8,128)(2,1)S(1)}, u32[]{:S(2)}, u32[]{:S(2)}) %collective-permute-start) | collective-permute-done | bytes 524320 | tf_op jit(solution)/shard_map/ppermute | solution.py:1214
  118.3 0.8 bitcast_dynamic-update-slice_fusion.2
  119.2 0.8 bitcast_dynamic-update-slice_fusion.1
  120.0 11.5 %collective-permute-done.2 = bf16[4,64,1024]{2,1,0:T(8,128)(2,1)S(1)} collective-permute-done((bf16[4,64,1024]{2,1,0:T(8,128)(2,1)S(1)}, bf16[4,64,1024]{2,1,0:T(8,128)(2,1)S(1)}, u32[]{:S(2)}, u32[]{:S(2)}) %collective-permute-start.2) | collective-permute-done | bytes 524320 | tf_op jit(solution)/shard_map/ppermute | solution.py:1214
  131.5 0.8 bitcast_dynamic-update-slice_fusion
  132.4 2.8 collective-permute-start.3
  135.5 0.9 fusion.17.gather
  136.4 18.0 %scan_forward.1 = (f32[1024,1024]{1,0:T(8,128)}, bf16[8,128,1024]{2,1,0:T(8,128)(2,1)S(1)}) custom-call(f32[1024,1408]{1,0:T(8,128)} %fusion.46.px.halo, f32[8,1280]{1,0:T(8,128)S(1)} %pad_maximum_fusion.3.taps, f32[8,128]{1,0:T(8,128)S(1)} %select_maximum_fusion.heads, f32[1,1024]{1,0:T(1,128)S(1)} %reshape_reshape.3.skip, bf16[128,1024]{1,0:T(8,128)(2,1)S(1)} %fusion.16.spread), custom_call_target="tpu_custom_call" | custom-call | flops 3000000000 | bytes 40000000 | tf_op jit(solution)/shard_map/scan_forward/pallas_call | solution.py:321
  154.4 2.1 convert_reduce_fusion
  156.5 1.6 copy-done.13
  158.1 3.0 fusion.1.normed
  161.2 4.1 maximum_select_fusion
  165.8 2.8 copy-done.29
  168.6 7.1 %multiply_convert_fusion.2 = (bf16[1024,1024]{1,0:T(8,128)(2,1)S(1)}, f32[1024,1024]{1,0:T(8,128)S(1)}, f32[1024,1024]{1,0:T(8,128)}) fusion(f32[1024]{0:T(1024)S(1)} %dynamic_slice.14, f32[1024,1024]{1,0:T(8,128)S(1)} %copy-done.29, bf16[1024,2048]{1,0:T(8,128)(2,1)S(1)} %bitcast.111, bf16[2048,1024]{1,0:T(8,128)(2,1)S(1)} %bitcast.99), kind=kOutput, calls=%fused_computation.20 | convolution fusion | flops 4302307328 | bytes 23072768 | tf_op jit(solution)/shard_map/dot_general | solution.py:44
  175.7 2.0 copy-done.19
  177.7 1.4 select_reduce_fusion.3
  179.3 1.6 fusion.7
  180.9 49.2 %swap.1.u = bf16[4,256,1152]{2,1,0:T(8,128)(2,1)} custom-call(bf16[4,256,1152]{2,1,0:T(8,128)(2,1)} %bitcast.105), custom_call_target="tpu_custom_call" | custom-call | tf_op jit(solution)/shard_map/swap/pallas_call | solution.py:564
  230.1 15.2 %all-gather.2.cloned.1.call-done.wo = bf16[4096,2048]{1,0:T(8,128)(2,1)} async-done(((bf16[128,2048]{1,0:T(8,128)(2,1)}), bf16[4096,2048]{1,0:T(8,128)(2,1)}) %all-gather.2.cloned.1.call-update) | async-done | bytes 16777232 | tf_op jit(solution)/shard_map/all_gather | solution.py:1204
  245.3 1.7 copy-done.3
  247.0 21.4 %widths.1 = (bf16[4,256,2048]{2,1,0:T(8,128)(2,1)}, bf16[4,256,1152]{2,1,0:T(8,128)(2,1)S(1)}, bf16[4,256,2048]{2,1,0:T(8,128)(2,1)}) custom-call(bf16[4,256,1152]{2,1,0:T(8,128)(2,1)S(1)} %copy-done.3, bf16[4096,2048]{1,0:T(8,128)(2,1)} %all-gather.2.cloned.1.call-done.wo, bf16[4,256,2048]{2,1,0:T(8,128)(2,1)} %bitcast.98, bf16[256,2048]{1,0:T(8,128)(2,1)S(1)} %bitcast.96), custom_call_target="tpu_custom_call" | custom-call | tf_op jit(solution)/shard_map/widths/pallas_call | solution.py:481
  268.4 1.5 copy-done.6
  269.9 33.6 %swap_back.1 = (bf16[4,256,1152]{2,1,0:T(8,128)(2,1)}, bf16[4,4,128,1024]{3,2,1,0:T(8,128)(2,1)}, bf16[4,4,128,1024]{3,2,1,0:T(8,128)(2,1)}) custom-call(bf16[4,256,1152]{2,1,0:T(8,128)(2,1)} %copy-done.6, bf16[4,256,1152]{2,1,0:T(8,128)(2,1)} %swap.1.u, bf16[4,256,2048]{2,1,0:T(8,128)(2,1)} %get-tuple-element.54.mixed), custom_call_target="tpu_custom_call" | custom-call | tf_op jit(solution)/shard_map/swap_back/pallas_call | solution.py:865
  303.5 1.1 slice_convert_fusion
  304.9 1.0 slice_reduce_fusion.3
  306.0 10.6 %multiply_convert_fusion.1 = (bf16[1024,1024]{1,0:T(8,128)(2,1)S(1)}, f32[1024,1024]{1,0:T(8,128)}, f32[1024]{0:T(1024)S(1)}) fusion(f32[1024,1024]{1,0:T(8,128)S(1)} %copy-done.30, f32[1024,1024]{1,0:T(8,128)S(1)} %copy-done.20, f32[1024,1024]{1,0:T(8,128)} %get-tuple-element.181, f32[1024]{0:T(1024)S(1)} %get-tuple-element.148, ...), kind=kLoop, calls=%fused_computation.14 | loop fusion | flops 20970496 | bytes 20999168 | tf_op jit(solution)/shard_map/convert_element_type | solution.py:1275
  316.5 6.2 %convolution_convert_fusion = bf16[2048,1024]{1,0:T(8,128)(2,1)} fusion(bf16[1024,2048]{1,0:T(8,128)(2,1)S(1)} %copy-done.17, bf16[1024,1024]{1,0:T(8,128)(2,1)S(1)} %get-tuple-element.167.dz), kind=kOutput, calls=%fused_computation.22 | convolution fusion | flops 4297064448 | bytes 10485760 | tf_op jit(solution)/shard_map/dot_general | solution.py:44
  322.8 62.6 %scan_backward.1 = (bf16[1024,1408]{1,0:T(8,128)(2,1)}, f32[8,1280]{1,0:T(8,128)}, f32[8,128]{1,0:T(8,128)}, f32[8,1024]{1,0:T(8,128)}, bf16[4,128,1024]{2,1,0:T(8,128)(2,1)}, /*index=5*/bf16[256,1024]{1,0:T(8,128)(2,1)}) custom-call(f32[1024,1408]{1,0:T(8,128)} %fusion.46.px.halo, f32[1024,1408]{1,0:T(8,128)} %fusion.46.px.halo, f32[8,1280]{1,0:T(8,128)} %copy-done.8, ...), custom_call_target="tpu_custom_call" | custom-call | flops 10000000000 | bytes 100000000 | tf_op jit(solution)/shard_map/scan_backward/pallas_call | solution.py:363
  385.3 0.8 reshape.279
  386.1 0.8 slice_reduce_fusion.6
  387.1 0.7 slice_bitcast_fusion.3
  388.5 116.4 %sum_to_owners.1 = (bf16[4,64,1408]{2,1,0:T(8,128)(2,1)}, f32[128,1024]{1,0:T(8,128)}, f32[128,1024]{1,0:T(8,128)}, bf16[4,64,1024]{2,1,0:T(8,128)(2,1)}, bf16[4...) custom-call(bf16[1024,2048]{1,0:T(8,128)(2,1)} %fusion.1.normed, bf16[4,128,1024]{2,1,0:T(8,128)(2,1)} %get-tuple-element.58.left, ...), custom_call_target="tpu_custom_call" | custom-call | tf_op jit(solution)/shard_map/sum_to_owners/pallas_call | solution.py:1131
  504.9 1.3 convert_element_type.92
  506.5 1.0 copy-done.25
  507.5 0.9 multiply_reduce_fusion.2
  508.4 1.1 copy.63
  509.6 1.1 copy.62
  510.6 0.8 convert_reduce_fusion.1
  511.5 1.8 reduce_sum.192.near
  513.2 2.7 multiply_reduce_fusion.1
  518.5 13.8 %broadcast.316 = (f32[24,128]{1,0:T(8,128)}, f32[4,64,128]{2,1,0:T(8,128)}) custom-call(f32[24,128]{1,0:T(8,128)} %concatenate.38.block, f32[64,128]{1,0:T(8,128)} %reduce_sum.192.near), custom_call_target="tpu_custom_call" | custom-call | tf_op jit(solution)/shard_map/broadcast/pallas_call | solution.py:617
  532.3 1.0 copy.71
  534.6 0.9 reshape.286
  535.6 0.7 slice_bitcast_fusion.1
  536.3 0.7 slice_bitcast_fusion.2
  537.0 1.2 slice.113
  538.2 1.3 multiply_reduce_fusion.4
  540.2 1.6 pad_maximum_fusion.2
  544.7 4.8 fusion.41
  549.5 5.2 fusion.43
  554.7 1.9 bitcast_add_fusion
  557.2 0.7 multiply_subtract_fusion.2
  (145 shorter events, 8.6 us)
Async XLA Ops:
  7.2 81.5 %copy-start.1 = (bf16[1,256,2048]{2,1,0:T(8,128)(2,1)S(1)}, bf16[1,256,2048]{2,1,0:T(8,128)(2,1)}, u32[]{:S(2)}) copy-start(bf16[1,256,2048]{2,1,0:T(8,128)(2,1)} %param.14) | copy-start | bytes 3145732
  7.2 81.4 %copy-start.37 = (f32[3,64]{1,0:T(4,128)S(1)}, f32[3,64]{1,0:T(4,128)}, u32[]{:S(2)}) copy-start(f32[3,64]{1,0:T(4,128)} %param.25) | copy-start | bytes 2308
  7.2 238.1 %all-gather.2.cloned.1.call-start = ((), (), s32[]{:S(2)}) async-start(), calls=%async_computation | async-start | bytes 17301504 | tf_op jit(solution)/shard_map/all_gather | solution.py:1204
  10.1 1.2 copy-start
  11.3 1.6 copy-start.4
  84.6 33.7 %collective-permute-start = (bf16[4,64,1024]{2,1,0:T(8,128)(2,1)S(1)}, bf16[4,64,1024]{2,1,0:T(8,128)(2,1)S(1)}, u32[]{:S(2)}, u32[]{:S(2)}) collective-permute-start(bf16[4,64,1024]{2,1,0:T(8,128)(2,1)S(1)} %get-tuple-element.50), channel_id=1, source_target_pairs={{0,8},{4,12},{8,0},{12,4},{16,24},{20,28},{24,16},{28,20},{1,9},{5... | collective-permute-start | bytes 1572872 | tf_op jit(solution)/shard_map/ppermute | solution.py:1214
  84.7 34.5 %collective-permute-start.1 = (bf16[4,64,1024]{2,1,0:T(8,128)(2,1)S(1)}, bf16[4,64,1024]{2,1,0:T(8,128)(2,1)S(1)}, u32[]{:S(2)}, u32[]{:S(2)}) collective-permute-start(bf16[4,64,1024]{2,1,0:T(8,128)(2,1)S(1)} %get-tuple-element.50), channel_id=1, source_target_pairs={{0,16},{4,20},{8,24},{12,28},{16,0},{20,4},{24,8},{28,12},{1,17},{... | collective-permute-start | bytes 1572872 | tf_op jit(solution)/shard_map/ppermute | solution.py:1214
  86.4 45.1 %collective-permute-start.2 = (bf16[4,64,1024]{2,1,0:T(8,128)(2,1)S(1)}, bf16[4,64,1024]{2,1,0:T(8,128)(2,1)S(1)}, u32[]{:S(2)}, u32[]{:S(2)}) collective-permute-start(bf16[4,64,1024]{2,1,0:T(8,128)(2,1)S(1)} %get-tuple-element.50), channel_id=1, source_target_pairs={{0,24},{4,28},{8,16},{12,20},{16,8},{20,12},{24,0},{28,4},{1,25},{... | collective-permute-start | bytes 1572872 | tf_op jit(solution)/shard_map/ppermute | solution.py:1214
  88.7 6.0 %copy-start.12 = (bf16[4,256,2048]{2,1,0:T(8,128)(2,1)S(1)}, bf16[4,256,2048]{2,1,0:T(8,128)(2,1)}, u32[]{:S(2)}) copy-start(bf16[4,256,2048]{2,1,0:T(8,128)(2,1)} %get-tuple-element.45) | copy-start | bytes 12582916
  92.2 3.6 slice-start
  94.6 1.6 slice-start.1
  95.7 9.1 %copy-start.27 = (bf16[4,256,2048]{2,1,0:T(8,128)(2,1)}, bf16[4,256,2048]{2,1,0:T(8,128)(2,1)S(1)}, u32[]{:S(2)}) copy-start(bf16[4,256,2048]{2,1,0:T(8,128)(2,1)S(1)} %multiply_convert_fusion) | copy-start | bytes 12582916
  104.8 49.6 %copy-start.10 = (f32[8,128]{1,0:T(8,128)}, f32[8,128]{1,0:T(8,128)S(1)}, u32[]{:S(2)}) copy-start(f32[8,128]{1,0:T(8,128)S(1)} %select_maximum_fusion.heads) | copy-start | bytes 12292
  132.4 28.8 %collective-permute-start.3 = (bf16[4,4,64,1024]{3,2,1,0:T(8,128)(2,1)}, bf16[4,4,64,1024]{3,2,1,0:T(8,128)(2,1)}, u32[]{:S(2)}, u32[]{:S(2)}) collective-permute-start(bf16[4,4,64,1024]{3,2,1,0:T(8,128)(2,1)} %bitcast_dynamic-update-slice_fusion), channel_id=1, source_target_pairs={{0,4},{4,0},{8,12},{12,8},{16,20},{20,16},{24,28},{28,24},{1,5},{5... | collective-permute-start | bytes 6291464 | tf_op jit(solution)/shard_map/ppermute | solution.py:1216
  135.4 19.0 %copy-start.9 = (f32[1,1024]{1,0:T(1,128)}, f32[1,1024]{1,0:T(1,128)S(1)}, u32[]{:S(2)}) copy-start(f32[1,1024]{1,0:T(1,128)S(1)} %reshape_reshape.3.skip) | copy-start | bytes 12292
  135.4 19.0 %copy-start.8 = (f32[8,1280]{1,0:T(8,128)}, f32[8,1280]{1,0:T(8,128)S(1)}, u32[]{:S(2)}) copy-start(f32[8,1280]{1,0:T(8,128)S(1)} %pad_maximum_fusion.3.taps) | copy-start | bytes 122884
  135.5 18.9 %copy-start.7 = (bf16[128,1024]{1,0:T(8,128)(2,1)}, bf16[128,1024]{1,0:T(8,128)(2,1)S(1)}, u32[]{:S(2)}) copy-start(bf16[128,1024]{1,0:T(8,128)(2,1)S(1)} %fusion.16.spread) | copy-start | bytes 786436
  136.4 18.0 %copy-start.16 = (bf16[4,1,256,2048]{3,2,1,0:T(8,128)(2,1)S(1)}, bf16[4,1,256,2048]{3,2,1,0:T(8,128)(2,1)}, u32[]{:S(2)}) copy-start(bf16[4,1,256,2048]{3,2,1,0:T(8,128)(2,1)} %param.15) | copy-start | bytes 12582916
  154.4 6.8 %copy-start.11 = (bf16[8,128,1024]{2,1,0:T(8,128)(2,1)}, bf16[8,128,1024]{2,1,0:T(8,128)(2,1)S(1)}, u32[]{:S(2)}) copy-start(bf16[8,128,1024]{2,1,0:T(8,128)(2,1)S(1)} %get-tuple-element.56.states) | copy-start | bytes 6291460
  154.4 3.7 copy-start.13
  161.2 4.7 copy-start.28
  161.2 7.4 %copy-start.29 = (f32[1024,1024]{1,0:T(8,128)S(1)}, f32[1024,1024]{1,0:T(8,128)}, u32[]{:S(2)}) copy-start(f32[1024,1024]{1,0:T(8,128)} %get-tuple-element.49.y) | copy-start | bytes 12582916
  165.3 10.4 %copy-start.18 = (bf16[4,2,4,64,1024]{4,3,2,1,0:T(8,128)(2,1)}, bf16[4,2,4,64,1024]{4,3,2,1,0:T(8,128)(2,1)S(1)}, u32[]{:S(2)}) copy-start(bf16[4,2,4,64,1024]{4,3,2,1,0:T(8,128)(2,1)S(1)} %maximum_select_fusion) | copy-start | bytes 12582916
  175.7 2.0 copy-start.19
  245.3 1.7 copy-start.3
  268.4 1.5 copy-start.6
  269.9 36.0 %copy-start.30 = (f32[1024,1024]{1,0:T(8,128)S(1)}, f32[1024,1024]{1,0:T(8,128)}, u32[]{:S(2)}) copy-start(f32[1024,1024]{1,0:T(8,128)} %get-tuple-element.49.y) | copy-start | bytes 12582916
  303.5 2.4 copy-start.20
  305.9 10.6 %copy-start.17 = (bf16[1024,2048]{1,0:T(8,128)(2,1)S(1)}, bf16[1024,2048]{1,0:T(8,128)(2,1)}, u32[]{:S(2)}) copy-start(bf16[1024,2048]{1,0:T(8,128)(2,1)} %fusion.1.normed) | copy-start | bytes 12582916
  316.5 6.2 %copy-start.24 = (bf16[1024,1024]{1,0:T(8,128)(2,1)}, bf16[1024,1024]{1,0:T(8,128)(2,1)S(1)}, u32[]{:S(2)}) copy-start(bf16[1024,1024]{1,0:T(8,128)(2,1)S(1)} %get-tuple-element.167.dz) | copy-start | bytes 6291460
  504.9 1.5 copy-start.34
  504.9 1.5 copy-start.33
  506.2 3.2 copy-start.32
  506.5 4.2 copy-start.26
  506.5 1.0 copy-start.25
  510.6 6.6 %copy-start.2 = (bf16[1,256,2048]{2,1,0:T(8,128)(2,1)S(1)}, bf16[1,256,2048]{2,1,0:T(8,128)(2,1)}, u32[]{:S(2)}) copy-start(bf16[1,256,2048]{2,1,0:T(8,128)(2,1)} %param.14) | copy-start | bytes 3145732
  511.5 28.0 %copy-start.14 = (f32[256,2048]{1,0:T(8,128)}, f32[256,2048]{1,0:T(8,128)S(1)}, u32[]{:S(2)}) copy-start(f32[256,2048]{1,0:T(8,128)S(1)} %convert_reduce_fusion.1) | copy-start | bytes 6291460
  533.3 0.7 copy-start.35
  539.5 9.9 %copy-start.5 = (f32[64,8512]{1,0:T(8,128)S(1)}, f32[64,8512]{1,0:T(8,128)}, u32[]{:S(2)}) copy-start(f32[64,8512]{1,0:T(8,128)} %w_in.1) | copy-start | bytes 6537220
  544.6 4.8 copy-start.21
  544.6 4.8 copy-start.22
  544.6 4.8 copy-start.31
  549.5 5.2 copy-start.15
  549.5 5.2 copy-start.23
  554.7 2.0 copy-start.40
  554.7 1.9 copy-start.41
  554.7 2.5 copy-start.36
  554.7 2.5 copy-start.38
  554.7 2.5 copy-start.39
Sparse Core Ops, SparseCore 0:
  84.7 160.5 all-gather.1

commit v4 on v3

--- a/solution.py
+++ b/solution.py
@@ -145,64 +145,63 @@
 
 
 def scan_backward_kernel(
-    groups, parts, cw,
+    groups, parts, cw, chunks,
     px, halo, taps, heads, skip, spread, gather, dy, y, states, wide, gate,
     dpx, dtaps, dheads, dskip, wide_sum, gate_sum,
     xbuf, dstate, dcbuf, slope, xact, xd_s, dxd_s, acc_s,
-    wide_in, gate_held, gate_acc, gate_in,
-    wide_s, wide_r, core_s, core_r, gate_s, gate_r,
+    first, second, wide_s, wide_r, gate_held, gate_acc, gate_up, gate_down,
+    core_s, core_r, up_s, up_r, down_s, down_r,
 ):
     line = groups // 2
     group, q = lax.axis_index("dp"), lax.axis_index("seq")
     z, core = group // 2, lax.rem(group, 2)
     sibling = (2 * z + 1 - core, q)
-    peers = seq_peers(parts)
-    places = [lax.rem(z + k, line) for k in range(1, line)]
-
-    def wide_copy(k):
-        return remote(wide.at[peers[k][1]], wide_in.at[k], wide_s, wide_r, k, peers[k])
+    last = chunks - 1
+    plane = PlaneSum(parts, group, q, wide, first, second, wide_s, wide_r)
+    rows = gate.shape[2] // 4
+    gates = LineSum(
+        line, z, core, q, gate_acc, gate_up, gate_down, up_s, up_r, down_s, down_r, rows, 4
+    )
 
     def core_copy(d):
         return remote(gate.at[d, 1 - core], gate_held.at[d], core_s, core_r, d, sibling)
 
-    def gate_copy(k):
-        to = (2 * places[k] + core, q)
-        return remote(gate_acc.at[places[k]], gate_in.at[k], gate_s, gate_r, k, to)
-
     @pl.when(pl.program_id(0) == 0)
     def _():
-        greet(peers + dp_peers(groups))
+        greet(seq_peers(parts) + dp_peers(groups))
         for d in range(line):
             core_copy(d).start()
-        for k in range(parts - 1):
-            wide_copy(k).start()
+        plane.start(0)
+        plane.start(1)
 
     @pl.when(pl.program_id(0) == 1)
     def _():
         for d in range(line):
             core_copy(d).wait()
-            add_blocks(gate_acc.at[d], gate.at[d, core], gate_held.at[d], 32, gate.shape[2] // 32)
-        for k in range(line - 1):
-            gate_copy(k).start()
+            add_blocks(gate_acc.at[d], gate.at[d, core], gate_held.at[d], rows, 4)
+        gates.step(0)
+
+    for t in range(1, line - 1):
+
+        @pl.when(pl.program_id(0) == min(1 + 3 * t, last))
+        def _(t=t):
+            gates.sent(t - 1)
+            gates.step(t)
+
+    @pl.when(pl.program_id(0) == min(6, last))
+    def _():
+        plane.turn(32)
 
     scan_backward_step(
         cw, px, halo, taps, heads, skip, spread, gather, dy, y, states,
         dpx, dtaps, dheads, dskip, xbuf, dstate, dcbuf, slope, xact, xd_s, dxd_s, acc_s,
     )
 
-    @pl.when(pl.program_id(0) == pl.num_programs(0) - 1)
+    @pl.when(pl.program_id(0) == last)
     def _():
-        for k in range(line - 1):
-            gate_copy(k).wait()
-        sum_blocks(gate_sum, [gate_acc.at[z]] + [gate_in.at[k] for k in range(line - 1)], 32)
-        for k in range(parts - 1):
-            wide_copy(k).wait()
-        for d in range(line):
-            sum_blocks(
-                wide_sum.at[d],
-                [wide.at[q, d]] + [wide_in.at[k, d] for k in range(parts - 1)],
-                16,
-            )
+        plane.finish(wide_sum, 32)
+        gates.finish(gate_sum)
+        gates.sent(line - 2)
 
 
 def scan_backward_step(
@@ -361,7 +360,7 @@
     sem = pltpu.SemaphoreType.DMA
     vmem = pl.BlockSpec(memory_space=pltpu.VMEM)
     return pl.pallas_call(
-        functools.partial(scan_backward_kernel, 2 * line, parts, cw),
+        functools.partial(scan_backward_kernel, 2 * line, parts, cw, chunks),
         grid=(chunks,),
         in_specs=[
             pl.BlockSpec((CHUNK, width), lambda i: (chunks - 1 - i, 0)),
@@ -404,15 +403,12 @@
             pltpu.VMEM((CHUNK, cw), BF16),
             pltpu.VMEM((CHUNK, cw), F32),
             pltpu.VMEM((CHUNK, CHUNK), F32),
-            pltpu.VMEM((parts - 1,) + wide.shape[1:], BF16),
-            pltpu.VMEM((line, span, cw), BF16),
-            pltpu.VMEM((line, span, cw), BF16),
-            pltpu.VMEM((line - 1, span, cw), BF16),
-            sem((parts - 1,)), sem((parts - 1,)), sem((line,)), sem((line,)),
-            sem((line - 1,)), sem((line - 1,)),
+            *PlaneSum.scratch(parts, wide.shape[1:], BF16),
+            *([pltpu.VMEM((line, span, cw), BF16)] * 4),
+            *([sem((line,))] * 6),
         ],
         compiler_params=pltpu.CompilerParams(
-            collective_id=collective_id, has_side_effects=True, vmem_limit_bytes=56 * 2**20
+            collective_id=collective_id, has_side_effects=True, vmem_limit_bytes=63 * 2**20
         ),
         cost_estimate=pl.CostEstimate(
             flops=10**10, bytes_accessed=100 * 10**6, transcendentals=10**7
@@ -498,7 +494,7 @@
             pltpu.VMEM((rows, LANES), F32),
             pltpu.VMEM((rows, LANES), F32),
         ],
-        compiler_params=pltpu.CompilerParams(vmem_limit_bytes=48 * 2**20),
+        compiler_params=pltpu.CompilerParams(vmem_limit_bytes=63 * 2**20),
         name="widths",
     )(u, wo, cotangent, tokens)
 
@@ -563,8 +559,8 @@
     count = len(arrays)
     return pl.pallas_call(
         functools.partial(swap_kernel, parts, count),
-        in_specs=[pl.BlockSpec(memory_space=pl.ANY)] * count,
-        out_specs=[pl.BlockSpec(memory_space=pl.ANY)] * count,
+        in_specs=[pl.BlockSpec(memory_space=pltpu.HBM)] * count,
+        out_specs=[pl.BlockSpec(memory_space=pltpu.HBM)] * count,
         out_shape=[jax.ShapeDtypeStruct(a.shape, a.dtype) for a in arrays],
         scratch_shapes=[
             pltpu.SemaphoreType.DMA(((parts - 1) * count,)),
@@ -586,50 +582,291 @@
     return peers
 
 
-def broadcast_kernel(
-    groups, parts, block, near, total, near_out, out, sends, recvs, near_s, near_r, local
+CHAN_ROWS = ((TAPS + 1) * CONV_CH + D + INNER) // LANES
+
+
+def adam_tile(weight, gradient, moment, second, step_rate, weight_decay):
+    new_moment = BETA * moment + (1.0 - BETA) * gradient
+    new_second = BETA * second + (1.0 - BETA) * gradient * gradient
+    correction = 1.0 - BETA**STEP
+    update = new_moment / correction / (jnp.sqrt(new_second / correction) + ADAM_EPS)
+    return weight - step_rate * (update + weight_decay * weight), new_moment, new_second
+
+
+def total_of(value):
+    return jnp.sum(jnp.sum(value, axis=1, keepdims=True), axis=0, keepdims=True)
+
+
+def norm_kernel(
+    groups, parts,
+    part_h, gate_h, left_h, right_h, back_h, small_h, hidden_h, gain, cotangent,
+    hidden_grad, chan, head, norm,
+    part, gate, left, right, back, small, hidden,
+    cot_v, block, near, all_block, all_near, sends, recvs, near_s, near_r, load, local,
 ):
     group, q = lax.axis_index("dp"), lax.axis_index("seq")
     me = group * parts + q
+    cw = INNER // parts
+    cc = cw + 2 * N
     everyone = all_peers(groups, parts)
-    greet(everyone)
+    fetches = [
+        pltpu.make_async_copy(source, target, load.at[k])
+        for k, (source, target) in enumerate(
+            [(back_h, back), (hidden_h, hidden), (part_h, part), (gate_h, gate),
+             (left_h, left), (right_h, right), (small_h, small), (cotangent, cot_v)]
+        )
+    ]
+    for copy in fetches:
+        copy.start()
+    barrier = pltpu.get_barrier_semaphore()
+    for device in everyone:
+        pl.semaphore_signal(barrier, inc=1, device_id=device, device_id_type=MESH)
+    for copy in fetches[:7]:
+        copy.wait()
+    total = small[0]
+    for k in range(1, groups):
+        total = total + small[k]
+    near[...] = total
+    rows = 32
+
+    def summed(at):
+        down = back[at, :]
+        tokens = hidden[at, :].astype(F32)
+        mean = jnp.sum(tokens * tokens, axis=-1, keepdims=True) / D
+        return down, tokens, lax.rsqrt(mean + EPS_IN)
+
+    def gain_rows(i, dgain):
+        at = pl.ds(pl.multiple_of(i * rows, rows), rows)
+        down, tokens, scale = summed(at)
+        return dgain + jnp.sum(down * tokens * scale, axis=0, keepdims=True)
+
+    dgain = lax.fori_loop(0, hidden.shape[0] // rows, gain_rows, jnp.zeros((1, D), F32))
+    tail = part[0, :, cw : cc + H].astype(F32)
+    for k in range(1, parts):
+        tail = tail + part[k, :, cw : cc + H].astype(F32)
+    squares = total_of(tail * tail)
+    for k in range(parts):
+        x = part[k, :, :cw].astype(F32)
+        g = gate[k].astype(F32)
+        squares = squares + total_of(x * x + g * g)
+    squares = squares + total_of(left[...] * left[...] + right[...] * right[...])
+    for k in range(D // LANES):
+        block[k : k + 1, :] = dgain[:, k * LANES : (k + 1) * LANES]
+    block[D // LANES :, :] = jnp.broadcast_to(squares, (8, LANES))
+    pl.semaphore_wait(barrier, len(everyone))
     copies = [
-        remote(block, out.at[me], sends, recvs, k, peer) for k, peer in enumerate(everyone)
+        remote(block, all_block.at[me], sends, recvs, k, peer) for k, peer in enumerate(everyone)
     ]
     copies += [
-        remote(near, near_out.at[q], near_s, near_r, k, peer)
+        remote(near, all_near.at[q], near_s, near_r, k, peer)
         for k, peer in enumerate(seq_peers(parts))
     ]
     copies += [
-        pltpu.make_async_copy(block, out.at[me], local.at[0]),
-        pltpu.make_async_copy(near, near_out.at[q], local.at[1]),
+        pltpu.make_async_copy(block, all_block.at[me], local.at[0]),
+        pltpu.make_async_copy(near, all_near.at[q], local.at[1]),
     ]
     for copy in copies:
         copy.start()
+    fetches[7].wait()
+
+    def grad_rows(i, carry):
+        at = pl.ds(pl.multiple_of(i * rows, rows), rows)
+        down, tokens, scale = summed(at)
+        scaled = down * gain[...]
+        inner = jnp.sum(scaled * tokens, axis=-1, keepdims=True) / D
+        direct = cot_v[0, at, :].astype(F32)
+        for k in range(1, LEVELS):
+            direct = direct + cot_v[k, at, :].astype(F32)
+        hidden_grad[at, :] = (
+            scale * scaled - tokens * (scale * scale * scale * inner) + direct
+        )
+        return carry
+
+    lax.fori_loop(0, hidden.shape[0] // rows, grad_rows, 0)
     for copy in copies:
         copy.wait()
-    total[...] = jnp.sum(out[...], axis=0)
-
-
-def broadcast(collective_id, block, near, groups, parts):
+    total = jnp.sum(all_block[...], axis=0)
+    own, wide = cw // LANES, cc // LANES
+    span = CONV_CH // LANES
+    for tap in range(TAPS + 1):
+        for k in range(parts):
+            at = tap * span + k * own
+            chan[at : at + own, :] = all_near[k, tap * wide : tap * wide + own, :]
+        shared = all_near[0, tap * wide + own : (tap + 1) * wide, :]
+        for k in range(1, parts):
+            shared = shared + all_near[k, tap * wide + own : (tap + 1) * wide, :]
+        chan[tap * span + INNER // LANES : (tap + 1) * span, :] = shared
+    at = (TAPS + 1) * span
+    chan[at : at + D // LANES, :] = total[: D // LANES]
+    at = at + D // LANES
+    for k in range(parts):
+        first = (TAPS + 1) * wide
+        chan[at + k * own : at + (k + 1) * own, :] = all_near[k, first : first + own, :]
+        head[k : k + 1, :] = all_near[k, first + own : first + own + 1, :]
+    squares = (
+        total[D // LANES : D // LANES + 1, :1]
+        + total_of(chan[:CHAN_ROWS, :] * chan[:CHAN_ROWS, :])
+        + total_of(head[:parts, :] * head[:parts, :])
+    )
+    grad_norm = jnp.sqrt(squares)
+    norm[0:1, :] = jnp.broadcast_to(grad_norm, (1, LANES))
+    norm[1:2, :] = jnp.broadcast_to(jnp.minimum(1.0, CLIP / grad_norm), (1, LANES))
+
+
+def gradient_norm(
+    collective_id, part, gate, left, right, back, small, hidden, gain, cotangent, groups
+):
+    parts = part.shape[0]
     devices = groups * parts
     sem = pltpu.SemaphoreType.DMA
+    vmem = pl.BlockSpec(memory_space=pltpu.VMEM)
+    hbm = pl.BlockSpec(memory_space=pltpu.HBM)
+    block = (D // LANES + 8, LANES)
+    chan_rows = -(-CHAN_ROWS // 8) * 8
     return pl.pallas_call(
-        functools.partial(broadcast_kernel, groups, parts),
-        in_specs=[pl.BlockSpec(memory_space=pltpu.VMEM)] * 2,
-        out_specs=[pl.BlockSpec(memory_space=pltpu.VMEM)] * 2,
+        functools.partial(norm_kernel, groups, parts),
+        in_specs=[*([hbm] * 7), vmem, hbm],
+        out_specs=[vmem] * 4,
         out_shape=[
-            jax.ShapeDtypeStruct(block.shape, block.dtype),
-            jax.ShapeDtypeStruct((parts,) + near.shape, near.dtype),
+            jax.ShapeDtypeStruct(hidden.shape, F32),
+            jax.ShapeDtypeStruct((chan_rows, LANES), F32),
+            jax.ShapeDtypeStruct((8, LANES), F32),
+            jax.ShapeDtypeStruct((8, LANES), F32),
         ],
         scratch_shapes=[
-            pltpu.VMEM((devices,) + block.shape, block.dtype),
+            *[pltpu.VMEM(a.shape, a.dtype) for a in (part, gate, left, right, back, small, hidden)],
+            pltpu.VMEM(cotangent.shape, BF16),
+            pltpu.VMEM(block, F32),
+            pltpu.VMEM(small.shape[1:], F32),
+            pltpu.VMEM((devices,) + block, F32),
+            pltpu.VMEM((parts,) + small.shape[1:], F32),
             sem((devices - 1,)), sem((devices - 1,)), sem((parts - 1,)), sem((parts - 1,)),
-            sem((2,)),
-        ],
-        compiler_params=pltpu.CompilerParams(collective_id=collective_id, has_side_effects=True),
-        name="broadcast",
-    )(block, near)
+            sem((8,)), sem((2,)),
+        ],
+        compiler_params=pltpu.CompilerParams(
+            collective_id=collective_id, has_side_effects=True, vmem_limit_bytes=63 * 2**20
+        ),
+        name="gradient_norm",
+    )(part, gate, left, right, back, small, hidden, gain, cotangent)
+
+
+BLOCKS = 4
+
+
+def update_kernel(
+    parts, norm, part_h, gate_h, left_h, right_h, hidden_grad, *refs
+):
+    ins, refs = refs[:6], refs[6:]
+    hidden_out, outs, refs = refs[0], refs[1:9], refs[9:]
+    held, made = refs[:6], refs[6:14]
+    part, gate, left, right, hidden_v, load, store, grads = refs[14:]
+    clip = norm[1:2, :1]
+    cw = INNER // parts
+    cc = cw + 2 * N
+    fetches = [
+        pltpu.make_async_copy(source, target, grads.at[k])
+        for k, (source, target) in enumerate(
+            [(part_h, part), (gate_h, gate), (left_h, left), (right_h, right),
+             (hidden_grad, hidden_v)]
+        )
+    ]
+    for copy in fetches:
+        copy.start()
+
+    def at(a, i):
+        rows = ins[a].shape[0] // BLOCKS
+        return pl.ds(i * rows, rows)
+
+    loads = [
+        [
+            pltpu.make_async_copy(ins[a].at[at(a, i)], held[a].at[at(a, i)], load.at[a * BLOCKS + i])
+            for a in range(6)
+        ]
+        for i in range(BLOCKS)
+    ]
+    for weight in (0, 3):
+        for i in range(BLOCKS):
+            for a in range(weight, weight + 3):
+                loads[i][a].start()
+    stores = []
+
+    def update(weight, rows, lanes, gradient, rate, decay):
+        first = 0 if weight == 0 else 4
+        new, moment, second = adam_tile(
+            held[weight][rows, lanes], clip * gradient, held[weight + 1][rows, lanes],
+            held[weight + 2][rows, lanes], rate, decay,
+        )
+        made[first][rows, lanes] = new
+        made[first + 1][rows, lanes] = moment
+        made[first + 2][rows, lanes] = second
+        made[first + 3][rows, lanes] = new.astype(BF16)
+
+    def send(first, rows, i):
+        for a in range(first, first + 4):
+            copy = pltpu.make_async_copy(
+                made[a].at[rows], outs[a].at[rows], store.at[a * BLOCKS + i]
+            )
+            copy.start()
+            stores.append(copy)
+
+    for copy in fetches[:4]:
+        copy.wait()
+    for i in range(BLOCKS):
+        rows = at(0, i)
+        for a in range(3):
+            loads[i][a].wait()
+        for source, first in ((gate, 0), (part, INNER)):
+
+            def step(k, carry, source=source, first=first, rows=rows):
+                to = pl.ds(pl.multiple_of(first + k * cw, cw), cw)
+                update(0, rows, to, source[k, rows, :cw].astype(F32), 0.02, 0.1)
+                return carry
+
+            lax.fori_loop(0, parts, step, 0)
+        tail = part[0, rows, cw : cc + H].astype(F32)
+        for k in range(1, parts):
+            tail = tail + part[k, rows, cw : cc + H].astype(F32)
+        update(0, rows, slice(2 * INNER, E_IN), tail, 0.02, 0.1)
+        send(0, rows, i)
+    fetches[4].wait()
+    pass_on = pltpu.make_async_copy(hidden_v, hidden_out, grads.at[5])
+    pass_on.start()
+    half = D // 2
+    for i in range(BLOCKS):
+        rows = at(3, i)
+        for a in range(3, 6):
+            loads[i][a].wait()
+        update(3, rows, slice(0, half), left[rows, :], 0.03, 0.1)
+        update(3, rows, slice(half, D), right[rows, :], 0.03, 0.1)
+        send(4, rows, i)
+    pass_on.wait()
+    for copy in stores:
+        copy.wait()
+
+
+def update_weights(norm, part, gate, left, right, hidden_grad, weights):
+    parts = part.shape[0]
+    w_in, w_out = weights[0], weights[3]
+    sem = pltpu.SemaphoreType.DMA
+    vmem = pl.BlockSpec(memory_space=pltpu.VMEM)
+    hbm = pl.BlockSpec(memory_space=pltpu.HBM)
+    made = [
+        jax.ShapeDtypeStruct(w.shape, dtype) for w in (w_in, w_out) for dtype in (F32, F32, F32, BF16)
+    ]
+    return pl.pallas_call(
+        functools.partial(update_kernel, parts),
+        in_specs=[vmem, *([hbm] * 11)],
+        out_specs=[hbm] * 9,
+        out_shape=[jax.ShapeDtypeStruct(hidden_grad.shape, F32), *made],
+        scratch_shapes=[
+            *[pltpu.VMEM(w.shape, F32) for w in weights],
+            *[pltpu.VMEM(m.shape, m.dtype) for m in made],
+            *[pltpu.VMEM(a.shape, a.dtype) for a in (part, gate, left, right, hidden_grad)],
+            sem((6 * BLOCKS,)), sem((8 * BLOCKS,)), sem((6,)),
+        ],
+        compiler_params=pltpu.CompilerParams(vmem_limit_bytes=63 * 2**20),
+        name="update_weights",
+    )(norm, part, gate, left, right, hidden_grad, *weights)
 
 
 def collect_kernel(
@@ -758,7 +995,7 @@
     cw = INNER // parts
     width = cw + 2 * N + LANES
     sem = pltpu.SemaphoreType.DMA
-    hbm = pl.BlockSpec(memory_space=pl.ANY)
+    hbm = pl.BlockSpec(memory_space=pltpu.HBM)
     return pl.pallas_call(
         functools.partial(collect_kernel, groups, parts),
         in_specs=[hbm, pl.BlockSpec(memory_space=pltpu.VMEM), hbm],
@@ -861,7 +1098,7 @@
     line, width = groups // 2, INNER // groups
     sem = pltpu.SemaphoreType.DMA
     vmem = pl.BlockSpec(memory_space=pltpu.VMEM)
-    hbm = pl.BlockSpec(memory_space=pl.ANY)
+    hbm = pl.BlockSpec(memory_space=pltpu.HBM)
     return pl.pallas_call(
         functools.partial(swap_back_kernel, groups, parts, wide - LANES),
         in_specs=[hbm, vmem, vmem],
@@ -876,7 +1113,7 @@
             sem((parts - 1,)), sem((parts - 1,)), sem((line,)), sem((line,)), sem,
         ],
         compiler_params=pltpu.CompilerParams(
-            collective_id=collective_id, has_side_effects=True, vmem_limit_bytes=56 * 2**20
+            collective_id=collective_id, has_side_effects=True, vmem_limit_bytes=63 * 2**20
         ),
         name="swap_back",
     )(back, u, mixed)
@@ -894,6 +1131,96 @@
     lax.fori_loop(0, out.shape[0] // rows, step, 0)
 
 
+class PlaneSum:
+    def __init__(self, parts, group, q, blocks, first, second, sends, recvs):
+        self.parts, self.group, self.q = parts, group, q
+        self.blocks, self.first, self.second = blocks, first, second
+        self.sends, self.recvs = sends, recvs
+        self.half = blocks.shape[1] // 2
+        if parts == 4:
+            self.near = [q + 1 - 2 * lax.rem(q, 2), lax.rem(q + 2, 4)]
+            self.far = 3 - q
+
+    @staticmethod
+    def scratch(parts, shape, dtype):
+        if parts == 4:
+            half = (shape[0] // 2,) + shape[1:]
+            first, second, count = (2, 2) + half, (2, 2) + half, 6
+        else:
+            first, second, count = (parts - 1,) + shape, (1, 16, LANES), parts - 1
+        sem = pltpu.SemaphoreType.DMA
+        return [pltpu.VMEM(first, dtype), pltpu.VMEM(second, dtype), sem((count,)), sem((count,))]
+
+    def piece(self, of, h):
+        return self.blocks.at[of, pl.ds(h * self.half, self.half)]
+
+    def early(self, h):
+        if self.parts != 4:
+            return []
+        near = self.near[h]
+        to = (self.group, near)
+        return [
+            remote(self.piece(of, h), self.first.at[h, k], self.sends, self.recvs, 2 * h + k, to)
+            for k, of in enumerate((near, self.far))
+        ]
+
+    def late(self, h):
+        to = (self.group, self.near[1 - h])
+        return remote(
+            self.second.at[h, 0], self.second.at[h, 1], self.sends, self.recvs, 4 + h, to
+        )
+
+    def direct(self):
+        peers = seq_peers(self.parts)
+        return [
+            remote(self.blocks.at[peer[1]], self.first.at[k], self.sends, self.recvs, k, peer)
+            for k, peer in enumerate(peers)
+        ]
+
+    def start(self, h):
+        for copy in self.early(h):
+            copy.start()
+        if self.parts != 4 and h == 1:
+            for copy in self.direct():
+                copy.start()
+
+    def turn(self, rows):
+        if self.parts != 4:
+            return
+        for h in range(2):
+            for copy in self.early(h):
+                copy.wait()
+            beyond = self.piece(self.near[1 - h], h)
+            each(self.second.at[h, 0], [beyond, self.first.at[h, 1]], rows)
+            self.late(h).start()
+
+    def finish(self, out, rows):
+        if self.parts != 4:
+            for copy in self.direct():
+                copy.wait()
+            each(
+                out,
+                [self.blocks.at[self.q]] + [self.first.at[k] for k in range(self.parts - 1)],
+                rows,
+            )
+            return
+        for h in range(2):
+            self.late(h).wait()
+            each(
+                out.at[pl.ds(h * self.half, self.half)],
+                [self.piece(self.q, h), self.first.at[h, 0], self.second.at[h, 1]],
+                rows,
+            )
+
+
+def each(out, blocks, rows):
+    if len(out.shape) == 2:
+        sum_blocks(out, blocks, rows)
+        return
+    for d in range(out.shape[0]):
+        sum_blocks(out.at[d], [block.at[d] for block in blocks], rows)
+
+
 class LineSum:
     def __init__(self, line, z, core, q, acc, up, down, up_s, up_r, down_s, down_r, rows, steps):
         self.line, self.z, self.core, self.q = line, z, core, q
@@ -983,11 +1310,11 @@
     groups, parts, rows,
     normed, left, right, gate, small, dz, dpx, wz, wx,
     part, left_out, right_out, gate_out, back_out, small_all,
-    made, held, acc, up, down, final, left_up, left_down, right_in, right_acc, right_up, right_down,
-    normed_v, dz_v, dpx_v, wz_v, wx_v, back,
+    made, held, acc, up, down, final, left_up, left_down, right_acc, right_up, right_down,
+    normed_v, dz_v, dpx_v, wz_v, wx_v, back, back_sum,
+    right_1, right_2, right_s, right_r, back_1, back_2, back_s, back_r,
     core_s, core_r, up_s, up_r, down_s, down_r, lup_s, lup_r, ldown_s, ldown_r,
-    rup_s, rup_r, rdown_s, rdown_r,
-    part_s, part_r, back_s, back_r, gate_s, gate_r, right_s, right_r, small_s, small_r,
+    rup_s, rup_r, rdown_s, rdown_r, part_s, part_r, gate_s, gate_r, small_s, small_r,
     load, local,
 ):
     line = groups // 2
@@ -1018,11 +1345,10 @@
         line, z, core, q, acc, up, down, up_s, up_r, down_s, down_r, rows, parts
     )
     lefts.step(0)
-    rights_in = []
-    for k, peer in enumerate(peers):
-        copy = remote(right.at[peer[1]], right_in.at[k], right_s, right_r, k, peer)
-        copy.start()
-        rights_in.append(copy)
+    right_plane = PlaneSum(parts, group, q, right, right_1, right_2, right_s, right_r)
+    back_plane = PlaneSum(parts, group, q, back, back_1, back_2, back_s, back_r)
+    right_plane.start(0)
+    right_plane.start(1)
     waiting = []
     for k, peer in enumerate(peers):
         copy = remote(gate.at[peer[1]], gate_out.at[q], gate_s, gate_r, k, peer)
@@ -1046,19 +1372,34 @@
         at = pl.ds(pl.multiple_of(of * span, span), span)
         out[...] = dot(normed_v[:, at], dpx_v[...], TN).astype(BF16)
 
-    cores = []
-    for d in range(line):
+    cores = {}
+    order = [d for k in range(line // 2) for d in (line - 1 - k, k)]
+
+    def share_core(d):
         dweight(2 * d + 1 - core, made.at[d])
         copy = remote(made.at[d], held.at[d], core_s, core_r, d, sibling)
         copy.start()
-        cores.append(copy)
-    for d in range(line):
+        cores[d] = copy
+
+    def sum_core(d):
         dweight(2 * d + core, acc.at[d])
-    for d in range(line):
         cores[d].wait()
         add_blocks(acc.at[d], acc.at[d], held.at[d], rows, parts)
+
+    share_core(order[0])
     lefts.sent(0)
+    lefts.step(1)
+    share_core(order[1])
+    sum_core(order[0])
+    for t in range(2, line - 1):
+        lefts.sent(t - 1)
+        lefts.step(t)
+    sum_core(order[1])
     wholes.step(0)
+    for d in order[2:]:
+        share_core(d)
+    for d in order[2:]:
+        sum_core(d)
     for copy in loads[2:]:
         copy.wait()
 
@@ -1074,29 +1415,27 @@
 
         lax.fori_loop(0, D // tile, step, 0)
 
-    for k, peer in enumerate(peers):
-        dnormed(peer[1])
-        copy = remote(back.at[peer[1]], back_out.at[q], back_s, back_r, k, peer)
-        copy.start()
-        waiting.append(copy)
+    right_plane.turn(32)
+    if parts == 4:
+        dnormed(back_plane.far)
+        dnormed(back_plane.near[0])
+        back_plane.start(0)
+    wholes.sent(0)
+    wholes.step(1)
+    if parts == 4:
+        dnormed(back_plane.near[1])
+    else:
+        for peer in peers:
+            dnormed(peer[1])
+    back_plane.start(1)
     dnormed(q)
-    copy = pltpu.make_async_copy(back.at[q], back_out.at[q], local.at[2])
-    copy.start()
-    own.append(copy)
-    for t in range(1, line - 1):
+    right_plane.finish(right_acc, 32)
+    for t in range(2, line - 1):
         wholes.sent(t - 1)
-        lefts.step(t)
-        lefts.sent(t)
         wholes.step(t)
+    back_plane.turn(32)
     lefts.finish(left_out)
-    for copy in rights_in:
-        copy.wait()
-    for d in range(line):
-        sum_blocks(
-            right_acc.at[d],
-            [right.at[q, d]] + [right_in.at[k, d] for k in range(parts - 1)],
-            16,
-        )
+    lefts.sent(line - 2)
     wholes.sent(line - 2)
     rights.step(0)
     wholes.finish(final)
@@ -1106,11 +1445,17 @@
         copy.start()
         waiting.append(copy)
     copy = pltpu.make_async_copy(
-        final.at[pl.ds(pl.multiple_of(q * rows, rows), rows)], part.at[q], local.at[3]
+        final.at[pl.ds(pl.multiple_of(q * rows, rows), rows)], part.at[q], local.at[2]
     )
     copy.start()
     own.append(copy)
-    for t in range(1, line - 1):
+    rights.sent(0)
+    rights.step(1)
+    back_plane.finish(back_sum, 32)
+    copy = pltpu.make_async_copy(back_sum, back_out, local.at[3])
+    copy.start()
+    own.append(copy)
+    for t in range(2, line - 1):
         rights.sent(t - 1)
         rights.step(t)
     rights.finish(right_out)
@@ -1127,7 +1472,7 @@
     tokens = dz.shape[0] // parts
     sem = pltpu.SemaphoreType.DMA
     vmem = pl.BlockSpec(memory_space=pltpu.VMEM)
-    hbm = pl.BlockSpec(memory_space=pl.ANY)
+    hbm = pl.BlockSpec(memory_space=pltpu.HBM)
     return pl.pallas_call(
         functools.partial(owners_kernel, groups, parts, rows),
         in_specs=[hbm, vmem, vmem, hbm, vmem, hbm, hbm, hbm, hbm],
@@ -1136,19 +1481,20 @@
             jax.ShapeDtypeStruct((parts, rows, width), BF16),
             *([jax.ShapeDtypeStruct((out_rows, half), F32)] * 2),
             jax.ShapeDtypeStruct(gate.shape, BF16),
-            jax.ShapeDtypeStruct((parts, tokens, D), BF16),
+            jax.ShapeDtypeStruct((tokens, D), F32),
             jax.ShapeDtypeStruct((groups,) + small.shape, F32),
         ],
         scratch_shapes=[
             *([pltpu.VMEM((line, span, width), BF16)] * 5),
             pltpu.VMEM((span, width), BF16),
-            *([pltpu.VMEM(left.shape, BF16)] * 2),
-            pltpu.VMEM((parts - 1,) + left.shape, BF16),
-            *([pltpu.VMEM(left.shape, BF16)] * 3),
+            *([pltpu.VMEM(left.shape, BF16)] * 5),
             *[pltpu.VMEM(a.shape, BF16) for a in (normed, dz, dpx, wz, wx)],
             pltpu.VMEM((parts, tokens, D), BF16),
+            pltpu.VMEM((tokens, D), F32),
+            *PlaneSum.scratch(parts, right.shape[1:], BF16),
+            *PlaneSum.scratch(parts, (tokens, D), BF16),
             *([sem((line,))] * 14),
-            *([sem((parts - 1,))] * 8),
+            *([sem((parts - 1,))] * 4),
             *([sem((groups - 1,))] * 2),
             sem((5,)),
             sem((4,)),
@@ -1158,14 +1504,6 @@
         ),
         name="sum_to_owners",
     )(normed, left, right, gate, small, dz, dpx, wz, wx)
-
-
-def adam_step(weight, gradient, moment, second, step_rate, weight_decay):
-    new_moment = BETA * moment + (1.0 - BETA) * gradient
-    new_second = BETA * second + (1.0 - BETA) * gradient * gradient
-    correction = 1.0 - BETA**STEP
-    update = new_moment / correction / (jnp.sqrt(new_second / correction) + ADAM_EPS)
-    return (weight - step_rate * (update + weight_decay * weight), new_moment, new_second)
 
 
 def pack_terms(values):
@@ -1208,14 +1546,9 @@
     line = groups // 2
     group = lax.axis_index("dp")
     core, place = group % 2, group // 2
-    wz_line = jnp.zeros((line,) + wz.shape, BF16)
-    wz_line = lax.dynamic_update_index_in_dim(wz_line, wz, place, 0)
-    for k in range(1, line):
-        block = lax.ppermute(wz, "dp", [(i, i ^ (2 * k)) for i in range(groups)])
-        wz_line = lax.dynamic_update_index_in_dim(wz_line, block, place ^ k, 0)
-    other = lax.ppermute(wz_line, "dp", [(i, i ^ 1) for i in range(groups)])
-    wz = jnp.where(core == 0, jnp.stack([wz_line, other], 1), jnp.stack([other, wz_line], 1))
-    wz = wz.reshape(D, cw)
+    wz_blocks = [
+        lax.ppermute(wz, "dp", [(i, i ^ (2 * k)) for i in range(groups)]) for k in range(1, line)
+    ]
 
     conv_taps = chan_full[: TAPS * CONV_CH].reshape(TAPS, CONV_CH)
     conv_bias = chan_full[TAPS * CONV_CH : (TAPS + 1) * CONV_CH].reshape(1, CONV_CH)
@@ -1243,6 +1576,15 @@
     normed = (tokens * scale * gain_in).astype(BF16)
     px = dot(normed, wx)
     y, states = scan_forward(px, taps, heads, skip, spread)
+    wz_blocks, y = lax.optimization_barrier((wz_blocks, y))
+    wz_line = lax.dynamic_update_index_in_dim(
+        jnp.zeros((line,) + wz.shape, BF16), wz, place, 0
+    )
+    for k in range(1, line):
+        wz_line = lax.dynamic_update_index_in_dim(wz_line, wz_blocks[k - 1], place ^ k, 0)
+    other = lax.ppermute(wz_line, "dp", [(i, i ^ 1) for i in range(groups)])
+    wz = jnp.where(core == 0, jnp.stack([wz_line, other], 1), jnp.stack([other, wz_line], 1))
+    wz = wz.reshape(D, cw)
     z = dot(normed, wz)
     sig = jax.nn.sigmoid(z)
     gate = z * sig
@@ -1288,77 +1630,33 @@
     x_part, left_part, right_part, z_part, dnormed, small = sum_to_owners(
         4, normed, dwo_left, dwo_right, dwz.reshape(parts, in_rows, cw), small, dz, dpx, wz, wx
     )
-    out_part = jnp.concatenate([left_part, right_part], axis=1)
-    dnormed = jnp.sum(dnormed.astype(F32), axis=0)
-    small = jnp.sum(small, axis=0)
-    own_scale = lax.rsqrt(jnp.mean(own_tokens * own_tokens, axis=-1, keepdims=True) + EPS_IN)
-    dgain_in = jnp.sum(dnormed * own_tokens * own_scale, axis=0)
-    scaled = dnormed * gain_in
-    hidden_grad = (
-        own_scale * scaled
-        - own_tokens
-        * (own_scale**3 * (jnp.sum(scaled * own_tokens, axis=-1, keepdims=True) / D))
-        + jnp.sum(cotangent.astype(F32), axis=0)
-    )[None]
-
-    z_part = z_part.astype(F32)
-    x_part = x_part.astype(F32)
-    in_part = jnp.concatenate(
-        [
-            z_part.transpose(1, 0, 2).reshape(in_rows, INNER),
-            x_part[:, :, :cw].transpose(1, 0, 2).reshape(in_rows, INNER),
-            jnp.sum(x_part[:, :, cw : cc + H], axis=0),
-        ],
-        axis=1,
-    )
-    local_squares = jnp.sum(in_part * in_part) + jnp.sum(out_part * out_part)
-    block = jnp.concatenate(
-        [dgain_in.reshape(D // LANES, LANES), jnp.full((8, LANES), local_squares)], axis=0
-    )
-    block, small = broadcast(6, block, small, groups, parts)
-    small = small.reshape(parts, small_rows * LANES)
-    taps_size = (TAPS + 1) * cc
-    taps_grad = small[:, :taps_size].reshape(parts, TAPS + 1, cc)
-    taps_grad = jnp.concatenate(
-        [
-            taps_grad[:, :, :cw].transpose(1, 0, 2).reshape(TAPS + 1, INNER),
-            jnp.sum(taps_grad[:, :, cw:], axis=0),
-        ],
-        axis=1,
-    )
-    head_total = small[:, taps_size + cw : taps_size + cw + 3 * hq]
-    head_total = head_total.reshape(parts, 3, hq).transpose(1, 0, 2).reshape(3, H)
-    chan_total = jnp.concatenate(
-        [
-            taps_grad.reshape(-1),
-            block[: D // LANES].reshape(-1),
-            small[:, taps_size : taps_size + cw].reshape(-1),
-        ]
-    )
-    owner = lax.axis_index("dp") * parts + q
-    chan_part = lax.dynamic_slice(chan_total, (owner * chan_len,), (chan_len,))
-    grad_norm = jnp.sqrt(
-        block[D // LANES, 0]
-        + jnp.sum(chan_total * chan_total)
-        + jnp.sum(head_total * head_total)
-    )
-    clip_factor = jnp.minimum(1.0, CLIP / grad_norm)
-    w_in_new, w_in_m_new, w_in_v_new = adam_step(
-        w_in, clip_factor * in_part, w_in_m, w_in_v, 0.02, 0.1
-    )
-    w_out_new, w_out_m_new, w_out_v_new = adam_step(
-        w_out, clip_factor * out_part, w_out_m, w_out_v, 0.03, 0.1
-    )
-    chan_new, chan_m_new, chan_v_new = adam_step(
+    hidden_grad, chan_total, head_total, norm = gradient_norm(
+        6, x_part, z_part, left_part, right_part, dnormed, small, hidden_in[0],
+        gain_in.reshape(1, D), cotangent, groups,
+    )
+    (
+        hidden_grad, w_in_new, w_in_m_new, w_in_v_new, w_in_copy,
+        w_out_new, w_out_m_new, w_out_v_new, w_out_copy,
+    ) = update_weights(
+        norm, x_part, z_part, left_part, right_part, hidden_grad,
+        (w_in, w_in_m, w_in_v, w_out, w_out_m, w_out_v),
+    )
+    hidden_grad = hidden_grad[None]
+    grad_norm, clip_factor = norm[0, 0], norm[1, 0]
+    owner = group * parts + q
+    chan_part = lax.dynamic_slice(chan_total.reshape(-1), (owner * chan_len,), (chan_len,))
+    head_total = head_total[:parts, : 3 * hq].reshape(parts, 3, hq)
+    head_total = head_total.transpose(1, 0, 2).reshape(3, H)
+    chan_new, chan_m_new, chan_v_new = adam_tile(
         chan_params, clip_factor * chan_part, chan_m, chan_v, 0.2, 0.0
     )
-    head_new, head_m_new, head_v_new = adam_step(
+    head_new, head_m_new, head_v_new = adam_tile(
         head_params, clip_factor * head_total, head_m, head_v, 1.0, 0.0
     )
     return (
         block_out, hidden_grad, grad_norm,
-        w_in_new, w_in_m_new, w_in_v_new, w_in_new.astype(BF16),
-        w_out_new, w_out_m_new, w_out_v_new, w_out_new.astype(BF16),
+        w_in_new, w_in_m_new, w_in_v_new, w_in_copy,
+        w_out_new, w_out_m_new, w_out_v_new, w_out_copy,
         chan_new, chan_m_new, chan_v_new, head_new, head_m_new, head_v_new,
     )
 

time: 576 us -> 530 us (0.920)
  Pallas kernels: 387 us -> 365 us
  other arithmetic: 57.7 us -> 37.4 us
  waiting for transfers between devices: 40.3 us -> 53.9 us
  local copies, waits for them, and re-layouts: 33.9 us -> 21.9 us
    all_gather x1, waiting for transfers between devices: 15.2 us -> 47.3 us  [on_device(): wo = lax.all_gather(out_low, ('dp', 'seq'), axis=0, tiled=True)]
    pallas_call x1, Pallas kernels: 116 us -> 91.6 us  [sum_to_owners(): pl.pallas_call(functools.partial(owners_kernel, groups, parts, rows), in_...]
    pallas_call x1 -> x2, Pallas kernels: 13.8 us -> 33.2 us  [the longest x1 22.3 us: gradient_norm(): pl.pallas_call(functools.partial(norm_kernel, groups, parts), in_specs=[*...]
    ppermute x3, waiting for transfers between devices: 25.1 us -> 6.63 us  [on_device(): lax.ppermute(wz, 'dp', [(i, i ^ 2 * k) for i in range(groups)])]
    pallas_call x1, Pallas kernels: 62.6 us -> 49.8 us  [scan_backward(): pl.pallas_call(functools.partial(scan_backward_kernel, 2 * line, parts, c...]
    convert_element_type x3 -> x0, other arithmetic: 11.3 us -> none  [the longest x1 5.18 us: on_device(): w_in_new.astype(BF16)]
    reduce_sum x10 -> x0, other arithmetic: 10.4 us -> none  [the longest x2 3.58 us: on_device(): local_squares = jnp.sum(in_part * in_part) + jnp.sum(out_part * out_part)]
    pallas_call x1, Pallas kernels: 49.2 us -> 42.7 us  [swap(): pl.pallas_call(functools.partial(swap_kernel, parts, count), in_specs=[pl...]
  transfers between devices with their start and end apart: 5 -> 5, of which waited for: 3 -> 2; matrix products, arithmetic and copies ran while one was open for 7% -> 7% of each run, Pallas kernels for 12% -> 12%
where the time goes in v4:
time: 530 us; the launch traced here: 520 us
  Pallas kernels  365 us (69%)
  waiting for transfers between devices  53.9 us (10%)
  other arithmetic  37.4 us (7%)
  local copies, waits for them, and re-layouts  21.9 us (4%)
  matrix products  21.7 us (4%)
  between operations  15 us (3%)
  starting transfers between devices  5.72 us (1%)
    pallas_call x1, Pallas kernels, sum_to_owners(): pl.pallas_call(functools.partial(owners_kernel, groups, parts, rows), in_...  91.6 us
    pallas_call x1, Pallas kernels, collect(): pl.pallas_call(functools.partial(collect_kernel, groups, parts), in_specs...  71.6 us
    pallas_call x1, Pallas kernels, scan_backward(): pl.pallas_call(functools.partial(scan_backward_kernel, 2 * line, parts, c...  49.8 us
    all_gather x1, waiting for transfers between devices, on_device(): wo = lax.all_gather(out_low, ('dp', 'seq'), axis=0, tiled=True)  47.3 us
    pallas_call x1, Pallas kernels, swap(): pl.pallas_call(functools.partial(swap_kernel, parts, count), in_specs=[pl...  42.7 us
    pallas_call x1, Pallas kernels, swap_back(): pl.pallas_call(functools.partial(swap_back_kernel, groups, parts, wide -...  34.6 us
    pallas_call x1, Pallas kernels, widths(): pl.pallas_call(functools.partial(widths_kernel, cw), grid=(INNER // WIDE,...  23.2 us
    pallas_call x1, Pallas kernels, gradient_norm(): pl.pallas_call(functools.partial(norm_kernel, groups, parts), in_specs=[*...  22.3 us
  transfers between devices with their start and end apart: 5, of which 2 were waited for; matrix products, arithmetic and copies ran while one was open for 7% of the time, Pallas kernels for 12%

profile of v4, /device:TPU:1, one launch (start us, length us, event | category | flops | bytes accessed | tf_op | source)
XLA Modules:
  0.0 520.3 jit_solution(2177716379769866163)
XLA Ops:
  7.2 0.0 all-gather.2.cloned.1.call-start
  7.2 0.7 reduce_precision.6
  7.9 2.1 convert_element_type.53
  10.0 1.2 copy-done
  11.3 1.6 copy-done.1
  12.9 71.6 %collect.1 = (bf16[4,256,2048]{2,1,0:T(8,128)(2,1)}, bf16[8,4,64,1408]{3,2,1,0:T(8,128)(2,1)}, bf16[4,64,1024]{2,1,0:T(8,128)(2,1)S(1)}, f32[32,8,128]{2,1,0:T(8,128)S(1)}) custom-call(bf16[256,2048]{1,0:T(8,128)(2,1)S(1)} %bitcast.64, f32[64,8512]{1,0:T(8,128)S(1)} %copy-done.1, f32[8,128]{1,0:T(8,128)S(1)} %pad_bitcast_fusion.1.chan), custom_call_target="tpu_custom_call" | custom-call | tf_op jit(solution)/shard_map/collect/pallas_call | solution.py:999
  84.5 0.1 collective-permute-start
  84.6 1.7 collective-permute-start.1
  86.3 1.8 collective-permute-start.2
  88.2 0.1 reshape.167
  88.4 0.1 pad.38.clone
  88.5 0.1 maximum_maximum_fusion
  88.6 0.1 constant_dynamic-slice_fusion
  88.7 0.1 broadcast_in_dim.118
  88.8 0.1 reshape_reshape.3.skip
  88.9 3.2 multiply_reduce_fusion
  92.2 0.1 fusion.8.spread
  92.3 0.3 copy-done.7
  92.6 1.0 multiply_convert_fusion
  93.6 3.3 copy-done.13
  96.9 8.5 %fusion.34.px.halo = f32[1024,1408]{1,0:T(8,128)} fusion(bf16[1024,2048]{1,0:T(8,128)(2,1)S(1)} %bitcast.74, bf16[2048,1408]{1,0:T(8,128)(2,1)S(1)} %bitcast.73), kind=kOutput, calls=%fused_computation.91 | convolution fusion | flops 5905580032 | bytes 15728640 | tf_op jit(solution)/shard_map/dot_general | solution.py:44
  105.3 0.3 broadcast_in_dim.119
  105.7 17.9 %scan_forward.1 = (f32[1024,1024]{1,0:T(8,128)}, bf16[8,128,1024]{2,1,0:T(8,128)(2,1)S(1)}) custom-call(f32[1024,1408]{1,0:T(8,128)} %fusion.34.px.halo, f32[8,1280]{1,0:T(8,128)S(1)} %pad_maximum_fusion.taps, f32[8,128]{1,0:T(8,128)S(1)} %select_maximum_fusion.heads, f32[1,1024]{1,0:T(1,128)S(1)} %reshape_reshape.3.skip, bf16[128,1024]{1,0:T(8,128)(2,1)S(1)} %fusion.8.spread), custom_call_target="tpu_custom_call" | custom-call | flops 3000000000 | bytes 40000000 | tf_op jit(solution)/shard_map/scan_forward/pallas_call | solution.py:320
  123.6 1.3 copy-done.6
  124.9 6.6 %collective-permute-done.2 = bf16[4,64,1024]{2,1,0:T(8,128)(2,1)} collective-permute-done((bf16[4,64,1024]{2,1,0:T(8,128)(2,1)S(1)}, bf16[4,64,1024]{2,1,0:T(8,128)(2,1)}, u32[]{:S(2)}, u32[]{:S(2)}) %collective-permute-start.2) | collective-permute-done | bytes 524320 | tf_op jit(solution)/shard_map/ppermute | solution.py:1550
  131.6 1.1 bitcast_dynamic-update-slice_fusion.1
  132.7 1.1 bitcast_dynamic-update-slice_fusion
  133.8 2.1 collective-permute-start.3
  135.9 0.9 fusion.9.gather
  136.8 5.3 %fusion.1.normed = bf16[1024,2048]{1,0:T(8,128)(2,1)} fusion(f32[2048]{0:T(1024)S(1)} %slice.97, f32[1024]{0:T(1024)S(1)} %bitcast.83, bf16[4,256,2048]{2,1,0:T(8,128)(2,1)} %get-tuple-element.61), kind=kLoop, calls=%fused_computation.2 | loop fusion | flops 8388608 | bytes 8400896 | tf_op jit(solution)/shard_map/convert_element_type | solution.py:1576
  142.1 2.9 maximum_select_fusion
  145.0 0.5 copy-done.15
  145.6 2.8 copy-done.16
  148.4 7.0 %multiply_convert_fusion.2 = (bf16[1024,1024]{1,0:T(8,128)(2,1)S(1)}, f32[1024,1024]{1,0:T(8,128)S(1)}, f32[1024,1024]{1,0:T(8,128)}) fusion(f32[1024]{0:T(1024)S(1)} %dynamic_slice.14, f32[1024,1024]{1,0:T(8,128)S(1)} %copy-done.16, bf16[1024,2048]{1,0:T(8,128)(2,1)S(1)} %bitcast.75, bf16[2048,1024]{1,0:T(8,128)(2,1)S(1)} %bitcast.68), kind=kOutput, calls=%fused_computation.18 | convolution fusion | flops 4302307328 | bytes 23072768 | tf_op jit(solution)/shard_map/dot_general | solution.py:44
  155.4 2.0 copy-done.10
  157.4 1.4 select_reduce_fusion.3
  158.9 0.2 copy.52
  159.0 1.6 fusion.7
  160.7 42.7 %swap.1.u = bf16[4,256,1152]{2,1,0:T(8,128)(2,1)} custom-call(bf16[4,256,1152]{2,1,0:T(8,128)(2,1)} %bitcast.70), custom_call_target="tpu_custom_call" | custom-call | tf_op jit(solution)/shard_map/swap/pallas_call | solution.py:560
  203.4 47.3 %all-gather.2.cloned.1.call-done.wo = bf16[4096,2048]{1,0:T(8,128)(2,1)} async-done(((bf16[128,2048]{1,0:T(8,128)(2,1)}), bf16[4096,2048]{1,0:T(8,128)(2,1)}) %all-gather.2.cloned.1.call-update) | async-done | bytes 16777232 | tf_op jit(solution)/shard_map/all_gather | solution.py:1542
  250.6 23.2 %widths.1 = (bf16[4,256,2048]{2,1,0:T(8,128)(2,1)}, bf16[4,256,1152]{2,1,0:T(8,128)(2,1)}, bf16[4,256,2048]{2,1,0:T(8,128)(2,1)}) custom-call(bf16[4,256,1152]{2,1,0:T(8,128)(2,1)} %swap.1.u, bf16[4096,2048]{1,0:T(8,128)(2,1)} %all-gather.2.cloned.1.call-done.wo, bf16[4,256,2048]{2,1,0:T(8,128)(2,1)} %bitcast.66, bf16[256,2048]{1,0:T(8,128)(2,1)} %bitcast.62), custom_call_target="tpu_custom_call" | custom-call | tf_op jit(solution)/shard_map/widths/pallas_call | solution.py:477
  273.8 34.6 %swap_back.1 = (bf16[4,256,1152]{2,1,0:T(8,128)(2,1)}, bf16[4,4,128,1024]{3,2,1,0:T(8,128)(2,1)}, bf16[4,4,128,1024]{3,2,1,0:T(8,128)(2,1)}) custom-call(bf16[4,256,1152]{2,1,0:T(8,128)(2,1)} %get-tuple-element.72.back, bf16[4,256,1152]{2,1,0:T(8,128)(2,1)} %swap.1.u, bf16[4,256,2048]{2,1,0:T(8,128)(2,1)} %get-tuple-element.73.mixed), custom_call_target="tpu_custom_call" | custom-call | tf_op jit(solution)/shard_map/swap_back/pallas_call | solution.py:1102
  308.5 1.1 slice_convert_fusion
  309.6 0.2 slice_add_fusion
  309.8 1.0 slice_reduce_fusion.3
  310.9 12.6 %multiply_convert_fusion.1 = (bf16[1024,1024]{1,0:T(8,128)(2,1)S(1)}, f32[1024,1024]{1,0:T(8,128)}, f32[1024]{0:T(1024)S(1)}) fusion(f32[1024,1024]{1,0:T(8,128)} %get-tuple-element.66.y, f32[1024,1024]{1,0:T(8,128)S(1)} %copy-done.11, f32[1024,1024]{1,0:T(8,128)} %get-tuple-element.201, f32[1024]{0:T(1024)S(1)} %get-tuple-element.176, ...), kind=kLoop, calls=%fused_computation.12 | loop fusion | flops 20970496 | bytes 20999168 | tf_op jit(solution)/shard_map/convert_element_type | solution.py:1617
  323.5 6.2 %convolution_convert_fusion = bf16[2048,1024]{1,0:T(8,128)(2,1)} fusion(bf16[1024,2048]{1,0:T(8,128)(2,1)S(1)} %copy-done.8, bf16[1024,1024]{1,0:T(8,128)(2,1)S(1)} %get-tuple-element.187.dz), kind=kOutput, calls=%fused_computation.20 | convolution fusion | flops 4297064448 | bytes 10485760 | tf_op jit(solution)/shard_map/dot_general | solution.py:44
  329.7 49.8 %scan_backward.1 = (bf16[1024,1408]{1,0:T(8,128)(2,1)}, f32[8,1280]{1,0:T(8,128)}, f32[8,128]{1,0:T(8,128)}, f32[8,1024]{1,0:T(8,128)}, bf16[4,128,1024]{2,1,0:T(8,128)(2,1)}, /*index=5*/bf16[256,1024]{1,0:T(8,128)(2,1)}) custom-call(f32[1024,1408]{1,0:T(8,128)} %fusion.34.px.halo, f32[1024,1408]{1,0:T(8,128)} %fusion.34.px.halo, f32[8,1280]{1,0:T(8,128)} %copy-done.3, ...), custom_call_target="tpu_custom_call" | custom-call | flops 10000000000 | bytes 100000000 | tf_op jit(solution)/shard_map/scan_backward/pallas_call | solution.py:362
  379.5 0.8 reshape.175
  380.3 0.8 slice_reduce_fusion.4
  381.0 0.1 reshape_squeeze.3
  381.1 0.1 reduce_sum.69
  381.2 0.8 slice_bitcast_fusion
  382.0 0.1 concatenate.20
  382.1 0.6 pad_bitcast_fusion.small
  382.7 91.6 %sum_to_owners.1 = (bf16[4,64,1408]{2,1,0:T(8,128)(2,1)}, f32[128,1024]{1,0:T(8,128)}, f32[128,1024]{1,0:T(8,128)}, bf16[4,64,1024]{2,1,0:T(8,128)(2,1)}, f32[256,2048]{1,0:T(8,128)}, /*index=5*/f32[8,64,128]{2,1,0:T(8,128)}) custom-call(bf16[1024,2048]{1,0:T(8,128)(2,1)} %fusion.1.normed, bf16[4,128,1024]{2,1,0:T(8,128)(2,1)} %get-tuple-element.77.left, ...), custom_call_target="tpu_custom_call" | custom-call | tf_op jit(solution)/shard_map/sum_to_owners/pallas_call | solution.py:1476
  474.3 22.3 %gradient_norm.1 = (f32[256,2048]{1,0:T(8,128)}, f32[224,128]{1,0:T(8,128)}, f32[8,128]{1,0:T(8,128)}, f32[8,128]{1,0:T(8,128)}) custom-call(bf16[4,64,1408]{2,1,0:T(8,128)(2,1)} %get-tuple-element.84.part_h, bf16[4,64,1024]{2,1,0:T(8,128)(2,1)} %get-tuple-element.85.gate_h, f32[128,1024]{1,0:T(8,128)} %get-tuple-element.86.left_h, ...), custom_call_target="tpu_custom_call" | custom-call | tf_op jit(solution)/shard_map/gradient_norm/pallas_call | solution.py:726
  496.6 1.3 fusion.33
  497.9 1.3 slice_multiply_fusion
  499.2 0.1 mul.193
  499.3 0.1 mul.195
  499.4 0.6 add_subtract_fusion
  500.0 2.0 multiply_subtract_fusion
  502.1 10.9 %update_weights.1 = (f32[256,2048]{1,0:T(8,128)}, f32[64,8512]{1,0:T(8,128)}, f32[64,8512]{1,0:T(8,128)}, f32[64,8512]{1,0:T(8,128)}, bf16[64,8512]{1,0:T(8,128)...) custom-call(f32[8,128]{1,0:T(8,128)} %get-tuple-element.90.norm, ...), custom_call_target="tpu_custom_call" | custom-call | tf_op jit(solution)/shard_map/update_weights/pallas_call | solution.py:856
  (72 shorter events, 0.5 us)
Async XLA Ops:
  7.2 81.4 %copy-start.19 = (f32[3,64]{1,0:T(4,128)S(1)}, f32[3,64]{1,0:T(4,128)}, u32[]{:S(2)}) copy-start(f32[3,64]{1,0:T(4,128)} %param.25) | copy-start | bytes 2308
  7.2 243.4 %all-gather.2.cloned.1.call-start = ((), (), s32[]{:S(2)}) async-start(), calls=%async_computation | async-start | bytes 17301504 | tf_op jit(solution)/shard_map/all_gather | solution.py:1542
  10.0 1.2 copy-start
  11.3 1.6 copy-start.1
  84.5 40.4 %collective-permute-start = (bf16[4,64,1024]{2,1,0:T(8,128)(2,1)S(1)}, bf16[4,64,1024]{2,1,0:T(8,128)(2,1)S(1)}, u32[]{:S(2)}, u32[]{:S(2)}) collective-permute-start(bf16[4,64,1024]{2,1,0:T(8,128)(2,1)S(1)} %get-tuple-element.60), channel_id=1, source_target_pairs={{0,8},{4,12},{8,0},{12,4},{16,24},{20,28},{24,16},{28,20},{1,9},{5... | collective-permute-start | bytes 1572872 | tf_op jit(solution)/shard_map/ppermute | solution.py:1550
  84.6 40.3 %collective-permute-start.1 = (bf16[4,64,1024]{2,1,0:T(8,128)(2,1)S(1)}, bf16[4,64,1024]{2,1,0:T(8,128)(2,1)}, u32[]{:S(2)}, u32[]{:S(2)}) collective-permute-start(bf16[4,64,1024]{2,1,0:T(8,128)(2,1)S(1)} %get-tuple-element.60), channel_id=1, source_target_pairs={{0,16},{4,20},{8,24},{12,28},{16,0},{20,4},{24,8},{28,12},{1,17},{... | collective-permute-start | bytes 1572872 | tf_op jit(solution)/shard_map/ppermute | solution.py:1550
  86.3 45.2 %collective-permute-start.2 = (bf16[4,64,1024]{2,1,0:T(8,128)(2,1)S(1)}, bf16[4,64,1024]{2,1,0:T(8,128)(2,1)}, u32[]{:S(2)}, u32[]{:S(2)}) collective-permute-start(bf16[4,64,1024]{2,1,0:T(8,128)(2,1)S(1)} %get-tuple-element.60), channel_id=1, source_target_pairs={{0,24},{4,28},{8,16},{12,20},{16,8},{20,12},{24,0},{28,4},{1,25},{... | collective-permute-start | bytes 1572872 | tf_op jit(solution)/shard_map/ppermute | solution.py:1550
  88.3 48.5 %copy-start.17 = (f32[2048]{0:T(1024)}, f32[2048]{0:T(1024)S(1)}, u32[]{:S(2)}) copy-start(f32[2048]{0:T(1024)S(1)} %slice.97) | copy-start | bytes 24580
  88.8 16.8 %copy-start.4 = (f32[1,1024]{1,0:T(1,128)}, f32[1,1024]{1,0:T(1,128)S(1)}, u32[]{:S(2)}) copy-start(f32[1,1024]{1,0:T(1,128)S(1)} %reshape_reshape.3.skip) | copy-start | bytes 12292
  88.8 3.7 copy-start.7
  88.9 16.8 %copy-start.5 = (f32[8,128]{1,0:T(8,128)}, f32[8,128]{1,0:T(8,128)S(1)}, u32[]{:S(2)}) copy-start(f32[8,128]{1,0:T(8,128)S(1)} %select_maximum_fusion.heads) | copy-start | bytes 12292
  92.2 13.5 %copy-start.3 = (f32[8,1280]{1,0:T(8,128)}, f32[8,1280]{1,0:T(8,128)S(1)}, u32[]{:S(2)}) copy-start(f32[8,1280]{1,0:T(8,128)S(1)} %pad_maximum_fusion.taps) | copy-start | bytes 122884
  92.2 13.5 %copy-start.2 = (bf16[128,1024]{1,0:T(8,128)(2,1)}, bf16[128,1024]{1,0:T(8,128)(2,1)S(1)}, u32[]{:S(2)}) copy-start(bf16[128,1024]{1,0:T(8,128)(2,1)S(1)} %fusion.8.spread) | copy-start | bytes 786436
  92.6 4.3 copy-start.13
  93.6 11.8 %copy-start.14 = (bf16[4,256,2048]{2,1,0:T(8,128)(2,1)}, bf16[4,256,2048]{2,1,0:T(8,128)(2,1)S(1)}, u32[]{:S(2)}) copy-start(bf16[4,256,2048]{2,1,0:T(8,128)(2,1)S(1)} %multiply_convert_fusion) | copy-start | bytes 12582916
  123.6 1.3 copy-start.6
  133.8 8.3 %collective-permute-start.3 = (bf16[4,4,64,1024]{3,2,1,0:T(8,128)(2,1)S(1)}, bf16[4,4,64,1024]{3,2,1,0:T(8,128)(2,1)}, u32[]{:S(2)}, u32[]{:S(2)}) collective-permute-start(bf16[4,4,64,1024]{3,2,1,0:T(8,128)(2,1)S(1)} %bitcast_dynamic-update-slice_fusion), channel_id=1, source_target_pairs={{0,4},{4,0},{8,12},{12,8},{16,20},{20,16},{24,28},{28,24},{1,5},{5... | collective-permute-start | bytes 6291464 | tf_op jit(solution)/shard_map/ppermute | solution.py:1585
  142.1 3.5 copy-start.15
  142.1 6.3 %copy-start.16 = (f32[1024,1024]{1,0:T(8,128)S(1)}, f32[1024,1024]{1,0:T(8,128)}, u32[]{:S(2)}) copy-start(f32[1024,1024]{1,0:T(8,128)} %get-tuple-element.66.y) | copy-start | bytes 12582916
  145.0 10.4 %copy-start.9 = (bf16[4,2,4,64,1024]{4,3,2,1,0:T(8,128)(2,1)}, bf16[4,2,4,64,1024]{4,3,2,1,0:T(8,128)(2,1)S(1)}, u32[]{:S(2)}) copy-start(bf16[4,2,4,64,1024]{4,3,2,1,0:T(8,128)(2,1)S(1)} %maximum_select_fusion) | copy-start | bytes 12582916
  155.4 2.0 copy-start.10
  308.4 2.4 copy-start.11
  310.8 12.6 %copy-start.8 = (bf16[1024,2048]{1,0:T(8,128)(2,1)S(1)}, bf16[1024,2048]{1,0:T(8,128)(2,1)}, u32[]{:S(2)}) copy-start(bf16[1024,2048]{1,0:T(8,128)(2,1)} %fusion.1.normed) | copy-start | bytes 12582916
  323.5 6.2 %copy-start.12 = (bf16[1024,1024]{1,0:T(8,128)(2,1)}, bf16[1024,1024]{1,0:T(8,128)(2,1)S(1)}, u32[]{:S(2)}) copy-start(bf16[1024,1024]{1,0:T(8,128)(2,1)S(1)} %get-tuple-element.187.dz) | copy-start | bytes 6291460
  474.3 25.1 %copy-start.22 = (f32[3,64]{1,0:T(4,128)S(1)}, f32[3,64]{1,0:T(4,128)}, u32[]{:S(2)}) copy-start(f32[3,64]{1,0:T(4,128)} %param.26) | copy-start | bytes 2308
  474.3 25.1 %copy-start.23 = (f32[3,64]{1,0:T(4,128)S(1)}, f32[3,64]{1,0:T(4,128)}, u32[]{:S(2)}) copy-start(f32[3,64]{1,0:T(4,128)} %param.27) | copy-start | bytes 2308
  474.3 25.7 %copy-start.18 = (f32[872]{0:T(1024)S(1)}, f32[872]{0:T(1024)}, u32[]{:S(2)}) copy-start(f32[872]{0:T(1024)} %param.22) | copy-start | bytes 10468
  474.3 25.7 %copy-start.20 = (f32[872]{0:T(1024)S(1)}, f32[872]{0:T(1024)}, u32[]{:S(2)}) copy-start(f32[872]{0:T(1024)} %param.23) | copy-start | bytes 10468
  474.3 25.7 %copy-start.21 = (f32[872]{0:T(1024)S(1)}, f32[872]{0:T(1024)}, u32[]{:S(2)}) copy-start(f32[872]{0:T(1024)} %param.24) | copy-start | bytes 10468
Sparse Core Ops, SparseCore 0:
  84.6 165.9 all-gather.1

commit v5 on v4

--- a/solution.py
+++ b/solution.py
@@ -90,14 +90,8 @@
     return jnp.exp(jnp.where(causal, gap, MASKED))
 
 
-def scan_forward_kernel(cw, px, taps, heads, skip, spread, y, states, xbuf, state, xdt, carried):
+def scan_forward_step(cw, px, taps, heads, skip, spread, y, states, xbuf, state, xdt, carried):
     cc = cw + 2 * N
-
-    @pl.when(pl.program_id(0) == 0)
-    def _():
-        state[...] = jnp.zeros_like(state)
-        xbuf[0:8, :] = jnp.zeros((8, cc), F32)
-
     xbuf[8 : 8 + CHUNK, :] = px[:, :cc]
     step, rate = rates(own_heads_first(px[:, cc:], cw // P_SIZE), heads)
     row, col = triangle(CHUNK)
@@ -117,7 +111,7 @@
     state_in = activated(slice(cw, cw + N))
     state_out = activated(slice(cw + N, cw + 2 * N))
     scores = dot(state_out, state_in, NT, EXACT)
-    states[0] = state[...].astype(BF16)
+    states[...] = state[...].astype(BF16)
     carried[...] = dot(state_out.astype(BF16), state[...].astype(BF16))
     first = lax.broadcasted_iota(jnp.int32, (1, LANES), 1) < P_SIZE
     for pair in range(cw // LANES):
@@ -312,43 +306,6 @@
     return pl.BlockSpec(shape, lambda i: (0,) * len(shape))
 
 
-def scan_forward(px, taps, heads, skip, spread):
-    length, width = px.shape
-    cw = skip.shape[1]
-    cc = cw + 2 * N
-    chunks = length // CHUNK
-    return pl.pallas_call(
-        functools.partial(scan_forward_kernel, cw),
-        grid=(chunks,),
-        in_specs=[
-            pl.BlockSpec((CHUNK, width), lambda i: (i, 0)),
-            whole(taps.shape),
-            whole(heads.shape),
-            whole(skip.shape),
-            whole(spread.shape),
-        ],
-        out_specs=[
-            pl.BlockSpec((CHUNK, cw), lambda i: (i, 0)),
-            pl.BlockSpec((1, N, cw), lambda i: (i, 0, 0)),
-        ],
-        out_shape=[
-            jax.ShapeDtypeStruct((length, cw), F32),
-            jax.ShapeDtypeStruct((chunks, N, cw), BF16),
-        ],
-        scratch_shapes=[
-            pltpu.VMEM((CHUNK + 8, cc), F32),
-            pltpu.VMEM((N, cw), F32),
-            pltpu.VMEM((CHUNK, cw), BF16),
-            pltpu.VMEM((CHUNK, cw), F32),
-        ],
-        compiler_params=pltpu.CompilerParams(vmem_limit_bytes=48 * 2**20),
-        cost_estimate=pl.CostEstimate(
-            flops=3 * 10**9, bytes_accessed=40 * 10**6, transcendentals=10**7
-        ),
-        name="scan_forward",
-    )(px, taps, heads, skip, spread)
-
-
 def scan_backward(collective_id, px, taps, heads, skip, spread, gather, dy, y, states, wide, gate):
     length, width = px.shape
     cw = skip.shape[1]
@@ -530,48 +487,6 @@
     return [(lax.rem(group + k, groups), q) for k in range(1, groups)]
 
 
-def swap_kernel(parts, count, *refs):
-    sources, results = refs[:count], refs[count : 2 * count]
-    sends, recvs, local = refs[2 * count :]
-    q = lax.axis_index("seq")
-    peers = seq_peers(parts)
-    greet(peers)
-    copies = []
-    for k, peer in enumerate(peers):
-        for a in range(count):
-            copy = remote(
-                sources[a].at[peer[1]], results[a].at[q], sends, recvs, k * count + a, peer
-            )
-            copy.start()
-            copies.append(copy)
-    own = [
-        pltpu.make_async_copy(sources[a].at[q], results[a].at[q], local.at[a])
-        for a in range(count)
-    ]
-    for copy in own:
-        copy.start()
-    for copy in own + copies:
-        copy.wait()
-
-
-def swap(collective_id, *arrays):
-    parts = arrays[0].shape[0]
-    count = len(arrays)
-    return pl.pallas_call(
-        functools.partial(swap_kernel, parts, count),
-        in_specs=[pl.BlockSpec(memory_space=pltpu.HBM)] * count,
-        out_specs=[pl.BlockSpec(memory_space=pltpu.HBM)] * count,
-        out_shape=[jax.ShapeDtypeStruct(a.shape, a.dtype) for a in arrays],
-        scratch_shapes=[
-            pltpu.SemaphoreType.DMA(((parts - 1) * count,)),
-            pltpu.SemaphoreType.DMA(((parts - 1) * count,)),
-            pltpu.SemaphoreType.DMA((count,)),
-        ],
-        compiler_params=pltpu.CompilerParams(collective_id=collective_id, has_side_effects=True),
-        name="swap",
-    )(*arrays)
-
-
 def all_peers(groups, parts):
     devices = groups * parts
     me = lax.axis_index("dp") * parts + lax.axis_index("seq")
@@ -869,10 +784,75 @@
     )(norm, part, gate, left, right, hidden_grad, *weights)
 
 
+class LineGather:
+    def __init__(self, line, z, core, q, slot, own, sends, recvs):
+        self.line, self.z, self.core, self.q = line, z, core, q
+        self.slot, self.own, self.sends, self.recvs = slot, own, sends, recvs
+
+    def along(self, from_z, up, first=False):
+        to = self.z + 1 if up else self.z - 1
+        return remote(
+            self.own if first else self.slot(from_z),
+            self.slot(from_z),
+            self.sends.at[0 if up else 1],
+            self.recvs.at[0 if up else 1],
+            from_z,
+            (2 * to + self.core, self.q),
+        )
+
+    def step(self, t, got=None):
+        line, z = self.line, self.z
+        low, high = z - t, z + t
+        if t == 0:
+
+            @pl.when(z < line - 1)
+            def _():
+                self.along(z, True, True).start()
+
+            @pl.when(z > 0)
+            def _():
+                self.along(z, False, True).start()
+
+            return
+
+        @pl.when(low >= 0)
+        def _():
+            self.along(low, True).wait_recv()
+
+            @pl.when(z < line - 1)
+            def _():
+                self.along(low, True).start()
+
+            if got is not None:
+                got(low)
+
+        @pl.when(high <= line - 1)
+        def _():
+            self.along(high, False).wait_recv()
+
+            @pl.when(z > 0)
+            def _():
+                self.along(high, False).start()
+
+            if got is not None:
+                got(high)
+
+    def sent(self):
+        for from_z in range(self.line):
+
+            @pl.when((from_z <= self.z) & (self.z < self.line - 1))
+            def _():
+                self.along(from_z, True).wait_send()
+
+            @pl.when((from_z >= self.z) & (self.z > 0))
+            def _():
+                self.along(from_z, False).wait_send()
+
+
 def collect_kernel(
-    groups, parts, hidden, w_in, chan, hid_out, w_out, gate_out, chan_out,
-    blocks, gates, chan_s, chan_r, hid_s, hid_r, swap_s, swap_r, gate_s, gate_r,
-    line_s, line_r, core_s, core_r, local,
+    groups, parts, hidden, w_in, w_own, chan, hid_out, w_out, gate_out, chan_out, wo_out,
+    blocks, gates, low, chan_s, chan_r, hid_s, hid_r, swap_s, swap_r, gate_s, gate_r,
+    wo_s, wo_r, line_s, line_r, lwo_s, lwo_r, core_s, core_r, local,
 ):
     line = groups // 2
     cw = INNER // parts
@@ -888,136 +868,352 @@
         blocks[part, :, :cw] = w_in[:, at : at + cw].astype(BF16)
         blocks[part, :, cw : cc + H] = shared
         blocks[part, :, cc + H :] = jnp.zeros((w_in.shape[0], LANES - H), BF16)
+    low[...] = w_own[...].astype(BF16)
     greet(everyone)
     swaps = []
     for k, peer in enumerate(peers):
         copy = remote(blocks.at[peer[1]], w_out.at[group, q], swap_s, swap_r, k, peer)
         copy.start()
         swaps.append(copy)
-    mine = pltpu.make_async_copy(blocks.at[q], w_out.at[group, q], local.at[0])
-    mine.start()
-    keep = pltpu.make_async_copy(hidden, hid_out.at[q], local.at[1])
-    keep.start()
-    chans = []
+    outs = LineGather(
+        line, z, core, q, lambda from_z: wo_out.at[2 * from_z + core, q], low, lwo_s, lwo_r
+    )
+    outs.step(0)
+    own = [
+        pltpu.make_async_copy(blocks.at[q], w_out.at[group, q], local.at[0]),
+        pltpu.make_async_copy(hidden, hid_out.at[q], local.at[1]),
+        pltpu.make_async_copy(chan, chan_out.at[group * parts + q], local.at[2]),
+        pltpu.make_async_copy(low, wo_out.at[group, q], local.at[3]),
+    ]
+    for copy in own:
+        copy.start()
+    waiting = []
     for k, peer in enumerate(everyone):
         copy = remote(chan, chan_out.at[group * parts + q], chan_s, chan_r, k, peer)
         copy.start()
-        chans.append(copy)
-    chan_keep = pltpu.make_async_copy(chan, chan_out.at[group * parts + q], local.at[2])
-    chan_keep.start()
+        waiting.append(copy)
     for part in range(parts):
         gates[part] = w_in[:, part * cw : (part + 1) * cw].astype(BF16)
-    mine.wait()
+    copy = pltpu.make_async_copy(gates.at[q], gate_out.at[q], local.at[4])
+    copy.start()
+    own.append(copy)
+    own[0].wait()
     for copy in swaps:
         copy.wait()
-    hids = []
     for k, peer in enumerate(peers):
-        copy = remote(hidden, hid_out.at[q], hid_s, hid_r, k, peer)
-        copy.start()
-        hids.append(copy)
-    for k, peer in enumerate(peers):
-        copy = remote(gates.at[peer[1]], gate_out.at[q], gate_s, gate_r, k, peer)
-        copy.start()
-        hids.append(copy)
-    gate_keep = pltpu.make_async_copy(gates.at[q], gate_out.at[q], local.at[3])
-    gate_keep.start()
-
-    def along(from_z, up):
-        block = w_out.at[2 * from_z + core]
-        to = z + 1 if up else z - 1
-        return remote(
-            block, block, line_s.at[0 if up else 1], line_r.at[0 if up else 1], from_z,
-            (2 * to + core, q),
-        )
+        for source, target, sends, recvs in (
+            (hidden, hid_out.at[q], hid_s, hid_r),
+            (gates.at[peer[1]], gate_out.at[q], gate_s, gate_r),
+            (low, wo_out.at[group, q], wo_s, wo_r),
+        ):
+            copy = remote(source, target, sends, recvs, k, peer)
+            copy.start()
+            waiting.append(copy)
 
     def across(from_z):
         block = w_out.at[2 * from_z + core]
         return remote(block, block, core_s, core_r, from_z, sibling)
 
-    for t in range(line):
-        low, high = z - t, z + t
-        if t == 0:
-            across(z).start()
-
-            @pl.when(z < line - 1)
-            def _():
-                along(z, True).start()
-
-            @pl.when(z > 0)
-            def _():
-                along(z, False).start()
-
-            continue
-
-        @pl.when(low >= 0)
-        def _():
-            along(low, True).wait_recv()
-
-            @pl.when(z < line - 1)
-            def _():
-                along(low, True).start()
-
-            across(low).start()
-
-        @pl.when(high <= line - 1)
-        def _():
-            along(high, False).wait_recv()
-
-            @pl.when(z > 0)
-            def _():
-                along(high, False).start()
-
-            across(high).start()
-
+    ins = LineGather(
+        line, z, core, q, lambda from_z: w_out.at[2 * from_z + core], w_out.at[group],
+        line_s, line_r,
+    )
+    across(z).start()
+    ins.step(0)
+    for t in range(1, line):
+        ins.step(t, lambda from_z: across(from_z).start())
+        if t == line - 2 or line == 2:
+            for s in range(1, line):
+                outs.step(s)
+    ins.sent()
+    outs.sent()
     for from_z in range(line):
         across(from_z).wait_send()
         block = w_out.at[2 * from_z + 1 - core]
         remote(block, block, core_s, core_r, from_z, sibling).wait_recv()
-
-        @pl.when((from_z <= z) & (z < line - 1))
-        def _():
-            along(from_z, True).wait_send()
-
-        @pl.when((from_z >= z) & (z > 0))
-        def _():
-            along(from_z, False).wait_send()
-
-    keep.wait()
-    chan_keep.wait()
-    gate_keep.wait()
-    for copy in hids + chans:
+    for copy in own[1:] + waiting:
         copy.wait()
 
 
-def collect(collective_id, hidden, w_in, chan, groups, parts):
+def collect(collective_id, hidden, w_in, w_own, chan, groups, parts):
     rows = w_in.shape[0]
     line = groups // 2
     cw = INNER // parts
     width = cw + 2 * N + LANES
     sem = pltpu.SemaphoreType.DMA
     hbm = pl.BlockSpec(memory_space=pltpu.HBM)
+    vmem = pl.BlockSpec(memory_space=pltpu.VMEM)
     return pl.pallas_call(
         functools.partial(collect_kernel, groups, parts),
-        in_specs=[hbm, pl.BlockSpec(memory_space=pltpu.VMEM), hbm],
-        out_specs=[hbm] * 4,
+        in_specs=[hbm, vmem, vmem, hbm],
+        out_specs=[hbm] * 5,
         out_shape=[
             jax.ShapeDtypeStruct((parts,) + hidden.shape, hidden.dtype),
             jax.ShapeDtypeStruct((groups, parts, rows, width), BF16),
             jax.ShapeDtypeStruct((parts, rows, cw), BF16),
             jax.ShapeDtypeStruct((groups * parts,) + chan.shape, chan.dtype),
+            jax.ShapeDtypeStruct((groups, parts) + w_own.shape, BF16),
         ],
         scratch_shapes=[
             pltpu.VMEM((parts, rows, width), BF16),
             pltpu.VMEM((parts, rows, cw), BF16),
+            pltpu.VMEM(w_own.shape, BF16),
             *([sem((groups * parts - 1,))] * 2),
-            *([sem((parts - 1,))] * 6),
-            sem((2, line)), sem((2, line)), sem((line,)), sem((line,)), sem((4,)),
+            *([sem((parts - 1,))] * 8),
+            *([sem((2, line))] * 4),
+            sem((line,)), sem((line,)), sem((5,)),
         ],
         compiler_params=pltpu.CompilerParams(
             collective_id=collective_id, has_side_effects=True, vmem_limit_bytes=48 * 2**20
         ),
         name="collect",
-    )(hidden, w_in, chan)
+    )(hidden, w_in, w_own, chan)
+
+
+def forward_kernel(
+    groups, parts, cw,
+    hidden_h, wx_h, gate_h, wo_in, gain_in, gain_out, taps, heads, skip, spread,
+    normed_h, px_h, y_h, states_h, z_h, u_h, wz_h, wo,
+    hidden, wx, wz, normed, px, y, states, zs, us, xbuf, state, xdt, carried,
+    line_s, line_r, core_s, core_r, out_s, out_r, load, store,
+):
+    line = groups // 2
+    cc = cw + 2 * N
+    length = px.shape[0]
+    chunks = length // CHUNK
+    group, q = lax.axis_index("dp"), lax.axis_index("seq")
+    z, core = group // 2, lax.rem(group, 2)
+    sibling = (2 * z + 1 - core, q)
+    peers = seq_peers(parts)
+    loads = [
+        pltpu.make_async_copy(source, target, load.at[k])
+        for k, (source, target) in enumerate(
+            [(hidden_h, hidden), (wx_h, wx), (gate_h, wz.at[group])]
+        )
+    ]
+    for copy in loads:
+        copy.start()
+    greet(peers + dp_peers(groups))
+
+    places = [lax.rem(z + k, line) for k in range(1, line)]
+
+    def plane(k, k_to, device, block):
+        return remote(block, block, out_s, out_r, k * (parts + 1) + k_to, device)
+
+    if parts == 4:
+        near = [q + 1 - 2 * lax.rem(q, 2), lax.rem(q + 2, 4)]
+        half = wo.shape[2] // 2
+
+    def early(k):
+        block = wo.at[2 * places[k] + core, q]
+        if parts == 4:
+            return [plane(k, h, (group, near[h]), block) for h in range(2)]
+        return [plane(k, j, peer, block) for j, peer in enumerate(peers)]
+
+    def late(k, h):
+        rows = pl.ds(h * half, half)
+        block = wo.at[2 * places[k] + core, near[h], rows]
+        return plane(k, 2 + h, (group, near[1 - h]), block)
+
+    for k in range(line - 1):
+        for copy in early(k):
+            copy.start()
+
+    def across(from_z):
+        block = wz.at[2 * from_z + core]
+        return remote(block, block, core_s, core_r, from_z, sibling)
+
+    gates = LineGather(
+        line, z, core, q, lambda from_z: wz.at[2 * from_z + core], wz.at[group], line_s, line_r
+    )
+    loads[2].wait()
+    across(z).start()
+    gates.step(0)
+    loads[0].wait()
+
+    def norm_rows(i, carry):
+        rows = pl.ds(pl.multiple_of(i * 32, 32), 32)
+        tokens = hidden[rows, :].astype(F32)
+        mean = jnp.sum(tokens * tokens, axis=-1, keepdims=True) / D
+        normed[rows, :] = (tokens * lax.rsqrt(mean + EPS_IN) * gain_in[...]).astype(BF16)
+        return carry
+
+    lax.fori_loop(0, length // 32, norm_rows, 0)
+    loads[1].wait()
+    tall = 256
+
+    def project_rows(i, carry):
+        rows = pl.ds(pl.multiple_of(i * tall, tall), tall)
+        px[rows, :] = dot(normed[rows, :], wx[...])
+        return carry
+
+    lax.fori_loop(0, length // tall, project_rows, 0)
+    stores = [
+        pltpu.make_async_copy(normed, normed_h, store.at[0]),
+        pltpu.make_async_copy(px, px_h, store.at[1]),
+    ]
+    for copy in stores:
+        copy.start()
+    state[...] = jnp.zeros_like(state)
+    xbuf[0:8, :] = jnp.zeros((8, cc), F32)
+
+    def scan_rows(i, carry):
+        for t in range(1, line):
+
+            @pl.when(i == min(3 * (t - 1), chunks - 1))
+            def _(t=t):
+                gates.step(t, lambda from_z: across(from_z).start())
+
+        rows = pl.ds(pl.multiple_of(i * CHUNK, CHUNK), CHUNK)
+        scan_forward_step(
+            cw, px.at[rows], taps, heads, skip, spread, y.at[rows], states.at[i],
+            xbuf, state, xdt, carried,
+        )
+        return carry
+
+    lax.fori_loop(0, chunks, scan_rows, 0)
+    for source, target, at in ((y, y_h, 2), (states, states_h, 3)):
+        copy = pltpu.make_async_copy(source, target, store.at[at])
+        copy.start()
+        stores.append(copy)
+    if parts == 4:
+        for k in range(line - 1):
+            for copy in early(k):
+                copy.wait()
+            for h in range(2):
+                late(k, h).start()
+    for from_z in range(line):
+        across(from_z).wait_send()
+        block = wz.at[2 * from_z + 1 - core]
+        remote(block, block, core_s, core_r, from_z, sibling).wait_recv()
+    gates.sent()
+    copy = pltpu.make_async_copy(wz, wz_h, store.at[4])
+    copy.start()
+    stores.append(copy)
+    lane = lax.broadcasted_iota(jnp.int32, (1, LANES), 1)
+    wide = 512
+
+    def gate_rows(i, carry):
+        rows = pl.ds(pl.multiple_of(i * tall, tall), tall)
+        weights = wz[...].reshape(D, cw)
+        gate_in = dot(normed[rows, :], weights)
+        zs[rows, :] = gate_in
+        gated = y[rows, :] * (gate_in * jax.nn.sigmoid(gate_in))
+        us[rows, :cw] = (gated * gain_out[...]).astype(BF16)
+        highs = jnp.zeros((tall, LANES), F32)
+        rests = jnp.zeros((tall, LANES), F32)
+        for b in range(cw // wide):
+            block = gated[:, b * wide : (b + 1) * wide]
+            total = jnp.sum(block * block, axis=-1, keepdims=True)
+            level = level_of(q * cw + b * wide, wide)
+            highs = highs + jnp.where(lane == level, total, 0.0)
+            rests = rests + jnp.where(lane == level + LEVELS, total, 0.0)
+        rests = rests - rests.astype(BF16).astype(F32)
+        us[rows, cw:] = jnp.where(lane < LEVELS, highs, rests).astype(BF16)
+        return carry
+
+    lax.fori_loop(0, length // tall, gate_rows, 0)
+    for source, target, at in ((zs, z_h, 5), (us, u_h, 6)):
+        copy = pltpu.make_async_copy(source, target, store.at[at])
+        copy.start()
+        stores.append(copy)
+    for k in range(line - 1):
+        if parts == 4:
+            for h in range(2):
+                late(k, h).wait()
+        else:
+            for copy in early(k):
+                copy.wait()
+    for copy in stores:
+        copy.wait()
+
+
+def forward(collective_id, hidden, wx, gate, wo, gain_in, gain_out, taps, heads, skip, spread):
+    groups, parts = wo.shape[:2]
+    line = groups // 2
+    length = hidden.shape[0]
+    rows, cw = gate.shape[1:]
+    cc = cw + 2 * N
+    width = cc + LANES
+    chunks = length // CHUNK
+    sem = pltpu.SemaphoreType.DMA
+    hbm = pl.BlockSpec(memory_space=pltpu.HBM)
+    vmem = pl.BlockSpec(memory_space=pltpu.VMEM)
+    made = [
+        jax.ShapeDtypeStruct((length, D), BF16),
+        jax.ShapeDtypeStruct((length, width), F32),
+        jax.ShapeDtypeStruct((length, cw), F32),
+        jax.ShapeDtypeStruct((chunks, N, cw), BF16),
+        jax.ShapeDtypeStruct((length, cw), F32),
+        jax.ShapeDtypeStruct((length, cw + LANES), BF16),
+    ]
+    wz = jax.ShapeDtypeStruct((groups, parts, rows, cw), BF16)
+    return pl.pallas_call(
+        functools.partial(forward_kernel, groups, parts, cw),
+        in_specs=[*([hbm] * 4), *([vmem] * 6)],
+        out_specs=[hbm] * 8,
+        out_shape=[*made, wz, jax.ShapeDtypeStruct(wo.shape, BF16)],
+        input_output_aliases={3: 7},
+        scratch_shapes=[
+            pltpu.VMEM(hidden.shape, BF16),
+            pltpu.VMEM(wx.shape, BF16),
+            pltpu.VMEM(wz.shape, BF16),
+            *[pltpu.VMEM(m.shape, m.dtype) for m in made],
+            pltpu.VMEM((CHUNK + 8, cc), F32),
+            pltpu.VMEM((N, cw), F32),
+            pltpu.VMEM((CHUNK, cw), BF16),
+            pltpu.VMEM((CHUNK, cw), F32),
+            sem((2, line)), sem((2, line)), sem((line,)), sem((line,)),
+            sem(((line - 1) * (parts + 1),)), sem(((line - 1) * (parts + 1),)),
+            sem((3,)), sem((7,)),
+        ],
+        compiler_params=pltpu.CompilerParams(
+            collective_id=collective_id, has_side_effects=True, vmem_limit_bytes=63 * 2**20
+        ),
+        name="forward",
+    )(hidden, wx, gate, wo, gain_in, gain_out, taps, heads, skip, spread)
+
+
+def swap_out_kernel(groups, parts, u, wo_in, u_out, wo, sends, recvs, core_s, core_r, local):
+    group, q = lax.axis_index("dp"), lax.axis_index("seq")
+    z, core = group // 2, lax.rem(group, 2)
+    sibling = (2 * z + 1 - core, q)
+    peers = seq_peers(parts)
+    greet(peers + [sibling])
+    copies = [
+        remote(u.at[peer[1]], u_out.at[q], sends, recvs, k, peer) for k, peer in enumerate(peers)
+    ]
+    for d in range(groups // 2):
+        block = wo.at[2 * d + core]
+        copies.append(remote(block, block, core_s, core_r, d, sibling))
+    copies.append(pltpu.make_async_copy(u.at[q], u_out.at[q], local))
+    for copy in copies:
+        copy.start()
+    for copy in copies[: parts - 1]:
+        copy.wait()
+    for d in range(groups // 2):
+        copies[parts - 1 + d].wait_send()
+        block = wo.at[2 * d + 1 - core]
+        remote(block, block, core_s, core_r, d, sibling).wait_recv()
+    copies[-1].wait()
+
+
+def swap_out(collective_id, u, wo):
+    groups, parts = wo.shape[:2]
+    sem = pltpu.SemaphoreType.DMA
+    hbm = pl.BlockSpec(memory_space=pltpu.HBM)
+    return pl.pallas_call(
+        functools.partial(swap_out_kernel, groups, parts),
+        in_specs=[hbm] * 2,
+        out_specs=[hbm] * 2,
+        out_shape=[jax.ShapeDtypeStruct(u.shape, BF16), jax.ShapeDtypeStruct(wo.shape, BF16)],
+        input_output_aliases={1: 1},
+        scratch_shapes=[
+            sem((parts - 1,)), sem((parts - 1,)), sem((groups // 2,)), sem((groups // 2,)), sem,
+        ],
+        compiler_params=pltpu.CompilerParams(collective_id=collective_id, has_side_effects=True),
+        name="swap_out",
+    )(u, wo)
 
 
 def add_blocks(out, a, b, rows, steps):
@@ -1506,12 +1702,6 @@
     )(normed, left, right, gate, small, dz, dpx, wz, wx)
 
 
-def pack_terms(values):
-    high = lax.reduce_precision(values, 8, 7)
-    packed = jnp.concatenate([high, values - high], axis=-1).astype(BF16)
-    return jnp.pad(packed, ((0, 0), (0, LANES - packed.shape[-1])))
-
-
 def unpack_terms(packed, count):
     packed = packed.astype(F32)
     return packed[..., :count] + packed[..., count : 2 * count]
@@ -1537,18 +1727,12 @@
     chan_block = jnp.pad(
         lax.reduce_precision(chan_params, 8, 7), (0, chan_rows * LANES - chan_len)
     ).reshape(chan_rows, LANES)
-    hidden, wx, wz, chan_full = collect(0, hidden_in[0], w_in, chan_block, groups, parts)
-    out_low, chan_full = lax.optimization_barrier((w_out.astype(BF16), chan_full))
-    wo = lax.all_gather(out_low, ("dp", "seq"), axis=0, tiled=True)
-    hidden = hidden.reshape(length, D)
-    wx = wx.reshape(D, cc + LANES)
+    hidden, wx, gate, chan_full, wo = collect(
+        0, hidden_in[0], w_in, w_out, chan_block, groups, parts
+    )
     chan_full = chan_full.reshape(groups * parts, chan_rows * LANES)[:, :chan_len].reshape(-1)
     line = groups // 2
     group = lax.axis_index("dp")
-    core, place = group % 2, group // 2
-    wz_blocks = [
-        lax.ppermute(wz, "dp", [(i, i ^ (2 * k)) for i in range(groups)]) for k in range(1, line)
-    ]
 
     conv_taps = chan_full[: TAPS * CONV_CH].reshape(TAPS, CONV_CH)
     conv_bias = chan_full[TAPS * CONV_CH : (TAPS + 1) * CONV_CH].reshape(1, CONV_CH)
@@ -1571,36 +1755,18 @@
         jnp.arange(LANES)[:, None] == (jnp.arange(cw) // P_SIZE)[None, :]
     ).astype(BF16)
 
-    tokens = hidden.astype(F32)
-    scale = lax.rsqrt(jnp.mean(tokens * tokens, axis=-1, keepdims=True) + EPS_IN)
-    normed = (tokens * scale * gain_in).astype(BF16)
-    px = dot(normed, wx)
-    y, states = scan_forward(px, taps, heads, skip, spread)
-    wz_blocks, y = lax.optimization_barrier((wz_blocks, y))
-    wz_line = lax.dynamic_update_index_in_dim(
-        jnp.zeros((line,) + wz.shape, BF16), wz, place, 0
-    )
-    for k in range(1, line):
-        wz_line = lax.dynamic_update_index_in_dim(wz_line, wz_blocks[k - 1], place ^ k, 0)
-    other = lax.ppermute(wz_line, "dp", [(i, i ^ 1) for i in range(groups)])
-    wz = jnp.where(core == 0, jnp.stack([wz_line, other], 1), jnp.stack([other, wz_line], 1))
-    wz = wz.reshape(D, cw)
-    z = dot(normed, wz)
+    normed, px, y, states, z, u_blocks, wz, wo = forward(
+        1, hidden.reshape(length, D), wx.reshape(D, cc + LANES), gate, wo, gain_in.reshape(1, D),
+        own_gain.reshape(1, cw), taps, heads, skip, spread,
+    )
+    wx, wz = wx.reshape(D, cc + LANES), wz.reshape(D, cw)
+    u, wo = swap_out(2, u_blocks.reshape(parts, rows, cw + LANES), wo)
+    wo = wo.reshape(INNER, D)
     sig = jax.nn.sigmoid(z)
     gate = z * sig
     gated = y * gate
     channel = q * cw + jnp.arange(cw)
-    squares = jnp.stack(
-        [
-            jnp.sum(jnp.where((channel >= low) & (channel < high), gated * gated, 0.0), axis=-1)
-            for low, high in SEGMENTS
-        ],
-        axis=-1,
-    )
-    u_blocks = jnp.concatenate([(gated * own_gain).astype(BF16), pack_terms(squares)], axis=-1)
-    u = swap(2, u_blocks.reshape(parts, rows, cw + LANES))[0]
-
-    own_tokens = hidden_in[0].astype(F32)
+
     cotangent = out_grads[:, 0]
     block_out, back_blocks, mixed = widths(u, wo, cotangent, hidden_in[0])
     block_out = block_out[:, None]

time: 530 us -> 474 us (0.89)
  Pallas kernels: 365 us -> 425 us
  waiting for transfers between devices: 53.9 us -> 0 us
  other arithmetic: 37.4 us -> 19.8 us
  matrix products: 21.7 us -> 6.11 us
  between operations: 15 us -> 1.4 us
  local copies, waits for them, and re-layouts: 21.9 us -> 12.8 us
  starting transfers between devices: 5.72 us -> 0 us
    all_gather x1 -> x0, waiting for transfers between devices: 47.3 us -> none  [on_device(): wo = lax.all_gather(out_low, ('dp', 'seq'), axis=0, tiled=True)]
    pallas_call x2, Pallas kernels: 60.6 us -> 94 us  [the longest x1 63.6 us: forward(): pl.pallas_call(functools.partial(forward_kernel, groups, parts, cw), in_s...]
    pallas_call x1, Pallas kernels: 71.6 us -> 98.3 us  [collect(): pl.pallas_call(functools.partial(collect_kernel, groups, parts), in_specs...]
    dot_general x3 -> x1, matrix products: 21.7 us -> 6.11 us  [dot(): lax.dot_general(a, b, (dims, ((), ())), precision=precision, preferred_el...]
    convert_element_type x3 -> x0, other arithmetic: 8.36 us -> none  [the longest x2 6.28 us: on_device(): normed = (tokens * scale * gain_in).astype(BF16)]
    unnamed x50 -> x29, local copies, waits for them, and re-layouts: 13.2 us -> 4.93 us
    ppermute x4 -> x0, waiting for transfers between devices: 6.63 us -> none  [the longest x3 6.63 us: on_device(): lax.ppermute(wz, 'dp', [(i, i ^ 2 * k) for i in range(groups)])]
    ppermute x4 -> x0, starting transfers between devices: 5.68 us -> none  [the longest x3 3.6 us: on_device(): lax.ppermute(wz, 'dp', [(i, i ^ 2 * k) for i in range(groups)])]
  transfers between devices with their start and end apart: 5 -> 0, of which waited for: 2 -> 0; matrix products, arithmetic and copies ran while one was open for 7% -> 0% of each run, Pallas kernels for 12% -> 0%
where the time goes in v5:
time: 474 us; the launch traced here: 465 us
  Pallas kernels  425 us (90%)
  other arithmetic  19.8 us (4%)
  local copies, waits for them, and re-layouts  12.8 us (3%)
  matrix products  6.11 us (1%)
    pallas_call x1, Pallas kernels, collect(): pl.pallas_call(functools.partial(collect_kernel, groups, parts), in_specs...  98.3 us
    pallas_call x1, Pallas kernels, sum_to_owners(): pl.pallas_call(functools.partial(owners_kernel, groups, parts, rows), in_...  92.2 us
    pallas_call x1, Pallas kernels, forward(): pl.pallas_call(functools.partial(forward_kernel, groups, parts, cw), in_s...  63.6 us
    pallas_call x1, Pallas kernels, scan_backward(): pl.pallas_call(functools.partial(scan_backward_kernel, 2 * line, parts, c...  50.1 us
    pallas_call x1, Pallas kernels, swap_back(): pl.pallas_call(functools.partial(swap_back_kernel, groups, parts, wide -...  34 us
    pallas_call x1, Pallas kernels, swap_out(): pl.pallas_call(functools.partial(swap_out_kernel, groups, parts), in_spec...  30.4 us
    pallas_call x1, Pallas kernels, widths(): pl.pallas_call(functools.partial(widths_kernel, cw), grid=(INNER // WIDE,...  23.2 us
    pallas_call x1, Pallas kernels, gradient_norm(): pl.pallas_call(functools.partial(norm_kernel, groups, parts), in_specs=[*...  22.1 us

profile of v5, /device:TPU:1, one launch (start us, length us, event | category | flops | bytes accessed | tf_op | source)
XLA Modules:
  0.0 464.8 jit_solution(5519205970973423144)
XLA Ops:
  0.7 0.0 copy-start.9
  0.7 0.7 reduce_precision.3
  1.4 1.2 copy-done
  2.6 1.6 copy-done.1
  4.2 1.2 copy-done.2
  5.4 98.3 %collect.1 = (bf16[4,256,2048]{2,1,0:T(8,128)(2,1)}, bf16[8,4,64,1408]{3,2,1,0:T(8,128)(2,1)}, bf16[4,64,1024]{2,1,0:T(8,128)(2,1)S(1)}, f32[32,8,128]{2,1,0:T(8,128)S(1)}, bf16[8,4,128,2048]{3,2,1,0:T(8,128)(2,1)}) custom-call(bf16[256,2048]{1,0:T(8,128)(2,1)S(1)} %bitcast.39, f32[64,8512]{1,0:T(8,128)S(1)} %copy-done.1, f32[128,2048]{1,0:T(8,128)S(1)} %copy-done.2, ...), custom_call_target="tpu_custom_call" | custom-call | tf_op jit(solution)/shard_map/collect/pallas_call | solution.py:946
  103.7 0.0 copy-start.3
  103.7 0.8 copy-done.3
  104.6 0.1 reshape.128
  104.8 0.1 pad.21.clone
  104.9 0.1 maximum_maximum_fusion
  105.0 0.6 pad_maximum_fusion.taps
  105.6 0.6 dynamic_slice.12
  106.2 0.0 copy-done.9
  106.2 0.1 constant_dynamic-slice_fusion
  106.3 0.6 select_maximum_fusion.heads
  106.9 0.1 broadcast_in_dim.77
  107.0 0.7 reshape_reshape.3.skip
  107.6 0.6 slice.97
  108.2 0.8 fusion.4.spread
  109.0 63.6 %forward.1 = (bf16[1024,2048]{1,0:T(8,128)(2,1)}, f32[1024,1408]{1,0:T(8,128)}, f32[1024,1024]{1,0:T(8,128)}, bf16[8,128,1024]{2,1,0:T(8,128)(2,1)}, f32[1024,10...) custom-call(bf16[1024,2048]{1,0:T(8,128)(2,1)} %bitcast.47, ...), custom_call_target="tpu_custom_call", output_to_operand_aliasing={{7}: (3, {})} | custom-call | tf_op jit(solution)/shard_map/forward/pallas_call | solution.py:1151
  172.6 30.4 %swap_out.1 = (bf16[4,256,1152]{2,1,0:T(8,128)(2,1)}, bf16[8,4,128,2048]{3,2,1,0:T(8,128)(2,1)}) custom-call(bf16[4,256,1152]{2,1,0:T(8,128)(2,1)} %bitcast.48, bf16[8,4,128,2048]{3,2,1,0:T(8,128)(2,1)} %get-tuple-element.69.wo_in), custom_call_target="tpu_custom_call", output_to_operand_aliasing={{1}: (1, {})} | custom-call | tf_op jit(solution)/shard_map/swap_out/pallas_call | solution.py:1205
  203.0 23.2 %widths.1 = (bf16[4,256,2048]{2,1,0:T(8,128)(2,1)}, bf16[4,256,1152]{2,1,0:T(8,128)(2,1)}, bf16[4,256,2048]{2,1,0:T(8,128)(2,1)}) custom-call(bf16[4,256,1152]{2,1,0:T(8,128)(2,1)} %get-tuple-element.70.u, bf16[4096,2048]{1,0:T(8,128)(2,1)} %bitcast.41, bf16[4,256,2048]{2,1,0:T(8,128)(2,1)} %bitcast.44, bf16[256,2048]{1,0:T(8,128)(2,1)} %bitcast.37), custom_call_target="tpu_custom_call" | custom-call | tf_op jit(solution)/shard_map/widths/pallas_call | solution.py:434
  226.2 34.0 %swap_back.1 = (bf16[4,256,1152]{2,1,0:T(8,128)(2,1)}, bf16[4,4,128,1024]{3,2,1,0:T(8,128)(2,1)}, bf16[4,4,128,1024]{3,2,1,0:T(8,128)(2,1)}) custom-call(bf16[4,256,1152]{2,1,0:T(8,128)(2,1)} %get-tuple-element.75.back, bf16[4,256,1152]{2,1,0:T(8,128)(2,1)} %get-tuple-element.70.u, bf16[4,256,2048]{2,1,0:T(8,128)(2,1)} %get-tuple-element.76.mixed), custom_call_target="tpu_custom_call" | custom-call | tf_op jit(solution)/shard_map/swap_back/pallas_call | solution.py:1298
  260.2 0.0 copy-start.5
  260.2 0.0 copy-start.7
  260.3 1.1 slice_convert_fusion
  261.4 0.2 slice_add_fusion
  261.6 1.0 slice_reduce_fusion.3
  262.7 0.0 copy-done.5
  262.7 0.0 copy-done.7
  262.7 0.0 copy-start.6
  262.7 10.6 %multiply_convert_fusion = (bf16[1024,1024]{1,0:T(8,128)(2,1)S(1)}, f32[1024,1024]{1,0:T(8,128)}, f32[1024]{0:T(1024)S(1)}) fusion(f32[1024,1024]{1,0:T(8,128)S(1)} %copy-done.5, f32[1024,1024]{1,0:T(8,128)} %get-tuple-element.79, f32[1024]{0:T(1024)S(1)} %get-tuple-element.161, f32[1024]{0:T(1024)S(1)} %get-tuple-element.162, ...), kind=kLoop, calls=%fused_computation.4 | loop fusion | flops 22019072 | bytes 16804864 | tf_op jit(solution)/shard_map/convert_element_type | solution.py:1783
  273.3 0.0 copy-done.6
  273.3 6.1 %convolution_convert_fusion = bf16[2048,1024]{1,0:T(8,128)(2,1)} fusion(bf16[1024,2048]{1,0:T(8,128)(2,1)S(1)} %copy-done.6, bf16[1024,1024]{1,0:T(8,128)(2,1)S(1)} %get-tuple-element.170.dz), kind=kOutput, calls=%fused_computation.7 | convolution fusion | flops 4297064448 | bytes 10485760 | tf_op jit(solution)/shard_map/dot_general | solution.py:44
  279.5 0.0 copy-done.4
  279.5 0.9 fusion.5.gather
  280.4 50.1 %scan_backward.1 = (bf16[1024,1408]{1,0:T(8,128)(2,1)}, f32[8,1280]{1,0:T(8,128)}, f32[8,128]{1,0:T(8,128)}, f32[8,1024]{1,0:T(8,128)}, bf16[4,128,1024]{2,1,0:T(8,128)(2,1)}, /*index=5*/bf16[256,1024]{1,0:T(8,128)(2,1)}) custom-call(f32[1024,1408]{1,0:T(8,128)} %get-tuple-element.74.px.halo, f32[1024,1408]{1,0:T(8,128)} %get-tuple-element.74.px.halo, ...), custom_call_target="tpu_custom_call" | custom-call | flops 10000000000 | bytes 100000000 | tf_op jit(solution)/shard_map/scan_backward/pallas_call | solution.py:319
  330.5 0.8 reshape.138
  331.3 0.8 slice_reduce_fusion.4
  332.0 0.1 reshape_squeeze.3
  332.1 0.1 reduce_sum.19
  332.2 0.8 slice_bitcast_fusion
  333.0 0.1 concatenate.11
  333.1 0.6 pad_bitcast_fusion.small
  333.7 92.2 %sum_to_owners.1 = (bf16[4,64,1408]{2,1,0:T(8,128)(2,1)}, f32[128,1024]{1,0:T(8,128)}, f32[128,1024]{1,0:T(8,128)}, bf16[4,64,1024]{2,1,0:T(8,128)(2,1)}, f32[256,2048]{1,0:T(8,128)}, /*index=5*/f32[8,64,128]{2,1,0:T(8,128)}) custom-call(bf16[1024,2048]{1,0:T(8,128)(2,1)} %get-tuple-element.73.normed, bf16[4,128,1024]{2,1,0:T(8,128)(2,1)} %get-tuple-element.82.left, ...), custom_call_target="tpu_custom_call" | custom-call | tf_op jit(solution)/shard_map/sum_to_owners/pallas_call | solution.py:1672
  425.9 0.0 copy-start.12
  425.9 0.0 copy-start.13
  425.9 0.0 copy-start.8
  425.9 0.0 copy-start.10
  425.9 0.0 copy-start.11
  425.9 22.1 %gradient_norm.1 = (f32[256,2048]{1,0:T(8,128)}, f32[224,128]{1,0:T(8,128)}, f32[8,128]{1,0:T(8,128)}, f32[8,128]{1,0:T(8,128)}) custom-call(bf16[4,64,1408]{2,1,0:T(8,128)(2,1)} %get-tuple-element.90.part_h, bf16[4,64,1024]{2,1,0:T(8,128)(2,1)} %get-tuple-element.91.gate_h, f32[128,1024]{1,0:T(8,128)} %get-tuple-element.92.left_h, ...), custom_call_target="tpu_custom_call" | custom-call | tf_op jit(solution)/shard_map/gradient_norm/pallas_call | solution.py:641
  448.0 1.3 fusion.16
  449.3 1.3 slice_multiply_fusion
  450.6 0.1 mul.138
  450.7 0.1 mul.140
  450.8 0.0 copy-done.12
  450.8 0.0 copy-done.13
  450.8 0.6 add_subtract_fusion
  451.4 0.0 copy-done.8
  451.4 0.0 copy-done.10
  451.4 0.0 copy-done.11
  451.4 2.0 multiply_subtract_fusion
  453.4 10.9 %update_weights.1 = (f32[256,2048]{1,0:T(8,128)}, f32[64,8512]{1,0:T(8,128)}, f32[64,8512]{1,0:T(8,128)}, f32[64,8512]{1,0:T(8,128)}, bf16[64,8512]{1,0:T(8,128)...) custom-call(f32[8,128]{1,0:T(8,128)} %get-tuple-element.96.norm, ...), custom_call_target="tpu_custom_call" | custom-call | tf_op jit(solution)/shard_map/update_weights/pallas_call | solution.py:771
  (20 shorter events, 0.2 us)
Async XLA Ops:
  0.7 105.6 %copy-start.9 = (f32[3,64]{1,0:T(4,128)S(1)}, f32[3,64]{1,0:T(4,128)}, u32[]{:S(2)}) copy-start(f32[3,64]{1,0:T(4,128)} %param.25) | copy-start | bytes 2308
  1.4 1.2 copy-start
  2.6 1.6 copy-start.1
  4.2 1.2 copy-start.2
  103.7 0.8 copy-start.3
  260.2 2.4 copy-start.5
  260.2 2.4 copy-start.7
  262.7 10.7 %copy-start.6 = (bf16[1024,2048]{1,0:T(8,128)(2,1)S(1)}, bf16[1024,2048]{1,0:T(8,128)(2,1)}, u32[]{:S(2)}) copy-start(bf16[1024,2048]{1,0:T(8,128)(2,1)} %get-tuple-element.73.normed) | copy-start | bytes 12582916
  273.3 6.1 %copy-start.4 = (bf16[1024,1024]{1,0:T(8,128)(2,1)}, bf16[1024,1024]{1,0:T(8,128)(2,1)S(1)}, u32[]{:S(2)}) copy-start(bf16[1024,1024]{1,0:T(8,128)(2,1)S(1)} %get-tuple-element.170.dz) | copy-start | bytes 6291460
  425.9 24.9 %copy-start.12 = (f32[3,64]{1,0:T(4,128)S(1)}, f32[3,64]{1,0:T(4,128)}, u32[]{:S(2)}) copy-start(f32[3,64]{1,0:T(4,128)} %param.26) | copy-start | bytes 2308
  425.9 24.9 %copy-start.13 = (f32[3,64]{1,0:T(4,128)S(1)}, f32[3,64]{1,0:T(4,128)}, u32[]{:S(2)}) copy-start(f32[3,64]{1,0:T(4,128)} %param.27) | copy-start | bytes 2308
  425.9 25.5 %copy-start.8 = (f32[872]{0:T(1024)S(1)}, f32[872]{0:T(1024)}, u32[]{:S(2)}) copy-start(f32[872]{0:T(1024)} %param.22) | copy-start | bytes 10468
  425.9 25.5 %copy-start.10 = (f32[872]{0:T(1024)S(1)}, f32[872]{0:T(1024)}, u32[]{:S(2)}) copy-start(f32[872]{0:T(1024)} %param.23) | copy-start | bytes 10468
  425.9 25.5 %copy-start.11 = (f32[872]{0:T(1024)S(1)}, f32[872]{0:T(1024)}, u32[]{:S(2)}) copy-start(f32[872]{0:T(1024)} %param.24) | copy-start | bytes 10468

commit v6 on v5

--- a/solution.py
+++ b/solution.py
@@ -138,83 +138,13 @@
     xbuf[0:8, :] = xbuf[CHUNK : CHUNK + 8, :]
 
 
-def scan_backward_kernel(
-    groups, parts, cw, chunks,
-    px, halo, taps, heads, skip, spread, gather, dy, y, states, wide, gate,
-    dpx, dtaps, dheads, dskip, wide_sum, gate_sum,
-    xbuf, dstate, dcbuf, slope, xact, xd_s, dxd_s, acc_s,
-    first, second, wide_s, wide_r, gate_held, gate_acc, gate_up, gate_down,
-    core_s, core_r, up_s, up_r, down_s, down_r,
-):
-    line = groups // 2
-    group, q = lax.axis_index("dp"), lax.axis_index("seq")
-    z, core = group // 2, lax.rem(group, 2)
-    sibling = (2 * z + 1 - core, q)
-    last = chunks - 1
-    plane = PlaneSum(parts, group, q, wide, first, second, wide_s, wide_r)
-    rows = gate.shape[2] // 4
-    gates = LineSum(
-        line, z, core, q, gate_acc, gate_up, gate_down, up_s, up_r, down_s, down_r, rows, 4
-    )
-
-    def core_copy(d):
-        return remote(gate.at[d, 1 - core], gate_held.at[d], core_s, core_r, d, sibling)
-
-    @pl.when(pl.program_id(0) == 0)
-    def _():
-        greet(seq_peers(parts) + dp_peers(groups))
-        for d in range(line):
-            core_copy(d).start()
-        plane.start(0)
-        plane.start(1)
-
-    @pl.when(pl.program_id(0) == 1)
-    def _():
-        for d in range(line):
-            core_copy(d).wait()
-            add_blocks(gate_acc.at[d], gate.at[d, core], gate_held.at[d], rows, 4)
-        gates.step(0)
-
-    for t in range(1, line - 1):
-
-        @pl.when(pl.program_id(0) == min(1 + 3 * t, last))
-        def _(t=t):
-            gates.sent(t - 1)
-            gates.step(t)
-
-    @pl.when(pl.program_id(0) == min(6, last))
-    def _():
-        plane.turn(32)
-
-    scan_backward_step(
-        cw, px, halo, taps, heads, skip, spread, gather, dy, y, states,
-        dpx, dtaps, dheads, dskip, xbuf, dstate, dcbuf, slope, xact, xd_s, dxd_s, acc_s,
-    )
-
-    @pl.when(pl.program_id(0) == last)
-    def _():
-        plane.finish(wide_sum, 32)
-        gates.finish(gate_sum)
-        gates.sent(line - 2)
-
-
 def scan_backward_step(
-    cw, px, halo, taps, heads, skip, spread, gather, dy, y, states,
+    cw, start, px, halo, taps, heads, skip, spread, gather, dy, y, states,
     dpx, dtaps, dheads, dskip,
     xbuf, dstate, dcbuf, slope, xact, xd_s, dxd_s, acc_s,
 ):
     cc = cw + 2 * N
-    at = pl.program_id(0)
-
-    @pl.when(at == 0)
-    def _():
-        dstate[...] = jnp.zeros_like(dstate)
-        dcbuf[CHUNK : CHUNK + 8, :] = jnp.zeros((8, cc), F32)
-        dtaps[...] = jnp.zeros_like(dtaps)
-        dheads[...] = jnp.zeros_like(dheads)
-        dskip[...] = jnp.zeros_like(dskip)
-
-    xbuf[0:8, :] = jnp.where(at == pl.num_programs(0) - 1, 0.0, halo[:, :cc])
+    xbuf[0:8, :] = jnp.where(start, 0.0, halo[:, :cc])
     xbuf[8 : 8 + CHUNK, :] = px[:, :cc]
     dt_raw = own_heads_first(px[:, cc:], cw // P_SIZE)
     step, rate = rates(dt_raw, heads)
@@ -248,7 +178,7 @@
     xd_s[...] = (xact[:, :cw] * step_x).astype(BF16)
     total = jnp.sum(xd_s[...].astype(F32) * dxd_s[...], axis=0, keepdims=True) + grow_x[
         CHUNK - 1 : CHUNK, :
-    ] * jnp.sum(dstate[...] * states[0].astype(F32), axis=0, keepdims=True)
+    ] * jnp.sum(dstate[...] * states[...].astype(F32), axis=0, keepdims=True)
     dscores = jnp.zeros((CHUNK, CHUNK), F32)
     for pair in range(cw // LANES):
         lanes = slice(pair * LANES, (pair + 1) * LANES)
@@ -277,7 +207,7 @@
     dheads[1:2, :] += jnp.sum(drate * rate, axis=0, keepdims=True)
     grown = (grow_x * dy_f).astype(BF16)
     dscores_low = dscores.astype(BF16)
-    dout = dot(dscores_low, in_low) + dot(grown, states[0], NT)
+    dout = dot(dscores_low, in_low) + dot(grown, states[...], NT)
     din = dot(dscores_low, out_low, TN) + dot((tail_x * xd_f).astype(BF16), dstate_low, NT)
     dstate[...] = grow_x[CHUNK - 1 : CHUNK, :] * dstate[...] + dot(out_low, grown, TN)
     dcbuf[:CHUNK, :cw] = (step_x * dxd + skip[...] * dy[...]) * slope[:, :cw]
@@ -302,158 +232,7 @@
     dcbuf[CHUNK : CHUNK + 8, :] = dcbuf[0:8, :]
 
 
-def whole(shape):
-    return pl.BlockSpec(shape, lambda i: (0,) * len(shape))
-
-
-def scan_backward(collective_id, px, taps, heads, skip, spread, gather, dy, y, states, wide, gate):
-    length, width = px.shape
-    cw = skip.shape[1]
-    cc = cw + 2 * N
-    chunks = length // CHUNK
-    eighths = CHUNK // 8
-    parts, line, out_rows, half = wide.shape
-    span = gate.shape[2]
-    sem = pltpu.SemaphoreType.DMA
-    vmem = pl.BlockSpec(memory_space=pltpu.VMEM)
-    return pl.pallas_call(
-        functools.partial(scan_backward_kernel, 2 * line, parts, cw, chunks),
-        grid=(chunks,),
-        in_specs=[
-            pl.BlockSpec((CHUNK, width), lambda i: (chunks - 1 - i, 0)),
-            pl.BlockSpec(
-                (8, width), lambda i: (jnp.maximum((chunks - 1 - i) * eighths - 1, 0), 0)
-            ),
-            whole(taps.shape),
-            whole(heads.shape),
-            whole(skip.shape),
-            whole(spread.shape),
-            whole(gather.shape),
-            pl.BlockSpec((CHUNK, cw), lambda i: (chunks - 1 - i, 0)),
-            pl.BlockSpec((CHUNK, cw), lambda i: (chunks - 1 - i, 0)),
-            pl.BlockSpec((1, N, cw), lambda i: (chunks - 1 - i, 0, 0)),
-            vmem,
-            vmem,
-        ],
-        out_specs=[
-            pl.BlockSpec((CHUNK, width), lambda i: (chunks - 1 - i, 0)),
-            whole((8, cc)),
-            whole((8, LANES)),
-            whole((8, cw)),
-            vmem,
-            vmem,
-        ],
-        out_shape=[
-            jax.ShapeDtypeStruct((length, width), BF16),
-            jax.ShapeDtypeStruct((8, cc), F32),
-            jax.ShapeDtypeStruct((8, LANES), F32),
-            jax.ShapeDtypeStruct((8, cw), F32),
-            jax.ShapeDtypeStruct(wide.shape[1:], BF16),
-            jax.ShapeDtypeStruct((span, cw), BF16),
-        ],
-        scratch_shapes=[
-            pltpu.VMEM((CHUNK + 8, cc), F32),
-            pltpu.VMEM((N, cw), F32),
-            pltpu.VMEM((CHUNK + 8, cc), F32),
-            pltpu.VMEM((CHUNK, cc), F32),
-            pltpu.VMEM((CHUNK, cc), F32),
-            pltpu.VMEM((CHUNK, cw), BF16),
-            pltpu.VMEM((CHUNK, cw), F32),
-            pltpu.VMEM((CHUNK, CHUNK), F32),
-            *PlaneSum.scratch(parts, wide.shape[1:], BF16),
-            *([pltpu.VMEM((line, span, cw), BF16)] * 4),
-            *([sem((line,))] * 6),
-        ],
-        compiler_params=pltpu.CompilerParams(
-            collective_id=collective_id, has_side_effects=True, vmem_limit_bytes=63 * 2**20
-        ),
-        cost_estimate=pl.CostEstimate(
-            flops=10**10, bytes_accessed=100 * 10**6, transcendentals=10**7
-        ),
-        name="scan_backward",
-    )(px, px, taps, heads, skip, spread, gather, dy, y, states, wide, gate)
-
-
 WIDE = 512
-
-
-def widths_kernel(cw, u, wo, cotangent, tokens, block_out, back, mixed, branch, norms, pulls):
-    at = pl.program_id(0)
-    ends = [level_width(k) // WIDE - 1 for k in range(LEVELS)]
-
-    @pl.when(at == 0)
-    def _():
-        terms = u[0, :, cw:].astype(F32)
-        for part in range(1, u.shape[0]):
-            terms = terms + u[part, :, cw:].astype(F32)
-        squares = jnp.zeros((terms.shape[0], 1), F32)
-        for k in range(LEVELS):
-            squares = squares + terms[:, k : k + 1] + terms[:, LEVELS + k : LEVELS + k + 1]
-            norms[:, k : k + 1] = lax.rsqrt(squares / level_width(k) + EPS_OUT)
-        running = jnp.zeros(branch.shape, F32)
-        for k in reversed(range(LEVELS)):
-            running = running + norms[:, k : k + 1] * cotangent[k].astype(F32)
-            mixed[k] = running.astype(BF16)
-        branch[...] = jnp.zeros_like(branch)
-
-    part = at * WIDE // cw
-    lanes = pl.ds(pl.multiple_of(lax.rem(at * WIDE, cw), WIDE), WIDE)
-    level = sum((at > end).astype(jnp.int32) for end in ends[:-1])
-    branch[...] += dot(u[part, :, lanes], wo[...])
-    back[part, :, lanes] = dot(mixed[level], wo[...], NT).astype(BF16)
-    for k in range(LEVELS):
-
-        @pl.when(at == ends[k])
-        def _():
-            norm = norms[:, k : k + 1]
-            block_out[k] = (tokens[...].astype(F32) + norm * branch[...]).astype(BF16)
-            inner = jnp.sum(cotangent[k].astype(F32) * branch[...], axis=-1, keepdims=True)
-            pulls[:, k : k + 1] = norm * norm * norm * (inner / level_width(k))
-
-    @pl.when(at == ends[-1])
-    def _():
-        coef = jnp.zeros((branch.shape[0], 1), F32)
-        lane = lax.broadcasted_iota(jnp.int32, (1, LANES), 1)
-        packed = jnp.zeros((branch.shape[0], LANES), F32)
-        for k in reversed(range(LEVELS)):
-            coef = coef + pulls[:, k : k + 1]
-            high, rest = two_terms(coef)
-            packed = jnp.where(lane == k, high.astype(F32), packed)
-            packed = jnp.where(lane == LEVELS + k, rest.astype(F32), packed)
-        for p in range(back.shape[0]):
-            back[p, :, cw:] = packed.astype(BF16)
-
-
-def widths(u, wo, cotangent, tokens):
-    parts, rows, wide = u.shape
-    cw = wide - LANES
-
-    def full(shape):
-        return pl.BlockSpec(shape, lambda i: (0,) * len(shape), pipeline_mode=pl.Buffered(1))
-
-    return pl.pallas_call(
-        functools.partial(widths_kernel, cw),
-        grid=(INNER // WIDE,),
-        in_specs=[
-            full(u.shape),
-            pl.BlockSpec((WIDE, D), lambda i: (i, 0)),
-            full(cotangent.shape),
-            full(tokens.shape),
-        ],
-        out_specs=[full(cotangent.shape), full(u.shape), full(cotangent.shape)],
-        out_shape=[
-            jax.ShapeDtypeStruct(cotangent.shape, BF16),
-            jax.ShapeDtypeStruct(u.shape, BF16),
-            jax.ShapeDtypeStruct(cotangent.shape, BF16),
-        ],
-        scratch_shapes=[
-            pltpu.VMEM((rows, D), F32),
-            pltpu.VMEM((rows, LANES), F32),
-            pltpu.VMEM((rows, LANES), F32),
-        ],
-        compiler_params=pltpu.CompilerParams(vmem_limit_bytes=63 * 2**20),
-        name="widths",
-    )(u, wo, cotangent, tokens)
 
 
 MESH = pl.DeviceIdType.MESH
@@ -1174,48 +953,6 @@
     )(hidden, wx, gate, wo, gain_in, gain_out, taps, heads, skip, spread)
 
 
-def swap_out_kernel(groups, parts, u, wo_in, u_out, wo, sends, recvs, core_s, core_r, local):
-    group, q = lax.axis_index("dp"), lax.axis_index("seq")
-    z, core = group // 2, lax.rem(group, 2)
-    sibling = (2 * z + 1 - core, q)
-    peers = seq_peers(parts)
-    greet(peers + [sibling])
-    copies = [
-        remote(u.at[peer[1]], u_out.at[q], sends, recvs, k, peer) for k, peer in enumerate(peers)
-    ]
-    for d in range(groups // 2):
-        block = wo.at[2 * d + core]
-        copies.append(remote(block, block, core_s, core_r, d, sibling))
-    copies.append(pltpu.make_async_copy(u.at[q], u_out.at[q], local))
-    for copy in copies:
-        copy.start()
-    for copy in copies[: parts - 1]:
-        copy.wait()
-    for d in range(groups // 2):
-        copies[parts - 1 + d].wait_send()
-        block = wo.at[2 * d + 1 - core]
-        remote(block, block, core_s, core_r, d, sibling).wait_recv()
-    copies[-1].wait()
-
-
-def swap_out(collective_id, u, wo):
-    groups, parts = wo.shape[:2]
-    sem = pltpu.SemaphoreType.DMA
-    hbm = pl.BlockSpec(memory_space=pltpu.HBM)
-    return pl.pallas_call(
-        functools.partial(swap_out_kernel, groups, parts),
-        in_specs=[hbm] * 2,
-        out_specs=[hbm] * 2,
-        out_shape=[jax.ShapeDtypeStruct(u.shape, BF16), jax.ShapeDtypeStruct(wo.shape, BF16)],
-        input_output_aliases={1: 1},
-        scratch_shapes=[
-            sem((parts - 1,)), sem((parts - 1,)), sem((groups // 2,)), sem((groups // 2,)), sem,
-        ],
-        compiler_params=pltpu.CompilerParams(collective_id=collective_id, has_side_effects=True),
-        name="swap_out",
-    )(u, wo)
-
-
 def add_blocks(out, a, b, rows, steps):
     def step(i, carry):
         at = pl.ds(pl.multiple_of(i * rows, rows), rows)
@@ -1229,25 +966,142 @@
     return sum((channel >= level_width(k)).astype(jnp.int32) for k in range(LEVELS - 1))
 
 
-def swap_back_kernel(
-    groups, parts, cw, back, u, mixed, back_out, left, right,
-    sent, held, sends, recvs, core_s, core_r, local,
+def mirror_peers(parts):
+    group, q = lax.axis_index("dp"), lax.axis_index("seq")
+    if parts != 4:
+        return seq_peers(parts)
+    return [(group, 3 - q), (group, q + 1 - 2 * lax.rem(q, 2)), (group, lax.rem(q + 2, 4))]
+
+
+def middle_kernel(
+    groups, parts, cw,
+    u_h, wo_in, cot_h, tokens_h,
+    back_h, coef_h, block_h, left_h, right_h, wo,
+    u, cot, tokens, mixed, branch, norms, pulls, back, coefs, weights, sent, held, left, right,
+    u_s, u_r, wo_s, wo_r, back_s, back_r, coef_s, coef_r, core_s, core_r, fetch, load, store, local,
 ):
     line = groups // 2
     group, q = lax.axis_index("dp"), lax.axis_index("seq")
     z, core = group // 2, lax.rem(group, 2)
     sibling = (2 * z + 1 - core, q)
-    peers = seq_peers(parts)
+    peers = mirror_peers(parts)
+    loads = [
+        pltpu.make_async_copy(u_h.at[q], u.at[q], load.at[0]),
+        pltpu.make_async_copy(cot_h, cot, load.at[1]),
+        pltpu.make_async_copy(tokens_h, tokens, load.at[2]),
+    ]
+    for copy in loads:
+        copy.start()
     greet(peers + [sibling])
-    copies = [
-        remote(back.at[peer[1]], back_out.at[q], sends, recvs, k, peer)
-        for k, peer in enumerate(peers)
-    ]
-    copies.append(pltpu.make_async_copy(back.at[q], back_out.at[q], local))
-    for copy in copies:
-        copy.start()
+    swaps = [remote(u_h.at[peer[1]], u.at[q], u_s, u_r, k, peer) for k, peer in enumerate(peers)]
+    for copy in swaps:
+        copy.start()
+
+    def parity(d, of):
+        block = wo.at[2 * d + of]
+        return remote(block, block, wo_s, wo_r, d, sibling)
+
+    for d in range(line):
+        parity(d, core).start()
+    for copy in loads + swaps:
+        copy.wait()
+
+    terms = u[0, :, cw:].astype(F32)
+    for part in range(1, parts):
+        terms = terms + u[part, :, cw:].astype(F32)
+    squares = jnp.zeros((terms.shape[0], 1), F32)
+    for k in range(LEVELS):
+        squares = squares + terms[:, k : k + 1] + terms[:, LEVELS + k : LEVELS + k + 1]
+        norms[:, k : k + 1] = lax.rsqrt(squares / level_width(k) + EPS_OUT)
+    rows = 32
+
+    def mix_rows(i, carry):
+        at = pl.ds(pl.multiple_of(i * rows, rows), rows)
+        running = norms[at, LEVELS - 1 : LEVELS] * cot[LEVELS - 1, at, :].astype(F32)
+        mixed[LEVELS - 1, at, :] = running.astype(BF16)
+        for k in reversed(range(LEVELS - 1)):
+            running = running + norms[at, k : k + 1] * cot[k, at, :].astype(F32)
+            mixed[k, at, :] = running.astype(BF16)
+        return carry
+
+    lax.fori_loop(0, tokens.shape[0] // rows, mix_rows, 0)
+    for d in range(line):
+        parity(d, core).wait_send()
+        parity(d, 1 - core).wait_recv()
+
     width = INNER // groups
-    rows = width // parts
+    per = WIDE // width
+    slots = weights.shape[0]
+    dests = [peer[1] for peer in peers] + [q]
+    firsts = [dest * cw + b * WIDE for dest in dests for b in range(cw // WIDE)]
+    firsts += [b * WIDE for b in range(INNER // WIDE)]
+
+    def get(i):
+        return pltpu.make_async_copy(
+            wo.at[pl.ds(firsts[i] // width, per)], weights.at[i % slots], fetch.at[i % slots]
+        )
+
+    def block_of(i):
+        get(i).wait()
+        return weights[i % slots].reshape(WIDE, D)
+
+    for i in range(slots - 1):
+        get(i).start()
+    outgoing = []
+    for i in range(len(dests) * (cw // WIDE)):
+        get(i + slots - 1).start()
+        at, b = divmod(i, cw // WIDE)
+        lanes = slice(b * WIDE, (b + 1) * WIDE)
+        level = level_of(firsts[i], WIDE)
+        back[dests[at], :, lanes] = dot(mixed[level], block_of(i), NT).astype(BF16)
+        if b == cw // WIDE - 1:
+            if at < len(peers):
+                copy = remote(back.at[dests[at]], back_h.at[q], back_s, back_r, at, peers[at])
+            else:
+                copy = pltpu.make_async_copy(back.at[q], back_h.at[q], local.at[0])
+            copy.start()
+            outgoing.append(copy)
+    first = len(dests) * (cw // WIDE)
+    branch[...] = jnp.zeros_like(branch)
+    for b in range(INNER // WIDE):
+        if first + b + slots - 1 < len(firsts):
+            get(first + b + slots - 1).start()
+        part, at = divmod(b * WIDE, cw)
+        branch[...] += dot(u[part, :, at : at + WIDE], block_of(first + b))
+        for k in range(LEVELS):
+            if level_width(k) == (b + 1) * WIDE:
+
+                def level_rows(i, carry, k=k):
+                    at = pl.ds(pl.multiple_of(i * rows, rows), rows)
+                    norm = norms[at, k : k + 1]
+                    total = branch[at, :]
+                    inner = jnp.sum(cot[k, at, :].astype(F32) * total, axis=-1, keepdims=True)
+                    pulls[at, k : k + 1] = norm * norm * norm * (inner / level_width(k))
+                    cot[k, at, :] = (tokens[at, :].astype(F32) + norm * total).astype(BF16)
+                    return carry
+
+                lax.fori_loop(0, tokens.shape[0] // rows, level_rows, 0)
+                copy = pltpu.make_async_copy(cot.at[k], block_h.at[k], store.at[k])
+                copy.start()
+                outgoing.append(copy)
+    coef = jnp.zeros((tokens.shape[0], 1), F32)
+    lane = lax.broadcasted_iota(jnp.int32, (1, LANES), 1)
+    packed = jnp.zeros((tokens.shape[0], LANES), F32)
+    for k in reversed(range(LEVELS)):
+        coef = coef + pulls[:, k : k + 1]
+        high, rest = two_terms(coef)
+        packed = jnp.where(lane == k, high.astype(F32), packed)
+        packed = jnp.where(lane == LEVELS + k, rest.astype(F32), packed)
+    coefs[...] = packed.astype(BF16)
+    for k, peer in enumerate(peers):
+        copy = remote(coefs, coef_h.at[q], coef_s, coef_r, k, peer)
+        copy.start()
+        outgoing.append(copy)
+    copy = pltpu.make_async_copy(coefs, coef_h.at[q], local.at[1])
+    copy.start()
+    outgoing.append(copy)
+
+    share = width // parts
     tile = 512
     halves = D // 2 // tile
 
@@ -1271,48 +1125,75 @@
         cores.append(copy)
     for d in range(line):
         cores[d].wait_recv()
-        for out, first in ((left, 0), (right, halves)):
+        for out, target, first, at in ((left, left_h, 0, 0), (right, right_h, halves, 1)):
 
             def keep_step(j, carry, d=d, out=out, first=first):
-                at = pl.ds(pl.multiple_of((j + first) * tile, tile), tile)
-                cols = pl.ds(pl.multiple_of(j * tile, tile), tile)
-                total = product(2 * d + core, j + first) + held[d, :, at].astype(F32)
+                cols = pl.ds(pl.multiple_of((j + first) * tile, tile), tile)
+                to = pl.ds(pl.multiple_of(j * tile, tile), tile)
+                total = product(2 * d + core, j + first) + held[d, :, cols].astype(F32)
                 total = total.astype(BF16)
                 for part in range(parts):
-                    out[part, d, :, cols] = total[part * rows : (part + 1) * rows]
+                    out[part, d, :, to] = total[part * share : (part + 1) * share]
                 return carry
 
             lax.fori_loop(0, halves, keep_step, 0)
+            copy = pltpu.make_async_copy(
+                out.at[:, d], target.at[:, d], store.at[LEVELS + 2 * d + at]
+            )
+            copy.start()
+            outgoing.append(copy)
     for copy in cores:
         copy.wait_send()
-    for copy in copies:
+    for copy in outgoing:
         copy.wait()
 
 
-def swap_back(collective_id, back, u, mixed, groups):
-    parts, rows, wide = back.shape
-    line, width = groups // 2, INNER // groups
+def middle(collective_id, u, wo, cotangent, tokens):
+    groups, parts, share = wo.shape[:3]
+    line = groups // 2
+    rows, wide = u.shape[1:]
+    cw = wide - LANES
+    width = share * parts
     sem = pltpu.SemaphoreType.DMA
-    vmem = pl.BlockSpec(memory_space=pltpu.VMEM)
     hbm = pl.BlockSpec(memory_space=pltpu.HBM)
+    half = (parts, line, share, D // 2)
     return pl.pallas_call(
-        functools.partial(swap_back_kernel, groups, parts, wide - LANES),
-        in_specs=[hbm, vmem, vmem],
-        out_specs=[hbm, vmem, vmem],
+        functools.partial(middle_kernel, groups, parts, cw),
+        in_specs=[hbm] * 4,
+        out_specs=[hbm] * 6,
         out_shape=[
-            jax.ShapeDtypeStruct(back.shape, back.dtype),
-            *([jax.ShapeDtypeStruct((parts, line, width // parts, D // 2), BF16)] * 2),
+            jax.ShapeDtypeStruct((parts, rows, cw), BF16),
+            jax.ShapeDtypeStruct((parts, rows, LANES), BF16),
+            jax.ShapeDtypeStruct(cotangent.shape, BF16),
+            jax.ShapeDtypeStruct(half, BF16),
+            jax.ShapeDtypeStruct(half, BF16),
+            jax.ShapeDtypeStruct(wo.shape, BF16),
         ],
+        input_output_aliases={1: 5},
         scratch_shapes=[
+            pltpu.VMEM(u.shape, BF16),
+            pltpu.VMEM(cotangent.shape, BF16),
+            pltpu.VMEM(tokens.shape, BF16),
+            pltpu.VMEM(cotangent.shape, BF16),
+            pltpu.VMEM((rows, D), F32),
+            pltpu.VMEM((rows, LANES), F32),
+            pltpu.VMEM((rows, LANES), F32),
+            pltpu.VMEM((parts, rows, cw), BF16),
+            pltpu.VMEM((rows, LANES), BF16),
+            pltpu.VMEM((3, WIDE // width, parts, share, D), BF16),
             pltpu.VMEM((line, width, D), BF16),
             pltpu.VMEM((line, width, D), BF16),
-            sem((parts - 1,)), sem((parts - 1,)), sem((line,)), sem((line,)), sem,
+            pltpu.VMEM(half, BF16),
+            pltpu.VMEM(half, BF16),
+            sem((parts - 1,)), sem((parts - 1,)), sem((line,)), sem((line,)),
+            *([sem((parts - 1,))] * 4),
+            sem((line,)), sem((line,)), sem((3,)), sem((3,)), sem((LEVELS + 2 * line,)), sem((2,)),
         ],
         compiler_params=pltpu.CompilerParams(
             collective_id=collective_id, has_side_effects=True, vmem_limit_bytes=63 * 2**20
         ),
-        name="swap_back",
-    )(back, u, mixed)
+        name="middle",
+    )(u, wo, cotangent, tokens)
 
 
 def sum_blocks(out, blocks, rows):
@@ -1500,6 +1381,196 @@
             self.add(self.up, z)
             self.behind(z, False).wait_recv()
             add_blocks(out, self.up.at[z], self.down.at[z], self.rows, self.steps)
+
+
+def backward_kernel(
+    groups, parts, cw,
+    back_h, coefs_h, normed_h, px_h, y_h, z_h, states_h, wide_h,
+    gain, taps, heads, skip, spread, gather,
+    dz_h, dpx_h, small, wide_sum, gate_sum,
+    dz, coefs, normed, px, y, dy, states, wide, dpx, dtaps, dheads, dskip, dgain,
+    xbuf, dstate, dcbuf, slope, xact, xd_s, dxd_s, acc_s,
+    first, second, wide_s, wide_r, gate_made, gate_held, gate_acc, gate_up, gate_down,
+    core_s, core_r, up_s, up_r, down_s, down_r, load, store,
+):
+    line = groups // 2
+    cc = cw + 2 * N
+    length = y.shape[0]
+    chunks = length // CHUNK
+    group, q = lax.axis_index("dp"), lax.axis_index("seq")
+    z, core = group // 2, lax.rem(group, 2)
+    sibling = (2 * z + 1 - core, q)
+    loads = [
+        pltpu.make_async_copy(source, target, load.at[k])
+        for k, (source, target) in enumerate(
+            [(wide_h, wide), (back_h, dz), (coefs_h, coefs), (y_h, y), (z_h, dy),
+             (normed_h, normed), (px_h, px), (states_h, states)]
+        )
+    ]
+    for copy in loads:
+        copy.start()
+    greet(seq_peers(parts) + dp_peers(groups))
+    plane = PlaneSum(parts, group, q, wide, first, second, wide_s, wide_r)
+    loads[0].wait()
+    plane.start(0)
+    plane.start(1)
+    for copy in loads[1:5]:
+        copy.wait()
+
+    rows = 32
+    lane = lax.broadcasted_iota(jnp.int32, (1, LANES), 1)
+    dgain[...] = jnp.zeros_like(dgain)
+
+    def gate_rows(i, carry):
+        at = pl.ds(pl.multiple_of(i * rows, rows), rows)
+        coef = coefs[at, :].astype(F32)
+        for b in range(cw // WIDE):
+            lanes = slice(b * WIDE, (b + 1) * WIDE)
+            level = level_of(q * cw + b * WIDE, WIDE)
+            ours = (lane == level) | (lane == level + LEVELS)
+            pull = jnp.sum(jnp.where(ours, coef, 0.0), axis=-1, keepdims=True)
+            gate_in = dy[at, lanes]
+            sig = jax.nn.sigmoid(gate_in)
+            gate = gate_in * sig
+            y_at = y[at, lanes]
+            gated = y_at * gate
+            back = dz[at, lanes].astype(F32)
+            dgated = gain[:, lanes] * back - gated * pull
+            dgain[0:1, lanes] += jnp.sum(back * gated, axis=0, keepdims=True)
+            dz[at, lanes] = (dgated * y_at * (sig + gate * (1.0 - sig))).astype(BF16)
+            dy[at, lanes] = dgated * gate
+        return carry
+
+    lax.fori_loop(0, length // rows, gate_rows, 0)
+    dz_out = pltpu.make_async_copy(dz, dz_h, store.at[0])
+    dz_out.start()
+    loads[5].wait()
+    span = gate_acc.shape[1]
+
+    def dweight(of, out):
+        at = pl.ds(pl.multiple_of(of * span, span), span)
+        out[...] = dot(normed[:, at], dz[...], TN).astype(BF16)
+
+    def core_copy(d):
+        return remote(gate_made.at[d], gate_held.at[d], core_s, core_r, d, sibling)
+
+    order = [d for k in range(line // 2) for d in (line - 1 - k, k)]
+    for d in order:
+        dweight(2 * d + 1 - core, gate_made.at[d])
+        core_copy(d).start()
+    for d in order:
+        dweight(2 * d + core, gate_acc.at[d])
+        core_copy(d).wait()
+        add_blocks(gate_acc.at[d], gate_acc.at[d], gate_held.at[d], span // 4, 4)
+    gates = LineSum(
+        line, z, core, q, gate_acc, gate_up, gate_down, up_s, up_r, down_s, down_r, span // 4, 4
+    )
+    gates.step(0)
+    dstate[...] = jnp.zeros_like(dstate)
+    dcbuf[CHUNK : CHUNK + 8, :] = jnp.zeros((8, cc), F32)
+    dtaps[...] = jnp.zeros_like(dtaps)
+    dheads[...] = jnp.zeros_like(dheads)
+    dskip[...] = jnp.zeros_like(dskip)
+    for copy in loads[6:]:
+        copy.wait()
+
+    def scan_rows(i, carry):
+        for t in range(1, line - 1):
+
+            @pl.when(i == min(4 * t - 1, chunks - 1))
+            def _(t=t):
+                gates.sent(t - 1)
+                gates.step(t)
+
+        @pl.when(i == 2)
+        def _():
+            plane.turn(32)
+
+        at = chunks - 1 - i
+        here = pl.ds(pl.multiple_of(at * CHUNK, CHUNK), CHUNK)
+        before = pl.ds(pl.multiple_of(jnp.maximum(at * CHUNK - 8, 0), 8), 8)
+        scan_backward_step(
+            cw, at == 0, px.at[here], px.at[before], taps, heads, skip, spread, gather,
+            dy.at[here], y.at[here], states.at[at], dpx.at[here], dtaps, dheads, dskip,
+            xbuf, dstate, dcbuf, slope, xact, xd_s, dxd_s, acc_s,
+        )
+        return carry
+
+    lax.fori_loop(0, chunks, scan_rows, 0)
+    dpx_out = pltpu.make_async_copy(dpx, dpx_h, store.at[1])
+    dpx_out.start()
+    small[...] = jnp.zeros_like(small)
+    wide_rows, own_rows = cc // LANES, cw // LANES
+    for tap in range(TAPS + 1):
+        for b in range(wide_rows):
+            to = tap * wide_rows + b
+            small[to : to + 1, :] = dtaps[tap : tap + 1, b * LANES : (b + 1) * LANES]
+    to = (TAPS + 1) * wide_rows
+    for b in range(own_rows):
+        small[to + b : to + b + 1, :] = dgain[0:1, b * LANES : (b + 1) * LANES]
+    hq = cw // P_SIZE
+    skips = spread_heads(dskip[...], gather[...])
+    small[to + own_rows : to + own_rows + 1, :] = (
+        dheads[0:1, :]
+        + pltpu.roll(dheads[...], hq, 1)[1:2, :]
+        + pltpu.roll(skips, 2 * hq, 1)[0:1, :]
+    )
+    plane.finish(wide_sum, 32)
+    gates.finish(gate_sum)
+    gates.sent(line - 2)
+    dz_out.wait()
+    dpx_out.wait()
+
+
+def backward(
+    collective_id, back, coefs, normed, px, y, z, states, wide, gain, taps, heads, skip, spread
+):
+    parts, line = wide.shape[:2]
+    length, width = px.shape
+    cw = skip.shape[1]
+    cc = cw + 2 * N
+    span = D // (2 * line)
+    sem = pltpu.SemaphoreType.DMA
+    vmem = pl.BlockSpec(memory_space=pltpu.VMEM)
+    hbm = pl.BlockSpec(memory_space=pltpu.HBM)
+    small_rows = (TAPS + 1) * (cc // LANES) + cw // LANES + 1
+    small_rows = -(-small_rows // 8) * 8
+    return pl.pallas_call(
+        functools.partial(backward_kernel, 2 * line, parts, cw),
+        in_specs=[*([hbm] * 8), *([vmem] * 6)],
+        out_specs=[hbm, hbm, vmem, vmem, vmem],
+        out_shape=[
+            jax.ShapeDtypeStruct((length, cw), BF16),
+            jax.ShapeDtypeStruct((length, width), BF16),
+            jax.ShapeDtypeStruct((small_rows, LANES), F32),
+            jax.ShapeDtypeStruct(wide.shape[1:], BF16),
+            jax.ShapeDtypeStruct((span, cw), BF16),
+        ],
+        scratch_shapes=[
+            *[pltpu.VMEM(a.shape, a.dtype) for a in (back, coefs, normed, px, y, z, states, wide)],
+            pltpu.VMEM((length, width), BF16),
+            pltpu.VMEM((8, cc), F32),
+            pltpu.VMEM((8, LANES), F32),
+            pltpu.VMEM((8, cw), F32),
+            pltpu.VMEM((8, cw), F32),
+            pltpu.VMEM((CHUNK + 8, cc), F32),
+            pltpu.VMEM((N, cw), F32),
+            pltpu.VMEM((CHUNK + 8, cc), F32),
+            pltpu.VMEM((CHUNK, cc), F32),
+            pltpu.VMEM((CHUNK, cc), F32),
+            pltpu.VMEM((CHUNK, cw), BF16),
+            pltpu.VMEM((CHUNK, cw), F32),
+            pltpu.VMEM((CHUNK, CHUNK), F32),
+            *PlaneSum.scratch(parts, wide.shape[1:], BF16),
+            *([pltpu.VMEM((line, span, cw), BF16)] * 5),
+            *([sem((line,))] * 6),
+            sem((8,)), sem((2,)),
+        ],
+        compiler_params=pltpu.CompilerParams(
+            collective_id=collective_id, has_side_effects=True, vmem_limit_bytes=63 * 2**20
+        ),
+        name="backward",
+    )(back, coefs, normed, px, y, z, states, wide, gain, taps, heads, skip, spread, spread.T)
 
 
 def owners_kernel(
@@ -1702,11 +1773,6 @@
     )(normed, left, right, gate, small, dz, dpx, wz, wx)
 
 
-def unpack_terms(packed, count):
-    packed = packed.astype(F32)
-    return packed[..., :count] + packed[..., count : 2 * count]
-
-
 def on_device(
     hidden_in, out_grads, w_in, w_in_m, w_in_v, w_out, w_out_m, w_out_v,
     chan_params, chan_m, chan_v, head_params, head_m, head_v,
@@ -1760,39 +1826,16 @@
         own_gain.reshape(1, cw), taps, heads, skip, spread,
     )
     wx, wz = wx.reshape(D, cc + LANES), wz.reshape(D, cw)
-    u, wo = swap_out(2, u_blocks.reshape(parts, rows, cw + LANES), wo)
-    wo = wo.reshape(INNER, D)
-    sig = jax.nn.sigmoid(z)
-    gate = z * sig
-    gated = y * gate
-    channel = q * cw + jnp.arange(cw)
-
     cotangent = out_grads[:, 0]
-    block_out, back_blocks, mixed = widths(u, wo, cotangent, hidden_in[0])
+    back_own, coefs, block_out, dwo_left, dwo_right, _ = middle(
+        2, u_blocks.reshape(parts, rows, cw + LANES), wo, cotangent, hidden_in[0]
+    )
     block_out = block_out[:, None]
-    back_own, dwo_left, dwo_right = swap_back(3, back_blocks, u, mixed, groups)
-    back_own = back_own.reshape(length, cw + LANES)
-
-    coefs = unpack_terms(back_own[:, cw:], LEVELS)
-    pull = coefs[:, LEVELS - 1 :]
-    for k in reversed(range(LEVELS - 1)):
-        pull = jnp.where(channel[None, :] < level_width(k), coefs[:, k : k + 1], pull)
-    back = back_own[:, :cw].astype(F32)
-    dgated = own_gain * back - gated * pull
-    dgain_out = jnp.sum(back * gated, axis=0)
-    dz = (dgated * y * (sig + gate * (1.0 - sig))).astype(BF16)
-    dy = dgated * gate
-    dwz = dot(normed, dz, TN).astype(BF16)
-    dwz = dwz.reshape(line, 2, parts * in_rows, cw)
-    dpx, dtaps, dheads, dskip, dwo_left, dwz = scan_backward(
-        5, px, taps, heads, skip, spread, spread.T, dy, y, states, dwo_left, dwz
-    )
-    skip_grad = jnp.sum(dskip[0].reshape(hq, P_SIZE), axis=-1)
-    small = jnp.concatenate(
-        [dtaps[: TAPS + 1].reshape(-1), dgain_out, dheads[0, :hq], dheads[1, :hq], skip_grad]
-    )
-    small_rows = -(-small.shape[0] // (8 * LANES)) * 8
-    small = jnp.pad(small, (0, small_rows * LANES - small.shape[0])).reshape(small_rows, LANES)
+
+    dz, dpx, small, dwo_left, dwz = backward(
+        5, back_own.reshape(length, cw), coefs.reshape(length, LANES), normed, px, y, z, states,
+        dwo_left, own_gain.reshape(1, cw), taps, heads, skip, spread,
+    )
     x_part, left_part, right_part, z_part, dnormed, small = sum_to_owners(
         4, normed, dwo_left, dwo_right, dwz.reshape(parts, in_rows, cw), small, dz, dpx, wz, wx
     )

time: 474 us -> 442 us (0.932)
  other arithmetic: 19.8 us -> 7.67 us
  Pallas kernels: 425 us -> 413 us
  matrix products: 6.11 us -> 0 us
    convert_element_type x2 -> x0, other arithmetic: 11.8 us -> none  [the longest x1 10.6 us: on_device(): dz = (dgated * y * (sig + gate * (1.0 - sig))).astype(BF16)]
    pallas_call x4 -> x2, Pallas kernels: 138 us -> 126 us  [the longest x1 68.6 us: middle(): pl.pallas_call(functools.partial(middle_kernel, groups, parts, cw), in_sp...]
    dot_general x1 -> x0, matrix products: 6.11 us -> none  [dot(): lax.dot_general(a, b, (dims, ((), ())), precision=precision, preferred_el...]
    unnamed x29 -> x22, local copies, waits for them, and re-layouts: 4.93 us -> 9.7 us
where the time goes in v6:
time: 442 us; the launch traced here: 436 us
  Pallas kernels  413 us (93%)
  local copies, waits for them, and re-layouts  13.4 us (3%)
  other arithmetic  7.67 us (2%)
    pallas_call x1, Pallas kernels, collect(): pl.pallas_call(functools.partial(collect_kernel, groups, parts), in_specs...  98.3 us
    pallas_call x1, Pallas kernels, sum_to_owners(): pl.pallas_call(functools.partial(owners_kernel, groups, parts, rows), in_...  91.2 us
    pallas_call x1, Pallas kernels, middle(): pl.pallas_call(functools.partial(middle_kernel, groups, parts, cw), in_sp...  68.6 us
    pallas_call x1, Pallas kernels, forward(): pl.pallas_call(functools.partial(forward_kernel, groups, parts, cw), in_s...  63.6 us
    pallas_call x1, Pallas kernels, backward(): pl.pallas_call(functools.partial(backward_kernel, 2 * line, parts, cw), i...  57.9 us
    pallas_call x1, Pallas kernels, gradient_norm(): pl.pallas_call(functools.partial(norm_kernel, groups, parts), in_specs=[*...  22.9 us
    pallas_call x1, Pallas kernels, update_weights(): pl.pallas_call(functools.partial(update_kernel, parts), in_specs=[vmem, *...  10.9 us
    unnamed x22, local copies, waits for them, and re-layouts  9.7 us

profile of v6, /device:TPU:1, one launch (start us, length us, event | category | flops | bytes accessed | tf_op | source)
XLA Modules:
  0.0 435.5 jit_solution(1675321741617081868)
XLA Ops:
  0.7 0.0 copy-start.5
  0.7 0.7 reduce_precision.3
  1.4 0.0 copy-start
  1.4 1.2 copy-done
  2.6 0.0 copy-start.1
  2.6 1.6 copy-done.1
  4.2 0.0 copy-start.2
  4.2 1.2 copy-done.2
  5.4 98.3 %collect.1 = (bf16[4,256,2048]{2,1,0:T(8,128)(2,1)}, bf16[8,4,64,1408]{3,2,1,0:T(8,128)(2,1)}, bf16[4,64,1024]{2,1,0:T(8,128)(2,1)S(1)}, f32[32,8,128]{2,1,0:T(8,128)S(1)}, bf16[8,4,128,2048]{3,2,1,0:T(8,128)(2,1)}) custom-call(bf16[256,2048]{1,0:T(8,128)(2,1)S(1)} %bitcast.29, f32[64,8512]{1,0:T(8,128)S(1)} %copy-done.1, f32[128,2048]{1,0:T(8,128)S(1)} %copy-done.2, ...), custom_call_target="tpu_custom_call" | custom-call | tf_op jit(solution)/shard_map/collect/pallas_call | solution.py:725
  103.7 0.0 copy-start.3
  103.7 0.8 copy-done.3
  104.6 0.1 reshape.105
  104.8 0.1 pad.16.clone
  104.9 0.1 maximum_maximum_fusion
  105.0 0.6 pad_maximum_fusion.taps
  105.6 0.0 copy-done.5
  105.6 0.1 constant_dynamic-slice_fusion
  105.7 0.6 select_maximum_fusion.heads
  106.3 0.6 dynamic_slice.12
  106.9 0.1 broadcast_in_dim.15
  107.0 0.7 reshape_reshape.3.skip
  107.6 0.6 slice.49
  108.2 0.8 fusion.spread
  109.0 63.6 %forward.1 = (bf16[1024,2048]{1,0:T(8,128)(2,1)}, f32[1024,1408]{1,0:T(8,128)}, f32[1024,1024]{1,0:T(8,128)}, bf16[8,128,1024]{2,1,0:T(8,128)(2,1)}, f32[1024,10...) custom-call(bf16[1024,2048]{1,0:T(8,128)(2,1)} %bitcast.36, ...), custom_call_target="tpu_custom_call", output_to_operand_aliasing={{7}: (3, {})} | custom-call | tf_op jit(solution)/shard_map/forward/pallas_call | solution.py:930
  172.6 68.6 %middle.1 = (bf16[4,256,1024]{2,1,0:T(8,128)(2,1)}, bf16[4,256,128]{2,1,0:T(8,128)(2,1)}, bf16[4,256,2048]{2,1,0:T(8,128)(2,1)}, bf16[4,4,128,1024]{3,2,1,0:T(8,...) custom-call(bf16[4,256,1152]{2,1,0:T(8,128)(2,1)} %bitcast.38, ...), custom_call_target="tpu_custom_call", output_to_operand_aliasing={{5}: (1, {})} | custom-call | tf_op jit(solution)/shard_map/middle/pallas_call | solution.py:1160
  241.2 0.9 fusion.1.gather
  242.1 57.9 %backward.1 = (bf16[1024,1024]{1,0:T(8,128)(2,1)}, bf16[1024,1408]{1,0:T(8,128)(2,1)}, f32[64,128]{1,0:T(8,128)}, bf16[4,128,1024]{2,1,0:T(8,128)(2,1)}, bf16[256,1024]{1,0:T(8,128)(2,1)}) custom-call(bf16[1024,1024]{1,0:T(8,128)(2,1)} %bitcast.39, bf16[1024,128]{1,0:T(8,128)(2,1)} %bitcast.42, bf16[1024,2048]{1,0:T(8,128)(2,1)} %get-tuple-element.67.normed_h.normed, ...), custom_call_target="tpu_custom_call" | custom-call | tf_op jit(solution)/shard_map/backward/pallas_call | solution.py:1538
  300.0 91.2 %sum_to_owners.1 = (bf16[4,64,1408]{2,1,0:T(8,128)(2,1)}, f32[128,1024]{1,0:T(8,128)}, f32[128,1024]{1,0:T(8,128)}, bf16[4,64,1024]{2,1,0:T(8,128)(2,1)}, f32[256,2048]{1,0:T(8,128)}, /*index=5*/f32[8,64,128]{2,1,0:T(8,128)}) custom-call(bf16[1024,2048]{1,0:T(8,128)(2,1)} %get-tuple-element.67.normed_h.normed, bf16[4,128,1024]{2,1,0:T(8,128)(2,1)} %get-tuple-element.75.left, ...), custom_call_target="tpu_custom_call" | custom-call | tf_op jit(solution)/shard_map/sum_to_owners/pallas_call | solution.py:1743
  391.2 0.0 copy-start.8
  391.2 0.0 copy-start.9
  391.2 0.0 copy-start.4
  391.2 0.0 copy-start.6
  391.2 0.0 copy-start.7
  391.2 22.9 %gradient_norm.1 = (f32[256,2048]{1,0:T(8,128)}, f32[224,128]{1,0:T(8,128)}, f32[8,128]{1,0:T(8,128)}, f32[8,128]{1,0:T(8,128)}) custom-call(bf16[4,64,1408]{2,1,0:T(8,128)(2,1)} %get-tuple-element.82.part_h, bf16[4,64,1024]{2,1,0:T(8,128)(2,1)} %get-tuple-element.83.gate_h, f32[128,1024]{1,0:T(8,128)} %get-tuple-element.84.left_h, ...), custom_call_target="tpu_custom_call" | custom-call | tf_op jit(solution)/shard_map/gradient_norm/pallas_call | solution.py:420
  414.2 1.3 fusion.9
  415.4 1.3 slice_multiply_fusion
  416.8 0.1 mul.95
  416.9 0.1 mul.97
  416.9 0.0 copy-done.8
  417.0 0.0 copy-done.9
  417.0 0.6 add_subtract_fusion
  417.6 0.0 copy-done.4
  417.6 0.0 copy-done.6
  417.6 0.0 copy-done.7
  417.6 2.1 multiply_subtract_fusion
  419.6 10.9 %update_weights.1 = (f32[256,2048]{1,0:T(8,128)}, f32[64,8512]{1,0:T(8,128)}, f32[64,8512]{1,0:T(8,128)}, f32[64,8512]{1,0:T(8,128)}, bf16[64,8512]{1,0:T(8,128)...) custom-call(f32[8,128]{1,0:T(8,128)} %get-tuple-element.88.norm, ...), custom_call_target="tpu_custom_call" | custom-call | tf_op jit(solution)/shard_map/update_weights/pallas_call | solution.py:550
  430.6 4.8 %copy.44 = bf16[4,1,256,2048]{3,2,1,0:T(8,128)(2,1)} copy(bf16[4,1,256,2048]{3,2,1,0:T(8,128)(2,1)} %bitcast.35) | data formatting | bytes 8388608
  (14 shorter events, 0.1 us)
Async XLA Ops:
  0.7 105.0 %copy-start.5 = (f32[3,64]{1,0:T(4,128)S(1)}, f32[3,64]{1,0:T(4,128)}, u32[]{:S(2)}) copy-start(f32[3,64]{1,0:T(4,128)} %param.25) | copy-start | bytes 2308
  1.4 1.2 copy-start
  2.6 1.6 copy-start.1
  4.2 1.2 copy-start.2
  103.7 0.8 copy-start.3
  391.2 25.8 %copy-start.8 = (f32[3,64]{1,0:T(4,128)S(1)}, f32[3,64]{1,0:T(4,128)}, u32[]{:S(2)}) copy-start(f32[3,64]{1,0:T(4,128)} %param.26) | copy-start | bytes 2308
  391.2 25.8 %copy-start.9 = (f32[3,64]{1,0:T(4,128)S(1)}, f32[3,64]{1,0:T(4,128)}, u32[]{:S(2)}) copy-start(f32[3,64]{1,0:T(4,128)} %param.27) | copy-start | bytes 2308
  391.2 26.3 %copy-start.4 = (f32[872]{0:T(1024)S(1)}, f32[872]{0:T(1024)}, u32[]{:S(2)}) copy-start(f32[872]{0:T(1024)} %param.22) | copy-start | bytes 10468
  391.2 26.3 %copy-start.6 = (f32[872]{0:T(1024)S(1)}, f32[872]{0:T(1024)}, u32[]{:S(2)}) copy-start(f32[872]{0:T(1024)} %param.23) | copy-start | bytes 10468
  391.2 26.3 %copy-start.7 = (f32[872]{0:T(1024)S(1)}, f32[872]{0:T(1024)}, u32[]{:S(2)}) copy-start(f32[872]{0:T(1024)} %param.24) | copy-start | bytes 10468

commit v7 on v6

--- a/solution.py
+++ b/solution.py
@@ -233,6 +233,7 @@
 
 
 WIDE = 512
+LEFT = 1280
 
 
 MESH = pl.DeviceIdType.MESH
@@ -293,9 +294,9 @@
 
 def norm_kernel(
     groups, parts,
-    part_h, gate_h, left_h, right_h, back_h, small_h, hidden_h, gain, cotangent,
+    part_h, rest_h, gate_h, left_h, right_h, back_h, small_h, hidden_h, gain, cotangent,
     hidden_grad, chan, head, norm,
-    part, gate, left, right, back, small, hidden,
+    part, rest, gate, left, right, back, small, hidden,
     cot_v, block, near, all_block, all_near, sends, recvs, near_s, near_r, load, local,
 ):
     group, q = lax.axis_index("dp"), lax.axis_index("seq")
@@ -307,7 +308,8 @@
         pltpu.make_async_copy(source, target, load.at[k])
         for k, (source, target) in enumerate(
             [(back_h, back), (hidden_h, hidden), (part_h, part), (gate_h, gate),
-             (left_h, left), (right_h, right), (small_h, small), (cotangent, cot_v)]
+             (left_h, left), (right_h, right), (small_h, small), (rest_h, rest),
+             (cotangent, cot_v)]
         )
     ]
     for copy in fetches:
@@ -315,7 +317,7 @@
     barrier = pltpu.get_barrier_semaphore()
     for device in everyone:
         pl.semaphore_signal(barrier, inc=1, device_id=device, device_id_type=MESH)
-    for copy in fetches[:7]:
+    for copy in fetches[:8]:
         copy.wait()
     total = small[0]
     for k in range(1, groups):
@@ -335,15 +337,13 @@
         return dgain + jnp.sum(down * tokens * scale, axis=0, keepdims=True)
 
     dgain = lax.fori_loop(0, hidden.shape[0] // rows, gain_rows, jnp.zeros((1, D), F32))
-    tail = part[0, :, cw : cc + H].astype(F32)
-    for k in range(1, parts):
-        tail = tail + part[k, :, cw : cc + H].astype(F32)
+    tail = rest[:, : 2 * N + H]
     squares = total_of(tail * tail)
     for k in range(parts):
-        x = part[k, :, :cw].astype(F32)
+        x = part[k].astype(F32)
         g = gate[k].astype(F32)
         squares = squares + total_of(x * x + g * g)
-    squares = squares + total_of(left[...] * left[...] + right[...] * right[...])
+    squares = squares + total_of(left[...] * left[...]) + total_of(right[...] * right[...])
     for k in range(D // LANES):
         block[k : k + 1, :] = dgain[:, k * LANES : (k + 1) * LANES]
     block[D // LANES :, :] = jnp.broadcast_to(squares, (8, LANES))
@@ -361,7 +361,7 @@
     ]
     for copy in copies:
         copy.start()
-    fetches[7].wait()
+    fetches[8].wait()
 
     def grad_rows(i, carry):
         at = pl.ds(pl.multiple_of(i * rows, rows), rows)
@@ -408,7 +408,7 @@
 
 
 def gradient_norm(
-    collective_id, part, gate, left, right, back, small, hidden, gain, cotangent, groups
+    collective_id, part, rest, gate, left, right, back, small, hidden, gain, cotangent, groups
 ):
     parts = part.shape[0]
     devices = groups * parts
@@ -419,7 +419,7 @@
     chan_rows = -(-CHAN_ROWS // 8) * 8
     return pl.pallas_call(
         functools.partial(norm_kernel, groups, parts),
-        in_specs=[*([hbm] * 7), vmem, hbm],
+        in_specs=[*([hbm] * 8), vmem, hbm],
         out_specs=[vmem] * 4,
         out_shape=[
             jax.ShapeDtypeStruct(hidden.shape, F32),
@@ -428,43 +428,45 @@
             jax.ShapeDtypeStruct((8, LANES), F32),
         ],
         scratch_shapes=[
-            *[pltpu.VMEM(a.shape, a.dtype) for a in (part, gate, left, right, back, small, hidden)],
+            *[
+                pltpu.VMEM(a.shape, a.dtype)
+                for a in (part, rest, gate, left, right, back, small, hidden)
+            ],
             pltpu.VMEM(cotangent.shape, BF16),
             pltpu.VMEM(block, F32),
             pltpu.VMEM(small.shape[1:], F32),
             pltpu.VMEM((devices,) + block, F32),
             pltpu.VMEM((parts,) + small.shape[1:], F32),
             sem((devices - 1,)), sem((devices - 1,)), sem((parts - 1,)), sem((parts - 1,)),
-            sem((8,)), sem((2,)),
+            sem((9,)), sem((2,)),
         ],
         compiler_params=pltpu.CompilerParams(
             collective_id=collective_id, has_side_effects=True, vmem_limit_bytes=63 * 2**20
         ),
         name="gradient_norm",
-    )(part, gate, left, right, back, small, hidden, gain, cotangent)
+    )(part, rest, gate, left, right, back, small, hidden, gain, cotangent)
 
 
 BLOCKS = 4
 
 
 def update_kernel(
-    parts, norm, part_h, gate_h, left_h, right_h, hidden_grad, *refs
+    parts, norm, part_h, rest_h, gate_h, left_h, right_h, hidden_grad, block, *refs
 ):
     ins, refs = refs[:6], refs[6:]
-    hidden_out, outs, refs = refs[0], refs[1:9], refs[9:]
+    hidden_out, block_out, outs, refs = refs[0], refs[1], refs[2:10], refs[10:]
     held, made = refs[:6], refs[6:14]
-    part, gate, left, right, hidden_v, load, store, grads = refs[14:]
+    part, rest, gate, left, right, hidden_v, block_v, load, store, grads = refs[14:]
     clip = norm[1:2, :1]
     cw = INNER // parts
-    cc = cw + 2 * N
     fetches = [
         pltpu.make_async_copy(source, target, grads.at[k])
         for k, (source, target) in enumerate(
-            [(part_h, part), (gate_h, gate), (left_h, left), (right_h, right),
-             (hidden_grad, hidden_v)]
+            [(part_h, part), (gate_h, gate), (left_h, left), (right_h, right), (rest_h, rest),
+             (hidden_grad, hidden_v), (block, block_v)]
         )
     ]
-    for copy in fetches:
+    for copy in fetches[:5]:
         copy.start()
 
     def at(a, i):
@@ -482,6 +484,8 @@
         for i in range(BLOCKS):
             for a in range(weight, weight + 3):
                 loads[i][a].start()
+    for copy in fetches[5:]:
+        copy.start()
     stores = []
 
     def update(weight, rows, lanes, gradient, rate, decay):
@@ -503,7 +507,7 @@
             copy.start()
             stores.append(copy)
 
-    for copy in fetches[:4]:
+    for copy in fetches[:5]:
         copy.wait()
     for i in range(BLOCKS):
         rows = at(0, i)
@@ -517,28 +521,26 @@
                 return carry
 
             lax.fori_loop(0, parts, step, 0)
-        tail = part[0, rows, cw : cc + H].astype(F32)
-        for k in range(1, parts):
-            tail = tail + part[k, rows, cw : cc + H].astype(F32)
-        update(0, rows, slice(2 * INNER, E_IN), tail, 0.02, 0.1)
+        update(0, rows, slice(2 * INNER, E_IN), rest[rows, : 2 * N + H], 0.02, 0.1)
         send(0, rows, i)
-    fetches[4].wait()
-    pass_on = pltpu.make_async_copy(hidden_v, hidden_out, grads.at[5])
-    pass_on.start()
-    half = D // 2
+    fetches[5].wait()
+    fetches[6].wait()
+    for source, target, k in ((hidden_v, hidden_out, 7), (block_v, block_out, 8)):
+        copy = pltpu.make_async_copy(source, target, grads.at[k])
+        copy.start()
+        stores.append(copy)
     for i in range(BLOCKS):
         rows = at(3, i)
         for a in range(3, 6):
             loads[i][a].wait()
-        update(3, rows, slice(0, half), left[rows, :], 0.03, 0.1)
-        update(3, rows, slice(half, D), right[rows, :], 0.03, 0.1)
+        update(3, rows, slice(0, LEFT), left[rows, :], 0.03, 0.1)
+        update(3, rows, slice(LEFT, D), right[rows, :], 0.03, 0.1)
         send(4, rows, i)
-    pass_on.wait()
     for copy in stores:
         copy.wait()
 
 
-def update_weights(norm, part, gate, left, right, hidden_grad, weights):
+def update_weights(norm, part, rest, gate, left, right, hidden_grad, block, weights):
     parts = part.shape[0]
     w_in, w_out = weights[0], weights[3]
     sem = pltpu.SemaphoreType.DMA
@@ -549,18 +551,25 @@
     ]
     return pl.pallas_call(
         functools.partial(update_kernel, parts),
-        in_specs=[vmem, *([hbm] * 11)],
-        out_specs=[hbm] * 9,
-        out_shape=[jax.ShapeDtypeStruct(hidden_grad.shape, F32), *made],
+        in_specs=[vmem, *([hbm] * 13)],
+        out_specs=[hbm] * 10,
+        out_shape=[
+            jax.ShapeDtypeStruct(hidden_grad.shape, F32),
+            jax.ShapeDtypeStruct(block.shape, BF16),
+            *made,
+        ],
         scratch_shapes=[
             *[pltpu.VMEM(w.shape, F32) for w in weights],
             *[pltpu.VMEM(m.shape, m.dtype) for m in made],
-            *[pltpu.VMEM(a.shape, a.dtype) for a in (part, gate, left, right, hidden_grad)],
-            sem((6 * BLOCKS,)), sem((8 * BLOCKS,)), sem((6,)),
+            *[
+                pltpu.VMEM(a.shape, a.dtype)
+                for a in (part, rest, gate, left, right, hidden_grad, block)
+            ],
+            sem((6 * BLOCKS,)), sem((8 * BLOCKS,)), sem((9,)),
         ],
         compiler_params=pltpu.CompilerParams(vmem_limit_bytes=63 * 2**20),
         name="update_weights",
-    )(norm, part, gate, left, right, hidden_grad, *weights)
+    )(norm, part, rest, gate, left, right, hidden_grad, block, *weights)
 
 
 class LineGather:
@@ -579,53 +588,128 @@
             (2 * to + self.core, self.q),
         )
 
-    def step(self, t, got=None):
-        line, z = self.line, self.z
-        low, high = z - t, z + t
-        if t == 0:
-
-            @pl.when(z < line - 1)
-            def _():
-                self.along(z, True, True).start()
-
-            @pl.when(z > 0)
-            def _():
-                self.along(z, False, True).start()
-
-            return
-
-        @pl.when(low >= 0)
-        def _():
-            self.along(low, True).wait_recv()
-
-            @pl.when(z < line - 1)
-            def _():
-                self.along(low, True).start()
+    def push(self, t):
+        z, line = self.z, self.line
+
+        @pl.when((z - t >= 0) & (z < line - 1))
+        def _():
+            self.along(z - t, True, t == 0).start()
+
+        @pl.when((z + t <= line - 1) & (z > 0))
+        def _():
+            self.along(z + t, False, t == 0).start()
+
+    def pushed(self, t):
+        z, line = self.z, self.line
+
+        @pl.when((z - t >= 0) & (z < line - 1))
+        def _():
+            self.along(z - t, True, t == 0).wait_send()
+
+        @pl.when((z + t <= line - 1) & (z > 0))
+        def _():
+            self.along(z + t, False, t == 0).wait_send()
+
+    def step(self, t, got=None, push=True):
+        z, line = self.z, self.line
+
+        @pl.when(z - t >= 0)
+        def _():
+            self.along(z - t, True).wait_recv()
+
+            if push:
+
+                @pl.when(z < line - 1)
+                def _():
+                    self.along(z - t, True).start()
 
             if got is not None:
-                got(low)
-
-        @pl.when(high <= line - 1)
-        def _():
-            self.along(high, False).wait_recv()
-
-            @pl.when(z > 0)
-            def _():
-                self.along(high, False).start()
+                got(z - t)
+
+        @pl.when(z + t <= line - 1)
+        def _():
+            self.along(z + t, False).wait_recv()
+
+            if push:
+
+                @pl.when(z > 0)
+                def _():
+                    self.along(z + t, False).start()
 
             if got is not None:
-                got(high)
-
-    def sent(self):
-        for from_z in range(self.line):
-
-            @pl.when((from_z <= self.z) & (self.z < self.line - 1))
-            def _():
-                self.along(from_z, True).wait_send()
-
-            @pl.when((from_z >= self.z) & (self.z > 0))
-            def _():
-                self.along(from_z, False).wait_send()
+                got(z + t)
+
+
+class LineGathers:
+    def __init__(self, line, z, core, q, slot, own, sends, recvs):
+        half = own.shape[0] // 2
+        self.line = line
+        self.halves = []
+        for h in range(2):
+            rows = pl.ds(h * half, half)
+            self.halves.append(
+                LineGather(
+                    line, z, core, q, lambda from_z, rows=rows: slot(from_z).at[rows],
+                    own.at[rows], sends.at[h], recvs.at[h],
+                )
+            )
+
+    def push(self, t):
+        for part in self.halves:
+            part.push(t)
+
+    def step(self, t, got=None, push=True):
+        self.halves[0].step(t, None, push)
+        self.halves[1].step(t, got, push)
+
+    def pushed(self):
+        for t in range(self.line - 1):
+            for part in self.halves:
+                part.pushed(t)
+
+
+class PlaneGather:
+    def __init__(self, parts, slot, own, sends, recvs, base=0):
+        self.parts, self.slot, self.own = parts, slot, own
+        self.sends, self.recvs, self.base = sends, recvs, base
+        self.group, self.q = lax.axis_index("dp"), lax.axis_index("seq")
+        if parts == 4:
+            self.near = [self.q + 1 - 2 * lax.rem(self.q, 2), lax.rem(self.q + 2, 4)]
+            self.half = own.shape[0] // 2
+
+    def early(self):
+        to = self.near if self.parts == 4 else [peer[1] for peer in seq_peers(self.parts)]
+        return [
+            remote(
+                self.own, self.slot(self.q), self.sends, self.recvs, self.base + k, (self.group, d)
+            )
+            for k, d in enumerate(to)
+        ]
+
+    def late(self):
+        if self.parts != 4:
+            return []
+        copies = []
+        for h in range(2):
+            block = self.slot(self.near[h]).at[pl.ds(h * self.half, self.half)]
+            to = (self.group, self.near[1 - h])
+            copies.append(remote(block, block, self.sends, self.recvs, self.base + 2 + h, to))
+        return copies
+
+    def start(self):
+        for copy in self.early():
+            copy.start()
+
+    def turn(self):
+        if self.parts == 4:
+            for copy in self.early():
+                copy.wait()
+            for copy in self.late():
+                copy.start()
+
+    def finish(self):
+        for copy in self.late() if self.parts == 4 else self.early():
+            copy.wait()
 
 
 def collect_kernel(
@@ -657,7 +741,7 @@
     outs = LineGather(
         line, z, core, q, lambda from_z: wo_out.at[2 * from_z + core, q], low, lwo_s, lwo_r
     )
-    outs.step(0)
+    outs.push(0)
     own = [
         pltpu.make_async_copy(blocks.at[q], w_out.at[group, q], local.at[0]),
         pltpu.make_async_copy(hidden, hid_out.at[q], local.at[1]),
@@ -679,33 +763,37 @@
     own[0].wait()
     for copy in swaps:
         copy.wait()
-    for k, peer in enumerate(peers):
-        for source, target, sends, recvs in (
-            (hidden, hid_out.at[q], hid_s, hid_r),
-            (gates.at[peer[1]], gate_out.at[q], gate_s, gate_r),
-            (low, wo_out.at[group, q], wo_s, wo_r),
-        ):
-            copy = remote(source, target, sends, recvs, k, peer)
-            copy.start()
-            waiting.append(copy)
+    hids = PlaneGather(parts, lambda of: hid_out.at[of], hidden, hid_s, hid_r)
+    lows = PlaneGather(parts, lambda of: wo_out.at[group, of], low, wo_s, wo_r)
+    hids.start()
 
     def across(from_z):
         block = w_out.at[2 * from_z + core]
         return remote(block, block, core_s, core_r, from_z, sibling)
 
-    ins = LineGather(
+    ins = LineGathers(
         line, z, core, q, lambda from_z: w_out.at[2 * from_z + core], w_out.at[group],
         line_s, line_r,
     )
     across(z).start()
-    ins.step(0)
+    ins.push(0)
+    lows.start()
     for t in range(1, line):
-        ins.step(t, lambda from_z: across(from_z).start())
-        if t == line - 2 or line == 2:
-            for s in range(1, line):
-                outs.step(s)
-    ins.sent()
-    outs.sent()
+        ins.step(t, lambda from_z: across(from_z).start(), t < line - 1)
+        if t == line - 2:
+            outs.step(1)
+            hids.turn()
+            lows.turn()
+            for k, peer in enumerate(peers):
+                copy = remote(gates.at[peer[1]], gate_out.at[q], gate_s, gate_r, k, peer)
+                copy.start()
+                waiting.append(copy)
+    ins.pushed()
+    outs.step(2, None, False)
+    outs.pushed(0)
+    outs.pushed(1)
+    hids.finish()
+    lows.finish()
     for from_z in range(line):
         across(from_z).wait_send()
         block = w_out.at[2 * from_z + 1 - core]
@@ -738,8 +826,8 @@
             pltpu.VMEM((parts, rows, cw), BF16),
             pltpu.VMEM(w_own.shape, BF16),
             *([sem((groups * parts - 1,))] * 2),
-            *([sem((parts - 1,))] * 8),
-            *([sem((2, line))] * 4),
+            *([sem((parts + 1,))] * 8),
+            *([sem((2, 2, line))] * 2), *([sem((2, line))] * 2),
             sem((line,)), sem((line,)), sem((5,)),
         ],
         compiler_params=pltpu.CompilerParams(
@@ -754,7 +842,7 @@
     hidden_h, wx_h, gate_h, wo_in, gain_in, gain_out, taps, heads, skip, spread,
     normed_h, px_h, y_h, states_h, z_h, u_h, wz_h, wo,
     hidden, wx, wz, normed, px, y, states, zs, us, xbuf, state, xdt, carried,
-    line_s, line_r, core_s, core_r, out_s, out_r, load, store,
+    line_s, line_r, lwo_s, lwo_r, core_s, core_r, wo_s, wo_r, out_s, out_r, u_s, u_r, load, store,
 ):
     line = groups // 2
     cc = cw + 2 * N
@@ -763,7 +851,7 @@
     group, q = lax.axis_index("dp"), lax.axis_index("seq")
     z, core = group // 2, lax.rem(group, 2)
     sibling = (2 * z + 1 - core, q)
-    peers = seq_peers(parts)
+    peers = mirror_peers(parts)
     loads = [
         pltpu.make_async_copy(source, target, load.at[k])
         for k, (source, target) in enumerate(
@@ -774,40 +862,37 @@
         copy.start()
     greet(peers + dp_peers(groups))
 
-    places = [lax.rem(z + k, line) for k in range(1, line)]
-
-    def plane(k, k_to, device, block):
-        return remote(block, block, out_s, out_r, k * (parts + 1) + k_to, device)
-
-    if parts == 4:
-        near = [q + 1 - 2 * lax.rem(q, 2), lax.rem(q + 2, 4)]
-        half = wo.shape[2] // 2
-
-    def early(k):
-        block = wo.at[2 * places[k] + core, q]
-        if parts == 4:
-            return [plane(k, h, (group, near[h]), block) for h in range(2)]
-        return [plane(k, j, peer, block) for j, peer in enumerate(peers)]
-
-    def late(k, h):
-        rows = pl.ds(h * half, half)
-        block = wo.at[2 * places[k] + core, near[h], rows]
-        return plane(k, 2 + h, (group, near[1 - h]), block)
-
-    for k in range(line - 1):
-        for copy in early(k):
-            copy.start()
+    outs = LineGather(
+        line, z, core, q, lambda from_z: wo.at[2 * from_z + core, q], wo.at[group, q], lwo_s, lwo_r
+    )
+
+    def planes(t, act):
+        for from_z, there in ((z - t, z - t >= 0), (z + t, z + t <= line - 1)):
+
+            @pl.when(there)
+            def _(from_z=from_z):
+                block = wo.at[2 * from_z + core]
+                act(
+                    PlaneGather(
+                        parts, lambda of: block.at[of], block.at[q], out_s, out_r,
+                        from_z * (parts + 1),
+                    )
+                )
+
+    outs.push(2)
+    planes(1, PlaneGather.start)
+    planes(2, PlaneGather.start)
 
     def across(from_z):
         block = wz.at[2 * from_z + core]
         return remote(block, block, core_s, core_r, from_z, sibling)
 
-    gates = LineGather(
+    gates = LineGathers(
         line, z, core, q, lambda from_z: wz.at[2 * from_z + core], wz.at[group], line_s, line_r
     )
     loads[2].wait()
     across(z).start()
-    gates.step(0)
+    gates.push(0)
     loads[0].wait()
 
     def norm_rows(i, carry):
@@ -837,11 +922,18 @@
     xbuf[0:8, :] = jnp.zeros((8, cc), F32)
 
     def scan_rows(i, carry):
-        for t in range(1, line):
-
-            @pl.when(i == min(3 * (t - 1), chunks - 1))
+        for t in range(1, line - 1):
+
+            @pl.when(i == min(5 * t - 4, chunks - 1))
             def _(t=t):
-                gates.step(t, lambda from_z: across(from_z).start())
+                gates.step(t, lambda from_z: across(from_z).start(), t < line - 1)
+
+        for t in range(3, line):
+
+            @pl.when(i == min(2 * t - 3, chunks - 1))
+            def _(t=t):
+                outs.step(t, None, t < line - 1)
+                planes(t, PlaneGather.start)
 
         rows = pl.ds(pl.multiple_of(i * CHUNK, CHUNK), CHUNK)
         scan_forward_step(
@@ -855,27 +947,24 @@
         copy = pltpu.make_async_copy(source, target, store.at[at])
         copy.start()
         stores.append(copy)
-    if parts == 4:
-        for k in range(line - 1):
-            for copy in early(k):
-                copy.wait()
-            for h in range(2):
-                late(k, h).start()
+    for t in range(1, line):
+        planes(t, PlaneGather.turn)
+    gates.step(line - 1, lambda from_z: across(from_z).start(), False)
     for from_z in range(line):
         across(from_z).wait_send()
         block = wz.at[2 * from_z + 1 - core]
         remote(block, block, core_s, core_r, from_z, sibling).wait_recv()
-    gates.sent()
+    gates.pushed()
+    for t in range(2, line - 1):
+        outs.pushed(t)
     copy = pltpu.make_async_copy(wz, wz_h, store.at[4])
     copy.start()
     stores.append(copy)
     lane = lax.broadcasted_iota(jnp.int32, (1, LANES), 1)
     wide = 512
 
-    def gate_rows(i, carry):
-        rows = pl.ds(pl.multiple_of(i * tall, tall), tall)
-        weights = wz[...].reshape(D, cw)
-        gate_in = dot(normed[rows, :], weights)
+    def gate_rows(rows):
+        gate_in = dot(normed[rows, :], wz[...].reshape(D, cw))
         zs[rows, :] = gate_in
         gated = y[rows, :] * (gate_in * jax.nn.sigmoid(gate_in))
         us[rows, :cw] = (gated * gain_out[...]).astype(BF16)
@@ -889,22 +978,40 @@
             rests = rests + jnp.where(lane == level + LEVELS, total, 0.0)
         rests = rests - rests.astype(BF16).astype(F32)
         us[rows, cw:] = jnp.where(lane < LEVELS, highs, rests).astype(BF16)
-        return carry
-
-    lax.fori_loop(0, length // tall, gate_rows, 0)
-    for source, target, at in ((zs, z_h, 5), (us, u_h, 6)):
-        copy = pltpu.make_async_copy(source, target, store.at[at])
-        copy.start()
-        stores.append(copy)
-    for k in range(line - 1):
-        if parts == 4:
-            for h in range(2):
-                late(k, h).wait()
+
+    waiting = []
+    tokens = length // parts
+    for k, dest in enumerate([peer[1] for peer in peers] + [q]):
+
+        def block_rows(i, carry, dest=dest):
+            gate_rows(pl.ds(pl.multiple_of(dest * tokens + i * tall, tall), tall))
+            return carry
+
+        lax.fori_loop(0, tokens // tall, block_rows, 0)
+        ours = us.at[pl.ds(pl.multiple_of(dest * tokens, tokens), tokens)]
+        if k < len(peers):
+            copy = remote(ours, u_h.at[q], u_s, u_r, k, peers[k])
         else:
-            for copy in early(k):
-                copy.wait()
-    for copy in stores:
+            copy = pltpu.make_async_copy(ours, u_h.at[q], store.at[6])
+        copy.start()
+        waiting.append(copy)
+    copy = pltpu.make_async_copy(zs, z_h, store.at[5])
+    copy.start()
+    stores.append(copy)
+
+    def parity(d, of):
+        block = wo.at[2 * d + of]
+        return remote(block, block, wo_s, wo_r, d, sibling)
+
+    for t in range(1, line):
+        planes(t, PlaneGather.finish)
+    for d in range(line):
+        parity(d, core).start()
+    for copy in waiting + stores:
         copy.wait()
+    for d in range(line):
+        parity(d, core).wait_send()
+        parity(d, 1 - core).wait_recv()
 
 
 def forward(collective_id, hidden, wx, gate, wo, gain_in, gain_out, taps, heads, skip, spread):
@@ -918,6 +1025,7 @@
     sem = pltpu.SemaphoreType.DMA
     hbm = pl.BlockSpec(memory_space=pltpu.HBM)
     vmem = pl.BlockSpec(memory_space=pltpu.VMEM)
+    u = jax.ShapeDtypeStruct((parts, length // parts, cw + LANES), BF16)
     made = [
         jax.ShapeDtypeStruct((length, D), BF16),
         jax.ShapeDtypeStruct((length, width), F32),
@@ -931,7 +1039,7 @@
         functools.partial(forward_kernel, groups, parts, cw),
         in_specs=[*([hbm] * 4), *([vmem] * 6)],
         out_specs=[hbm] * 8,
-        out_shape=[*made, wz, jax.ShapeDtypeStruct(wo.shape, BF16)],
+        out_shape=[*made[:-1], u, wz, jax.ShapeDtypeStruct(wo.shape, BF16)],
         input_output_aliases={3: 7},
         scratch_shapes=[
             pltpu.VMEM(hidden.shape, BF16),
@@ -942,8 +1050,10 @@
             pltpu.VMEM((N, cw), F32),
             pltpu.VMEM((CHUNK, cw), BF16),
             pltpu.VMEM((CHUNK, cw), F32),
-            sem((2, line)), sem((2, line)), sem((line,)), sem((line,)),
-            sem(((line - 1) * (parts + 1),)), sem(((line - 1) * (parts + 1),)),
+            *([sem((2, 2, line))] * 2), *([sem((2, line))] * 2),
+            *([sem((line,))] * 4),
+            sem((line * (parts + 1),)), sem((line * (parts + 1),)),
+            sem((parts - 1,)), sem((parts - 1,)),
             sem((3,)), sem((7,)),
         ],
         compiler_params=pltpu.CompilerParams(
@@ -975,10 +1085,10 @@
 
 def middle_kernel(
     groups, parts, cw,
-    u_h, wo_in, cot_h, tokens_h,
-    back_h, coef_h, block_h, left_h, right_h, wo,
+    u_h, wo, cot_h, tokens_h,
+    back_h, coef_h, block_h, left_h, right_h,
     u, cot, tokens, mixed, branch, norms, pulls, back, coefs, weights, sent, held, left, right,
-    u_s, u_r, wo_s, wo_r, back_s, back_r, coef_s, coef_r, core_s, core_r, fetch, load, store, local,
+    back_s, back_r, coef_s, coef_r, core_s, core_r, fetch, load, store, local,
 ):
     line = groups // 2
     group, q = lax.axis_index("dp"), lax.axis_index("seq")
@@ -986,24 +1096,14 @@
     sibling = (2 * z + 1 - core, q)
     peers = mirror_peers(parts)
     loads = [
-        pltpu.make_async_copy(u_h.at[q], u.at[q], load.at[0]),
+        pltpu.make_async_copy(u_h, u, load.at[0]),
         pltpu.make_async_copy(cot_h, cot, load.at[1]),
         pltpu.make_async_copy(tokens_h, tokens, load.at[2]),
     ]
     for copy in loads:
         copy.start()
     greet(peers + [sibling])
-    swaps = [remote(u_h.at[peer[1]], u.at[q], u_s, u_r, k, peer) for k, peer in enumerate(peers)]
-    for copy in swaps:
-        copy.start()
-
-    def parity(d, of):
-        block = wo.at[2 * d + of]
-        return remote(block, block, wo_s, wo_r, d, sibling)
-
-    for d in range(line):
-        parity(d, core).start()
-    for copy in loads + swaps:
+    for copy in loads:
         copy.wait()
 
     terms = u[0, :, cw:].astype(F32)
@@ -1025,9 +1125,6 @@
         return carry
 
     lax.fori_loop(0, tokens.shape[0] // rows, mix_rows, 0)
-    for d in range(line):
-        parity(d, core).wait_send()
-        parity(d, 1 - core).wait_recv()
 
     width = INNER // groups
     per = WIDE // width
@@ -1102,8 +1199,8 @@
     outgoing.append(copy)
 
     share = width // parts
-    tile = 512
-    halves = D // 2 // tile
+    tile = 256
+    turns = LEFT // tile
 
     def product(of, j):
         channel = of * width
@@ -1119,13 +1216,13 @@
             sent[d, :, cols] = product(2 * d + 1 - core, j).astype(BF16)
             return carry
 
-        lax.fori_loop(0, 2 * halves, send_step, 0)
+        lax.fori_loop(0, D // tile, send_step, 0)
         copy = remote(sent.at[d], held.at[d], core_s, core_r, d, sibling)
         copy.start()
         cores.append(copy)
     for d in range(line):
         cores[d].wait_recv()
-        for out, target, first, at in ((left, left_h, 0, 0), (right, right_h, halves, 1)):
+        for out, target, first, at in ((left, left_h, 0, 0), (right, right_h, turns, 1)):
 
             def keep_step(j, carry, d=d, out=out, first=first):
                 cols = pl.ds(pl.multiple_of((j + first) * tile, tile), tile)
@@ -1136,7 +1233,7 @@
                     out[part, d, :, to] = total[part * share : (part + 1) * share]
                 return carry
 
-            lax.fori_loop(0, halves, keep_step, 0)
+            lax.fori_loop(0, out.shape[-1] // tile, keep_step, 0)
             copy = pltpu.make_async_copy(
                 out.at[:, d], target.at[:, d], store.at[LEVELS + 2 * d + at]
             )
@@ -1156,20 +1253,19 @@
     width = share * parts
     sem = pltpu.SemaphoreType.DMA
     hbm = pl.BlockSpec(memory_space=pltpu.HBM)
-    half = (parts, line, share, D // 2)
+    left = (parts, line, share, LEFT)
+    right = (parts, line, share, D - LEFT)
     return pl.pallas_call(
         functools.partial(middle_kernel, groups, parts, cw),
         in_specs=[hbm] * 4,
-        out_specs=[hbm] * 6,
+        out_specs=[hbm] * 5,
         out_shape=[
             jax.ShapeDtypeStruct((parts, rows, cw), BF16),
             jax.ShapeDtypeStruct((parts, rows, LANES), BF16),
             jax.ShapeDtypeStruct(cotangent.shape, BF16),
-            jax.ShapeDtypeStruct(half, BF16),
-            jax.ShapeDtypeStruct(half, BF16),
-            jax.ShapeDtypeStruct(wo.shape, BF16),
+            jax.ShapeDtypeStruct(left, BF16),
+            jax.ShapeDtypeStruct(right, BF16),
         ],
-        input_output_aliases={1: 5},
         scratch_shapes=[
             pltpu.VMEM(u.shape, BF16),
             pltpu.VMEM(cotangent.shape, BF16),
@@ -1183,9 +1279,8 @@
             pltpu.VMEM((3, WIDE // width, parts, share, D), BF16),
             pltpu.VMEM((line, width, D), BF16),
             pltpu.VMEM((line, width, D), BF16),
-            pltpu.VMEM(half, BF16),
-            pltpu.VMEM(half, BF16),
-            sem((parts - 1,)), sem((parts - 1,)), sem((line,)), sem((line,)),
+            pltpu.VMEM(left, BF16),
+            pltpu.VMEM(right, BF16),
             *([sem((parts - 1,))] * 4),
             sem((line,)), sem((line,)), sem((3,)), sem((3,)), sem((LEVELS + 2 * line,)), sem((2,)),
         ],
@@ -1209,8 +1304,9 @@
 
 
 class PlaneSum:
-    def __init__(self, parts, group, q, blocks, first, second, sends, recvs):
+    def __init__(self, parts, group, q, blocks, first, second, sends, recvs, source=None):
         self.parts, self.group, self.q = parts, group, q
+        self.source = blocks if source is None else source
         self.blocks, self.first, self.second = blocks, first, second
         self.sends, self.recvs = sends, recvs
         self.half = blocks.shape[1] // 2
@@ -1228,8 +1324,9 @@
         sem = pltpu.SemaphoreType.DMA
         return [pltpu.VMEM(first, dtype), pltpu.VMEM(second, dtype), sem((count,)), sem((count,))]
 
-    def piece(self, of, h):
-        return self.blocks.at[of, pl.ds(h * self.half, self.half)]
+    def piece(self, of, h, source=None):
+        blocks = self.blocks if source is None else source
+        return blocks.at[of, pl.ds(h * self.half, self.half)]
 
     def early(self, h):
         if self.parts != 4:
@@ -1237,7 +1334,10 @@
         near = self.near[h]
         to = (self.group, near)
         return [
-            remote(self.piece(of, h), self.first.at[h, k], self.sends, self.recvs, 2 * h + k, to)
+            remote(
+                self.piece(of, h, self.source), self.first.at[h, k],
+                self.sends, self.recvs, 2 * h + k, to,
+            )
             for k, of in enumerate((near, self.far))
         ]
 
@@ -1250,7 +1350,7 @@
     def direct(self):
         peers = seq_peers(self.parts)
         return [
-            remote(self.blocks.at[peer[1]], self.first.at[k], self.sends, self.recvs, k, peer)
+            remote(self.source.at[peer[1]], self.first.at[k], self.sends, self.recvs, k, peer)
             for k, peer in enumerate(peers)
         ]
 
@@ -1381,6 +1481,33 @@
             self.add(self.up, z)
             self.behind(z, False).wait_recv()
             add_blocks(out, self.up.at[z], self.down.at[z], self.rows, self.steps)
+
+
+class LineSums:
+    def __init__(self, line, z, core, q, acc, up, down, sems, rows):
+        half = acc.shape[1] // 2
+        self.line = line
+        self.halves = [
+            LineSum(
+                line, z, core, q, *[a.at[:, pl.ds(h * half, half)] for a in (acc, up, down)],
+                *[s.at[h] for s in sems], rows, half // rows,
+            )
+            for h in range(2)
+        ]
+        self.half = half
+
+    def step(self, t):
+        for part in self.halves:
+            part.step(t)
+
+    def finish(self, out):
+        for h, part in enumerate(self.halves):
+            part.finish(out.at[pl.ds(h * self.half, self.half)])
+
+    def sent(self):
+        for t in range(self.line - 1):
+            for part in self.halves:
+                part.sent(t)
 
 
 def backward_kernel(
@@ -1404,18 +1531,31 @@
         pltpu.make_async_copy(source, target, load.at[k])
         for k, (source, target) in enumerate(
             [(wide_h, wide), (back_h, dz), (coefs_h, coefs), (y_h, y), (z_h, dy),
-             (normed_h, normed), (px_h, px), (states_h, states)]
+             (normed_h, normed), (states_h, states)]
         )
     ]
-    for copy in loads:
-        copy.start()
+    for copy in loads[1:5]:
+        copy.start()
+
+    def fetch(at, first=False):
+        slot = lax.rem(at, 2)
+        if first:
+            return pltpu.make_async_copy(
+                px_h.at[pl.ds(0, CHUNK)], px.at[0, pl.ds(8, CHUNK)], load.at[7]
+            )
+        rows = pl.ds(pl.multiple_of(at * CHUNK - 8, 8), CHUNK + 8)
+        return pltpu.make_async_copy(px_h.at[rows], px.at[slot], load.at[7 + slot])
+
     greet(seq_peers(parts) + dp_peers(groups))
-    plane = PlaneSum(parts, group, q, wide, first, second, wide_s, wide_r)
-    loads[0].wait()
+    plane = PlaneSum(parts, group, q, wide, first, second, wide_s, wide_r, wide_h)
     plane.start(0)
     plane.start(1)
     for copy in loads[1:5]:
         copy.wait()
+    loads[5].start()
+    loads[6].start()
+    loads[0].start()
+    fetch(chunks - 1).start()
 
     rows = 32
     lane = lax.broadcasted_iota(jnp.int32, (1, LANES), 1)
@@ -1455,42 +1595,60 @@
         return remote(gate_made.at[d], gate_held.at[d], core_s, core_r, d, sibling)
 
     order = [d for k in range(line // 2) for d in (line - 1 - k, k)]
-    for d in order:
-        dweight(2 * d + 1 - core, gate_made.at[d])
-        core_copy(d).start()
-    for d in order:
-        dweight(2 * d + core, gate_acc.at[d])
-        core_copy(d).wait()
-        add_blocks(gate_acc.at[d], gate_acc.at[d], gate_held.at[d], span // 4, 4)
-    gates = LineSum(
-        line, z, core, q, gate_acc, gate_up, gate_down, up_s, up_r, down_s, down_r, span // 4, 4
-    )
-    gates.step(0)
+    gates = LineSums(
+        line, z, core, q, gate_acc, gate_up, gate_down, (up_s, up_r, down_s, down_r), span // 8
+    )
+    for some in (order[:2], order[2:]):
+        for d in some:
+            dweight(2 * d + 1 - core, gate_made.at[d])
+            core_copy(d).start()
+        for d in some:
+            dweight(2 * d + core, gate_acc.at[d])
+            core_copy(d).wait()
+            add_blocks(gate_acc.at[d], gate_acc.at[d], gate_held.at[d], span // 4, 4)
+        if some[0] == order[0]:
+            gates.step(0)
     dstate[...] = jnp.zeros_like(dstate)
     dcbuf[CHUNK : CHUNK + 8, :] = jnp.zeros((8, cc), F32)
     dtaps[...] = jnp.zeros_like(dtaps)
     dheads[...] = jnp.zeros_like(dheads)
     dskip[...] = jnp.zeros_like(dskip)
-    for copy in loads[6:]:
-        copy.wait()
+    loads[6].wait()
+    loads[0].wait()
 
     def scan_rows(i, carry):
         for t in range(1, line - 1):
 
-            @pl.when(i == min(4 * t - 1, chunks - 1))
+            @pl.when(i == min(3 * t - 2, chunks - 1))
             def _(t=t):
-                gates.sent(t - 1)
                 gates.step(t)
 
-        @pl.when(i == 2)
+        @pl.when(i == 3)
         def _():
             plane.turn(32)
 
         at = chunks - 1 - i
         here = pl.ds(pl.multiple_of(at * CHUNK, CHUNK), CHUNK)
-        before = pl.ds(pl.multiple_of(jnp.maximum(at * CHUNK - 8, 0), 8), 8)
+
+        @pl.when(at > 0)
+        def _():
+            fetch(at).wait()
+
+        @pl.when(at == 0)
+        def _():
+            fetch(0, True).wait()
+
+        @pl.when(at > 1)
+        def _():
+            fetch(at - 1).start()
+
+        @pl.when(at == 1)
+        def _():
+            fetch(0, True).start()
+
+        rows = px.at[lax.rem(at, 2)]
         scan_backward_step(
-            cw, at == 0, px.at[here], px.at[before], taps, heads, skip, spread, gather,
+            cw, at == 0, rows.at[pl.ds(8, CHUNK)], rows.at[pl.ds(0, 8)], taps, heads, skip, spread, gather,
             dy.at[here], y.at[here], states.at[at], dpx.at[here], dtaps, dheads, dskip,
             xbuf, dstate, dcbuf, slope, xact, xd_s, dxd_s, acc_s,
         )
@@ -1517,7 +1675,7 @@
     )
     plane.finish(wide_sum, 32)
     gates.finish(gate_sum)
-    gates.sent(line - 2)
+    gates.sent()
     dz_out.wait()
     dpx_out.wait()
 
@@ -1547,7 +1705,9 @@
             jax.ShapeDtypeStruct((span, cw), BF16),
         ],
         scratch_shapes=[
-            *[pltpu.VMEM(a.shape, a.dtype) for a in (back, coefs, normed, px, y, z, states, wide)],
+            *[pltpu.VMEM(a.shape, a.dtype) for a in (back, coefs, normed)],
+            pltpu.VMEM((2, CHUNK + 8, width), F32),
+            *[pltpu.VMEM(a.shape, a.dtype) for a in (y, z, states, wide)],
             pltpu.VMEM((length, width), BF16),
             pltpu.VMEM((8, cc), F32),
             pltpu.VMEM((8, LANES), F32),
@@ -1563,8 +1723,8 @@
             pltpu.VMEM((CHUNK, CHUNK), F32),
             *PlaneSum.scratch(parts, wide.shape[1:], BF16),
             *([pltpu.VMEM((line, span, cw), BF16)] * 5),
-            *([sem((line,))] * 6),
-            sem((8,)), sem((2,)),
+            sem((line,)), sem((line,)), *([sem((2, line))] * 4),
+            sem((9,)), sem((2,)),
         ],
         compiler_params=pltpu.CompilerParams(
             collective_id=collective_id, has_side_effects=True, vmem_limit_bytes=63 * 2**20
@@ -1574,15 +1734,17 @@
 
 
 def owners_kernel(
-    groups, parts, rows,
+    groups, parts, rows, cw,
     normed, left, right, gate, small, dz, dpx, wz, wx,
-    part, left_out, right_out, gate_out, back_out, small_all,
+    part, rest_out, left_out, right_out, gate_out, back_out, small_all,
     made, held, acc, up, down, final, left_up, left_down, right_acc, right_up, right_down,
+    rest_made, rest_held, rest, rest_acc, rest_up, rest_down,
     normed_v, dz_v, dpx_v, wz_v, wx_v, back, back_sum,
     right_1, right_2, right_s, right_r, back_1, back_2, back_s, back_r,
+    rest_1, rest_2, rest_s, rest_r,
     core_s, core_r, up_s, up_r, down_s, down_r, lup_s, lup_r, ldown_s, ldown_r,
-    rup_s, rup_r, rdown_s, rdown_r, part_s, part_r, gate_s, gate_r, small_s, small_r,
-    load, local,
+    rup_s, rup_r, rdown_s, rdown_r, tup_s, tup_r, tdown_s, tdown_r, rcore_s, rcore_r,
+    part_s, part_r, gate_s, gate_r, small_s, small_r, load, local,
 ):
     line = groups // 2
     span = parts * rows
@@ -1597,7 +1759,7 @@
             [(normed, normed_v), (dpx, dpx_v), (dz, dz_v), (wz, wz_v), (wx, wx_v)]
         )
     ]
-    for copy in loads:
+    for copy in loads[:2]:
         copy.start()
     greet(peers + others)
     half_rows = left.shape[1] // 2
@@ -1613,6 +1775,10 @@
     )
     lefts.step(0)
     right_plane = PlaneSum(parts, group, q, right, right_1, right_2, right_s, right_r)
+    rest_plane = PlaneSum(parts, group, q, rest, rest_1, rest_2, rest_s, rest_r)
+    rests = LineSum(
+        line, z, core, q, rest_acc, rest_up, rest_down, tup_s, tup_r, tdown_s, tdown_r, rows, 1
+    )
     back_plane = PlaneSum(parts, group, q, back, back_1, back_2, back_s, back_r)
     right_plane.start(0)
     right_plane.start(1)
@@ -1633,25 +1799,36 @@
         copy.start()
     loads[0].wait()
     loads[1].wait()
+    for copy in loads[2:]:
+        copy.start()
     tile = 512
 
-    def dweight(of, out):
+    def dweight(of):
         at = pl.ds(pl.multiple_of(of * span, span), span)
-        out[...] = dot(normed_v[:, at], dpx_v[...], TN).astype(BF16)
+        return dot(normed_v[:, at], dpx_v[...], TN)
 
     cores = {}
     order = [d for k in range(line // 2) for d in (line - 1 - k, k)]
 
     def share_core(d):
-        dweight(2 * d + 1 - core, made.at[d])
-        copy = remote(made.at[d], held.at[d], core_s, core_r, d, sibling)
-        copy.start()
-        cores[d] = copy
+        total = dweight(2 * d + 1 - core)
+        made[d] = total[:, :cw].astype(BF16)
+        rest_made[d] = total[:, cw:].astype(BF16)
+        cores[d] = [
+            remote(made.at[d], held.at[d], core_s, core_r, d, sibling),
+            remote(rest_made.at[d], rest_held.at[d], rcore_s, rcore_r, d, sibling),
+        ]
+        for copy in cores[d]:
+            copy.start()
 
     def sum_core(d):
-        dweight(2 * d + core, acc.at[d])
-        cores[d].wait()
-        add_blocks(acc.at[d], acc.at[d], held.at[d], rows, parts)
+        total = dweight(2 * d + core)
+        for copy in cores[d]:
+            copy.wait()
+        acc[d] = (total[:, :cw] + held[d].astype(F32)).astype(BF16)
+        others = (total[:, cw:] + rest_held[d].astype(F32)).astype(BF16)
+        for k in range(parts):
+            rest[k, d] = others[k * rows : (k + 1) * rows]
 
     share_core(order[0])
     lefts.sent(0)
@@ -1667,6 +1844,8 @@
         share_core(d)
     for d in order[2:]:
         sum_core(d)
+    rest_plane.start(0)
+    rest_plane.start(1)
     for copy in loads[2:]:
         copy.wait()
 
@@ -1683,6 +1862,7 @@
         lax.fori_loop(0, D // tile, step, 0)
 
     right_plane.turn(32)
+    rest_plane.turn(rows)
     if parts == 4:
         dnormed(back_plane.far)
         dnormed(back_plane.near[0])
@@ -1697,13 +1877,19 @@
     back_plane.start(1)
     dnormed(q)
     right_plane.finish(right_acc, 32)
+    rest_plane.finish(rest_acc, rows)
+    rests.step(0)
     for t in range(2, line - 1):
         wholes.sent(t - 1)
         wholes.step(t)
+        rests.sent(t - 2)
+        rests.step(t - 1)
     back_plane.turn(32)
     lefts.finish(left_out)
     lefts.sent(line - 2)
     wholes.sent(line - 2)
+    rests.sent(line - 3)
+    rests.step(line - 2)
     rights.step(0)
     wholes.finish(final)
     for k, peer in enumerate(peers):
@@ -1725,6 +1911,8 @@
     for t in range(2, line - 1):
         rights.sent(t - 1)
         rights.step(t)
+    rests.finish(rest_out)
+    rests.sent(line - 2)
     rights.finish(right_out)
     rights.sent(line - 2)
     for copy in own + waiting:
@@ -1732,35 +1920,45 @@
 
 
 def sum_to_owners(collective_id, normed, left, right, gate, small, dz, dpx, wz, wx):
-    parts, line, out_rows, half = right.shape
+    parts, line, out_rows, slim = right.shape
     groups = 2 * line
-    rows = gate.shape[1]
-    span, width = rows * parts, dpx.shape[1]
+    rows, cw = gate.shape[1:]
+    span = rows * parts
+    extra = dpx.shape[1] - cw
     tokens = dz.shape[0] // parts
     sem = pltpu.SemaphoreType.DMA
     vmem = pl.BlockSpec(memory_space=pltpu.VMEM)
     hbm = pl.BlockSpec(memory_space=pltpu.HBM)
+    right_sum = (line, out_rows, slim)
+    rest = (parts, line, rows, extra)
     return pl.pallas_call(
-        functools.partial(owners_kernel, groups, parts, rows),
+        functools.partial(owners_kernel, groups, parts, rows, cw),
         in_specs=[hbm, vmem, vmem, hbm, vmem, hbm, hbm, hbm, hbm],
-        out_specs=[hbm, vmem, vmem, hbm, hbm, vmem],
+        out_specs=[hbm, vmem, vmem, vmem, hbm, hbm, vmem],
         out_shape=[
-            jax.ShapeDtypeStruct((parts, rows, width), BF16),
-            *([jax.ShapeDtypeStruct((out_rows, half), F32)] * 2),
+            jax.ShapeDtypeStruct((parts, rows, cw), BF16),
+            jax.ShapeDtypeStruct((rows, extra), F32),
+            jax.ShapeDtypeStruct((out_rows, left.shape[-1]), F32),
+            jax.ShapeDtypeStruct((out_rows, slim), F32),
             jax.ShapeDtypeStruct(gate.shape, BF16),
             jax.ShapeDtypeStruct((tokens, D), F32),
             jax.ShapeDtypeStruct((groups,) + small.shape, F32),
         ],
         scratch_shapes=[
-            *([pltpu.VMEM((line, span, width), BF16)] * 5),
-            pltpu.VMEM((span, width), BF16),
-            *([pltpu.VMEM(left.shape, BF16)] * 5),
+            *([pltpu.VMEM((line, span, cw), BF16)] * 5),
+            pltpu.VMEM((span, cw), BF16),
+            *([pltpu.VMEM(left.shape, BF16)] * 2),
+            *([pltpu.VMEM(right_sum, BF16)] * 3),
+            *([pltpu.VMEM((line, span, extra), BF16)] * 2),
+            pltpu.VMEM(rest, BF16),
+            *([pltpu.VMEM(rest[1:], BF16)] * 3),
             *[pltpu.VMEM(a.shape, BF16) for a in (normed, dz, dpx, wz, wx)],
             pltpu.VMEM((parts, tokens, D), BF16),
             pltpu.VMEM((tokens, D), F32),
             *PlaneSum.scratch(parts, right.shape[1:], BF16),
             *PlaneSum.scratch(parts, (tokens, D), BF16),
-            *([sem((line,))] * 14),
+            *PlaneSum.scratch(parts, rest[1:], BF16),
+            *([sem((line,))] * 20),
             *([sem((parts - 1,))] * 4),
             *([sem((groups - 1,))] * 2),
             sem((5,)),
@@ -1827,30 +2025,29 @@
     )
     wx, wz = wx.reshape(D, cc + LANES), wz.reshape(D, cw)
     cotangent = out_grads[:, 0]
-    back_own, coefs, block_out, dwo_left, dwo_right, _ = middle(
-        2, u_blocks.reshape(parts, rows, cw + LANES), wo, cotangent, hidden_in[0]
-    )
-    block_out = block_out[:, None]
+    back_own, coefs, block_out, dwo_left, dwo_right = middle(
+        2, u_blocks, wo, cotangent, hidden_in[0]
+    )
 
     dz, dpx, small, dwo_left, dwz = backward(
         5, back_own.reshape(length, cw), coefs.reshape(length, LANES), normed, px, y, z, states,
         dwo_left, own_gain.reshape(1, cw), taps, heads, skip, spread,
     )
-    x_part, left_part, right_part, z_part, dnormed, small = sum_to_owners(
+    x_part, rest, left_part, right_part, z_part, dnormed, small = sum_to_owners(
         4, normed, dwo_left, dwo_right, dwz.reshape(parts, in_rows, cw), small, dz, dpx, wz, wx
     )
     hidden_grad, chan_total, head_total, norm = gradient_norm(
-        6, x_part, z_part, left_part, right_part, dnormed, small, hidden_in[0],
+        6, x_part, rest, z_part, left_part, right_part, dnormed, small, hidden_in[0],
         gain_in.reshape(1, D), cotangent, groups,
     )
     (
-        hidden_grad, w_in_new, w_in_m_new, w_in_v_new, w_in_copy,
+        hidden_grad, block_out, w_in_new, w_in_m_new, w_in_v_new, w_in_copy,
         w_out_new, w_out_m_new, w_out_v_new, w_out_copy,
     ) = update_weights(
-        norm, x_part, z_part, left_part, right_part, hidden_grad,
+        norm, x_part, rest, z_part, left_part, right_part, hidden_grad, block_out,
         (w_in, w_in_m, w_in_v, w_out, w_out_m, w_out_v),
     )
-    hidden_grad = hidden_grad[None]
+    hidden_grad, block_out = hidden_grad[None], block_out[:, None]
     grad_norm, clip_factor = norm[0, 0], norm[1, 0]
     owner = group * parts + q
     chan_part = lax.dynamic_slice(chan_total.reshape(-1), (owner * chan_len,), (chan_len,))

time: 442 us -> 415 us (0.939)
  Pallas kernels: 413 us -> 390 us
  local copies, waits for them, and re-layouts: 13.4 us -> 8.64 us
    pallas_call x1, Pallas kernels: 63.6 us -> 89.4 us  [forward(): pl.pallas_call(functools.partial(forward_kernel, groups, parts, cw), in_s...]
    pallas_call x1, Pallas kernels: 68.6 us -> 43.7 us  [middle(): pl.pallas_call(functools.partial(middle_kernel, groups, parts, cw), in_sp...]
    pallas_call x1, Pallas kernels: 98.3 us -> 80.7 us  [collect(): pl.pallas_call(functools.partial(collect_kernel, groups, parts), in_specs...]
    unnamed x22 -> x21, local copies, waits for them, and re-layouts: 9.7 us -> 4.92 us
where the time goes in v7:
time: 415 us; the launch traced here: 407 us
  Pallas kernels  390 us (94%)
  local copies, waits for them, and re-layouts  8.64 us (2%)
  other arithmetic  7.66 us (2%)
    pallas_call x1, Pallas kernels, sum_to_owners(): pl.pallas_call(functools.partial(owners_kernel, groups, parts, rows, cw),...  89.8 us
    pallas_call x1, Pallas kernels, forward(): pl.pallas_call(functools.partial(forward_kernel, groups, parts, cw), in_s...  89.4 us
    pallas_call x1, Pallas kernels, collect(): pl.pallas_call(functools.partial(collect_kernel, groups, parts), in_specs...  80.7 us
    pallas_call x1, Pallas kernels, backward(): pl.pallas_call(functools.partial(backward_kernel, 2 * line, parts, cw), i...  54.6 us
    pallas_call x1, Pallas kernels, middle(): pl.pallas_call(functools.partial(middle_kernel, groups, parts, cw), in_sp...  43.7 us
    pallas_call x1, Pallas kernels, gradient_norm(): pl.pallas_call(functools.partial(norm_kernel, groups, parts), in_specs=[*...  19 us
    pallas_call x1, Pallas kernels, update_weights(): pl.pallas_call(functools.partial(update_kernel, parts), in_specs=[vmem, *...  12.3 us

profile of v7, /device:TPU:1, one launch (start us, length us, event | category | flops | bytes accessed | tf_op | source)
XLA Modules:
  0.0 407.2 jit_solution(1607804113683315767)
XLA Ops:
  0.7 0.7 reduce_precision.3
  1.4 0.0 copy-start
  1.4 1.2 copy-done
  2.6 0.0 copy-start.1
  2.6 1.6 copy-done.1
  4.2 0.0 copy-start.2
  4.2 1.2 copy-done.2
  5.4 0.0 copy-start.5
  5.4 80.7 %collect.1 = (bf16[4,256,2048]{2,1,0:T(8,128)(2,1)}, bf16[8,4,64,1408]{3,2,1,0:T(8,128)(2,1)}, bf16[4,64,1024]{2,1,0:T(8,128)(2,1)S(1)}, f32[32,8,128]{2,1,0:T(8,128)S(1)}, bf16[8,4,128,2048]{3,2,1,0:T(8,128)(2,1)}) custom-call(bf16[256,2048]{1,0:T(8,128)(2,1)S(1)} %bitcast.28, f32[64,8512]{1,0:T(8,128)S(1)} %copy-done.1, f32[128,2048]{1,0:T(8,128)S(1)} %copy-done.2, ...), custom_call_target="tpu_custom_call" | custom-call | tf_op jit(solution)/shard_map/collect/pallas_call | solution.py:813
  86.1 0.0 copy-start.3
  86.1 0.8 copy-done.3
  87.0 0.1 reshape.102
  87.2 0.1 pad.16.clone
  87.3 0.1 maximum_maximum_fusion
  87.4 0.6 pad_maximum_fusion.taps
  88.0 0.0 copy-done.5
  88.0 0.1 constant_dynamic-slice_fusion
  88.1 0.6 select_maximum_fusion.heads
  88.7 0.6 dynamic_slice.12
  89.3 0.1 broadcast_in_dim.15
  89.4 0.7 reshape_reshape.3.skip
  90.0 0.6 slice.49
  90.6 0.8 fusion.spread
  91.4 89.4 %forward.1 = (bf16[1024,2048]{1,0:T(8,128)(2,1)}, f32[1024,1408]{1,0:T(8,128)}, f32[1024,1024]{1,0:T(8,128)}, bf16[8,128,1024]{2,1,0:T(8,128)(2,1)}, f32[1024,10...) custom-call(bf16[1024,2048]{1,0:T(8,128)(2,1)} %bitcast.34, ...), custom_call_target="tpu_custom_call", output_to_operand_aliasing={{7}: (3, {})} | custom-call | tf_op jit(solution)/shard_map/forward/pallas_call | solution.py:1038
  180.8 43.7 %middle.1 = (bf16[4,256,1024]{2,1,0:T(8,128)(2,1)}, bf16[4,256,128]{2,1,0:T(8,128)(2,1)}, bf16[4,256,2048]{2,1,0:T(8,128)(2,1)}, bf16[4,4,128,1280]{3,2,1,0:T(8,128)(2,1)}, bf16[4,4,128,768]{3,2,1,0:T(8,128)(2,1)}) custom-call(bf16[4,256,1152]{2,1,0:T(8,128)(2,1)} %get-tuple-element.67.u_h, bf16[8,4,128,2048]{3,2,1,0:T(8,128)(2,1)} %get-tuple-element.68.wo, ...), custom_call_target="tpu_custom_call" | custom-call | tf_op jit(solution)/shard_map/middle/pallas_call | solution.py:1258
  224.6 0.9 fusion.1.gather
  225.5 54.6 %backward.1 = (bf16[1024,1024]{1,0:T(8,128)(2,1)}, bf16[1024,1408]{1,0:T(8,128)(2,1)}, f32[64,128]{1,0:T(8,128)}, bf16[4,128,1280]{2,1,0:T(8,128)(2,1)}, bf16[256,1024]{1,0:T(8,128)(2,1)}) custom-call(bf16[1024,1024]{1,0:T(8,128)(2,1)} %bitcast.36, bf16[1024,128]{1,0:T(8,128)(2,1)} %bitcast.39, bf16[1024,2048]{1,0:T(8,128)(2,1)} %get-tuple-element.66.normed_h.normed, ...), custom_call_target="tpu_custom_call" | custom-call | tf_op jit(solution)/shard_map/backward/pallas_call | solution.py:1696
  280.1 89.8 %sum_to_owners.1 = (bf16[4,64,1024]{2,1,0:T(8,128)(2,1)}, f32[64,384]{1,0:T(8,128)}, f32[128,1280]{1,0:T(8,128)}, f32[128,768]{1,0:T(8,128)}, bf16[4,64,1024]{2,...) custom-call(bf16[1024,2048]{1,0:T(8,128)(2,1)} %get-tuple-element.66.normed_h.normed, ...), custom_call_target="tpu_custom_call" | custom-call | tf_op jit(solution)/shard_map/sum_to_owners/pallas_call | solution.py:1934
  369.9 0.0 copy-start.8
  370.0 0.0 copy-start.9
  370.0 0.0 copy-start.4
  370.0 0.0 copy-start.6
  370.0 0.0 copy-start.7
  370.0 19.0 %gradient_norm.1 = (f32[256,2048]{1,0:T(8,128)}, f32[224,128]{1,0:T(8,128)}, f32[8,128]{1,0:T(8,128)}, f32[8,128]{1,0:T(8,128)}) custom-call(bf16[4,64,1024]{2,1,0:T(8,128)(2,1)} %get-tuple-element.83.part_h, f32[64,384]{1,0:T(8,128)} %get-tuple-element.84.rest_h, bf16[4,64,1024]{2,1,0:T(8,128)(2,1)} %get-tuple-element.85.gate_h, ...), custom_call_target="tpu_custom_call" | custom-call | tf_op jit(solution)/shard_map/gradient_norm/pallas_call | solution.py:420
  389.0 1.3 fusion.9
  390.2 1.3 slice_multiply_fusion
  391.6 0.1 mul.95
  391.7 0.1 mul.97
  391.7 0.0 copy-done.8
  391.7 0.0 copy-done.9
  391.8 0.6 add_subtract_fusion
  392.4 0.0 copy-done.4
  392.4 0.0 copy-done.6
  392.4 0.0 copy-done.7
  392.4 2.0 multiply_subtract_fusion
  394.4 12.3 %update_weights.1 = (f32[256,2048]{1,0:T(8,128)}, bf16[4,256,2048]{2,1,0:T(8,128)(2,1)}, f32[64,8512]{1,0:T(8,128)}, f32[64,8512]{1,0:T(8,128)}, f32[64,8512]{1,...) custom-call(f32[8,128]{1,0:T(8,128)} %get-tuple-element.90.norm, ...), custom_call_target="tpu_custom_call" | custom-call | tf_op jit(solution)/shard_map/update_weights/pallas_call | solution.py:552
  (14 shorter events, 0.1 us)
Async XLA Ops:
  1.4 1.2 copy-start
  2.6 1.6 copy-start.1
  4.2 1.2 copy-start.2
  5.4 82.6 %copy-start.5 = (f32[3,64]{1,0:T(4,128)S(1)}, f32[3,64]{1,0:T(4,128)}, u32[]{:S(2)}) copy-start(f32[3,64]{1,0:T(4,128)} %param.25) | copy-start | bytes 2308
  86.1 0.8 copy-start.3
  369.9 21.8 %copy-start.8 = (f32[3,64]{1,0:T(4,128)S(1)}, f32[3,64]{1,0:T(4,128)}, u32[]{:S(2)}) copy-start(f32[3,64]{1,0:T(4,128)} %param.26) | copy-start | bytes 2308
  370.0 21.8 %copy-start.9 = (f32[3,64]{1,0:T(4,128)S(1)}, f32[3,64]{1,0:T(4,128)}, u32[]{:S(2)}) copy-start(f32[3,64]{1,0:T(4,128)} %param.27) | copy-start | bytes 2308
  370.0 22.4 %copy-start.4 = (f32[872]{0:T(1024)S(1)}, f32[872]{0:T(1024)}, u32[]{:S(2)}) copy-start(f32[872]{0:T(1024)} %param.22) | copy-start | bytes 10468
  370.0 22.4 %copy-start.6 = (f32[872]{0:T(1024)S(1)}, f32[872]{0:T(1024)}, u32[]{:S(2)}) copy-start(f32[872]{0:T(1024)} %param.23) | copy-start | bytes 10468
  370.0 22.4 %copy-start.7 = (f32[872]{0:T(1024)S(1)}, f32[872]{0:T(1024)}, u32[]{:S(2)}) copy-start(f32[872]{0:T(1024)} %param.24) | copy-start | bytes 10468
